TPU v7x, 32 devices: a whole 2x2x4 slice. The times are simulated.
32 devices in a mesh: dp: 8 (over z, x), tensor: 4 (over y, core).
Axes of the slice: x: 2, y: 2, z: 4, core: 2. Of those that a mesh axis runs over, the one named last changes fastest.
Arguments:
- tokens: bfloat16 [8192, 1536], P(('dp', 'tensor')), may hold values from -6 to 6
- segment: int32 [8192], P('dp'), may hold values from 0 to 8191, as said below
- gain_attn: float32 [1536], replicated, may hold values from 0.5 to 1.5
- w_query: bfloat16 [1536, 1536], P('dp', 'tensor'), may hold values from -0.15625 to 0.15625
- b_query: float32 [1536], P('tensor'), may hold values from -3 to 3
- w_key: bfloat16 [1536, 256], P(('dp', 'tensor')), may hold values from -0.15625 to 0.15625
- b_key: float32 [256], replicated, may hold values from -3 to 3
- w_value: bfloat16 [1536, 256], P(('dp', 'tensor')), may hold values from -0.15625 to 0.15625
- b_value: float32 [256], replicated, may hold values from -3 to 3
- w_out: bfloat16 [1536, 1536], P('tensor', 'dp'), may hold values from -0.625 to 0.625
- gain_ffn: float32 [1536], replicated, may hold values from 0.5 to 1.5
- w_gate: bfloat16 [1536, 8960], P('dp', 'tensor'), may hold values from -0.15625 to 0.15625
- w_up: bfloat16 [1536, 8960], P('dp', 'tensor'), may hold values from -0.15625 to 0.15625
- w_down: bfloat16 [8960, 1536], P('tensor', 'dp'), may hold values from -0.125 to 0.125
- grad_out: bfloat16 [8192, 1536], P(('dp', 'tensor')), may hold values from -6 to 6
Outputs:
- layer_out: bfloat16 [8192, 1536], P(('dp', 'tensor'))
- grad_tokens: float32 [8192, 1536], P(('dp', 'tensor'))
- grad_gain_attn: float32 [1536], P(('dp', 'tensor'))
- grad_w_query: float32 [1536, 1536], P('dp', 'tensor')
- grad_b_query: float32 [1536], P(('dp', 'tensor'))
- grad_w_key: float32 [1536, 256], P(('dp', 'tensor'))
- grad_b_key: float32 [256], P(('dp', 'tensor'))
- grad_w_value: float32 [1536, 256], P(('dp', 'tensor'))
- grad_b_value: float32 [256], P(('dp', 'tensor'))
- grad_w_out: float32 [1536, 1536], P('tensor', 'dp')
- grad_gain_ffn: float32 [1536], P(('dp', 'tensor'))
- grad_w_gate: float32 [1536, 8960], P('dp', 'tensor')
- grad_w_up: float32 [1536, 8960], P('dp', 'tensor')
- grad_w_down: float32 [8960, 1536], P('tensor', 'dp')
Inputs may be any that keep to these rules, and one draw needn't show every extreme that they name: `segment`: document numbers never fall, and no document crosses an aligned block of 1024 rows.
All inputs are finite; a program needn't handle non-finite values.
Results may differ from a plain program's by a relative error of at most 0.025.
Values may be sent and summed in bfloat16 or wider, within the bound.
No kernel may reach another device: no remote copies, remote signals or barrier semaphores. Data moves between devices by JAX's collectives and lax.ppermute only.
A program may use at most 320 MiB of HBM per device.

v0:
```python
import jax
import jax.numpy as jnp
from jax import lax
from jax.sharding import PartitionSpec as P

HEADS = 12
KV_HEADS = 2
HD = 128


eps_norm = 1e-06
rope_base = 1000000.0
masked = -1e30


def from_partner(block, axis, apart):
    count = lax.axis_size(axis)
    route = []
    for low in range(count):
        high = low | 1 << apart
        if high != low and high < count:
            route += [(low, high), (high, low)]
    return lax.ppermute(block, axis, route)


def positions_of(segment):
    row_index = jnp.arange(segment.shape[0], dtype=jnp.int32)
    before = jnp.concatenate([segment[:1] - 1, segment[:-1]])
    starts = jnp.where(segment != before, row_index, 0)
    return row_index - lax.cummax(starts, axis=0)


def angles_of(segment, head_width):
    position = positions_of(segment).astype(jnp.float32)
    freqs = rope_base ** (-(jnp.arange(head_width // 2, dtype=jnp.float32) * 2.0) / head_width)
    angle = position[:, None] * freqs[None, :]
    angle = jnp.concatenate([angle, angle], axis=1)
    return (jnp.cos(angle), jnp.sin(angle))


def rotate(values, cosine, sine):
    half = values.shape[-1] // 2
    turned = jnp.concatenate([-values[..., half:], values[..., :half]], axis=-1)
    return values * cosine + turned * sine


def rotate_back(grads, cosine, sine):
    half = grads.shape[-1] // 2
    turned = grads * sine
    return grads * cosine + jnp.concatenate([turned[..., half:], -turned[..., :half]], axis=-1)


def norm_scale(values):
    return lax.rsqrt(jnp.mean(values * values, axis=1, keepdims=True) + eps_norm)


def norm_back(values, scale, gain, grad_normed):
    weighted = grad_normed * gain
    grad_values = scale * weighted - values * scale**3 * jnp.mean(
        values * weighted, axis=1, keepdims=True
    )
    grad_gain = jnp.sum(grad_normed * values * scale, axis=0)
    return (grad_values, grad_gain)


def product(operand, weight_mat):
    return jnp.dot(operand, weight_mat, preferred_element_type=jnp.float32)


def product_tail(operand, weight_mat):
    return lax.dot_general(
        operand, weight_mat, (((1,), (1,)), ((), ())), preferred_element_type=jnp.float32
    )


def product_head(operand, weight_mat):
    return lax.dot_general(
        operand, weight_mat, (((0,), (0,)), ((), ())), preferred_element_type=jnp.float32
    )


def spread_rows(values):
    return lax.all_gather(values, "tensor", axis=0, tiled=True)


def collect_rows(values):
    return lax.psum_scatter(
        values.astype(jnp.bfloat16), "tensor", scatter_dimension=0, tiled=True
    ).astype(jnp.float32)


def on_device(
    tokens,
    segment,
    gain_attn,
    w_query,
    b_query,
    w_key,
    b_key,
    w_value,
    b_value,
    w_out,
    gain_ffn,
    w_gate,
    w_up,
    w_down,
    grad_out,
):
    width = tokens.shape[1]
    tensor_count = lax.axis_size("tensor")
    tensor_rank = lax.axis_index("tensor")
    kv_head = tensor_rank // (tensor_count // KV_HEADS)
    length = segment.shape[0]
    heads_here = w_query.shape[1] // HD
    query_cols = heads_here * HD
    ffn_cols = w_gate.shape[1]
    factor = HD ** (-0.5)
    block_rows = min(512, length)
    cosine, sine = angles_of(segment, HD)
    row_index = jnp.arange(length, dtype=jnp.int32)
    query_full, out_full = (
        lax.all_gather(w_query, "dp", axis=0, tiled=True),
        lax.all_gather(w_out, "dp", axis=1, tiled=True),
    )
    key_full, value_full = (
        lax.all_gather(w_key, ("dp", "tensor"), axis=0, tiled=True),
        lax.all_gather(w_value, ("dp", "tensor"), axis=0, tiled=True),
    )
    key_head = lax.dynamic_slice_in_dim(key_full, kv_head * HD, HD, 1)
    value_head = lax.dynamic_slice_in_dim(value_full, kv_head * HD, HD, 1)
    key_bias = lax.dynamic_slice_in_dim(b_key, kv_head * HD, HD, 0)
    value_bias = lax.dynamic_slice_in_dim(b_value, kv_head * HD, HD, 0)
    x_rows = tokens.astype(jnp.float32)
    scale_one = norm_scale(x_rows)
    normed_one = (x_rows * scale_one * gain_attn).astype(jnp.bfloat16)
    rows_one = spread_rows(normed_one)
    query_lin = (product(rows_one, query_full) + b_query).reshape(length, heads_here, HD)
    key_lin = product(rows_one, key_head) + key_bias
    value_low = (product(rows_one, value_head) + value_bias).astype(jnp.bfloat16)
    query_rot = rotate(query_lin, cosine[:, None, :], sine[:, None, :]).astype(jnp.bfloat16)
    key_rot = rotate(key_lin, cosine, sine).astype(jnp.bfloat16)

    def block_scores(first_row, last_row):
        allowed = (segment[first_row:last_row, None] == segment[None, :last_row]) & (
            row_index[first_row:last_row, None] >= row_index[None, :last_row]
        )
        scores = (
            jnp.einsum(
                "qhd,kd->hqk",
                query_rot[first_row:last_row],
                key_rot[:last_row],
                preferred_element_type=jnp.float32,
            )
            * factor
        )
        return jnp.where(allowed[None], scores, masked)

    outputs = []
    totals = []
    for first_row in range(0, length, block_rows):
        last_row = first_row + block_rows
        scores = block_scores(first_row, last_row)
        row_max = jnp.max(scores, axis=2, keepdims=True)
        weights = jnp.exp(scores - row_max)
        row_total = jnp.sum(weights, axis=2, keepdims=True)
        weights_low = (weights / row_total).astype(jnp.bfloat16)
        outputs.append(
            jnp.einsum(
                "hqk,kd->qhd", weights_low, value_low[:last_row], preferred_element_type=jnp.float32
            )
        )
        totals.append(row_max + jnp.log(row_total))
    heads_low = jnp.concatenate(outputs, axis=0).reshape(length, query_cols).astype(jnp.bfloat16)
    log_totals = jnp.concatenate(totals, axis=1)
    mid_rows = x_rows + collect_rows(product(heads_low, out_full))
    scale_two = norm_scale(mid_rows)
    normed_two = (mid_rows * scale_two * gain_ffn).astype(jnp.bfloat16)
    rows_two = spread_rows(normed_two)
    gate_full, up_full, down_full = (
        lax.all_gather(w_gate, "dp", axis=0, tiled=True),
        lax.all_gather(w_up, "dp", axis=0, tiled=True),
        lax.all_gather(w_down, "dp", axis=1, tiled=True),
    )
    gate = product(rows_two, gate_full)
    upward = product(rows_two, up_full)
    sigma = jax.nn.sigmoid(gate)
    active = gate * sigma
    hidden = (active * upward).astype(jnp.bfloat16)
    ffn_rows = collect_rows(product(hidden, down_full))
    layer_out = (mid_rows + ffn_rows).astype(jnp.bfloat16)
    grad_rows = grad_out.astype(jnp.float32)
    grad_ffn = spread_rows(grad_out)
    grad_hidden = product_tail(grad_ffn, down_full)
    grad_gate = (grad_hidden * upward * sigma * (1.0 + gate * (1.0 - sigma))).astype(jnp.bfloat16)
    grad_up = (grad_hidden * active).astype(jnp.bfloat16)
    grad_two = collect_rows(product_tail(grad_gate, gate_full) + product_tail(grad_up, up_full))
    grad_norm_two, gain_two_part = norm_back(mid_rows, scale_two, gain_ffn, grad_two)
    grad_mid = grad_rows + grad_norm_two
    grad_attn = spread_rows(grad_mid.astype(jnp.bfloat16))
    grad_heads = (
        product_tail(grad_attn, out_full).astype(jnp.bfloat16).reshape(length, heads_here, HD)
    )
    query_parts = []
    grad_key = jnp.zeros((length, HD), jnp.float32)
    grad_value = jnp.zeros((length, HD), jnp.float32)
    for first_row in range(0, length, block_rows):
        last_row = first_row + block_rows
        scores = block_scores(first_row, last_row)
        weights = jnp.exp(scores - log_totals[:, first_row:last_row])
        weights_low = weights.astype(jnp.bfloat16)
        grad_part = grad_heads[first_row:last_row]
        grad_weights = jnp.einsum(
            "qhd,kd->hqk", grad_part, value_low[:last_row], preferred_element_type=jnp.float32
        )
        inner = jnp.sum(weights * grad_weights, axis=2, keepdims=True)
        grad_scores = (weights * (grad_weights - inner)).astype(jnp.bfloat16)
        query_parts.append(
            jnp.einsum(
                "hqk,kd->qhd", grad_scores, key_rot[:last_row], preferred_element_type=jnp.float32
            )
            * factor
        )
        grad_key = grad_key.at[:last_row].add(
            jnp.einsum(
                "hqk,qhd->kd",
                grad_scores,
                query_rot[first_row:last_row],
                preferred_element_type=jnp.float32,
            )
            * factor
        )
        grad_value = grad_value.at[:last_row].add(
            jnp.einsum("hqk,qhd->kd", weights_low, grad_part, preferred_element_type=jnp.float32)
        )
    partial_pair = jnp.stack([grad_key, grad_value])
    full_pair = partial_pair + from_partner(partial_pair.astype(jnp.bfloat16), "tensor", 0).astype(
        partial_pair.dtype
    )
    grad_query_rot = jnp.concatenate(query_parts, axis=0)
    grad_query = (
        rotate_back(grad_query_rot, cosine[:, None, :], sine[:, None, :])
        .reshape(length, query_cols)
        .astype(jnp.bfloat16)
    )
    grad_key_low = rotate_back(full_pair[0], cosine, sine).astype(jnp.bfloat16)
    grad_value_low = full_pair[1].astype(jnp.bfloat16)
    grad_one = collect_rows(
        product_tail(grad_query, query_full)
        + 0.5 * (product_tail(grad_key_low, key_head) + product_tail(grad_value_low, value_head))
    )
    grad_norm_one, gain_one_part = norm_back(x_rows, scale_one, gain_attn, grad_one)
    grad_tokens = grad_mid + grad_norm_one
    joint_sums = lax.psum_scatter(
        jnp.concatenate(
            [
                jnp.concatenate(
                    [product_head(rows_one, grad_query), product_head(grad_attn, heads_low)], axis=1
                ),
                jnp.concatenate(
                    [
                        product_head(rows_two, grad_gate),
                        product_head(rows_two, grad_up),
                        product_head(grad_ffn, hidden),
                    ],
                    axis=1,
                ),
            ],
            axis=1,
        ).astype(jnp.bfloat16),
        "dp",
        scatter_dimension=0,
        tiled=True,
    ).astype(jnp.float32)
    attn_sums = joint_sums[:, : 2 * query_cols]
    ffn_sums = joint_sums[:, 2 * query_cols :]
    bias_query = lax.dynamic_update_slice_in_dim(
        jnp.zeros((HEADS * HD,), jnp.float32),
        jnp.sum(grad_query, axis=0, dtype=jnp.float32),
        tensor_rank * query_cols,
        0,
    )
    bias_key = lax.dynamic_update_slice_in_dim(
        jnp.zeros((KV_HEADS * HD,), jnp.float32),
        0.5 * jnp.sum(grad_key_low, axis=0, dtype=jnp.float32),
        kv_head * HD,
        0,
    )
    bias_value = lax.dynamic_update_slice_in_dim(
        jnp.zeros((KV_HEADS * HD,), jnp.float32),
        0.5 * jnp.sum(grad_value_low, axis=0, dtype=jnp.float32),
        kv_head * HD,
        0,
    )
    weight_key = lax.dynamic_update_slice_in_dim(
        jnp.zeros((width, KV_HEADS * HD), jnp.float32),
        0.5 * product_head(rows_one, grad_key_low),
        kv_head * HD,
        1,
    )
    weight_value = lax.dynamic_update_slice_in_dim(
        jnp.zeros((width, KV_HEADS * HD), jnp.float32),
        0.5 * product_head(rows_one, grad_value_low),
        kv_head * HD,
        1,
    )
    small_sums = (
        lax.psum_scatter(weight_key, ("dp", "tensor"), scatter_dimension=0, tiled=True),
        lax.psum_scatter(weight_value, ("dp", "tensor"), scatter_dimension=0, tiled=True),
        lax.psum_scatter(bias_query, ("dp", "tensor"), scatter_dimension=0, tiled=True),
        lax.psum_scatter(bias_key, ("dp", "tensor"), scatter_dimension=0, tiled=True),
        lax.psum_scatter(bias_value, ("dp", "tensor"), scatter_dimension=0, tiled=True),
        lax.psum_scatter(gain_one_part, ("dp", "tensor"), scatter_dimension=0, tiled=True),
        lax.psum_scatter(gain_two_part, ("dp", "tensor"), scatter_dimension=0, tiled=True),
    )
    grad_w_query = attn_sums[:, :query_cols]
    grad_w_out = attn_sums[:, query_cols:].T
    grad_w_gate = ffn_sums[:, :ffn_cols]
    grad_w_up = ffn_sums[:, ffn_cols : 2 * ffn_cols]
    grad_w_down = ffn_sums[:, 2 * ffn_cols :].T
    return (
        layer_out,
        grad_tokens,
        small_sums[5],
        grad_w_query,
        small_sums[2],
        small_sums[0],
        small_sums[3],
        small_sums[1],
        small_sums[4],
        grad_w_out,
        small_sums[6],
        grad_w_gate,
        grad_w_up,
        grad_w_down,
    )


def solution(mesh):
    return jax.shard_map(
        on_device,
        mesh=mesh,
        in_specs=(
            P(("dp", "tensor"), None),
            P("dp"),
            P(),
            P("dp", "tensor"),
            P("tensor"),
            P(("dp", "tensor"), None),
            P(),
            P(("dp", "tensor"), None),
            P(),
            P("tensor", "dp"),
            P(),
            P("dp", "tensor"),
            P("dp", "tensor"),
            P("tensor", "dp"),
            P(("dp", "tensor"), None),
        ),
        out_specs=(
            P(("dp", "tensor"), None),
            P(("dp", "tensor"), None),
            P(("dp", "tensor")),
            P("dp", "tensor"),
            P(("dp", "tensor")),
            P(("dp", "tensor"), None),
            P(("dp", "tensor")),
            P(("dp", "tensor"), None),
            P(("dp", "tensor")),
            P("tensor", "dp"),
            P(("dp", "tensor")),
            P("dp", "tensor"),
            P("dp", "tensor"),
            P("tensor", "dp"),
        ),
        check_vma=False,
    )
```

profile of v0, /device:TPU:0, one launch (start us, length us, event | category | flops | bytes accessed | tf_op | source)
XLA Modules:
  0.0 1387.8 jit_solution(9779161032657018858)
XLA Ops:
  10.6 2.3 fusion.38
  14.2 49.0 %all_gather.35 = bf16[1536,256]{1,0:T(8,128)(2,1)} all-gather(bf16[48,256]{1,0:T(8,128)(2,1)S(1)} %copy-done.41), channel_id=1, replica_groups=mesh['dp'=8,'tensor'=4] {'dp','tensor'}, dimensions={0}, use_global_device_ids=true | all-gather | bytes 811008 | tf_op jit(solution)/shard_map/all_gather | solution.py:126
  64.5 41.9 %all_gather.34 = bf16[1536,256]{1,0:T(8,128)(2,1)} all-gather(bf16[48,256]{1,0:T(8,128)(2,1)S(1)} %copy-done.42), channel_id=1, replica_groups=mesh['dp'=8,'tensor'=4] {'dp','tensor'}, dimensions={0}, use_global_device_ids=true | all-gather | bytes 811008 | tf_op jit(solution)/shard_map/all_gather | solution.py:127
  109.0 3.6 convolution_add_fusion
  117.0 3.0 fusion.77
  120.0 2.0 copy.93
  122.0 2.0 copy.89
  124.1 2.2 fusion.44
  128.6 3.4 copy-done.3
  137.5 5.0 convolution_convert_fusion.4
  143.2 35.0 %reduce-scatter.10.cloned.1.call-done = bf16[256,1536]{1,0:T(8,128)(2,1)} async-done(((bf16[1024,1536]{1,0:T(8,128)(2,1)}), bf16[256,1536]{1,0:T(8,128)(2,1)}) %reduce-scatter.10.cloned.1.call-update) | async-done | bytes 786448 | tf_op jit(solution)/shard_map/reduce_scatter | solution.py:87
  179.8 2.5 multiply_convert_fusion.3
  184.7 104.5 %all-gather.18.cloned.1.call-done = bf16[1536,2240]{1,0:T(8,128)(2,1)} async-done(((bf16[192,2240]{1,0:T(8,128)(2,1)}), bf16[1536,2240]{1,0:T(8,128)(2,1)}) %all-gather.18.cloned.1.call-update) | async-done | bytes 6881296 | tf_op jit(solution)/shard_map/all_gather | solution.py:180
  289.2 28.8 %all-gather.16.cloned.1.call-done = bf16[1024,1536]{1,0:T(8,128)(2,1)} async-done(((bf16[256,1536]{1,0:T(8,128)(2,1)}), bf16[1024,1536]{1,0:T(8,128)(2,1)}) %all-gather.16.cloned.1.call-update) | async-done | bytes 3145744 | tf_op jit(solution)/shard_map/all_gather | solution.py:83
  318.0 13.8 fusion.112
  331.8 97.4 %all-gather.20.cloned.1.call-done = bf16[1536,2240]{1,0:T(8,128)(2,1)} async-done(((bf16[192,2240]{1,0:T(8,128)(2,1)}), bf16[1536,2240]{1,0:T(8,128)(2,1)}) %all-gather.20.cloned.1.call-update) | async-done | bytes 6881296 | tf_op jit(solution)/shard_map/all_gather | solution.py:181
  429.3 13.2 fusion.113
  442.5 15.2 %all-gather.24.cloned.1.call-done = bf16[1024,1536]{1,0:T(8,128)(2,1)} async-done(((bf16[256,1536]{1,0:T(8,128)(2,1)}), bf16[1024,1536]{1,0:T(8,128)(2,1)}) %all-gather.24.cloned.1.call-update) | async-done | bytes 3145744 | tf_op jit(solution)/shard_map/all_gather | solution.py:83
  457.7 111.3 %all-gather.22.cloned.1.call-done = bf16[2240,1536]{0,1:T(8,128)(2,1)} async-done(((bf16[2240,192]{0,1:T(8,128)(2,1)}), bf16[2240,1536]{0,1:T(8,128)(2,1)}) %all-gather.22.cloned.1.call-update) | async-done | bytes 6881296 | tf_op jit(solution)/shard_map/all_gather | solution.py:182
  568.9 20.2 %multiply_convert_fusion = (bf16[1024,2240]{0,1:T(8,128)(2,1)}, bf16[1024,2240]{0,1:T(8,128)(2,1)}, bf16[1024,2240]{0,1:T(8,128)(2,1)}) fusion(f32[1024,2240]{0,1:T(8,128)} %fusion.112, f32[1024,2240]{0,1:T(8,128)} %fusion.113, bf16[1024,1536]{1,0:T(8,128)(2,1)} %all-gather.24.cloned.1.call-done, bf16[2240,1536]{0,1:T(8,128)(2,1)} %all-gather.22.cloned.1.call-done), kind=kOutput, calls=%fused_computation.7 | convolution fusion | flops 7080837120 | bytes 42139648 | tf_op jit(solution)/shard_map/dot_general | solution.py:71
  589.1 11.4 fusion.114
  600.5 9.2 add_convert_fusion.1
  609.8 36.2 %reduce-scatter.14.cloned.1.call-done = bf16[256,1536]{1,0:T(8,128)(2,1)} async-done(((bf16[1024,1536]{1,0:T(8,128)(2,1)}), bf16[256,1536]{1,0:T(8,128)(2,1)}) %reduce-scatter.14.cloned.1.call-update) | async-done | bytes 786448 | tf_op jit(solution)/shard_map/reduce_scatter | solution.py:87
  646.0 2.2 fusion.33
  648.2 3.3 fusion.103
  652.0 28.2 %all-gather.26.cloned.1.call-done = bf16[1024,1536]{1,0:T(8,128)(2,1)} async-done(((bf16[256,1536]{1,0:T(8,128)(2,1)}), bf16[1024,1536]{1,0:T(8,128)(2,1)}) %all-gather.26.cloned.1.call-update) | async-done | bytes 3145744 | tf_op jit(solution)/shard_map/all_gather | solution.py:83
  680.2 3.7 convolution_convert_fusion.7
  712.7 2.8 add_convert_fusion
  715.5 12.4 convolution_convert_fusion.3
  729.9 3.7 fusion.18
  733.6 2.5 fusion.17
  736.1 11.6 fusion.1
  747.7 9.3 fusion
  757.0 9.3 fusion.3
  766.3 29.4 %copy.143 = bf16[1536,7488]{1,0:T(8,128)(2,1)} copy(bf16[1536,7488]{0,1:T(8,128)(2,1)} %fusion.3) | data formatting | bytes 46006272
  797.1 1.9 fusion.21
  801.0 4.0 fusion.20
  805.1 2.0 fusion.42
  807.2 3.9 fusion.28
  811.1 44.1 %all-reduce.7 = (f32[1536]{0:T(1024)S(1)}, f32[1536]{0:T(1024)S(1)}, f32[256]{0:T(256)S(1)}, f32[256]{0:T(256)S(1)}, f32[1536]{0:T(1024)S(1)}) all-reduce(f32[1536]{0:T(1024)S(1)} %get-tuple-element.122, f32[1536]{0:T(1024)S(1)} %bitcast_dynamic-update-slice_fusion, ...), channel_id=6, replica_groups=mesh['dp'=8,'tensor'=4] {'dp','tensor'}, use_global_device_ids=true, to_apply=%region_17.18.clone | all-reduce | flops 5120 | bytes 40960
  858.2 317.5 %reduce-scatter.22.cloned.1.call-done = bf16[192,7488]{1,0:T(8,128)(2,1)} async-done(((bf16[1536,7488]{1,0:T(8,128)(2,1)}), bf16[192,7488]{1,0:T(8,128)(2,1)}) %reduce-scatter.22.cloned.1.call-update) | async-done | bytes 2875408
  1175.6 5.6 copy.144
  1182.2 5.7 convert_element_type.159
  1190.7 3.4 fusion.105
  1194.1 2.9 copy.118
  1200.7 1.9 copy.120
  1202.7 75.7 %reduce-scatter.18.cloned.1.call-done = f32[48,256]{1,0:T(8,128)} async-done(((f32[1536,256]{1,0:T(8,128)}), f32[48,256]{1,0:T(8,128)}) %reduce-scatter.18.cloned.1.call-update) | async-done | bytes 49168 | tf_op jit(solution)/shard_map/reduce_scatter | solution.py:307
  1278.4 102.6 %reduce-scatter.20.cloned.1.call-done = f32[48,256]{1,0:T(8,128)} async-done(((f32[1536,256]{1,0:T(8,128)}), f32[48,256]{1,0:T(8,128)}) %reduce-scatter.20.cloned.1.call-update) | async-done | bytes 49168 | tf_op jit(solution)/shard_map/reduce_scatter | solution.py:308
  (243 shorter events, 69.0 us)
Async XLA Ops:
  7.2 6.5 copy-start.40
  7.2 7.0 copy-start.41
  7.2 57.3 %copy-start.42 = (bf16[48,256]{1,0:T(8,128)(2,1)S(1)}, bf16[48,256]{1,0:T(8,128)(2,1)}, u32[]{:S(2)}) copy-start(bf16[48,256]{1,0:T(8,128)(2,1)} %param.34) | copy-start | bytes 73732
  7.2 99.3 %copy-start.51 = (f32[256]{0:T(256)S(1)}, f32[256]{0:T(256)}, u32[]{:S(2)}) copy-start(f32[256]{0:T(256)} %param.33) | copy-start | bytes 3076
  7.2 99.3 %copy-start.52 = (f32[256]{0:T(256)S(1)}, f32[256]{0:T(256)}, u32[]{:S(2)}) copy-start(f32[256]{0:T(256)} %param.35) | copy-start | bytes 3076
  7.2 101.8 %all-gather.12.cloned.1.call-start = ((), (), s32[]{:S(2)}) async-start(), calls=%async_computation.8 | async-start | bytes 1327104 | tf_op jit(solution)/shard_map/all_gather | solution.py:122
  7.3 101.7 %copy-start.50 = (f32[384]{0:T(512)S(1)}, f32[384]{0:T(512)}, u32[]{:S(2)}) copy-start(f32[384]{0:T(512)} %param.31) | copy-start | bytes 4612
  8.0 101.0 %all-gather.10.cloned.1.call-start = ((), (), s32[]{:S(2)}) async-start(), calls=%async_computation.7 | async-start | bytes 3932160 | tf_op jit(solution)/shard_map/all_gather | solution.py:83
  12.9 124.6 %all-gather.14.cloned.1.call-start = ((), (), s32[]{:S(2)}) async-start(), calls=%async_computation.9 | async-start | bytes 1327104 | tf_op jit(solution)/shard_map/all_gather | solution.py:123
  13.6 164.5 %reduce-scatter.10.cloned.1.call-start = ((), (), s32[]{:S(2)}) async-start(), calls=%async_computation.10 | async-start | bytes 3932160 | tf_op jit(solution)/shard_map/reduce_scatter | solution.py:87
  113.1 2.6 copy-start.21
  127.8 7.4 copy-start
  127.8 4.2 copy-start.3
  127.8 4.3 copy-start.26
  142.5 37.3 %copy-start.38 = (f32[1536]{0:T(1024)S(1)}, f32[1536]{0:T(1024)}, u32[]{:S(2)}) copy-start(f32[1536]{0:T(1024)} %param.37) | copy-start | bytes 18436
  142.5 146.7 %all-gather.18.cloned.1.call-start = ((), (), s32[]{:S(2)}) async-start(), calls=%async_computation.12 | async-start | bytes 7962624 | tf_op jit(solution)/shard_map/all_gather | solution.py:180
  143.1 174.9 %all-gather.16.cloned.1.call-start = ((), (), s32[]{:S(2)}) async-start(), calls=%async_computation.11 | async-start | bytes 3932160 | tf_op jit(solution)/shard_map/all_gather | solution.py:83
  182.4 246.9 %all-gather.20.cloned.1.call-start = ((), (), s32[]{:S(2)}) async-start(), calls=%async_computation.13 | async-start | bytes 7962624 | tf_op jit(solution)/shard_map/all_gather | solution.py:181
  183.2 274.5 %all-gather.24.cloned.1.call-start = ((), (), s32[]{:S(2)}) async-start(), calls=%async_computation.16 | async-start | bytes 3932160 | tf_op jit(solution)/shard_map/all_gather | solution.py:83
  183.9 385.0 %all-gather.22.cloned.1.call-start = ((), (), s32[]{:S(2)}) async-start(), calls=%async_computation.14 | async-start | bytes 7962624 | tf_op jit(solution)/shard_map/all_gather | solution.py:182
  184.6 461.4 %reduce-scatter.14.cloned.1.call-start = ((), (), s32[]{:S(2)}) async-start(), calls=%async_computation.17 | async-start | bytes 3932160 | tf_op jit(solution)/shard_map/reduce_scatter | solution.py:87
  589.1 11.4 copy-start.46
  589.1 11.4 copy-start.53
  609.7 70.5 %all-gather.26.cloned.1.call-start = ((), (), s32[]{:S(2)}) async-start(), calls=%async_computation.18 | async-start | bytes 3932160 | tf_op jit(solution)/shard_map/all_gather | solution.py:83
  651.5 153.5 %reduce-scatter.16.cloned.1.call-start = ((), (), s32[]{:S(2)}) async-start(), calls=%async_computation.19 | async-start | bytes 3932160 | tf_op jit(solution)/shard_map/reduce_scatter | solution.py:87
  680.2 3.8 copy-start.35
  684.0 4.6 copy-start.17
  686.1 3.2 slice-start.1
  698.1 7.6 collective-permute-start
  705.7 5.9 copy-start.22
  707.0 5.5 copy-start.6
  715.5 91.6 %reduce-scatter.12.cloned.1.call-start = ((), (), s32[]{:S(2)}) async-start(), calls=%async_computation.15 | async-start | bytes 3932160 | tf_op jit(solution)/shard_map/reduce_scatter | solution.py:87
  728.0 447.6 %reduce-scatter.22.cloned.1.call-start = ((), (), s32[]{:S(2)}) async-start(), calls=%async_computation.22 | async-start | bytes 26099712
  729.9 3.7 copy-start.33
  729.9 3.7 copy-start.49
  733.6 14.1 %slice-start.2 = ((s8[4587520]{0:T(1024)(128)(4,1)}), s8[4194304]{0:T(1024)(128)(4,1)S(1)}, s32[]{:S(2)}) async-start(s8[4587520]{0:T(1024)(128)(4,1)} %bitcast.181), calls=%async_computation.25 | async-start | bytes 8388608
  736.1 11.6 slice-start.3
  736.1 20.9 %slice-start.4 = ((s8[4587520]{0:T(1024)(128)(4,1)}), s8[4194304]{0:T(1024)(128)(4,1)S(1)}, s32[]{:S(2)}) async-start(s8[4587520]{0:T(1024)(128)(4,1)} %bitcast.183), calls=%async_computation.27 | async-start | bytes 8388608
  747.7 9.3 copy-start.48
  747.7 9.3 slice-start.5
  795.8 482.6 %reduce-scatter.18.cloned.1.call-start = ((), (), s32[]{:S(2)}) async-start(), calls=%async_computation.20 | async-start | bytes 1622016 | tf_op jit(solution)/shard_map/reduce_scatter | solution.py:307
  799.0 582.0 %reduce-scatter.20.cloned.1.call-start = ((), (), s32[]{:S(2)}) async-start(), calls=%async_computation.21 | async-start | bytes 1622016 | tf_op jit(solution)/shard_map/reduce_scatter | solution.py:308
  801.0 4.1 copy-start.1
  801.0 4.1 copy-start.39
  801.0 4.1 copy-start.44
  801.0 6.2 copy-start.5
  801.0 6.2 copy-start.8
  801.0 6.2 copy-start.45
  (29 other events, 49.7 us)
Sparse Core Ops, SparseCore 0:
  10.2 44.9 all-gather.11
  57.4 31.2 all-gather.9
  90.9 40.7 all-gather.13
  142.6 35.4 reduce-scatter.9
  180.4 108.7 all-gather.17
  291.3 26.7 all-gather.15
  320.5 108.7 all-gather.19
  430.9 26.7 all-gather.23
  460.1 108.7 all-gather.21
  609.8 36.1 reduce-scatter.13
  651.7 28.5 all-gather.25
  715.6 37.9 reduce-scatter.15
  756.3 37.9 reduce-scatter.11
  798.0 377.5 reduce-scatter.21
  1182.2 96.2 reduce-scatter.17
  1284.9 96.0 reduce-scatter.19
where the time goes:
time: 1390 us
  waiting for transfers between devices  957 us (69%)
  matrix products  155 us (11%)
  blocking collectives  135 us (10%)
  local copies, waits for them, and re-layouts  73.9 us (5%)
  other arithmetic  49.9 us (4%)
  between operations  15.8 us (1%)
    unnamed x17, waiting for transfers between devices  322 us
    all_gather x1, waiting for transfers between devices, on_device(): lax.all_gather(w_down, 'dp', axis=1, tiled=True)  111 us
    all_gather x1, waiting for transfers between devices, on_device(): lax.all_gather(w_gate, 'dp', axis=0, tiled=True)  105 us
    reduce_scatter x1, waiting for transfers between devices, on_device(): lax.psum_scatter(weight_value, ('dp', 'tensor'), scatter_dimension=0, til...  103 us
    all_gather x1, waiting for transfers between devices, on_device(): lax.all_gather(w_up, 'dp', axis=0, tiled=True)  97.4 us
    reduce_scatter x1, waiting for transfers between devices, on_device(): lax.psum_scatter(weight_key, ('dp', 'tensor'), scatter_dimension=0, tiled...  75.7 us
    all_gather x4, waiting for transfers between devices, spread_rows(): return lax.all_gather(values, 'tensor', axis=0, tiled=True)  72.2 us
    reduce_scatter x4, waiting for transfers between devices, collect_rows(): lax.psum_scatter(values.astype(jnp.bfloat16), 'tensor', scatter_dimension...  71.2 us
  transfers between devices with their start and end apart: 17, of which 11 were waited for; matrix products, arithmetic and copies ran while one was open for 14% of the time, Pallas kernels for 0%

commit v1 on v0

v1 whole, which is shorter than its diff:
```python
import jax
import jax.numpy as jnp
from jax import lax
from jax.experimental import pallas as pl
from jax.experimental.pallas import tpu as pltpu
from jax.sharding import PartitionSpec as P

HEADS = 12
KV_HEADS = 2
HD = 128


eps_norm = 1e-06
rope_base = 1000000.0
masked = -1e30
low = jnp.bfloat16
wide = jnp.float32


def positions_of(segment):
    row_index = jnp.arange(segment.shape[0], dtype=jnp.int32)
    before = jnp.concatenate([segment[:1] - 1, segment[:-1]])
    starts = jnp.where(segment != before, row_index, 0)
    return row_index - lax.cummax(starts, axis=0)


def angles_of(segment, head_width):
    position = positions_of(segment).astype(jnp.float32)
    freqs = rope_base ** (-(jnp.arange(head_width // 2, dtype=jnp.float32) * 2.0) / head_width)
    angle = position[:, None] * freqs[None, :]
    angle = jnp.concatenate([angle, angle], axis=1)
    return (jnp.cos(angle), jnp.sin(angle))


def dot_nn(left, right):
    return jnp.dot(left, right, preferred_element_type=wide)


def dot_nt(left, right):
    return lax.dot_general(left, right, (((1,), (1,)), ((), ())), preferred_element_type=wide)


def dot_tn(left, right):
    return lax.dot_general(left, right, (((0,), (0,)), ((), ())), preferred_element_type=wide)


def moved(block, axis, target):
    route = [(index, target(index)) for index in range(lax.axis_size(axis))]
    return lax.ppermute(block, axis, route)


def across_x(block):
    return moved(block, "dp", lambda index: index ^ 1)


def across_y(block):
    return moved(block, "tensor", lambda index: index ^ 2)


def across_core(block):
    return moved(block, "tensor", lambda index: index ^ 1)


def across_both(block):
    return moved(block, "tensor", lambda index: index ^ 3)


def up_line(block):
    count = lax.axis_size("dp")
    return moved(block, "dp", lambda index: (index + 2) % count)


def in_order(first, second, rank, axis):
    return jnp.where(
        rank == 0, jnp.stack([first, second], axis), jnp.stack([second, first], axis)
    )


def pick(values, rank, axis):
    return lax.dynamic_index_in_dim(values, rank, axis, keepdims=False)


def after(value, *others):
    return lax.optimization_barrier((value, *others))[0]


def all_sum(vector):
    total = vector
    for axis in ("tensor", "dp"):
        for bit in range(lax.axis_size(axis).bit_length() - 1):
            total = total + moved(total, axis, lambda index: index ^ (1 << bit))
    return total


def cuts_of(columns):
    pieces = [(first, 256) for first in range(0, columns // 512 * 512, 512)]
    if columns % 512:
        pieces.append((columns // 512 * 512, columns % 512 // 2))
    cuts = [pieces[:-3], pieces[-3:-2], pieces[-2:]]
    return [cut for cut in cuts if cut]


def size_of(cut):
    return -(-sum(size for _, size in cut) // 128) * 128


anywhere = pl.BlockSpec(memory_space=pl.ANY)
in_vmem = pl.BlockSpec(memory_space=pltpu.VMEM)
in_smem = pl.BlockSpec(memory_space=pltpu.SMEM)


def shaped(shape, kind=low):
    return jax.ShapeDtypeStruct(tuple(shape), kind)


def call(kernel, args, specs, outs, scratch=(), tokens=(), out_specs=None, room=16):
    tokens = list(tokens)

    def body(*refs):
        kernel(*refs[: len(args)], *refs[len(args) + len(tokens) :])

    return pl.pallas_call(
        body,
        out_shape=outs,
        in_specs=list(specs) + [anywhere] * len(tokens),
        out_specs=[in_vmem] * len(outs) if out_specs is None else out_specs,
        scratch_shapes=list(scratch),
        compiler_params=pltpu.CompilerParams(vmem_limit_bytes=room * 2**20),
        cost_estimate=pl.CostEstimate(flops=1, bytes_accessed=1, transcendentals=0),
    )(*args, *tokens)


def start_rows(sources, target, offsets, sems):
    copies = []
    for index, (source, offset) in enumerate(zip(sources, offsets)):
        size = source.shape[0]
        place = pl.ds(pl.multiple_of(offset, size), size)
        copies.append(pltpu.make_async_copy(source, target.at[place], sems.at[index]))
        copies[-1].start()
    return copies


def dp_offsets(ranks, count, size):
    return [
        (lax.rem(ranks[0] + slot // 2, count // 2) * 2 + lax.rem(ranks[1] + slot % 2, 2)) * size
        for slot in range(count)
    ]


def tensor_offsets(ranks, count, size):
    return [(ranks[2] ^ slot) * size for slot in range(count)]


def pack(ranks, matrices, cuts, tokens=()):
    share = matrices[0].shape[0]

    def kernel(ranks_ref, gate_ref, up_ref, down_ref, *outs):
        x_rank = ranks_ref[1]
        for index, cut in enumerate(cuts):
            sent_ref, block_ref = outs[2 * index : 2 * index + 2]
            begin = 0
            for first, size in cut:
                here = slice(begin, begin + size)
                for matrix, source in enumerate((gate_ref, up_ref, down_ref)):
                    halves = [
                        source[:, first + which * size : first + (which + 1) * size]
                        for which in range(2)
                    ]
                    sent_ref[matrix, :, here] = jnp.where(x_rank == 0, halves[1], halves[0])
                    mine = jnp.where(x_rank == 0, halves[0], halves[1])
                    block_ref[matrix, :share, here] = mine
                    block_ref[matrix, share:, here] = mine
                begin += size
            if begin < sent_ref.shape[2]:
                for out in (sent_ref, block_ref):
                    rest = out.shape[2] - begin
                    out[:, :, begin:] = jnp.zeros((3, out.shape[1], rest), low)

    outs = []
    for cut in cuts:
        outs += [shaped((3, share, size_of(cut))), shaped((3, 2 * share, size_of(cut)))]
    return call(
        kernel, [ranks, *matrices], [in_smem] + [in_vmem] * 3, outs, tokens=tokens
    )


def attention_block(ranks, w_query, parts):
    share, query_cols = w_query.shape
    rows = parts[0].shape[0]
    if rows % 16:
        block = jnp.zeros((share, query_cols + 2 * HD), low).at[:, :query_cols].set(w_query)
        for slot, part in enumerate(parts):
            heads = pick(part.reshape(rows, 2, KV_HEADS, HD), ranks[2] // 2, 2)
            block = lax.dynamic_update_slice(
                block, heads.reshape(rows, 2 * HD), ((ranks[2] ^ slot) * rows, query_cols)
            )
        return block

    def kernel(ranks_ref, query_ref, *refs):
        out_ref = refs[-1]
        out_ref[:, :query_cols] = query_ref[...]
        first = ranks_ref[2] // 2 == 0
        for slot, ref in enumerate(refs[:-1]):
            place = pl.ds(pl.multiple_of((ranks_ref[2] ^ slot) * rows, rows), rows)
            for which in range(2):
                begin = which * KV_HEADS * HD
                column = query_cols + which * HD
                out_ref[place, column : column + HD] = jnp.where(
                    first, ref[:, begin : begin + HD], ref[:, begin + HD : begin + 2 * HD]
                )

    return call(
        kernel,
        [ranks, w_query, *parts],
        [in_smem] + [in_vmem] * (1 + len(parts)),
        [shaped((share, query_cols + 2 * HD))],
    )[0]


def normalize(rows, gain, tokens=()):
    def kernel(rows_ref, gain_ref, out_ref):
        x = rows_ref[...].astype(wide)
        scale = lax.rsqrt(jnp.mean(x * x, axis=1, keepdims=True) + eps_norm)
        out_ref[...] = (x * scale * gain_ref[...]).astype(low)

    return call(kernel, [rows, gain[None]], [in_vmem] * 2, [shaped(rows.shape)], tokens=tokens)[0]


def join_near(ranks, keep, came, tokens=()):
    def kernel(ranks_ref, keep_ref, first_ref, second_ref, sent_ref, own_ref):
        y_rank = ranks_ref[2] // 2
        other = 1 - y_rank
        first, second = first_ref[...], second_ref[...]
        here = jnp.where(y_rank == 0, first, second).astype(wide)
        there = jnp.where(y_rank == 0, second, first).astype(wide)
        sent_ref[...] = (keep_ref[other].astype(wide) + there).astype(low)
        own_ref[...] = keep_ref[y_rank].astype(wide) + here

    shape = keep.shape[1:]
    return call(
        kernel,
        [ranks, keep, *came],
        [in_smem, in_vmem, in_vmem, in_vmem],
        [shaped(shape), shaped(shape, wide)],
        tokens=tokens,
    )


def middle(rows, own, came, gain, tokens=()):
    half = rows.shape[0] // 2

    def kernel(rows_ref, own_ref, came_ref, gain_ref, mid_ref, top_ref, bottom_ref):
        mid = rows_ref[...].astype(wide) + own_ref[...] + came_ref[...].astype(wide)
        mid_ref[...] = mid
        scale = lax.rsqrt(jnp.mean(mid * mid, axis=1, keepdims=True) + eps_norm)
        normed = (mid * scale * gain_ref[...]).astype(low)
        top_ref[...] = normed[:half]
        bottom_ref[...] = normed[half:]

    shape = (half, rows.shape[1])
    return call(
        kernel,
        [rows, own, came, gain[None]],
        [in_vmem] * 4,
        [shaped(rows.shape, wide), shaped(shape), shaped(shape)],
        tokens=tokens,
    )


def stack_pairs(pairs, tokens=()):
    def kernel(*refs):
        outs = refs[2 * len(pairs) :]
        for index, out in enumerate(outs):
            half = out.shape[0] // 2
            out[:half] = refs[2 * index][...]
            out[half:] = refs[2 * index + 1][...]

    args = [one for pair in pairs for one in pair]
    return call(
        kernel,
        args,
        [in_vmem] * len(args),
        [shaped((2 * pair[0].shape[0], pair[0].shape[1])) for pair in pairs],
        tokens=tokens,
    )


def join_plane(keep, came, tokens=()):
    quarter = keep.shape[0] // 4

    def kernel(keep_ref, *refs):
        came_refs, (top_ref, bottom_ref, own_ref) = refs[:4], refs[4:]
        for part, came_ref in enumerate(came_refs):
            here = slice(part * quarter, (part + 1) * quarter)
            total = keep_ref[here].astype(wide) + came_ref[...].astype(wide)
            if part < 2:
                own_ref[here] = total
            else:
                (top_ref, bottom_ref)[part - 2][...] = total.astype(low)

    shape = (quarter, keep.shape[1])
    return call(
        kernel,
        [keep, *came],
        [in_vmem] * 5,
        [shaped(shape), shaped(shape), shaped((2 * quarter, keep.shape[1]), wide)],
        tokens=tokens,
    )


def join_pair(own, came_top, came_bottom, tokens=()):
    half = own.shape[0] // 4

    def kernel(own_ref, came_top_ref, came_bottom_ref, top_ref, bottom_ref, out_ref):
        for index, (came, sent) in enumerate(
            ((came_top_ref, top_ref), (came_bottom_ref, bottom_ref))
        ):
            total = own_ref[2 * index * half : 2 * (index + 1) * half] + came[...].astype(wide)
            out_ref[index * half : (index + 1) * half] = total[:half]
            sent[...] = total[half:].astype(low)

    shape = (half, own.shape[1])
    return call(
        kernel,
        [own, came_top, came_bottom],
        [in_vmem] * 3,
        [shaped(shape), shaped(shape), shaped((2 * half, own.shape[1]), wide)],
        tokens=tokens,
    )


def back_of_norm(values, gain, grad_normed):
    scale = lax.rsqrt(jnp.mean(values * values, axis=1, keepdims=True) + eps_norm)
    weighted = grad_normed * gain
    inner = jnp.mean(values * weighted, axis=1, keepdims=True)
    return scale * weighted - values * (scale * scale * scale * inner), scale


def middle_back(mid, gain, grad_out, own, came_top, came_bottom, tokens=()):
    half = came_top.shape[0]

    def kernel(mid_ref, gain_ref, grad_ref, own_ref, top_ref, bottom_ref, out_ref, low_ref, sum_ref):
        sum_ref[...] = jnp.zeros_like(sum_ref)
        for index, came in enumerate((top_ref, bottom_ref)):
            here = slice(index * half, (index + 1) * half)
            grad_two = own_ref[here] + came[...].astype(wide)
            values = mid_ref[here]
            grad_values, scale = back_of_norm(values, gain_ref[...], grad_two)
            total = grad_ref[here].astype(wide) + grad_values
            out_ref[here] = total
            low_ref[here] = total.astype(low)
            sum_ref[...] += jnp.sum(grad_two * values * scale, axis=0, keepdims=True)

    return call(
        kernel,
        [mid, gain[None], grad_out, own, came_top, came_bottom],
        [in_vmem] * 6,
        [shaped(mid.shape, wide), shaped(mid.shape), shaped((1, mid.shape[1]), wide)],
        tokens=tokens,
    )


def tokens_back(rows, gain, grad_mid, own, came, tokens=()):
    def kernel(rows_ref, gain_ref, grad_ref, own_ref, came_ref, out_ref):
        values = rows_ref[...].astype(wide)
        grad_one = own_ref[...] + came_ref[...].astype(wide)
        out_ref[...] = grad_ref[...] + back_of_norm(values, gain_ref[...], grad_one)[0]

    return call(
        kernel,
        [rows, gain[None], grad_mid, own, came],
        [in_vmem] * 5,
        [shaped(rows.shape, wide)],
        tokens=tokens,
    )[0]


def layer_rows(mid, own, came_top, came_bottom, tokens=()):
    half = came_top.shape[0]

    def kernel(mid_ref, own_ref, top_ref, bottom_ref, out_ref):
        for index, came in enumerate((top_ref, bottom_ref)):
            here = slice(index * half, (index + 1) * half)
            out_ref[here] = (mid_ref[here] + own_ref[here] + came[...].astype(wide)).astype(low)

    return call(
        kernel, [mid, own, came_top, came_bottom], [in_vmem] * 4, [shaped(mid.shape)], tokens=tokens
    )[0]


def added(came, part):
    return (came.astype(wide) + part.astype(wide)).astype(low)


def store_split(ranks_ref, compute, keep_ref, send_refs):
    core = lax.rem(ranks_ref[2], 2)
    for y_rank in range(2):
        send_refs[y_rank][...] = compute(y_rank * 2 + 1 - core).astype(low)
        keep_ref[y_rank] = compute(y_rank * 2 + core).astype(low)


def project_out(ranks, heads_low, weights, tokens=()):
    length, width = heads_low.shape[0], weights.shape[0]
    rows = length // 4

    def kernel(ranks_ref, heads_ref, weights_ref, keep_ref, *send_refs):
        def compute(index):
            here = pl.ds(pl.multiple_of(index * rows, rows), rows)
            return dot_nt(heads_ref[here], weights_ref[...])

        store_split(ranks_ref, compute, keep_ref, send_refs)

    return call(
        kernel,
        [ranks, heads_low, weights],
        [in_smem, in_vmem, in_vmem],
        [shaped((2, rows, width)), shaped((rows, width)), shaped((rows, width))],
        tokens=tokens,
    )


def attend(ranks, pieces, weights, bias, cosine, sine, segment, tokens=()):
    rows, width = pieces[0].shape
    count = len(pieces)
    length = rows * count
    columns = weights[0].shape[1]
    share = weights[0].shape[0]
    query_cols = columns - 2 * HD
    heads = query_cols // HD
    factor = HD ** (-0.5)

    def kernel(ranks_ref, *refs):
        piece_refs, refs = refs[:count], refs[count:]
        weight_refs, refs = refs[: len(weights)], refs[len(weights) :]
        bias_ref, cos_ref, sin_ref, col_ref, row_ref = refs[:5]
        query_ref, key_ref, value_ref, heads_ref = refs[5:9]
        prob_refs = refs[9 : 9 + count]
        rows_v, weights_v, piece_sems, weight_sems = refs[9 + count :]
        copies = start_rows(
            piece_refs, rows_v, tensor_offsets(ranks_ref, count, rows), piece_sems
        ) + start_rows(
            weight_refs, weights_v, dp_offsets(ranks_ref, len(weights), share), weight_sems
        )
        for copy in copies:
            copy.wait()
        for block in range(count):
            here = slice(block * rows, (block + 1) * rows)
            lin = dot_nn(rows_v[here], weights_v[...]) + bias_ref[...]
            cos, sin = cos_ref[here], sin_ref[here]
            for head in range(heads + 1):
                part = lin[:, head * HD : (head + 1) * HD]
                turned = (part * cos + pltpu.roll(part, HD // 2, 1) * sin).astype(low)
                if head < heads:
                    query_ref[here, head * HD : (head + 1) * HD] = turned
                else:
                    key_ref[here] = turned
            value_ref[here] = lin[:, (heads + 1) * HD :].astype(low)
        for block in range(count):
            here = slice(block * rows, (block + 1) * rows)
            seen = (block + 1) * rows
            stacked = jnp.concatenate(
                [query_ref[here, head * HD : (head + 1) * HD] for head in range(heads)], axis=0
            )
            scores = dot_nt(stacked, key_ref[:seen]) * factor
            row_id = lax.broadcasted_iota(jnp.int32, (rows, seen), 0) + block * rows
            col_id = lax.broadcasted_iota(jnp.int32, (rows, seen), 1)
            allowed = (col_ref[here] == row_ref[:, :seen]) & (row_id >= col_id)
            shift = jnp.where(allowed, 0.0, masked)
            scores = scores + jnp.concatenate([shift] * heads, axis=0)
            weight = jnp.exp(scores - jnp.max(scores, axis=1, keepdims=True))
            weight = weight * (1.0 / jnp.sum(weight, axis=1, keepdims=True))
            weight_low = weight.astype(low)
            prob_refs[block][...] = weight_low
            out = dot_nn(weight_low, value_ref[:seen]).astype(low)
            for head in range(heads):
                heads_ref[here, head * HD : (head + 1) * HD] = out[head * rows : (head + 1) * rows]

    outs = [
        shaped((length, query_cols)),
        shaped((length, HD)),
        shaped((length, HD)),
        shaped((length, query_cols)),
    ] + [shaped((heads * rows, (block + 1) * rows)) for block in range(count)]
    out = call(
        kernel,
        [ranks, *pieces, *weights, bias[None], cosine, sine, segment[:, None], segment[None]],
        [in_smem] + [anywhere] * (count + len(weights)) + [in_vmem] * 5,
        outs,
        [
            pltpu.VMEM((length, width), low),
            pltpu.VMEM((width, columns), low),
            pltpu.SemaphoreType.DMA((count,)),
            pltpu.SemaphoreType.DMA((len(weights),)),
        ],
        tokens,
        room=40,
    )
    return out[:4], out[4:]


def attend_back(
    ranks, pieces, normed, gain, out_weights, weights, kept, probs, cosine, sine, tokens=()
):
    query, key, value = kept
    rows, width = pieces[0].shape
    count = len(pieces)
    length = rows * count
    share = weights[0].shape[0]
    columns = weights[0].shape[1]
    query_cols = query.shape[1]
    heads = query_cols // HD
    factor = HD ** (-0.5)
    blocks = len(weights)

    def kernel(ranks_ref, *refs):
        piece_refs, refs = refs[:count], refs[count:]
        normed_refs, refs = refs[:count], refs[count:]
        out_ref, refs = refs[0], refs[1:]
        weight_refs, refs = refs[:blocks], refs[blocks:]
        query_ref, key_ref, value_ref = refs[:3]
        prob_refs, refs = refs[3 : 3 + count], refs[3 + count :]
        cos_ref, sin_ref, gain_ref = refs[:3]
        grad_ref, bias_ref, gain_sum_ref, keep_ref, *send_refs = refs[3:9]
        rows_v, normed_v, out_v, weights_v, do_v, dk_v, dv_v = refs[9:16]
        piece_sems, normed_sems, out_sem, weight_sems = refs[16:]
        copies = [pltpu.make_async_copy(out_ref, out_v, out_sem)]
        copies[0].start()
        copies += start_rows(
            piece_refs, rows_v, tensor_offsets(ranks_ref, count, rows), piece_sems
        )
        late = start_rows(
            weight_refs, weights_v, dp_offsets(ranks_ref, blocks, share), weight_sems
        ) + start_rows(
            normed_refs, normed_v, tensor_offsets(ranks_ref, count, rows), normed_sems
        )
        for copy in copies:
            copy.wait()
        for block in range(count):
            here = slice(block * rows, (block + 1) * rows)
            do_v[here] = dot_nn(rows_v[here], out_v[...]).astype(low)
        dk_v[...] = jnp.zeros_like(dk_v)
        dv_v[...] = jnp.zeros_like(dv_v)
        for block in range(count):
            here = slice(block * rows, (block + 1) * rows)
            seen = (block + 1) * rows
            stacked = jnp.concatenate(
                [do_v[here, head * HD : (head + 1) * HD] for head in range(heads)], axis=0
            )
            query_here = jnp.concatenate(
                [query_ref[here, head * HD : (head + 1) * HD] for head in range(heads)], axis=0
            )
            weight_low = prob_refs[block][...]
            grad_weight = dot_nt(stacked, value_ref[:seen])
            weight = weight_low.astype(wide)
            inner = jnp.sum(weight * grad_weight, axis=1, keepdims=True)
            grad_scores = (weight * (grad_weight - inner)).astype(low)
            grad_query = dot_nn(grad_scores, key_ref[:seen]) * factor
            dk_v[:seen] += dot_tn(grad_scores, query_here) * factor
            dv_v[:seen] += dot_tn(weight_low, stacked)
            cos, sin = cos_ref[here], sin_ref[here]
            for head in range(heads):
                part = grad_query[head * rows : (head + 1) * rows]
                grad_ref[here, head * HD : (head + 1) * HD] = (
                    part * cos - pltpu.roll(part, HD // 2, 1) * sin
                ).astype(low)
        part = dk_v[...]
        grad_ref[:, query_cols : query_cols + HD] = (
            part * cos_ref[...] - pltpu.roll(part, HD // 2, 1) * sin_ref[...]
        ).astype(low)
        grad_ref[:, query_cols + HD :] = dv_v[...].astype(low)
        bias_ref[...] = jnp.sum(grad_ref[...].astype(wide), axis=0, keepdims=True)
        for copy in late:
            copy.wait()
        gain_sum_ref[...] = jnp.zeros_like(gain_sum_ref)

        def compute(index):
            here = pl.ds(pl.multiple_of(index * rows, rows), rows)
            part = dot_nt(grad_ref[here], weights_v[...])
            gain_sum_ref[...] += jnp.sum(part * normed_v[here].astype(wide), axis=0, keepdims=True)
            return part

        store_split(ranks_ref, compute, keep_ref, send_refs)
        gain_sum_ref[...] = gain_sum_ref[...] / gain_ref[...]

    return call(
        kernel,
        [ranks, *pieces, *normed, out_weights, *weights, query, key, value, *probs]
        + [cosine, sine, gain[None]],
        [in_smem] + [anywhere] * (2 * count + 1 + blocks) + [in_vmem] * (6 + count),
        [
            shaped((length, columns)),
            shaped((1, columns), wide),
            shaped((1, width), wide),
            shaped((2, rows, width)),
            shaped((rows, width)),
            shaped((rows, width)),
        ],
        [
            pltpu.VMEM((length, width), low),
            pltpu.VMEM((length, width), low),
            pltpu.VMEM((width, query_cols), low),
            pltpu.VMEM((width, columns), low),
            pltpu.VMEM((length, query_cols), low),
            pltpu.VMEM((length, HD), wide),
            pltpu.VMEM((length, HD), wide),
            pltpu.SemaphoreType.DMA((count,)),
            pltpu.SemaphoreType.DMA((count,)),
            pltpu.SemaphoreType.DMA,
            pltpu.SemaphoreType.DMA((blocks,)),
        ],
        tokens,
        room=40,
    )


def weight_sums(ranks, pairs, blocks, tokens=()):
    rows, width = pairs[0][0][0].shape
    count = len(pairs[0][0])
    share = width // blocks
    columns = sum(grads.shape[1] for _, grads in pairs)
    group = max(width // 4, share)

    def kernel(ranks_ref, *refs):
        piece_refs = [refs[index * (count + 1) : (index + 1) * (count + 1)] for index in range(len(pairs))]
        refs = refs[len(pairs) * (count + 1) :]
        sums_refs, sums_v = refs[:blocks], refs[blocks]
        rows_vs, sems = refs[blocks + 1 : -1], refs[-1]
        copies = [
            start_rows(
                one[:count], rows_v, tensor_offsets(ranks_ref, count, rows), sems.at[index]
            )
            for index, (one, rows_v) in enumerate(zip(piece_refs, rows_vs))
        ]
        begin = 0
        for index, (one, rows_v) in enumerate(zip(piece_refs, rows_vs)):
            for copy in copies[index]:
                copy.wait()
            end = begin + one[count].shape[1]
            for first in range(0, width, group):
                part = dot_tn(rows_v[:, first : first + group], one[count][...]).astype(low)
                for place in range(0, group, share):
                    block = (first + place) // share
                    slot = lax.rem(block // 2 + blocks // 2 - ranks_ref[0], blocks // 2) * 2
                    sums_v[slot + lax.rem(block % 2 + ranks_ref[1], 2), :, begin:end] = part[
                        place : place + share
                    ]
            begin = end
        for slot in range(blocks):
            sums_refs[slot][...] = sums_v[slot]

    args, specs = [ranks], [in_smem]
    for pieces, grads in pairs:
        args += [*pieces, grads]
        specs += [anywhere] * count + [in_vmem]
    return call(
        kernel,
        args,
        specs,
        [shaped((share, columns))] * blocks,
        [pltpu.VMEM((blocks, share, columns), low)]
        + [pltpu.VMEM((rows * count, width), low)] * len(pairs)
        + [pltpu.SemaphoreType.DMA((len(pairs), count))],
        tokens,
        room=40,
    )


def row_places(ranks, rows):
    half = rows // 2
    places = []
    for other in range(2):
        for pair, part in (
            (((0, 0), (1, 0)), 0),
            (((0, 0), (0, 1)), 1),
            (((0, 1), (1, 1)), 0),
            (((1, 0), (1, 1)), 1),
        ):
            for flip_x, flip_y in pair:
                device = (ranks[1] ^ flip_x) * 4 + (ranks[2] ^ (flip_y * 2 + other))
                places.append(device * rows + part * half)
    return places


def start_weights(ranks, sources, target, sems, matrices=None):
    copies = []
    blocks = len(sources)
    for slot, source in enumerate(sources):
        share = source.shape[1]
        place = pl.ds(pl.multiple_of(lax.rem(ranks[0] + slot, blocks) * share, share), share)
        if matrices is None:
            copies.append(pltpu.make_async_copy(source, target.at[:, place], sems.at[slot, 0]))
            copies[-1].start()
        else:
            for index, matrix in enumerate(matrices):
                copies.append(
                    pltpu.make_async_copy(
                        source.at[matrix], target.at[index, place], sems.at[slot, index]
                    )
                )
                copies[-1].start()
    return copies


def ffn(ranks, normed, grads, weights, saved, sums, tokens=()):
    acts = saved is None
    count = len(normed)
    rows, width = normed[0].shape
    length = rows * count
    blocks = len(weights)
    share = weights[0].shape[1]
    size = weights[0].shape[2]
    step = 2 * rows
    group = max(width // 2, share)

    def kernel(ranks_ref, *refs):
        refs = list(refs)

        def take(number):
            taken = refs[:number]
            del refs[:number]
            return taken

        normed_refs = take(count)
        (grads_ref,) = take(1)
        weight_refs = take(blocks) if acts else []
        saved_refs = take(3)
        sums_refs = take(blocks) if sums else []
        normed_v, grads_v, row_sems = take(3)
        leaving = []

        def leave(source, target, sem):
            leaving.append(pltpu.make_async_copy(source, target, sem))
            leaving[-1].start()

        copies = []
        if acts:
            weights_v, weight_sems, *saved_vs, saved_sems = take(6)
            copies = start_weights(ranks_ref, weight_refs, weights_v, weight_sems)
        places = row_places(ranks_ref, rows)
        half = rows // 2
        waits = []
        for k in range(count):
            waits.append(
                pltpu.make_async_copy(
                    normed_refs[k], normed_v.at[pl.ds(k * rows, rows)], row_sems.at[k, 0]
                )
            )
            for part in range(2):
                source = pl.ds(pl.multiple_of(places[2 * k + part], half), half)
                waits.append(
                    pltpu.make_async_copy(
                        grads_ref.at[source],
                        grads_v.at[pl.ds(k * rows + part * half, half)],
                        row_sems.at[k, 1 + part],
                    )
                )
        for wait in waits:
            wait.start()
        for copy in copies:
            copy.wait()
        for k in range(length // step):
            here = pl.ds(k * step, step)
            for wait in waits[6 * k : 6 * k + 6]:
                wait.wait()
            if not acts:
                continue
            gate = dot_nn(normed_v[here], weights_v[0])
            upward = dot_nn(normed_v[here], weights_v[1])
            grad_hidden = dot_nn(grads_v[here], weights_v[2])
            sigma = 0.5 * jnp.tanh(0.5 * gate) + 0.5
            active = gate * sigma
            saved_vs[0][here] = (active * upward).astype(low)
            saved_vs[1][here] = (grad_hidden * upward * (sigma + active * (1.0 - sigma))).astype(low)
            saved_vs[2][here] = (grad_hidden * active).astype(low)
            for index in range(3):
                leave(saved_vs[index].at[here], saved_refs[index].at[here], saved_sems.at[k, index])
        if sums:
            sums_v, sums_sems = take(2)
            lefts = saved_vs if acts else saved_refs
            for index, (left, right) in enumerate(
                ((lefts[1], normed_v), (lefts[2], normed_v), (lefts[0], grads_v))
            ):
                turned = left[...].T
                for first in range(0, width, group):
                    part = dot_nn(turned, right[:, first : first + group]).T.astype(low)
                    for place in range(0, group, share):
                        block = (first + place) // share
                        slot = lax.rem(block + blocks - ranks_ref[0], blocks)
                        sums_v[slot, index] = part[place : place + share]
                for slot in range(blocks):
                    leave(sums_v.at[slot, index], sums_refs[slot].at[index], sums_sems.at[index, slot])
        for copy in leaving:
            copy.wait()

    args = [ranks, *normed, grads]
    specs = [in_smem] + [anywhere] * (count + 1)
    outs = []
    scratch = [
        pltpu.VMEM((length, width), low),
        pltpu.VMEM((length, width), low),
        pltpu.SemaphoreType.DMA((count, 3)),
    ]
    if acts:
        args += weights
        specs += [anywhere] * blocks
        scratch += [pltpu.VMEM((3, width, size), low), pltpu.SemaphoreType.DMA((blocks, 1))]
        scratch += [pltpu.VMEM((length, size), low)] * 3
        scratch += [pltpu.SemaphoreType.DMA((length // step, 3))]
        outs += [shaped((length, size))] * 3
    else:
        args += saved
        specs += [in_vmem] * 3
    if sums:
        outs += [shaped((3, share, size))] * blocks
        scratch += [
            pltpu.VMEM((blocks, 3, share, size), low),
            pltpu.SemaphoreType.DMA((3, blocks)),
        ]
    return call(kernel, args, specs, outs, scratch, tokens, [anywhere] * len(outs), 60)


def back_rows(ranks, lefts, chunks, which, tokens=()):
    length = lefts[0][0].shape[0]
    blocks = len(chunks[0])
    share = chunks[0][0].shape[1]
    width = share * blocks
    sizes = [chunk[0].shape[2] for chunk in chunks]
    step = length // 4

    def kernel(ranks_ref, *refs):
        refs = list(refs)

        def take(number):
            taken = refs[:number]
            del refs[:number]
            return taken

        left_refs = [take(len(which)) for _ in chunks]
        weight_refs = [take(blocks) for _ in chunks]
        keep_ref, *send_refs = take(5)
        weight_vs = take(len(chunks))
        (sems,) = refs
        copies = []
        for chunk, sources in enumerate(weight_refs):
            copies += start_weights(ranks_ref, sources, weight_vs[chunk], sems.at[chunk], which)
        for copy in copies:
            copy.wait()
        for k in (2, 3, 0, 1):
            here = pl.ds(k * step, step)
            total = None
            for chunk in range(len(chunks)):
                for index in range(len(which)):
                    term = dot_nt(left_refs[chunk][index][here], weight_vs[chunk][index])
                    total = term if total is None else total + term
            if k < 2:
                keep_ref[here] = total.astype(low)
            else:
                send_refs[2 * (k - 2)][...] = total[: step // 2].astype(low)
                send_refs[2 * (k - 2) + 1][...] = total[step // 2 :].astype(low)

    args = [ranks] + [one for left in lefts for one in left]
    args += [block for chunk in chunks for block in chunk]
    return call(
        kernel,
        args,
        [in_smem] + [in_vmem] * (len(which) * len(chunks)) + [anywhere] * (blocks * len(chunks)),
        [shaped((length // 2, width))] + [shaped((length // 8, width))] * 4,
        [pltpu.VMEM((len(which), width, size), low) for size in sizes]
        + [pltpu.SemaphoreType.DMA((len(chunks), blocks, len(which)))],
        tokens,
        room=60,
    )


def split_x(ranks, total, tokens=()):
    share = total.shape[1] // 2

    def kernel(ranks_ref, total_ref, out_ref):
        place = pl.ds(pl.multiple_of((1 - ranks_ref[1]) * share, share), share)
        out_ref[...] = total_ref[:, place]

    return call(
        kernel,
        [ranks, total],
        [in_smem, in_vmem],
        [shaped((3, share, total.shape[2]))],
        tokens=tokens,
    )[0]


def lay_out(ranks, totals, cames, cuts, columns, tokens=()):
    share = cames[0].shape[1]

    def kernel(ranks_ref, *refs):
        total_refs, came_refs = refs[: len(cuts)], refs[len(cuts) : 2 * len(cuts)]
        outs = refs[2 * len(cuts) :]
        x_rank = ranks_ref[1]
        place = pl.ds(pl.multiple_of(x_rank * share, share), share)
        for index, cut in enumerate(cuts):
            begin = 0
            for first, size in cut:
                here = slice(begin, begin + size)
                for matrix in range(3):
                    own = total_refs[index][matrix, place, here].astype(wide)
                    came = came_refs[index][matrix, :, here].astype(wide)
                    for which in range(2):
                        half = jnp.where(x_rank == which, own, came)
                        to = slice(first + which * size, first + (which + 1) * size)
                        outs[matrix][:, to] = half
                begin += size

    return call(
        kernel,
        [ranks, *totals, *cames],
        [in_smem] + [in_vmem] * (2 * len(cuts)),
        [shaped((share, columns), wide)] * 3,
        tokens=tokens,
        room=40,
    )


def on_device(
    tokens,
    segment,
    gain_attn,
    w_query,
    b_query,
    w_key,
    b_key,
    w_value,
    b_value,
    w_out,
    gain_ffn,
    w_gate,
    w_up,
    w_down,
    grad_out,
):
    width = tokens.shape[1]
    dp_count, tensor_count = lax.axis_size("dp"), lax.axis_size("tensor")
    dp_rank, tensor_rank = lax.axis_index("dp"), lax.axis_index("tensor")
    z_count = dp_count // 2
    z_rank, x_rank = dp_rank // 2, dp_rank % 2
    y_rank, core = tensor_rank // 2, tensor_rank % 2
    ranks = jnp.stack([z_rank, x_rank, tensor_rank]).astype(jnp.int32)
    share = width // dp_count
    query_cols = w_query.shape[1]
    qkv_cols = query_cols + 2 * HD
    ffn_cols = w_gate.shape[1]
    cuts = cuts_of(ffn_cols)
    planes = [
        [plane * 2 * tensor_count + device for device in range(2 * tensor_count)]
        for plane in range(z_count)
    ]

    out_full = lax.all_gather(w_out.T, "dp", axis=0, tiled=True)
    pair_kv = jnp.concatenate([w_key, w_value], axis=1)
    parts_kv = [pair_kv, across_core(pair_kv), across_y(pair_kv), across_both(pair_kv)]
    normed_one = normalize(tokens, gain_attn, [pair_kv])
    far_one = across_y(normed_one)
    rows_one = [normed_one, across_core(normed_one), far_one, across_core(far_one)]

    line = [attention_block(ranks, w_query, parts_kv)]
    for _ in range(z_count - 1):
        line.append(up_line(line[-1]))
    crossed = [across_x(block) for block in line]
    qkv_blocks = []
    for slot in range(z_count):
        qkv_blocks += [line[-slot % z_count], crossed[-slot % z_count]]
    grad_ffn = lax.all_gather(
        after(grad_out, line[0]), ("dp", "tensor"), axis=0, tiled=True, axis_index_groups=planes
    )

    packed = pack(ranks, (w_gate, w_up, w_down.T), cuts, [line[0]])
    came_ffn = [across_x(sent) for sent in packed[::2]]
    lines = [
        [
            lax.dynamic_update_slice_in_dim(
                packed[2 * index + 1], after(came, line[-1]), (1 - x_rank) * share, 1
            )
        ]
        for index, came in enumerate(came_ffn)
    ]
    chunk_count = len(lines)
    stages = [0]

    def advance(*others):
        for index, one in enumerate(lines):
            if index <= stages[0] and len(one) < z_count:
                one.append(up_line(after(one[-1], *others)))
        stages[0] += 1

    def newest():
        return [one[-1] for one in lines]

    advance(line[-1])
    cosine, sine = angles_of(segment, HD)
    sine = jnp.where(jnp.arange(HD) < HD // 2, -sine, sine)
    key_bias = lax.dynamic_slice_in_dim(b_key, y_rank * HD, HD, 0)
    value_bias = lax.dynamic_slice_in_dim(b_value, y_rank * HD, HD, 0)
    bias = jnp.concatenate([b_query, key_bias, value_bias])
    (query, key, value, heads_low), probs = attend(
        ranks, rows_one, qkv_blocks, bias, cosine, sine, segment, [one[0] for one in lines]
    )
    keep, *send = project_out(ranks, heads_low, out_full)
    came = [across_core(one) for one in send]
    waited = newest()
    advance(send[0])
    sent, own = join_near(ranks, keep, came, waited)
    mid_rows, top, bottom = middle(tokens, own, across_y(sent), gain_ffn)
    top_x, bottom_y = across_x(top), across_y(bottom)
    waited = newest()
    advance(mid_rows)
    top, bottom = stack_pairs([(top, top_x), (bottom, bottom_y)], waited)
    pieces = [top, bottom, across_y(top), across_x(bottom)]
    rows_two = pieces + [across_core(piece) for piece in pieces]

    saved, hops, terms, slots, lines_held = [], [], [], [], []

    def start_sums(sums):
        terms.append(sums)
        hops.append(up_line(sums[-1]))
        slots.append(z_count - 2)

    def add_next(index, token):
        if index >= len(slots) or slots[index] < 0:
            return token
        total = added(hops[index], after(terms[index][slots[index]], token))
        hops[index] = up_line(total) if slots[index] else total
        slots[index] -= 1
        return total

    token = top
    for index in range(chunk_count):
        waited = newest()
        if stages[0] < z_count - 1 + index:
            advance(token)
        while len(lines[index]) < z_count:
            waited = newest()
            advance(token)
        chunk = lines[index][:1] + lines[index][:0:-1]
        lines_held.append(chunk)
        some = ffn(
            ranks, rows_two, grad_ffn, chunk, None, index < chunk_count - 1, [token, *waited]
        )
        saved.append(some[:3])
        if index < chunk_count - 1:
            start_sums(some[3:])
        token = some[0]
    held = lines_held
    keep, *send = back_rows(ranks, [some[1:] for some in saved], held, (0, 1), [token])
    came = [across_core(one) for one in send]
    token = add_next(0, send[0])
    top, bottom, own = join_plane(keep, came, [token])
    came_top, came_bottom = across_y(top), across_x(bottom)
    start_sums(ffn(ranks, rows_two, grad_ffn, held[-1], saved[-1], True, [top]))
    token = add_next(1, terms[-1][-1])
    top, bottom, own = join_pair(own, came_top, came_bottom, [token])
    came_top, came_bottom = across_x(top), across_y(bottom)
    keep_out, *send_out = back_rows(ranks, [some[:1] for some in saved], held, (2,), [top])
    came_out = [across_core(one) for one in send_out]
    grad_mid, grad_mid_low, gain_two_part = middle_back(
        mid_rows, gain_ffn, grad_out, own, came_top, came_bottom, [send_out[0]]
    )

    far_attn = across_y(grad_mid_low)
    grad_attn = [grad_mid_low, across_core(grad_mid_low), far_attn, across_core(far_attn)]
    token = add_next(0, grad_mid_low)
    top_out, bottom_out, own_out = join_plane(keep_out, came_out, [token])
    came_top_out, came_bottom_out = across_y(top_out), across_x(bottom_out)
    token = add_next(1, top_out)
    token = add_next(2, token)
    grad_qkv, bias_sums, gain_one_part, keep, *send = attend_back(
        ranks, grad_attn, rows_one, gain_attn, out_full, qkv_blocks, (query, key, value), probs,
        cosine, sine, [token],
    )
    came_one = [across_core(one) for one in send]
    both_terms = weight_sums(
        ranks, [(rows_one, grad_qkv), (grad_attn, heads_low)], dp_count, [send[0]]
    )
    both_far = [across_x(both_terms[2 * slot + 1]) for slot in range(z_count)]
    sent, own = join_near(ranks, keep, came_one, [both_terms[0]])
    came_one = across_y(sent)
    token = add_next(0, sent)
    top_out, bottom_out, own_out = join_pair(own_out, came_top_out, came_bottom_out, [token])
    came_top_out, came_bottom_out = across_x(top_out), across_y(bottom_out)
    token = add_next(1, top_out)
    token = add_next(2, token)

    both_sums = None
    for slot in range(z_count - 1, -1, -1):
        part = both_terms[2 * slot].astype(wide) + both_far[slot].astype(wide)
        if both_sums is not None:
            part = part + up_line(both_sums).astype(wide)
        both_sums = part.astype(low)
    grad_w_query = both_sums[:, :query_cols].astype(wide)
    grad_w_out = both_sums[:, qkv_cols:].astype(wide).T

    grad_tokens = tokens_back(tokens, gain_attn, grad_mid, own, came_one, [token])
    token = grad_tokens
    layer_out = layer_rows(mid_rows, own_out, came_top_out, came_bottom_out, [token])
    token = layer_out
    while any(slot >= 0 for slot in slots):
        for index in range(chunk_count):
            token = add_next(index, token)
    sent_ffn = [split_x(ranks, hop) for hop in hops]
    grad_w_gate, grad_w_up, grad_w_down = lay_out(
        ranks, hops, [across_x(sent) for sent in sent_ffn], cuts, ffn_cols
    )
    grad_w_down = grad_w_down.T

    kv_sums = both_sums[:, query_cols:qkv_cols].reshape(2, 2, -1, 2 * HD)
    near_kv = pick(kv_sums, core, 1).astype(wide) + across_core(
        pick(kv_sums, 1 - core, 1)
    ).astype(wide)
    came_kv = across_y(pick(near_kv, 1 - y_rank, 0).astype(low)).astype(wide)
    both_kv = in_order(pick(near_kv, y_rank, 0), came_kv, y_rank, 0).reshape(2, -1, 2, HD)
    grad_w_key = both_kv[:, :, 0].transpose(1, 0, 2).reshape(-1, KV_HEADS * HD)
    grad_w_value = both_kv[:, :, 1].transpose(1, 0, 2).reshape(-1, KV_HEADS * HD)
    bias_sums, gain_one_part, gain_two_part = bias_sums[0], gain_one_part[0], gain_two_part[0]

    def spread(values, count, rank):
        return lax.dynamic_update_slice_in_dim(
            jnp.zeros((count,), wide), values, rank * values.shape[0], 0
        )

    sizes = (HEADS * HD, KV_HEADS * HD, KV_HEADS * HD, width, width)
    small = all_sum(
        jnp.concatenate(
            [
                spread(bias_sums[:query_cols], sizes[0], tensor_rank),
                spread(bias_sums[query_cols : query_cols + HD], sizes[1], y_rank),
                spread(bias_sums[query_cols + HD :], sizes[2], y_rank),
                gain_two_part,
                gain_one_part,
            ]
        ).reshape(-1, 128)
    ).reshape(-1)
    device = dp_rank * lax.axis_size("tensor") + tensor_rank
    small_sums = []
    first = 0
    for size in sizes:
        each = size // (dp_count * lax.axis_size("tensor"))
        small_sums.append(lax.dynamic_slice_in_dim(small, first + device * each, each, 0))
        first += size

    return (
        layer_out,
        grad_tokens,
        small_sums[4],
        grad_w_query,
        small_sums[0],
        grad_w_key,
        small_sums[1],
        grad_w_value,
        small_sums[2],
        grad_w_out,
        small_sums[3],
        grad_w_gate,
        grad_w_up,
        grad_w_down,
    )


def solution(mesh):
    return jax.shard_map(
        on_device,
        mesh=mesh,
        in_specs=(
            P(("dp", "tensor"), None),
            P("dp"),
            P(),
            P("dp", "tensor"),
            P("tensor"),
            P(("dp", "tensor"), None),
            P(),
            P(("dp", "tensor"), None),
            P(),
            P("tensor", "dp"),
            P(),
            P("dp", "tensor"),
            P("dp", "tensor"),
            P("tensor", "dp"),
            P(("dp", "tensor"), None),
        ),
        out_specs=(
            P(("dp", "tensor"), None),
            P(("dp", "tensor"), None),
            P(("dp", "tensor")),
            P("dp", "tensor"),
            P(("dp", "tensor")),
            P(("dp", "tensor"), None),
            P(("dp", "tensor")),
            P(("dp", "tensor"), None),
            P(("dp", "tensor")),
            P("tensor", "dp"),
            P(("dp", "tensor")),
            P("dp", "tensor"),
            P("dp", "tensor"),
            P("tensor", "dp"),
        ),
        check_vma=False,
    )
```

time: 1390 us -> 680 us (0.49)
  waiting for transfers between devices: 957 us -> 323 us
  Pallas kernels: 0 us -> 183 us
  matrix products: 155 us -> 0 us
  blocking collectives: 135 us -> 0 us
  starting transfers between devices: 1.51 us -> 64.4 us
  other arithmetic: 49.9 us -> 26.9 us
    all_gather x9 -> x2, waiting for transfers between devices: 385 us -> 0.01 us  [the longest x1 0.01 us: on_device(): out_full = lax.all_gather(w_out.T, 'dp', axis=0, tiled=True)]
    ppermute x1 -> x84, waiting for transfers between devices: 0.01 us -> 323 us  [moved(): return lax.ppermute(block, axis, route)]
    unnamed x17 -> x2, waiting for transfers between devices: 322 us -> 0.7 us
    reduce_scatter x6 -> x0, waiting for transfers between devices: 250 us -> none  [the longest x1 103 us: on_device(): lax.psum_scatter(weight_value, ('dp', 'tensor'), scatter_dimension=0, til...]
    pallas_call x0 -> x28, Pallas kernels: none -> 183 us  [call(): pl.pallas_call(body, out_shape=outs, in_specs=list(specs) + [anywhere] *...]
    dot_general x33 -> x0, matrix products: 155 us -> none  [the longest x7 50.2 us: product(): return jnp.dot(operand, weight_mat, preferred_element_type=jnp.float32)]
    all_gather x2 -> x0, blocking collectives: 91 us -> none  [the longest x1 49 us: on_device(): lax.all_gather(w_key, ('dp', 'tensor'), axis=0, tiled=True)]
    ppermute x1 -> x84, starting transfers between devices: 0.25 us -> 64.3 us  [moved(): return lax.ppermute(block, axis, route)]
  transfers between devices with their start and end apart: 17 -> 86, of which waited for: 11 -> 39; matrix products, arithmetic and copies ran while one was open for 14% -> 5% of each run, Pallas kernels for 0% -> 20%
where the time goes in v1:
time: 680 us; the launch traced here: 675 us
  waiting for transfers between devices  323 us (48%)
  Pallas kernels  183 us (27%)
  starting transfers between devices  64.4 us (9%)
  local copies, waits for them, and re-layouts  61.3 us (9%)
  other arithmetic  26.9 us (4%)
  between operations  16.1 us (2%)
    ppermute x84, waiting for transfers between devices, moved(): return lax.ppermute(block, axis, route)  323 us
    pallas_call x28, Pallas kernels, call(): pl.pallas_call(body, out_shape=outs, in_specs=list(specs) + [anywhere] *...  183 us
    ppermute x84, starting transfers between devices, moved(): return lax.ppermute(block, axis, route)  64.3 us
    unnamed x225, local copies, waits for them, and re-layouts  50.5 us
    convert_element_type x9, other arithmetic, added(): return (came.astype(wide) + part.astype(wide)).astype(low)  15 us
  transfers between devices with their start and end apart: 86, of which 39 were waited for; matrix products, arithmetic and copies ran while one was open for 5% of the time, Pallas kernels for 20%

profile of v1, /device:TPU:0, one launch (start us, length us, event | category | flops | bytes accessed | tf_op | source)
XLA Modules:
  0.0 675.2 jit_solution(5479827471448100869)
XLA Ops:
  9.9 2.5 collective-permute-start.4
  32.5 7.6 %collective-permute-done.8.refs_9_.refs_14_ = bf16[192,640]{1,0:T(8,128)(2,1)S(1)} collective-permute-done((bf16[192,640]{1,0:T(8,128)(2,1)}, bf16[192,640]{1,0:T(8,128)(2,1)S(1)}, u32[]{:S(2)}, u32[]{:S(2)}) %collective-permute-start.8) | collective-permute-done | bytes 245792 | tf_op jit(solution)/shard_map/ppermute | solution.py:49
  49.9 5.8 collective-permute-done.6.refs_6_.refs_11_
  55.7 2.5 collective-permute-start.12
  58.2 5.3 collective-permute-done.14
  65.2 4.3 negate_select_fusion
  69.7 3.3 collective-permute-done.15
  74.5 4.4 collective-permute-done.12.refs_12_.refs_17_
  78.9 2.5 collective-permute-start.10
  84.8 4.6 collective-permute-done.11.refs_10_.refs_15_
  89.4 6.4 collective-permute-done.10.refs_8_.refs_13_
  96.9 11.2 %shard_map.257 = (bf16[1024,384]{1,0:T(8,128)(2,1)S(1)}, bf16[1024,128]{1,0:T(8,128)(2,1)S(1)}, bf16[1024,128]{1,0:T(8,128)(2,1)S(1)}, bf16[1024,384]{1,0:T(8,12...) custom-call(s32[3]{0:T(128)S(1)} %pad_add_fusion.refs_0_, ...), custom_call_target="tpu_custom_call" | custom-call | flops 1 | bytes 1 | tf_op jit(solution)/shard_map/pallas_call | solution.py:122
  116.4 2.4 shard_map.258
  127.3 15.9 %collective-permute-done.19.refs_2_ = bf16[256,1536]{1,0:T(8,128)(2,1)S(1)} collective-permute-done((bf16[256,1536]{1,0:T(8,128)(2,1)S(1)}, bf16[256,1536]{1,0:T(8,128)(2,1)S(1)}, u32[]{:S(2)}, u32[]{:S(2)}) %collective-permute-start.19) | collective-permute-done | bytes 786464 | tf_op jit(solution)/shard_map/ppermute | solution.py:49
  147.5 20.3 %collective-permute-done.23.refs_5_.refs_13_.refs_14_.refs_11_ = bf16[3,384,256]{2,1,0:T(8,128)(2,1)S(1)} collective-permute-done((bf16[3,384,256]{2,1,0:T(8,128)(2,1)S(1)}, bf16[3,384,256]{2,1,0:T(8,128)(2,1)S(1)}, u32[]{:S(2)}, u32[]{:S(2)}) %collective-permute-start.23) | collective-permute-done | bytes 589856 | tf_op jit(solution)/shard_map/ppermute | solution.py:49
  172.0 27.4 %collective-permute-done.31.refs_16_.refs_12_.refs_13_.refs_10_ = bf16[3,384,256]{2,1,0:T(8,128)(2,1)S(1)} collective-permute-done((bf16[3,384,256]{2,1,0:T(8,128)(2,1)S(1)}, bf16[3,384,256]{2,1,0:T(8,128)(2,1)S(1)}, u32[]{:S(2)}, u32[]{:S(2)}) %collective-permute-start.31) | collective-permute-done | bytes 589856 | tf_op jit(solution)/shard_map/ppermute | solution.py:49
  200.4 23.1 %collective-permute-done.30.refs_11_.refs_15_.refs_8_.refs_5_ = bf16[3,384,512]{2,1,0:T(8,128)(2,1)S(1)} collective-permute-done((bf16[3,384,512]{2,1,0:T(8,128)(2,1)S(1)}, bf16[3,384,512]{2,1,0:T(8,128)(2,1)S(1)}, u32[]{:S(2)}, u32[]{:S(2)}) %collective-permute-start.30) | collective-permute-done | bytes 1179680 | tf_op jit(solution)/shard_map/ppermute | solution.py:49
  226.4 29.8 %shard_map.262 = (bf16[2048,512]{1,0:T(8,128)(2,1)}, bf16[2048,512]{1,0:T(8,128)(2,1)}, bf16[2048,512]{1,0:T(8,128)(2,1)}, bf16[3,384,512]{2,1,0:T(8,128)(2,1)},...) custom-call(s32[3]{0:T(128)} %copy-done.72, ...), custom_call_target="tpu_custom_call" | custom-call | flops 1 | bytes 1 | tf_op jit(solution)/shard_map/pallas_call | solution.py:122
  257.5 33.8 %collective-permute-done.33.refs_11_.refs_16_.refs_12_.refs_9_ = bf16[3,384,256]{2,1,0:T(8,128)(2,1)S(1)} collective-permute-done((bf16[3,384,256]{2,1,0:T(8,128)(2,1)}, bf16[3,384,256]{2,1,0:T(8,128)(2,1)S(1)}, u32[]{:S(2)}, u32[]{:S(2)}) %collective-permute-start.33) | collective-permute-done | bytes 589856 | tf_op jit(solution)/shard_map/ppermute | solution.py:49
  292.1 19.7 %shard_map.263 = (bf16[2048,256]{1,0:T(8,128)(2,1)}, bf16[2048,256]{1,0:T(8,128)(2,1)}, bf16[2048,256]{1,0:T(8,128)(2,1)}, bf16[3,384,256]{2,1,0:T(8,128)(2,1)},...) custom-call(s32[3]{0:T(128)} %copy-done.72, ...), custom_call_target="tpu_custom_call" | custom-call | flops 1 | bytes 1 | tf_op jit(solution)/shard_map/pallas_call | solution.py:122
  312.1 24.1 %collective-permute-done.35.refs_11_.refs_16_.refs_13_ = bf16[3,384,384]{2,1,0:T(8,128)(2,1)S(1)} collective-permute-done((bf16[3,384,384]{2,1,0:T(8,128)(2,1)S(1)}, bf16[3,384,384]{2,1,0:T(8,128)(2,1)S(1)}, u32[]{:S(2)}, u32[]{:S(2)}) %collective-permute-start.35) | collective-permute-done | bytes 884768 | tf_op jit(solution)/shard_map/ppermute | solution.py:49
  337.2 18.2 %shard_map.264 = (bf16[2048,384]{1,0:T(8,128)(2,1)}, bf16[2048,384]{1,0:T(8,128)(2,1)}, bf16[2048,384]{1,0:T(8,128)(2,1)}) custom-call(s32[3]{0:T(128)} %copy-done.72, bf16[256,1536]{1,0:T(8,128)(2,1)} %copy-done.1, bf16[256,1536]{1,0:T(8,128)(2,1)} %copy-done.5, bf16[256,1536]{1,0:T(8,128)(2,1)} %copy-done.88, bf16[256,1536]{1,0:T(8,128)(2,1)} %copy-done.89, ...), custom_call_target="tpu_custom_call" | custom-call | flops 1 | bytes 1 | tf_op jit(solution)/shard_map/pallas_call | solution.py:122
  355.4 25.2 %shard_map.265 = (bf16[1024,1536]{1,0:T(8,128)(2,1)}, bf16[256,1536]{1,0:T(8,128)(2,1)}, bf16[256,1536]{1,0:T(8,128)(2,1)}, bf16[256,1536]{1,0:T(8,128)(2,1)}, bf16[256,1536]{1,0:T(8,128)(2,1)}) custom-call(s32[3]{0:T(128)} %copy-done.72, bf16[2048,512]{1,0:T(8,128)(2,1)} %get-tuple-element.158.refs_1_, bf16[2048,512]{1,0:T(8,128)(2,1)} %get-tuple-element.159.refs_2_, ...), custom_call_target="tpu_custom_call" | custom-call | flops 1 | bytes 1 | tf_op jit(solution)/shard_map/pallas_call | solution.py:122
  393.2 15.9 %shard_map.267 = (bf16[3,384,384]{2,1,0:T(8,128)(2,1)}, bf16[3,384,384]{2,1,0:T(8,128)(2,1)}, bf16[3,384,384]{2,1,0:T(8,128)(2,1)}, bf16[3,384,384]{2,1,0:T(8,128)(2,1)}) custom-call(s32[3]{0:T(128)} %copy-done.72, bf16[256,1536]{1,0:T(8,128)(2,1)} %copy-done.1, bf16[256,1536]{1,0:T(8,128)(2,1)} %copy-done.5, bf16[256,1536]{1,0:T(8,128)(2,1)} %copy-done.88, ...), custom_call_target="tpu_custom_call" | custom-call | flops 1 | bytes 1 | tf_op jit(solution)/shard_map/pallas_call | solution.py:122
  409.1 2.2 add_convert_fusion.8.refs_3_
  416.7 14.5 %shard_map.269 = (bf16[1024,1536]{1,0:T(8,128)(2,1)}, bf16[256,1536]{1,0:T(8,128)(2,1)}, bf16[256,1536]{1,0:T(8,128)(2,1)}, bf16[256,1536]{1,0:T(8,128)(2,1)}, bf16[256,1536]{1,0:T(8,128)(2,1)}) custom-call(s32[3]{0:T(128)} %copy-done.72, bf16[2048,512]{1,0:T(8,128)(2,1)} %get-tuple-element.152.refs_14_.refs_1_, ...), custom_call_target="tpu_custom_call" | custom-call | flops 1 | bytes 1 | tf_op jit(solution)/shard_map/pallas_call | solution.py:122
  443.5 15.9 %collective-permute-done.55.refs_3_.refs_8_ = bf16[256,1536]{1,0:T(8,128)(2,1)} collective-permute-done((bf16[256,1536]{1,0:T(8,128)(2,1)S(1)}, bf16[256,1536]{1,0:T(8,128)(2,1)}, u32[]{:S(2)}, u32[]{:S(2)}) %collective-permute-start.55) | collective-permute-done | bytes 786464 | tf_op jit(solution)/shard_map/ppermute | solution.py:49
  459.4 3.0 add_convert_fusion.1.refs_5_
  464.7 2.8 shard_map.271
  469.2 9.5 %collective-permute-done.58 = bf16[3,384,256]{2,1,0:T(8,128)(2,1)} collective-permute-done((bf16[3,384,256]{2,1,0:T(8,128)(2,1)}, bf16[3,384,256]{2,1,0:T(8,128)(2,1)}, u32[]{:S(2)}, u32[]{:S(2)}) %collective-permute-start.58) | collective-permute-done | bytes 589856 | tf_op jit(solution)/shard_map/ppermute | solution.py:49
  478.7 2.2 add_convert_fusion.7
  480.9 2.6 add_convert_fusion.5.refs_28_
  483.6 15.9 %shard_map.272 = (bf16[1024,640]{1,0:T(8,128)(2,1)}, f32[1,640]{1,0:T(1,128)S(1)}, f32[1,1536]{1,0:T(1,128)S(1)}, bf16[2,256,1536]{2,1,0:T(8,128)(2,1)}, bf16[25...) custom-call(s32[3]{0:T(128)S(1)} %copy-done.73, bf16[256,1536]{1,0:T(8,128)(2,1)S(1)} %get-tuple-element.188.refs_1_.refs_6_, ...), custom_call_target="tpu_custom_call" | custom-call | flops 1 | bytes 1 | tf_op jit(solution)/shard_map/pallas_call | solution.py:122
  511.5 7.1 %shard_map.273 = (bf16[192,1024]{1,0:T(8,128)(2,1)S(1)}, bf16[192,1024]{1,0:T(8,128)(2,1)S(1)}, bf16[192,1024]{1,0:T(8,128)(2,1)S(1)}, bf16[192,1024]{1,0:T(8,12...) custom-call(s32[3]{0:T(128)S(1)} %copy-done.73, ...), custom_call_target="tpu_custom_call" | custom-call | flops 1 | bytes 1 | tf_op jit(solution)/shard_map/pallas_call | solution.py:122
  522.7 2.6 collective-permute-done.67
  526.7 13.1 %collective-permute-done.68 = f32[40,128]{1,0:T(8,128)S(1)} collective-permute-done((f32[40,128]{1,0:T(8,128)S(1)}, f32[40,128]{1,0:T(8,128)S(1)}, u32[]{:S(2)}, u32[]{:S(2)}) %collective-permute-start.68) | collective-permute-done | bytes 20512 | tf_op jit(solution)/shard_map/ppermute | solution.py:49
  539.9 12.4 %collective-permute-done.69 = f32[40,128]{1,0:T(8,128)S(1)} collective-permute-done((f32[40,128]{1,0:T(8,128)S(1)}, f32[40,128]{1,0:T(8,128)S(1)}, u32[]{:S(2)}, u32[]{:S(2)}) %collective-permute-start.69) | collective-permute-done | bytes 20512 | tf_op jit(solution)/shard_map/ppermute | solution.py:49
  554.4 2.6 collective-permute-done.70
  560.0 12.4 %collective-permute-done.75 = bf16[192,1024]{1,0:T(8,128)(2,1)} collective-permute-done((bf16[192,1024]{1,0:T(8,128)(2,1)}, bf16[192,1024]{1,0:T(8,128)(2,1)}, u32[]{:S(2)}, u32[]{:S(2)}) %collective-permute-start.75) | collective-permute-done | bytes 393248 | tf_op jit(solution)/shard_map/ppermute | solution.py:49
  582.7 10.4 %collective-permute-done.52.refs_2_ = bf16[256,1536]{1,0:T(8,128)(2,1)S(1)} collective-permute-done((bf16[256,1536]{1,0:T(8,128)(2,1)}, bf16[256,1536]{1,0:T(8,128)(2,1)S(1)}, u32[]{:S(2)}, u32[]{:S(2)}) %collective-permute-start.52) | collective-permute-done | bytes 786464 | tf_op jit(solution)/shard_map/ppermute | solution.py:49
  594.0 7.4 %collective-permute-done.72 = bf16[192,1024]{1,0:T(8,128)(2,1)S(1)} collective-permute-done((bf16[192,1024]{1,0:T(8,128)(2,1)S(1)}, bf16[192,1024]{1,0:T(8,128)(2,1)S(1)}, u32[]{:S(2)}, u32[]{:S(2)}) %collective-permute-start.72) | collective-permute-done | bytes 393248 | tf_op jit(solution)/shard_map/ppermute | solution.py:49
  603.0 15.5 %collective-permute-done.76 = bf16[192,1024]{1,0:T(8,128)(2,1)S(1)} collective-permute-done((bf16[192,1024]{1,0:T(8,128)(2,1)S(1)}, bf16[192,1024]{1,0:T(8,128)(2,1)S(1)}, u32[]{:S(2)}, u32[]{:S(2)}) %collective-permute-start.76) | collective-permute-done | bytes 393248 | tf_op jit(solution)/shard_map/ppermute | solution.py:49
  625.8 5.6 collective-permute-done.77
  639.0 2.7 collective-permute-start.79
  643.6 5.1 collective-permute-done.80
  653.1 2.2 collective-permute-done.81.refs_4_
  655.3 9.1 %collective-permute-done.83.refs_6_ = bf16[3,192,384]{2,1,0:T(8,128)(2,1)S(1)} collective-permute-done((bf16[3,192,384]{2,1,0:T(8,128)(2,1)S(1)}, bf16[3,192,384]{2,1,0:T(8,128)(2,1)S(1)}, u32[]{:S(2)}, u32[]{:S(2)}) %collective-permute-start.83) | collective-permute-done | bytes 442400 | tf_op jit(solution)/shard_map/ppermute | solution.py:49
  664.4 3.8 shard_map.281
  (444 shorter events, 162.6 us)
Async XLA Ops:
  7.2 106.8 %all-gather.3.cloned.1.call-start = ((), (), s32[]{:S(2)}) async-start(), calls=%async_computation | async-start | bytes 1327104 | tf_op jit(solution)/shard_map/all_gather | solution.py:956
  7.9 218.5 %all-gather.5.cloned.1.call-start = ((), (), s32[]{:S(2)}) async-start(), calls=%async_computation.1 | async-start | bytes 7077888 | tf_op jit(solution)/shard_map/all_gather | solution.py:970
  21.0 24.5 %collective-permute-start.1 = (bf16[256,1536]{1,0:T(8,128)(2,1)S(1)}, bf16[256,1536]{1,0:T(8,128)(2,1)}, u32[]{:S(2)}, u32[]{:S(2)}) collective-permute-start(bf16[256,1536]{1,0:T(8,128)(2,1)S(1)} %shard_map.254.refs_1_.refs_5_), channel_id=1, source_target_pairs={{0,2},{1,3},{2,0},{3,1},{4,6},{5,7},{6,4},{7,5},{8,10},{9,11},{10,... | collective-permute-start | bytes 2359304 | tf_op jit(solution)/shard_map/ppermute | solution.py:49
  41.9 21.6 %collective-permute-start.14 = (bf16[3,192,256]{2,1,0:T(8,128)(2,1)}, bf16[3,192,256]{2,1,0:T(8,128)(2,1)}, u32[]{:S(2)}, u32[]{:S(2)}) collective-permute-start(bf16[3,192,256]{2,1,0:T(8,128)(2,1)} %get-tuple-element.129), channel_id=1, source_target_pairs={{0,4},{4,0},{8,12},{12,8},{16,20},{20,16},{24,28},{28,24},{1,5},{5... | collective-permute-start | bytes 884744 | tf_op jit(solution)/shard_map/ppermute | solution.py:49
  45.5 39.3 %collective-permute-start = (bf16[256,1536]{1,0:T(8,128)(2,1)S(1)}, bf16[256,1536]{1,0:T(8,128)(2,1)}, u32[]{:S(2)}, u32[]{:S(2)}) collective-permute-start(bf16[256,1536]{1,0:T(8,128)(2,1)S(1)} %shard_map.254.refs_1_.refs_5_), channel_id=1, source_target_pairs={{0,1},{1,0},{2,3},{3,2},{4,5},{5,4},{6,7},{7,6},{8,9},{9,8},{10,11... | collective-permute-start | bytes 2359304 | tf_op jit(solution)/shard_map/ppermute | solution.py:49
  45.5 27.5 %collective-permute-start.15 = (bf16[3,192,384]{2,1,0:T(8,128)(2,1)}, bf16[3,192,384]{2,1,0:T(8,128)(2,1)}, u32[]{:S(2)}, u32[]{:S(2)}) collective-permute-start(bf16[3,192,384]{2,1,0:T(8,128)(2,1)} %get-tuple-element.132), channel_id=1, source_target_pairs={{0,4},{4,0},{8,12},{12,8},{16,20},{20,16},{24,28},{28,24},{1,5},{5... | collective-permute-start | bytes 1327112 | tf_op jit(solution)/shard_map/ppermute | solution.py:49
  48.7 47.1 %collective-permute-start.2 = (bf16[256,1536]{1,0:T(8,128)(2,1)}, bf16[256,1536]{1,0:T(8,128)(2,1)}, u32[]{:S(2)}, u32[]{:S(2)}) collective-permute-start(bf16[256,1536]{1,0:T(8,128)(2,1)} %collective-permute-done.1.refs_3_.refs_7_), channel_id=1, source_target_pairs={{0,1},{1,0},{2,3},{3,2},{4,5},{5,4},{6,7},{7,6},{8,9},{9,8},{10,11... | collective-permute-start | bytes 2359304 | tf_op jit(solution)/shard_map/ppermute | solution.py:49
  55.7 23.2 %collective-permute-start.12 = (bf16[192,640]{1,0:T(8,128)(2,1)}, bf16[192,640]{1,0:T(8,128)(2,1)}, u32[]{:S(2)}, u32[]{:S(2)}) collective-permute-start(bf16[192,640]{1,0:T(8,128)(2,1)} %collective-permute-done.7.refs_11_.refs_16_), channel_id=1, source_target_pairs={{0,4},{4,0},{8,12},{12,8},{16,20},{20,16},{24,28},{28,24},{1,5},{5... | collective-permute-start | bytes 737288 | tf_op jit(solution)/shard_map/ppermute | solution.py:49
  63.5 55.9 %collective-permute-start.18 = (bf16[3,384,512]{2,1,0:T(8,128)(2,1)S(1)}, bf16[3,384,512]{2,1,0:T(8,128)(2,1)}, u32[]{:S(2)}, u32[]{:S(2)}) collective-permute-start(bf16[3,384,512]{2,1,0:T(8,128)(2,1)S(1)} %constant_dynamic-update-slice_fusion.9.refs_18_.refs_10_.refs_7_.refs_4_), channel_id=1, source_target_pairs={{0,8},{4,12},{8,16},{12,20},{16,24},{20,28},{24,0},{28,4},{1,9},{5... | collective-permute-start | bytes 3538952 | tf_op jit(solution)/shard_map/ppermute | solution.py:49
  124.3 43.5 %collective-permute-start.22 = (bf16[3,384,512]{2,1,0:T(8,128)(2,1)}, bf16[3,384,512]{2,1,0:T(8,128)(2,1)S(1)}, u32[]{:S(2)}, u32[]{:S(2)}) collective-permute-start(bf16[3,384,512]{2,1,0:T(8,128)(2,1)} %collective-permute-done.18.refs_4_.refs_13_.refs_10_.refs_7_), channel_id=1, source_target_pairs={{0,8},{4,12},{8,16},{12,20},{16,24},{20,28},{24,0},{28,4},{1,9},{5... | collective-permute-start | bytes 3538952 | tf_op jit(solution)/shard_map/ppermute | solution.py:49
  125.8 42.0 %collective-permute-start.23 = (bf16[3,384,256]{2,1,0:T(8,128)(2,1)S(1)}, bf16[3,384,256]{2,1,0:T(8,128)(2,1)S(1)}, u32[]{:S(2)}, u32[]{:S(2)}) collective-permute-start(bf16[3,384,256]{2,1,0:T(8,128)(2,1)S(1)} %constant_dynamic-update-slice_fusion.8.refs_19_.refs_5_.refs_10_.refs_11_.refs_8_), channel_id=1, source_target_pairs={{0,8},{4,12},{8,16},{12,20},{16,24},{20,28},{24,0},{28,4},{1,9},{5... | collective-permute-start | bytes 1769480 | tf_op jit(solution)/shard_map/ppermute | solution.py:49
  143.9 23.9 %collective-permute-start.20 = (bf16[128,1536]{1,0:T(8,128)(2,1)S(1)}, bf16[128,1536]{1,0:T(8,128)(2,1)S(1)}, u32[]{:S(2)}, u32[]{:S(2)}) collective-permute-start(bf16[128,1536]{1,0:T(8,128)(2,1)S(1)} %get-tuple-element.142.refs_0_), channel_id=1, source_target_pairs={{0,4},{4,0},{8,12},{12,8},{16,20},{20,16},{24,28},{28,24},{1,5},{5... | collective-permute-start | bytes 1179656 | tf_op jit(solution)/shard_map/ppermute | solution.py:49
  145.4 22.4 %collective-permute-start.21 = (bf16[128,1536]{1,0:T(8,128)(2,1)S(1)}, bf16[128,1536]{1,0:T(8,128)(2,1)S(1)}, u32[]{:S(2)}, u32[]{:S(2)}) collective-permute-start(bf16[128,1536]{1,0:T(8,128)(2,1)S(1)} %get-tuple-element.143.refs_2_), channel_id=1, source_target_pairs={{0,2},{1,3},{2,0},{3,1},{4,6},{5,7},{6,4},{7,5},{8,10},{9,11},{10,... | collective-permute-start | bytes 1179656 | tf_op jit(solution)/shard_map/ppermute | solution.py:49
  146.0 53.4 %collective-permute-start.32 = (bf16[3,384,384]{2,1,0:T(8,128)(2,1)S(1)}, bf16[3,384,384]{2,1,0:T(8,128)(2,1)S(1)}, u32[]{:S(2)}, u32[]{:S(2)}) collective-permute-start(bf16[3,384,384]{2,1,0:T(8,128)(2,1)S(1)} %constant_dynamic-update-slice_fusion.7.refs_20_.refs_6_.refs_10_.refs_15_.refs_12_), channel_id=1, source_target_pairs={{0,8},{4,12},{8,16},{12,20},{16,24},{20,28},{24,0},{28,4},{1,9},{5... | collective-permute-start | bytes 2654216 | tf_op jit(solution)/shard_map/ppermute | solution.py:49
  168.0 31.9 %collective-permute-start.24 = (bf16[256,1536]{1,0:T(8,128)(2,1)S(1)}, bf16[256,1536]{1,0:T(8,128)(2,1)S(1)}, u32[]{:S(2)}, u32[]{:S(2)}) collective-permute-start(bf16[256,1536]{1,0:T(8,128)(2,1)S(1)} %get-tuple-element.146.refs_1_.refs_14_), channel_id=1, source_target_pairs={{0,2},{1,3},{2,0},{3,1},{4,6},{5,7},{6,4},{7,5},{8,10},{9,11},{10,... | collective-permute-start | bytes 2359304 | tf_op jit(solution)/shard_map/ppermute | solution.py:49
  169.1 30.9 %collective-permute-start.25 = (bf16[256,1536]{1,0:T(8,128)(2,1)S(1)}, bf16[256,1536]{1,0:T(8,128)(2,1)S(1)}, u32[]{:S(2)}, u32[]{:S(2)}) collective-permute-start(bf16[256,1536]{1,0:T(8,128)(2,1)S(1)} %get-tuple-element.147.refs_2_), channel_id=1, source_target_pairs={{0,4},{4,0},{8,12},{12,8},{16,20},{20,16},{24,28},{28,24},{1,5},{5... | collective-permute-start | bytes 2359304 | tf_op jit(solution)/shard_map/ppermute | solution.py:49
  170.5 28.9 %collective-permute-start.31 = (bf16[3,384,256]{2,1,0:T(8,128)(2,1)S(1)}, bf16[3,384,256]{2,1,0:T(8,128)(2,1)S(1)}, u32[]{:S(2)}, u32[]{:S(2)}) collective-permute-start(bf16[3,384,256]{2,1,0:T(8,128)(2,1)S(1)} %collective-permute-done.23.refs_5_.refs_13_.refs_14_.refs_11_), channel_id=1, source_target_pairs={{0,8},{4,12},{8,16},{12,20},{16,24},{20,28},{24,0},{28,4},{1,9},{5... | collective-permute-start | bytes 1769480 | tf_op jit(solution)/shard_map/ppermute | solution.py:49
  170.5 53.0 %collective-permute-start.30 = (bf16[3,384,512]{2,1,0:T(8,128)(2,1)S(1)}, bf16[3,384,512]{2,1,0:T(8,128)(2,1)S(1)}, u32[]{:S(2)}, u32[]{:S(2)}) collective-permute-start(bf16[3,384,512]{2,1,0:T(8,128)(2,1)S(1)} %collective-permute-done.22.refs_4_.refs_12_.refs_9_.refs_6_), channel_id=1, source_target_pairs={{0,8},{4,12},{8,16},{12,20},{16,24},{20,28},{24,0},{28,4},{1,9},{5... | collective-permute-start | bytes 3538952 | tf_op jit(solution)/shard_map/ppermute | solution.py:49
  199.4 24.2 %collective-permute-start.26 = (bf16[256,1536]{1,0:T(8,128)(2,1)S(1)}, bf16[256,1536]{1,0:T(8,128)(2,1)S(1)}, u32[]{:S(2)}, u32[]{:S(2)}) collective-permute-start(bf16[256,1536]{1,0:T(8,128)(2,1)S(1)} %get-tuple-element.146.refs_1_.refs_14_), channel_id=1, source_target_pairs={{0,1},{1,0},{2,3},{3,2},{4,5},{5,4},{6,7},{7,6},{8,9},{9,8},{10,11... | collective-permute-start | bytes 2359304 | tf_op jit(solution)/shard_map/ppermute | solution.py:49
  199.4 24.2 %collective-permute-start.27 = (bf16[256,1536]{1,0:T(8,128)(2,1)S(1)}, bf16[256,1536]{1,0:T(8,128)(2,1)S(1)}, u32[]{:S(2)}, u32[]{:S(2)}) collective-permute-start(bf16[256,1536]{1,0:T(8,128)(2,1)S(1)} %get-tuple-element.147.refs_2_), channel_id=1, source_target_pairs={{0,1},{1,0},{2,3},{3,2},{4,5},{5,4},{6,7},{7,6},{8,9},{9,8},{10,11... | collective-permute-start | bytes 2359304 | tf_op jit(solution)/shard_map/ppermute | solution.py:49
  199.9 24.7 %collective-permute-start.28 = (bf16[256,1536]{1,0:T(8,128)(2,1)S(1)}, bf16[256,1536]{1,0:T(8,128)(2,1)S(1)}, u32[]{:S(2)}, u32[]{:S(2)}) collective-permute-start(bf16[256,1536]{1,0:T(8,128)(2,1)S(1)} %collective-permute-done.24.refs_3_), channel_id=1, source_target_pairs={{0,1},{1,0},{2,3},{3,2},{4,5},{5,4},{6,7},{7,6},{8,9},{9,8},{10,11... | collective-permute-start | bytes 2359304 | tf_op jit(solution)/shard_map/ppermute | solution.py:49
  200.0 26.4 %collective-permute-start.29 = (bf16[256,1536]{1,0:T(8,128)(2,1)S(1)}, bf16[256,1536]{1,0:T(8,128)(2,1)}, u32[]{:S(2)}, u32[]{:S(2)}) collective-permute-start(bf16[256,1536]{1,0:T(8,128)(2,1)S(1)} %collective-permute-done.25.refs_4_), channel_id=1, source_target_pairs={{0,1},{1,0},{2,3},{3,2},{4,5},{5,4},{6,7},{7,6},{8,9},{9,8},{10,11... | collective-permute-start | bytes 2359304 | tf_op jit(solution)/shard_map/ppermute | solution.py:49
  256.3 55.5 %collective-permute-start.34 = (bf16[3,384,384]{2,1,0:T(8,128)(2,1)S(1)}, bf16[3,384,384]{2,1,0:T(8,128)(2,1)S(1)}, u32[]{:S(2)}, u32[]{:S(2)}) collective-permute-start(bf16[3,384,384]{2,1,0:T(8,128)(2,1)S(1)} %copy-done.85), channel_id=1, source_target_pairs={{0,8},{4,12},{8,16},{12,20},{16,24},{20,28},{24,0},{28,4},{1,9},{5... | collective-permute-start | bytes 2654216 | tf_op jit(solution)/shard_map/ppermute | solution.py:49
  256.3 35.0 %collective-permute-start.33 = (bf16[3,384,256]{2,1,0:T(8,128)(2,1)}, bf16[3,384,256]{2,1,0:T(8,128)(2,1)S(1)}, u32[]{:S(2)}, u32[]{:S(2)}) collective-permute-start(bf16[3,384,256]{2,1,0:T(8,128)(2,1)} %copy-done.86), channel_id=1, source_target_pairs={{0,8},{4,12},{8,16},{12,20},{16,24},{20,28},{24,0},{28,4},{1,9},{5... | collective-permute-start | bytes 1769480 | tf_op jit(solution)/shard_map/ppermute | solution.py:49
  311.8 24.4 %collective-permute-start.35 = (bf16[3,384,384]{2,1,0:T(8,128)(2,1)S(1)}, bf16[3,384,384]{2,1,0:T(8,128)(2,1)S(1)}, u32[]{:S(2)}, u32[]{:S(2)}) collective-permute-start(bf16[3,384,384]{2,1,0:T(8,128)(2,1)S(1)} %collective-permute-done.34.refs_12_.refs_17_.refs_14_), channel_id=1, source_target_pairs={{0,8},{4,12},{8,16},{12,20},{16,24},{20,28},{24,0},{28,4},{1,9},{5... | collective-permute-start | bytes 2654216 | tf_op jit(solution)/shard_map/ppermute | solution.py:49
  311.9 69.8 %collective-permute-start.40 = (bf16[3,384,512]{2,1,0:T(8,128)(2,1)}, bf16[3,384,512]{2,1,0:T(8,128)(2,1)S(1)}, u32[]{:S(2)}, u32[]{:S(2)}) collective-permute-start(bf16[3,384,512]{2,1,0:T(8,128)(2,1)} %get-tuple-element.169), channel_id=1, source_target_pairs={{0,8},{4,12},{8,16},{12,20},{16,24},{20,28},{24,0},{28,4},{1,9},{5... | collective-permute-start | bytes 3538952 | tf_op jit(solution)/shard_map/ppermute | solution.py:49
  381.7 27.3 %collective-permute-start.43 = (bf16[3,384,256]{2,1,0:T(8,128)(2,1)}, bf16[3,384,256]{2,1,0:T(8,128)(2,1)}, u32[]{:S(2)}, u32[]{:S(2)}) collective-permute-start(bf16[3,384,256]{2,1,0:T(8,128)(2,1)} %get-tuple-element.175), channel_id=1, source_target_pairs={{0,8},{4,12},{8,16},{12,20},{16,24},{20,28},{24,0},{28,4},{1,9},{5... | collective-permute-start | bytes 1769480 | tf_op jit(solution)/shard_map/ppermute | solution.py:49
  389.7 21.6 %collective-permute-start.41 = (bf16[256,1536]{1,0:T(8,128)(2,1)S(1)}, bf16[256,1536]{1,0:T(8,128)(2,1)S(1)}, u32[]{:S(2)}, u32[]{:S(2)}) collective-permute-start(bf16[256,1536]{1,0:T(8,128)(2,1)S(1)} %get-tuple-element.173.refs_13_), channel_id=1, source_target_pairs={{0,2},{1,3},{2,0},{3,1},{4,6},{5,7},{6,4},{7,5},{8,10},{9,11},{10,... | collective-permute-start | bytes 2359304 | tf_op jit(solution)/shard_map/ppermute | solution.py:49
  392.8 48.2 %collective-permute-start.48 = (bf16[3,384,512]{2,1,0:T(8,128)(2,1)S(1)}, bf16[3,384,512]{2,1,0:T(8,128)(2,1)}, u32[]{:S(2)}, u32[]{:S(2)}) collective-permute-start(bf16[3,384,512]{2,1,0:T(8,128)(2,1)S(1)} %add_convert_fusion.2.refs_5_), channel_id=1, source_target_pairs={{0,8},{4,12},{8,16},{12,20},{16,24},{20,28},{24,0},{28,4},{1,9},{5... | collective-permute-start | bytes 3538952 | tf_op jit(solution)/shard_map/ppermute | solution.py:49
  439.4 20.0 %collective-permute-start.55 = (bf16[256,1536]{1,0:T(8,128)(2,1)S(1)}, bf16[256,1536]{1,0:T(8,128)(2,1)}, u32[]{:S(2)}, u32[]{:S(2)}) collective-permute-start(bf16[256,1536]{1,0:T(8,128)(2,1)S(1)} %get-tuple-element.188.refs_1_.refs_6_), channel_id=1, source_target_pairs={{0,2},{1,3},{2,0},{3,1},{4,6},{5,7},{6,4},{7,5},{8,10},{9,11},{10,... | collective-permute-start | bytes 2359304 | tf_op jit(solution)/shard_map/ppermute | solution.py:49
  441.0 21.5 %collective-permute-start.47 = (bf16[256,1536]{1,0:T(8,128)(2,1)}, bf16[256,1536]{1,0:T(8,128)(2,1)S(1)}, u32[]{:S(2)}, u32[]{:S(2)}) collective-permute-start(bf16[256,1536]{1,0:T(8,128)(2,1)} %get-tuple-element.184), channel_id=1, source_target_pairs={{0,1},{1,0},{2,3},{3,2},{4,5},{5,4},{6,7},{7,6},{8,9},{9,8},{10,11... | collective-permute-start | bytes 2359304 | tf_op jit(solution)/shard_map/ppermute | solution.py:49
  442.0 38.9 %collective-permute-start.57 = (bf16[3,384,384]{2,1,0:T(8,128)(2,1)}, bf16[3,384,384]{2,1,0:T(8,128)(2,1)}, u32[]{:S(2)}, u32[]{:S(2)}) collective-permute-start(bf16[3,384,384]{2,1,0:T(8,128)(2,1)} %get-tuple-element.177), channel_id=1, source_target_pairs={{0,8},{4,12},{8,16},{12,20},{16,24},{20,28},{24,0},{28,4},{1,9},{5... | collective-permute-start | bytes 2654216 | tf_op jit(solution)/shard_map/ppermute | solution.py:49
  442.9 35.8 %collective-permute-start.58 = (bf16[3,384,256]{2,1,0:T(8,128)(2,1)}, bf16[3,384,256]{2,1,0:T(8,128)(2,1)}, u32[]{:S(2)}, u32[]{:S(2)}) collective-permute-start(bf16[3,384,256]{2,1,0:T(8,128)(2,1)} %add_convert_fusion.8.refs_3_), channel_id=1, source_target_pairs={{0,8},{4,12},{8,16},{12,20},{16,24},{20,28},{24,0},{28,4},{1,9},{5... | collective-permute-start | bytes 1769480 | tf_op jit(solution)/shard_map/ppermute | solution.py:49
  443.4 40.1 %collective-permute-start.54 = (bf16[256,1536]{1,0:T(8,128)(2,1)S(1)}, bf16[256,1536]{1,0:T(8,128)(2,1)S(1)}, u32[]{:S(2)}, u32[]{:S(2)}) collective-permute-start(bf16[256,1536]{1,0:T(8,128)(2,1)S(1)} %get-tuple-element.188.refs_1_.refs_6_), channel_id=1, source_target_pairs={{0,1},{1,0},{2,3},{3,2},{4,5},{5,4},{6,7},{7,6},{8,9},{9,8},{10,11... | collective-permute-start | bytes 2359304 | tf_op jit(solution)/shard_map/ppermute | solution.py:49
  459.4 24.1 %collective-permute-start.56 = (bf16[256,1536]{1,0:T(8,128)(2,1)}, bf16[256,1536]{1,0:T(8,128)(2,1)S(1)}, u32[]{:S(2)}, u32[]{:S(2)}) collective-permute-start(bf16[256,1536]{1,0:T(8,128)(2,1)} %collective-permute-done.55.refs_3_.refs_8_), channel_id=1, source_target_pairs={{0,1},{1,0},{2,3},{3,2},{4,5},{5,4},{6,7},{7,6},{8,9},{9,8},{10,11... | collective-permute-start | bytes 2359304 | tf_op jit(solution)/shard_map/ppermute | solution.py:49
  519.4 37.6 %collective-permute-start.74 = (bf16[192,1024]{1,0:T(8,128)(2,1)S(1)}, bf16[192,1024]{1,0:T(8,128)(2,1)S(1)}, u32[]{:S(2)}, u32[]{:S(2)}) collective-permute-start(bf16[192,1024]{1,0:T(8,128)(2,1)S(1)} %get-tuple-element.230), channel_id=1, source_target_pairs={{0,4},{4,0},{8,12},{12,8},{16,20},{20,16},{24,28},{28,24},{1,5},{5... | collective-permute-start | bytes 1179656 | tf_op jit(solution)/shard_map/ppermute | solution.py:49
  522.0 53.1 %collective-permute-start.53 = (bf16[3,384,512]{2,1,0:T(8,128)(2,1)}, bf16[3,384,512]{2,1,0:T(8,128)(2,1)}, u32[]{:S(2)}, u32[]{:S(2)}) collective-permute-start(bf16[3,384,512]{2,1,0:T(8,128)(2,1)} %add_convert_fusion.1.refs_5_), channel_id=1, source_target_pairs={{0,8},{4,12},{8,16},{12,20},{16,24},{20,28},{24,0},{28,4},{1,9},{5... | collective-permute-start | bytes 3538952 | tf_op jit(solution)/shard_map/ppermute | solution.py:49
  522.0 36.4 %collective-permute-start.73 = (bf16[192,1024]{1,0:T(8,128)(2,1)S(1)}, bf16[192,1024]{1,0:T(8,128)(2,1)S(1)}, u32[]{:S(2)}, u32[]{:S(2)}) collective-permute-start(bf16[192,1024]{1,0:T(8,128)(2,1)S(1)} %get-tuple-element.228), channel_id=1, source_target_pairs={{0,4},{4,0},{8,12},{12,8},{16,20},{20,16},{24,28},{28,24},{1,5},{5... | collective-permute-start | bytes 1179656 | tf_op jit(solution)/shard_map/ppermute | solution.py:49
  552.8 22.3 %collective-permute-start.51 = (bf16[256,1536]{1,0:T(8,128)(2,1)}, bf16[256,1536]{1,0:T(8,128)(2,1)S(1)}, u32[]{:S(2)}, u32[]{:S(2)}) collective-permute-start(bf16[256,1536]{1,0:T(8,128)(2,1)} %get-tuple-element.191), channel_id=1, source_target_pairs={{0,2},{1,3},{2,0},{3,1},{4,6},{5,7},{6,4},{7,5},{8,10},{9,11},{10,... | collective-permute-start | bytes 2359304 | tf_op jit(solution)/shard_map/ppermute | solution.py:49
  572.3 20.7 %collective-permute-start.52 = (bf16[256,1536]{1,0:T(8,128)(2,1)}, bf16[256,1536]{1,0:T(8,128)(2,1)S(1)}, u32[]{:S(2)}, u32[]{:S(2)}) collective-permute-start(bf16[256,1536]{1,0:T(8,128)(2,1)} %copy-done.78), channel_id=1, source_target_pairs={{0,4},{4,0},{8,12},{12,8},{16,20},{20,16},{24,28},{28,24},{1,5},{5... | collective-permute-start | bytes 2359304 | tf_op jit(solution)/shard_map/ppermute | solution.py:49
  575.1 43.7 %collective-permute-start.65 = (bf16[3,384,256]{2,1,0:T(8,128)(2,1)S(1)}, bf16[3,384,256]{2,1,0:T(8,128)(2,1)S(1)}, u32[]{:S(2)}, u32[]{:S(2)}) collective-permute-start(bf16[3,384,256]{2,1,0:T(8,128)(2,1)S(1)} %copy-done.100), channel_id=1, source_target_pairs={{0,8},{4,12},{8,16},{12,20},{16,24},{20,28},{24,0},{28,4},{1,9},{5... | collective-permute-start | bytes 1769480 | tf_op jit(solution)/shard_map/ppermute | solution.py:49
  575.2 47.9 %collective-permute-start.64 = (bf16[3,384,384]{2,1,0:T(8,128)(2,1)}, bf16[3,384,384]{2,1,0:T(8,128)(2,1)S(1)}, u32[]{:S(2)}, u32[]{:S(2)}) collective-permute-start(bf16[3,384,384]{2,1,0:T(8,128)(2,1)} %add_convert_fusion.5.refs_28_), channel_id=1, source_target_pairs={{0,8},{4,12},{8,16},{12,20},{16,24},{20,28},{24,0},{28,4},{1,9},{5... | collective-permute-start | bytes 2654216 | tf_op jit(solution)/shard_map/ppermute | solution.py:49
  575.3 26.2 %collective-permute-start.72 = (bf16[192,1024]{1,0:T(8,128)(2,1)S(1)}, bf16[192,1024]{1,0:T(8,128)(2,1)S(1)}, u32[]{:S(2)}, u32[]{:S(2)}) collective-permute-start(bf16[192,1024]{1,0:T(8,128)(2,1)S(1)} %copy-done.82), channel_id=1, source_target_pairs={{0,4},{4,0},{8,12},{12,8},{16,20},{20,16},{24,28},{28,24},{1,5},{5... | collective-permute-start | bytes 1179656 | tf_op jit(solution)/shard_map/ppermute | solution.py:49
  576.7 41.9 %collective-permute-start.76 = (bf16[192,1024]{1,0:T(8,128)(2,1)S(1)}, bf16[192,1024]{1,0:T(8,128)(2,1)S(1)}, u32[]{:S(2)}, u32[]{:S(2)}) collective-permute-start(bf16[192,1024]{1,0:T(8,128)(2,1)S(1)} %add_convert_fusion.11), channel_id=1, source_target_pairs={{0,8},{4,12},{8,16},{12,20},{16,24},{20,28},{24,0},{28,4},{1,9},{5... | collective-permute-start | bytes 1179656 | tf_op jit(solution)/shard_map/ppermute | solution.py:49
  593.0 32.7 %collective-permute-start.71 = (bf16[192,1024]{1,0:T(8,128)(2,1)S(1)}, bf16[192,1024]{1,0:T(8,128)(2,1)S(1)}, u32[]{:S(2)}, u32[]{:S(2)}) collective-permute-start(bf16[192,1024]{1,0:T(8,128)(2,1)S(1)} %copy-done.80), channel_id=1, source_target_pairs={{0,4},{4,0},{8,12},{12,8},{16,20},{20,16},{24,28},{28,24},{1,5},{5... | collective-permute-start | bytes 1179656 | tf_op jit(solution)/shard_map/ppermute | solution.py:49
  601.5 31.1 %collective-permute-start.63 = (bf16[256,1536]{1,0:T(8,128)(2,1)S(1)}, bf16[256,1536]{1,0:T(8,128)(2,1)S(1)}, u32[]{:S(2)}, u32[]{:S(2)}) collective-permute-start(bf16[256,1536]{1,0:T(8,128)(2,1)S(1)} %get-tuple-element.210), channel_id=1, source_target_pairs={{0,2},{1,3},{2,0},{3,1},{4,6},{5,7},{6,4},{7,5},{8,10},{9,11},{10,... | collective-permute-start | bytes 2359304 | tf_op jit(solution)/shard_map/ppermute | solution.py:49
  625.8 22.9 %collective-permute-start.80 = (bf16[3,384,384]{2,1,0:T(8,128)(2,1)}, bf16[3,384,384]{2,1,0:T(8,128)(2,1)}, u32[]{:S(2)}, u32[]{:S(2)}) collective-permute-start(bf16[3,384,384]{2,1,0:T(8,128)(2,1)} %add_convert_fusion.4.refs_5_), channel_id=1, source_target_pairs={{0,8},{4,12},{8,16},{12,20},{16,24},{20,28},{24,0},{28,4},{1,9},{5... | collective-permute-start | bytes 2654216 | tf_op jit(solution)/shard_map/ppermute | solution.py:49
  632.6 20.6 %collective-permute-start.82 = (bf16[3,192,256]{2,1,0:T(8,128)(2,1)}, bf16[3,192,256]{2,1,0:T(8,128)(2,1)}, u32[]{:S(2)}, u32[]{:S(2)}) collective-permute-start(bf16[3,192,256]{2,1,0:T(8,128)(2,1)} %shard_map.279), channel_id=1, source_target_pairs={{0,4},{4,0},{8,12},{12,8},{16,20},{20,16},{24,28},{28,24},{1,5},{5... | collective-permute-start | bytes 884744 | tf_op jit(solution)/shard_map/ppermute | solution.py:49
  (148 other events, 1859.9 us)
Sparse Core Ops, SparseCore 0:
  10.2 55.3 all-gather.2
  67.4 53.6 all-gather.4

commit v2 on v1

v2 whole, which is shorter than its diff:
```python
import jax
import jax.numpy as jnp
from jax import lax
from jax.experimental import pallas as pl
from jax.experimental.pallas import tpu as pltpu
from jax.sharding import PartitionSpec as P

HEADS = 12
KV_HEADS = 2
HD = 128


eps_norm = 1e-06
rope_base = 1000000.0
masked = -1e30
low = jnp.bfloat16
wide = jnp.float32


def positions_of(segment):
    row_index = jnp.arange(segment.shape[0], dtype=jnp.int32)
    before = jnp.concatenate([segment[:1] - 1, segment[:-1]])
    starts = jnp.where(segment != before, row_index, 0)
    return row_index - lax.cummax(starts, axis=0)


def angles_of(segment, head_width):
    position = positions_of(segment).astype(jnp.float32)
    freqs = rope_base ** (-(jnp.arange(head_width // 2, dtype=jnp.float32) * 2.0) / head_width)
    angle = position[:, None] * freqs[None, :]
    angle = jnp.concatenate([angle, angle], axis=1)
    return (jnp.cos(angle), jnp.sin(angle))


def dot_nn(left, right):
    return jnp.dot(left, right, preferred_element_type=wide)


def dot_nt(left, right):
    return lax.dot_general(left, right, (((1,), (1,)), ((), ())), preferred_element_type=wide)


def dot_tn(left, right):
    return lax.dot_general(left, right, (((0,), (0,)), ((), ())), preferred_element_type=wide)


def moved(block, axis, target):
    route = [(index, target(index)) for index in range(lax.axis_size(axis))]
    return lax.ppermute(block, axis, route)


def across_x(block):
    return moved(block, "dp", lambda index: index ^ 1)


def across_y(block):
    return moved(block, "tensor", lambda index: index ^ 2)


def across_core(block):
    return moved(block, "tensor", lambda index: index ^ 1)


def across_both(block):
    return moved(block, "tensor", lambda index: index ^ 3)


def up_line(block):
    count = lax.axis_size("dp")
    return moved(block, "dp", lambda index: (index + 2) % count)


def in_order(first, second, rank, axis):
    return jnp.where(
        rank == 0, jnp.stack([first, second], axis), jnp.stack([second, first], axis)
    )


def pick(values, rank, axis):
    return lax.dynamic_index_in_dim(values, rank, axis, keepdims=False)


def stage(work, *args):
    kinds = jax.eval_shape(work, *args)
    empty = lambda *_: jax.tree.map(lambda kind: jnp.zeros(kind.shape, kind.dtype), kinds)
    return lax.cond(lax.axis_index("tensor") >= 0, work, empty, *args)


def all_sum(vector):
    total = vector
    for axis in ("tensor", "dp"):
        for bit in range(lax.axis_size(axis).bit_length() - 1):
            total = total + moved(total, axis, lambda index: index ^ (1 << bit))
    return total


def cuts_of(columns):
    pieces = [(first, 256) for first in range(0, columns // 512 * 512, 512)]
    if columns % 512:
        pieces.append((columns // 512 * 512, columns % 512 // 2))
    return [pieces[:2] + pieces[4:], pieces[2:4]]


def size_of(cut):
    return -(-sum(size for _, size in cut) // 128) * 128


anywhere = pl.BlockSpec(memory_space=pl.ANY)
in_vmem = pl.BlockSpec(memory_space=pltpu.VMEM)
in_smem = pl.BlockSpec(memory_space=pltpu.SMEM)


def shaped(shape, kind=low):
    return jax.ShapeDtypeStruct(tuple(shape), kind)


def call(kernel, args, specs, outs, scratch=(), tokens=(), out_specs=None, room=16):
    tokens = list(tokens)

    def body(*refs):
        kernel(*refs[: len(args)], *refs[len(args) + len(tokens) :])

    return pl.pallas_call(
        body,
        out_shape=outs,
        in_specs=list(specs) + [anywhere] * len(tokens),
        out_specs=[in_vmem] * len(outs) if out_specs is None else out_specs,
        scratch_shapes=list(scratch),
        compiler_params=pltpu.CompilerParams(vmem_limit_bytes=room * 2**20),
        cost_estimate=pl.CostEstimate(flops=2 * 10**11, bytes_accessed=1, transcendentals=0),
    )(*args, *tokens)


def start_rows(sources, target, offsets, sems):
    copies = []
    for index, (source, offset) in enumerate(zip(sources, offsets)):
        size = source.shape[0]
        place = pl.ds(pl.multiple_of(offset, size), size)
        copies.append(pltpu.make_async_copy(source, target.at[place], sems.at[index]))
        copies[-1].start()
    return copies


def dp_offsets(ranks, count, size):
    return [
        (lax.rem(ranks[0] // 2 + slot // 2, count // 2) * 2 + (lax.rem(ranks[0], 2) ^ slot % 2)) * size
        for slot in range(count)
    ]


def tensor_offsets(ranks, count, size):
    return [(ranks[1] ^ slot) * size for slot in range(count)]


def pack(ranks, matrices, cuts, tokens=()):
    share = matrices[0].shape[0]

    def kernel(ranks_ref, gate_ref, up_ref, down_ref, *outs):
        rank = lax.rem(ranks_ref[0], 2)
        for index, cut in enumerate(cuts):
            sent_ref, block_ref = outs[2 * index : 2 * index + 2]
            begin = 0
            for first, size in cut:
                here = slice(begin, begin + size)
                for matrix, source in enumerate((gate_ref, up_ref, down_ref)):
                    halves = [
                        source[:, first + which * size : first + (which + 1) * size]
                        for which in range(2)
                    ]
                    sent_ref[matrix, :, here] = jnp.where(rank == 0, halves[1], halves[0])
                    mine = jnp.where(rank == 0, halves[0], halves[1])
                    block_ref[matrix, :share, here] = mine
                    block_ref[matrix, share:, here] = mine
                begin += size
            if begin < sent_ref.shape[2]:
                for out in (sent_ref, block_ref):
                    rest = out.shape[2] - begin
                    out[:, :, begin:] = jnp.zeros((3, out.shape[1], rest), low)

    outs = []
    for cut in cuts:
        outs += [shaped((3, share, size_of(cut))), shaped((3, 2 * share, size_of(cut)))]
    return call(
        kernel, [ranks, *matrices], [in_smem] + [in_vmem] * 3, outs, tokens=tokens
    )


def attention_block(ranks, w_query, out_turned, parts):
    share, query_cols = w_query.shape
    rows = parts[0].shape[0]
    if rows % 16:
        block = jnp.zeros((share, query_cols + 2 * HD), low).at[:, :query_cols].set(w_query)
        block = jnp.concatenate([block, out_turned], axis=1)
        for slot, part in enumerate(parts):
            heads = pick(part.reshape(rows, 2, KV_HEADS, HD), ranks[1] // 2, 2)
            block = lax.dynamic_update_slice(
                block, heads.reshape(rows, 2 * HD), ((ranks[1] ^ slot) * rows, query_cols)
            )
        return block

    def kernel(ranks_ref, query_ref, turned_ref, *refs):
        out_ref = refs[-1]
        out_ref[:, :query_cols] = query_ref[...]
        out_ref[:, query_cols + 2 * HD :] = turned_ref[...]
        first = ranks_ref[1] // 2 == 0
        for slot, ref in enumerate(refs[:-1]):
            place = pl.ds(pl.multiple_of((ranks_ref[1] ^ slot) * rows, rows), rows)
            for which in range(2):
                begin = which * KV_HEADS * HD
                column = query_cols + which * HD
                out_ref[place, column : column + HD] = jnp.where(
                    first, ref[:, begin : begin + HD], ref[:, begin + HD : begin + 2 * HD]
                )

    return call(
        kernel,
        [ranks, w_query, out_turned, *parts],
        [in_smem] + [in_vmem] * (2 + len(parts)),
        [shaped((share, 2 * query_cols + 2 * HD))],
    )[0]


def normalize(rows, gain, tokens=()):
    def kernel(rows_ref, gain_ref, out_ref):
        x = rows_ref[...].astype(wide)
        scale = lax.rsqrt(jnp.mean(x * x, axis=1, keepdims=True) + eps_norm)
        out_ref[...] = (x * scale * gain_ref[...]).astype(low)

    return call(kernel, [rows, gain[None]], [in_vmem] * 2, [shaped(rows.shape)], tokens=tokens)[0]


def join_near(ranks, keep, came, tokens=()):
    def kernel(ranks_ref, keep_ref, came_ref, sent_ref, own_ref):
        y_rank = ranks_ref[1] // 2
        other = 1 - y_rank
        sent_ref[...] = (keep_ref[other].astype(wide) + came_ref[other].astype(wide)).astype(low)
        own_ref[...] = keep_ref[y_rank].astype(wide) + came_ref[y_rank].astype(wide)

    shape = keep.shape[1:]
    return call(
        kernel,
        [ranks, keep, came],
        [in_smem, in_vmem, in_vmem],
        [shaped(shape), shaped(shape, wide)],
        tokens=tokens,
    )


def middle(rows, own, came, gain, tokens=()):
    half = rows.shape[0] // 2

    def kernel(rows_ref, own_ref, came_ref, gain_ref, mid_ref, top_ref, bottom_ref):
        mid = rows_ref[...].astype(wide) + own_ref[...] + came_ref[...].astype(wide)
        mid_ref[...] = mid
        scale = lax.rsqrt(jnp.mean(mid * mid, axis=1, keepdims=True) + eps_norm)
        normed = (mid * scale * gain_ref[...]).astype(low)
        top_ref[...] = normed[:half]
        bottom_ref[...] = normed[half:]

    shape = (half, rows.shape[1])
    return call(
        kernel,
        [rows, own, came, gain[None]],
        [in_vmem] * 4,
        [shaped(rows.shape, wide), shaped(shape), shaped(shape)],
        tokens=tokens,
    )


def stack_rows(parts, outs):
    def kernel(*refs):
        for index, numbers in enumerate(outs):
            begin = 0
            for number in numbers:
                ref = refs[number]
                refs[len(parts) + index][begin : begin + ref.shape[0]] = ref[...]
                begin += ref.shape[0]

    width = parts[0].shape[1]
    return call(
        kernel,
        parts,
        [in_vmem] * len(parts),
        [shaped((sum(parts[number].shape[0] for number in numbers), width)) for numbers in outs],
        room=24,
    )


def join_group(keep, came, tokens=()):
    quarter = keep.shape[0] // 4

    def kernel(keep_ref, came_ref, top_ref, bottom_ref, own_ref):
        for part in range(4):
            here = slice(part * quarter, (part + 1) * quarter)
            total = keep_ref[here].astype(wide) + came_ref[here].astype(wide)
            if part < 2:
                own_ref[here] = total
            else:
                (top_ref, bottom_ref)[part - 2][...] = total.astype(low)

    shape = (quarter, keep.shape[1])
    return call(
        kernel,
        [keep, came],
        [in_vmem] * 2,
        [shaped(shape), shaped(shape), shaped((2 * quarter, keep.shape[1]), wide)],
        tokens=tokens,
    )


def join_pair(own, came_top, came_bottom, tokens=()):
    half = own.shape[0] // 4

    def kernel(own_ref, came_top_ref, came_bottom_ref, top_ref, bottom_ref, out_ref):
        for index, (came, sent) in enumerate(
            ((came_top_ref, top_ref), (came_bottom_ref, bottom_ref))
        ):
            total = own_ref[2 * index * half : 2 * (index + 1) * half] + came[...].astype(wide)
            out_ref[index * half : (index + 1) * half] = total[:half]
            sent[...] = total[half:].astype(low)

    shape = (half, own.shape[1])
    return call(
        kernel,
        [own, came_top, came_bottom],
        [in_vmem] * 3,
        [shaped(shape), shaped(shape), shaped((2 * half, own.shape[1]), wide)],
        tokens=tokens,
    )


def back_of_norm(values, gain, grad_normed):
    scale = lax.rsqrt(jnp.mean(values * values, axis=1, keepdims=True) + eps_norm)
    weighted = grad_normed * gain
    inner = jnp.mean(values * weighted, axis=1, keepdims=True)
    return scale * weighted - values * (scale * scale * scale * inner), scale


def middle_back(mid, gain, grad_out, own, came_top, came_bottom, tokens=()):
    half = came_top.shape[0]

    def kernel(mid_ref, gain_ref, grad_ref, own_ref, top_ref, bottom_ref, out_ref, low_ref, sum_ref):
        sum_ref[...] = jnp.zeros_like(sum_ref)
        for index, came in enumerate((top_ref, bottom_ref)):
            here = slice(index * half, (index + 1) * half)
            grad_two = own_ref[here] + came[...].astype(wide)
            values = mid_ref[here]
            grad_values, scale = back_of_norm(values, gain_ref[...], grad_two)
            total = grad_ref[here].astype(wide) + grad_values
            out_ref[here] = total
            low_ref[here] = total.astype(low)
            sum_ref[...] += jnp.sum(grad_two * values * scale, axis=0, keepdims=True)

    return call(
        kernel,
        [mid, gain[None], grad_out, own, came_top, came_bottom],
        [in_vmem] * 6,
        [shaped(mid.shape, wide), shaped(mid.shape), shaped((1, mid.shape[1]), wide)],
        tokens=tokens,
    )


def tokens_back(rows, gain, grad_mid, own, came, tokens=()):
    def kernel(rows_ref, gain_ref, grad_ref, own_ref, came_ref, out_ref):
        values = rows_ref[...].astype(wide)
        grad_one = own_ref[...] + came_ref[...].astype(wide)
        out_ref[...] = grad_ref[...] + back_of_norm(values, gain_ref[...], grad_one)[0]

    return call(
        kernel,
        [rows, gain[None], grad_mid, own, came],
        [in_vmem] * 5,
        [shaped(rows.shape, wide)],
        tokens=tokens,
    )[0]


def layer_rows(mid, own, came_top, came_bottom, tokens=()):
    half = came_top.shape[0]

    def kernel(mid_ref, own_ref, top_ref, bottom_ref, out_ref):
        for index, came in enumerate((top_ref, bottom_ref)):
            here = slice(index * half, (index + 1) * half)
            out_ref[here] = (mid_ref[here] + own_ref[here] + came[...].astype(wide)).astype(low)

    return call(
        kernel, [mid, own, came_top, came_bottom], [in_vmem] * 4, [shaped(mid.shape)], tokens=tokens
    )[0]


def added(came, part):
    return (came.astype(wide) + part.astype(wide)).astype(low)


def after(value, *others, cost=1):
    def kernel(*refs):
        pass

    return pl.pallas_call(
        kernel,
        out_shape=shaped(value.shape, value.dtype),
        in_specs=[anywhere] * (1 + len(others)),
        out_specs=anywhere,
        input_output_aliases={0: 0},
        cost_estimate=pl.CostEstimate(flops=cost, bytes_accessed=1, transcendentals=0),
    )(value, *others)


def gate(value, *others):
    return after(value, *others, cost=2 * 10**11)


def store_split(ranks_ref, compute, keep_ref, send_ref):
    core = lax.rem(ranks_ref[1], 2)
    for y_rank in range(2):
        send_ref[y_rank] = compute(y_rank * 2 + 1 - core).astype(low)
        keep_ref[y_rank] = compute(y_rank * 2 + core).astype(low)


def attend(ranks, pieces, weights, bias, cosine, sine, segment, tokens=()):
    rows, width = pieces[0].shape
    count = len(pieces)
    length = rows * count
    share, all_columns = weights[0].shape
    query_cols = (all_columns - 2 * HD) // 2
    columns = query_cols + 2 * HD
    heads = query_cols // HD
    factor = HD ** (-0.5)

    def kernel(ranks_ref, *refs):
        piece_refs, refs = refs[:count], refs[count:]
        weight_refs, refs = refs[: len(weights)], refs[len(weights) :]
        bias_ref, cos_ref, sin_ref, col_ref, row_ref = refs[:5]
        query_ref, key_ref, value_ref, heads_ref, keep_ref, send_ref = refs[5:11]
        prob_refs = refs[11 : 11 + count]
        rows_v, weights_v, piece_sems, weight_sems = refs[11 + count :]
        copies = start_rows(
            piece_refs, rows_v, tensor_offsets(ranks_ref, count, rows), piece_sems
        ) + start_rows(
            weight_refs, weights_v, dp_offsets(ranks_ref, len(weights), share), weight_sems
        )
        for copy in copies:
            copy.wait()
        for block in range(count):
            here = slice(block * rows, (block + 1) * rows)
            lin = dot_nn(rows_v[here], weights_v[:, :columns]) + bias_ref[...]
            cos, sin = cos_ref[here], sin_ref[here]
            for head in range(heads + 1):
                part = lin[:, head * HD : (head + 1) * HD]
                turned = (part * cos + pltpu.roll(part, HD // 2, 1) * sin).astype(low)
                if head < heads:
                    query_ref[here, head * HD : (head + 1) * HD] = turned
                else:
                    key_ref[here] = turned
            value_ref[here] = lin[:, (heads + 1) * HD :].astype(low)
        for block in range(count):
            here = slice(block * rows, (block + 1) * rows)
            seen = (block + 1) * rows
            stacked = jnp.concatenate(
                [query_ref[here, head * HD : (head + 1) * HD] for head in range(heads)], axis=0
            )
            scores = dot_nt(stacked, key_ref[:seen]) * factor
            row_id = lax.broadcasted_iota(jnp.int32, (rows, seen), 0) + block * rows
            col_id = lax.broadcasted_iota(jnp.int32, (rows, seen), 1)
            allowed = (col_ref[here] == row_ref[:, :seen]) & (row_id >= col_id)
            shift = jnp.where(allowed, 0.0, masked)
            scores = scores + jnp.concatenate([shift] * heads, axis=0)
            weight = jnp.exp(scores - jnp.max(scores, axis=1, keepdims=True))
            weight = weight * (1.0 / jnp.sum(weight, axis=1, keepdims=True))
            weight_low = weight.astype(low)
            prob_refs[block][...] = weight_low
            out = dot_nn(weight_low, value_ref[:seen]).astype(low)
            for head in range(heads):
                heads_ref[here, head * HD : (head + 1) * HD] = out[head * rows : (head + 1) * rows]

        def compute(index):
            here = pl.ds(pl.multiple_of(index * rows, rows), rows)
            return dot_nt(heads_ref[here], weights_v[:, columns:])

        store_split(ranks_ref, compute, keep_ref, send_ref)

    outs = [
        shaped((length, query_cols)),
        shaped((length, HD)),
        shaped((length, HD)),
        shaped((length, query_cols)),
        shaped((2, rows, width)),
        shaped((2, rows, width)),
    ] + [shaped((heads * rows, (block + 1) * rows)) for block in range(count)]
    out = call(
        kernel,
        [ranks, *pieces, *weights, bias[None], cosine, sine]
        + [segment[:, None], segment[None]],
        [in_smem] + [anywhere] * (count + len(weights)) + [in_vmem] * 5,
        outs,
        [
            pltpu.VMEM((length, width), low),
            pltpu.VMEM((width, all_columns), low),
            pltpu.SemaphoreType.DMA((count,)),
            pltpu.SemaphoreType.DMA((len(weights),)),
        ],
        tokens,
        room=40,
    )
    return out[:4], out[4], out[5], out[6:]


def attend_back(
    ranks, pieces, normed, gain, weights, kept, probs, cosine, sine, tokens=()
):
    query, key, value = kept
    rows, width = pieces[0].shape
    count = len(pieces)
    length = rows * count
    share, all_columns = weights[0].shape
    query_cols = query.shape[1]
    columns = query_cols + 2 * HD
    heads = query_cols // HD
    factor = HD ** (-0.5)
    blocks = len(weights)

    def kernel(ranks_ref, *refs):
        piece_refs, refs = refs[:count], refs[count:]
        normed_refs, refs = refs[:count], refs[count:]
        weight_refs, refs = refs[:blocks], refs[blocks:]
        query_ref, key_ref, value_ref = refs[:3]
        prob_refs, refs = refs[3 : 3 + count], refs[3 + count :]
        cos_ref, sin_ref, gain_ref = refs[:3]
        grad_ref, bias_ref, gain_sum_ref, keep_ref, send_ref = refs[3:8]
        rows_v, normed_v, weights_v, do_v, dk_v, dv_v = refs[8:14]
        piece_sems, normed_sems, weight_sems = refs[14:]
        copies = start_rows(
            weight_refs, weights_v, dp_offsets(ranks_ref, blocks, share), weight_sems
        ) + start_rows(
            piece_refs, rows_v, tensor_offsets(ranks_ref, count, rows), piece_sems
        )
        late = start_rows(
            normed_refs, normed_v, tensor_offsets(ranks_ref, count, rows), normed_sems
        )
        for copy in copies:
            copy.wait()
        for block in range(count):
            here = slice(block * rows, (block + 1) * rows)
            do_v[here] = dot_nn(rows_v[here], weights_v[:, columns:]).astype(low)
        dk_v[...] = jnp.zeros_like(dk_v)
        dv_v[...] = jnp.zeros_like(dv_v)
        for block in range(count):
            here = slice(block * rows, (block + 1) * rows)
            seen = (block + 1) * rows
            stacked = jnp.concatenate(
                [do_v[here, head * HD : (head + 1) * HD] for head in range(heads)], axis=0
            )
            query_here = jnp.concatenate(
                [query_ref[here, head * HD : (head + 1) * HD] for head in range(heads)], axis=0
            )
            weight_low = prob_refs[block][...]
            grad_weight = dot_nt(stacked, value_ref[:seen])
            weight = weight_low.astype(wide)
            inner = jnp.sum(weight * grad_weight, axis=1, keepdims=True)
            grad_scores = (weight * (grad_weight - inner)).astype(low)
            grad_query = dot_nn(grad_scores, key_ref[:seen]) * factor
            dk_v[:seen] += dot_tn(grad_scores, query_here) * factor
            dv_v[:seen] += dot_tn(weight_low, stacked)
            cos, sin = cos_ref[here], sin_ref[here]
            for head in range(heads):
                part = grad_query[head * rows : (head + 1) * rows]
                grad_ref[here, head * HD : (head + 1) * HD] = (
                    part * cos - pltpu.roll(part, HD // 2, 1) * sin
                ).astype(low)
        part = dk_v[...]
        grad_ref[:, query_cols : query_cols + HD] = (
            part * cos_ref[...] - pltpu.roll(part, HD // 2, 1) * sin_ref[...]
        ).astype(low)
        grad_ref[:, query_cols + HD :] = dv_v[...].astype(low)
        bias_ref[...] = jnp.sum(grad_ref[...].astype(wide), axis=0, keepdims=True)
        for copy in late:
            copy.wait()
        gain_sum_ref[...] = jnp.zeros_like(gain_sum_ref)

        def compute(index):
            here = pl.ds(pl.multiple_of(index * rows, rows), rows)
            part = dot_nt(grad_ref[here], weights_v[:, :columns])
            gain_sum_ref[...] += jnp.sum(part * normed_v[here].astype(wide), axis=0, keepdims=True)
            return part

        store_split(ranks_ref, compute, keep_ref, send_ref)
        gain_sum_ref[...] = gain_sum_ref[...] / gain_ref[...]

    return call(
        kernel,
        [ranks, *pieces, *normed, *weights, query, key, value, *probs]
        + [cosine, sine, gain[None]],
        [in_smem] + [anywhere] * (2 * count + blocks) + [in_vmem] * (6 + count),
        [
            shaped((length, columns)),
            shaped((1, columns), wide),
            shaped((1, width), wide),
            shaped((2, rows, width)),
            shaped((2, rows, width)),
        ],
        [
            pltpu.VMEM((length, width), low),
            pltpu.VMEM((length, width), low),
            pltpu.VMEM((width, all_columns), low),
            pltpu.VMEM((length, query_cols), low),
            pltpu.VMEM((length, HD), wide),
            pltpu.VMEM((length, HD), wide),
            pltpu.SemaphoreType.DMA((count,)),
            pltpu.SemaphoreType.DMA((count,)),
            pltpu.SemaphoreType.DMA((blocks,)),
        ],
        tokens,
        room=40,
    )


def weight_sums(ranks, pairs, blocks, tokens=()):
    rows, width = pairs[0][0][0].shape
    count = len(pairs[0][0])
    share = width // blocks
    columns = sum(grads.shape[1] for _, grads in pairs)
    group = max(width // 4, share)

    def kernel(ranks_ref, *refs):
        piece_refs = [refs[index * (count + 1) : (index + 1) * (count + 1)] for index in range(len(pairs))]
        refs = refs[len(pairs) * (count + 1) :]
        near_ref, far_refs, sums_v = refs[0], refs[1 : 1 + blocks // 2], refs[1 + blocks // 2]
        rows_vs, sems = refs[2 + blocks // 2 : -1], refs[-1]
        copies = [
            start_rows(
                one[:count], rows_v, tensor_offsets(ranks_ref, count, rows), sems.at[index]
            )
            for index, (one, rows_v) in enumerate(zip(piece_refs, rows_vs))
        ]
        begin = 0
        for index, (one, rows_v) in enumerate(zip(piece_refs, rows_vs)):
            for copy in copies[index]:
                copy.wait()
            end = begin + one[count].shape[1]
            for first in range(0, width, group):
                part = dot_tn(rows_v[:, first : first + group], one[count][...]).astype(low)
                for place in range(0, group, share):
                    block = (first + place) // share
                    slot = lax.rem(block // 2 + blocks // 2 - ranks_ref[0] // 2, blocks // 2) * 2
                    sums_v[slot + (block % 2 ^ lax.rem(ranks_ref[0], 2)), :, begin:end] = part[
                        place : place + share
                    ]
            begin = end
        for slot in range(blocks // 2):
            near_ref[slot] = sums_v[2 * slot]
            far_refs[slot][...] = sums_v[2 * slot + 1]

    args, specs = [ranks], [in_smem]
    for pieces, grads in pairs:
        args += [*pieces, grads]
        specs += [anywhere] * count + [in_vmem]
    near, *far = call(
        kernel,
        args,
        specs,
        [shaped((blocks // 2, share, columns))] + [shaped((share, columns))] * (blocks // 2),
        [pltpu.VMEM((blocks, share, columns), low)]
        + [pltpu.VMEM((rows * count, width), low)] * len(pairs)
        + [pltpu.SemaphoreType.DMA((len(pairs), count))],
        tokens,
        room=40,
    )
    return near, far


def row_places(rows):
    own, x, y, xy = (0, 0), (1, 0), (0, rows), (1, rows)
    places = []
    for other in range(2):
        for pair, part in (((own, x), 0), ((own, y), 1), ((y, xy), 0), ((x, xy), 1)):
            places += [(other * 2 + array, row + part * (rows // 2)) for array, row in pair]
    return places


def start_weights(ranks, sources, places, sems):
    copies = []
    for slot, source in enumerate(sources):
        share, size = source.shape[1], source.shape[2]
        offset = lax.rem(ranks[0] // 2 + slot, len(sources)) * share
        rows = pl.ds(pl.multiple_of(offset, share), share)
        for matrix, place in enumerate(places):
            if place is None:
                continue
            target, column = place
            copies.append(
                pltpu.make_async_copy(
                    source.at[matrix], target.at[rows, column : column + size], sems.at[slot, matrix]
                )
            )
            copies[-1].start()
    return copies


def ffn(ranks, normed, normed_places, grads, weights, saved, tokens=()):
    count = len(normed_places)
    rows, width = grads[0].shape[0] // 2, grads[0].shape[1]
    length = rows * count
    blocks = lax.axis_size("dp") // 2
    share = width // blocks
    step = 2 * rows
    group = max(width // 2, share)
    if weights:
        sizes = [weights[0].shape[2]]
    else:
        sizes = [hidden.shape[1] for hidden, _ in saved]
    size = sum(sizes)

    def kernel(ranks_ref, *refs):
        refs = list(refs)

        def take(number):
            taken = refs[:number]
            del refs[:number]
            return taken

        normed_refs = take(len(normed))
        grad_refs = take(4)
        if weights:
            weight_refs = take(blocks)
            hidden_ref, pair_ref = take(2)
        else:
            saved_refs = [take(2) for _ in saved]
            sums_refs = take(2)
        normed_v, grads_v, row_sems = take(3)
        leaving = []

        def leave(source, target, sem):
            leaving.append(pltpu.make_async_copy(source, target, sem))
            leaving[-1].start()

        copies = []
        if weights:
            in_v, down_v, weight_sems, hidden_v, pair_v, saved_sems = take(6)
            copies = start_weights(
                ranks_ref, weight_refs, ((in_v, 0), (in_v, size), (down_v, 0)), weight_sems
            )
        places = row_places(rows)
        half = rows // 2
        waits = []
        for k in range(count):
            piece, first = normed_places[k]
            waits.append(
                pltpu.make_async_copy(
                    normed_refs[piece].at[pl.ds(first, rows)],
                    normed_v.at[pl.ds(k * rows, rows)],
                    row_sems.at[k, 0],
                )
            )
            for part in range(2):
                piece, first = places[2 * k + part]
                waits.append(
                    pltpu.make_async_copy(
                        grad_refs[piece].at[pl.ds(first, half)],
                        grads_v.at[pl.ds(k * rows + part * half, half)],
                        row_sems.at[k, 1 + part],
                    )
                )
        for wait in waits:
            wait.start()
        for copy in copies:
            copy.wait()
        for k in range(length // step):
            here = pl.ds(k * step, step)
            for wait in waits[6 * k : 6 * k + 6]:
                wait.wait()
            if not weights:
                continue
            both = dot_nn(normed_v[here], in_v[...])
            gate, upward = both[:, :size], both[:, size:]
            grad_hidden = dot_nn(grads_v[here], down_v[...])
            sigma = 0.5 * jnp.tanh(0.5 * gate) + 0.5
            active = gate * sigma
            hidden_v[here] = (active * upward).astype(low)
            pair_v[here, :size] = (grad_hidden * upward * (sigma + active * (1.0 - sigma))).astype(
                low
            )
            pair_v[here, size:] = (grad_hidden * active).astype(low)
            leave(hidden_v.at[here], hidden_ref.at[here], saved_sems.at[k, 0])
            leave(pair_v.at[here], pair_ref.at[here], saved_sems.at[k, 1])
        if not weights:
            sums_v, sums_sems = take(2)
            begin = 0
            for chunk, (hidden, pairs) in enumerate(saved_refs):
                here = slice(begin, begin + sizes[chunk])
                begin += sizes[chunk]
                for left, right, matrix in ((hidden, grads_v, 2), (pairs, normed_v, 0)):
                    turned = left[...].T
                    matrices = left.shape[1] // sizes[chunk]
                    for first in range(0, width, group):
                        part = dot_nn(turned, right[:, first : first + group]).T.astype(low)
                        for place in range(0, group, share):
                            block = (first + place) // share
                            slot = lax.rem(block + blocks - ranks_ref[0] // 2, blocks)
                            for index in range(matrices):
                                sums_v[slot, matrix + index, :, here] = part[
                                    place : place + share,
                                    index * sizes[chunk] : (index + 1) * sizes[chunk],
                                ]
                    if chunk == len(saved_refs) - 1:
                        for index in range(matrix, matrix + matrices):
                            leave(
                                sums_v.at[blocks - 1, index],
                                sums_refs[0].at[index],
                                sums_sems.at[index, blocks - 1],
                            )
                            for slot in range(blocks - 1):
                                leave(
                                    sums_v.at[slot, index],
                                    sums_refs[1].at[slot, index],
                                    sums_sems.at[index, slot],
                                )
        for copy in leaving:
            copy.wait()

    args = [ranks, *normed, *grads]
    specs = [in_smem] + [anywhere] * (len(normed) + 4)
    scratch = [
        pltpu.VMEM((length, width), low),
        pltpu.VMEM((length, width), low),
        pltpu.SemaphoreType.DMA((count, 3)),
    ]
    if weights:
        args += weights
        specs += [anywhere] * blocks
        scratch += [
            pltpu.VMEM((width, 2 * size), low),
            pltpu.VMEM((width, size), low),
            pltpu.SemaphoreType.DMA((blocks, 3)),
            pltpu.VMEM((length, size), low),
            pltpu.VMEM((length, 2 * size), low),
            pltpu.SemaphoreType.DMA((length // step, 2)),
        ]
        outs = [shaped((length, size)), shaped((length, 2 * size))]
    else:
        args += [one for chunk in saved for one in chunk]
        specs += [in_vmem] * (2 * len(saved))
        outs = [shaped((3, share, size)), shaped((blocks - 1, 3, share, size))]
        scratch += [
            pltpu.VMEM((blocks, 3, share, size), low),
            pltpu.SemaphoreType.DMA((3, blocks)),
        ]
    return call(kernel, args, specs, outs, scratch, tokens, [anywhere] * len(outs), 62)


def back_rows(ranks, lefts, chunks, inner, tokens=()):
    length = lefts[0].shape[0]
    blocks = len(chunks[0])
    width = chunks[0][0].shape[1] * blocks
    sizes = [chunk[0].shape[2] for chunk in chunks]
    wide_sizes = [left.shape[1] for left in lefts]
    step = length // 4

    def kernel(ranks_ref, *refs):
        refs = list(refs)

        def take(number):
            taken = refs[:number]
            del refs[:number]
            return taken

        left_refs = take(len(chunks))
        weight_refs = [take(blocks) for _ in chunks]
        keep_ref, send_ref = take(2)
        weight_vs = take(len(chunks))
        left_vs = take(len(chunks))
        total_v, weight_sems, left_sems, out_sems = refs
        copies = []
        for chunk, sources in enumerate(weight_refs):
            target = weight_vs[chunk]
            places = ((target, 0), (target, sizes[chunk]), None) if inner else (None, None, (target, 0))
            copies.append(start_weights(ranks_ref, sources, places, weight_sems.at[chunk]))
        order = (2, 3, 0, 1)
        arriving = []
        for k in order:
            here = pl.ds(k * step, step)
            arriving.append(
                [
                    pltpu.make_async_copy(
                        left_refs[chunk].at[here], left_vs[chunk].at[here], left_sems.at[chunk, k]
                    )
                    for chunk in range(len(chunks))
                ]
            )
            for copy in arriving[-1]:
                copy.start()
        leaving = []
        for number, k in enumerate(order):
            here = pl.ds(k * step, step)
            total = None
            for chunk in range(len(chunks)):
                if number == 0:
                    for copy in copies[chunk]:
                        copy.wait()
                arriving[number][chunk].wait()
                term = dot_nt(left_vs[chunk][here], weight_vs[chunk][...])
                total = term if total is None else total + term
            total_v[here] = total.astype(low)
            target = keep_ref if k < 2 else send_ref
            leaving.append(
                pltpu.make_async_copy(
                    total_v.at[here], target.at[pl.ds(k % 2 * step, step)], out_sems.at[k]
                )
            )
            leaving[-1].start()
        for copy in leaving:
            copy.wait()

    return call(
        kernel,
        [ranks, *lefts] + [block for chunk in chunks for block in chunk],
        [in_smem] + [anywhere] * (len(chunks) * (1 + blocks)),
        [shaped((length // 2, width))] * 2,
        [pltpu.VMEM((width, size), low) for size in wide_sizes]
        + [pltpu.VMEM((length, size), low) for size in wide_sizes]
        + [
            pltpu.VMEM((length, width), low),
            pltpu.SemaphoreType.DMA((len(chunks), blocks, 3)),
            pltpu.SemaphoreType.DMA((len(chunks), 4)),
            pltpu.SemaphoreType.DMA((4,)),
        ],
        tokens,
        [anywhere] * 2,
        60,
    )


def small_rows(ranks, biases, gains):
    query_rows = biases.shape[1] // HD - 2
    bias_rows = HEADS + 2 * KV_HEADS
    gain_rows = gains[0].shape[1] // HD

    def kernel(ranks_ref, bias_ref, *refs):
        out_ref = refs[-1]
        for row in range(HEADS):
            column = row % query_rows * HD
            here = ranks_ref[1] == row // query_rows
            out_ref[row : row + 1] = jnp.where(here, bias_ref[:, column : column + HD], 0.0)
        for which in range(2):
            column = (query_rows + which) * HD
            for head in range(KV_HEADS):
                row = HEADS + which * KV_HEADS + head
                here = ranks_ref[1] // 2 == head
                out_ref[row : row + 1] = jnp.where(here, bias_ref[:, column : column + HD], 0.0)
        for index, ref in enumerate(refs[:-1]):
            for row in range(gain_rows):
                place = bias_rows + index * gain_rows + row
                out_ref[place : place + 1] = ref[:, row * HD : (row + 1) * HD]

    return call(
        kernel,
        [ranks, biases, *gains],
        [in_smem] + [in_vmem] * (1 + len(gains)),
        [shaped((bias_rows + len(gains) * gain_rows, HD), wide)],
    )[0]


def split_pair(ranks, total, tokens=()):
    share = total.shape[1] // 2

    def kernel(ranks_ref, total_ref, out_ref):
        place = pl.ds(pl.multiple_of((1 - lax.rem(ranks_ref[0], 2)) * share, share), share)
        out_ref[...] = total_ref[:, place]

    return call(
        kernel,
        [ranks, total],
        [in_smem, in_vmem],
        [shaped((3, share, total.shape[2]))],
        tokens=tokens,
    )[0]


def lay_out(ranks, totals, cames, cuts, columns, tokens=()):
    share = cames[0].shape[1]

    def kernel(ranks_ref, *refs):
        total_refs, came_refs = refs[: len(cuts)], refs[len(cuts) : 2 * len(cuts)]
        outs = refs[2 * len(cuts) :]
        rank = lax.rem(ranks_ref[0], 2)
        place = pl.ds(pl.multiple_of(rank * share, share), share)
        for index, cut in enumerate(cuts):
            begin = 0
            for first, size in cut:
                here = slice(begin, begin + size)
                for matrix in range(3):
                    own = total_refs[index][matrix, place, here].astype(wide)
                    came = came_refs[index][matrix, :, here].astype(wide)
                    for which in range(2):
                        half = jnp.where(rank == which, own, came)
                        to = slice(first + which * size, first + (which + 1) * size)
                        outs[matrix][:, to] = half
                begin += size

    return call(
        kernel,
        [ranks, *totals, *cames],
        [in_smem] + [in_vmem] * (2 * len(cuts)),
        [shaped((share, columns), wide)] * 3,
        tokens=tokens,
        room=40,
    )


def on_device(
    tokens,
    segment,
    gain_attn,
    w_query,
    b_query,
    w_key,
    b_key,
    w_value,
    b_value,
    w_out,
    gain_ffn,
    w_gate,
    w_up,
    w_down,
    grad_out,
):
    width = tokens.shape[1]
    dp_count, tensor_count = lax.axis_size("dp"), lax.axis_size("tensor")
    dp_rank, tensor_rank = lax.axis_index("dp"), lax.axis_index("tensor")
    z_count = dp_count // 2
    y_rank, core = tensor_rank // 2, tensor_rank % 2
    ranks = jnp.stack([dp_rank, tensor_rank]).astype(jnp.int32)
    share = width // dp_count
    query_cols = w_query.shape[1]
    qkv_cols = query_cols + 2 * HD
    ffn_cols = w_gate.shape[1]
    cuts = cuts_of(ffn_cols)

    def begin():
        pair_kv = jnp.concatenate([w_key, w_value], axis=1)
        parts_kv = [pair_kv, across_core(pair_kv), across_y(pair_kv), across_both(pair_kv)]
        normed = normalize(tokens, gain_attn, [pair_kv])
        packed = pack(ranks, (w_gate, w_up, w_down.T), cuts, [normed])
        return attention_block(ranks, w_query, w_out.T, parts_kv), normed, packed

    def along_z(block, normed, *sent):
        far = across_y(normed)
        rows = [normed, across_core(normed), far, across_core(far)]
        line, crossed = [block], []
        for _ in range(z_count - 1):
            crossed.append(across_x(line[-1]))
            line.append(up_line(line[-1]))
        came = [across_x(after(sent[1], crossed[0]))]
        came = [across_x(after(sent[0], came[0])), *came]
        (grads,) = stack_rows([grad_out, across_y(after(grad_out, line[1]))], [(0, 1)])
        cosine, sine = angles_of(segment, HD)
        sine = jnp.where(jnp.arange(HD) < HD // 2, -sine, sine)
        return rows, line, crossed, came, grads, cosine, sine

    block, normed_one, packed = stage(begin)
    rows_one, line, crossed, came_ffn, grad_near, cosine, sine = stage(
        along_z, block, normed_one, *packed[::2]
    )
    crossed.append(across_x(line[-1]))
    qkv_blocks = []
    for slot in range(z_count):
        qkv_blocks += [line[-slot % z_count], crossed[-slot % z_count]]

    def pair_block(index, came):
        return lax.dynamic_update_slice_in_dim(
            packed[2 * index + 1], came, (1 - dp_rank % 2) * share, 1
        )

    def next_hop(blocks, *others):
        if others:
            blocks[-1] = after(blocks[-1], *others)
        blocks.append(up_line(blocks[-1]))

    def in_slots(blocks):
        return blocks[:1] + blocks[:0:-1]

    early, late = ([pair_block(index, came)] for index, came in enumerate(came_ffn))
    next_hop(early)
    next_hop(late, crossed[-1])
    grad_near = after(grad_near, crossed[-1])
    grad_far = across_x(grad_near)
    rows_one[0] = gate(rows_one[0], early[0], late[0], crossed[-1])
    key_bias = lax.dynamic_slice_in_dim(b_key, y_rank * HD, HD, 0)
    value_bias = lax.dynamic_slice_in_dim(b_value, y_rank * HD, HD, 0)
    bias = jnp.concatenate([b_query, key_bias, value_bias])

    def attention(*others):
        kept, keep, send, probs = attend(
            ranks, rows_one, qkv_blocks, bias, cosine, sine, segment, others
        )
        sent, own = join_near(ranks, keep, across_core(send))
        mid, top, bottom = middle(tokens, own, across_y(sent), gain_ffn)
        top, bottom, both = stack_rows(
            [top, across_x(top), bottom, across_y(bottom)], [(0, 1), (2, 3), (0, 1, 2, 3)]
        )
        return kept, probs, mid, top, bottom, both

    (query, key, value, heads_low), probs, mid_rows, top, bottom, both = stage(attention)
    next_hop(early, both)
    grad_far, late[1] = after(grad_far, both), after(late[1], both)

    top = gate(top, late[1], grad_far, early[1])

    def spread():
        far_top, far_bottom = across_y(top), across_x(bottom)
        return [
            both,
            far_top,
            far_bottom,
            across_core(both),
            across_core(far_top),
            across_core(far_bottom),
        ]

    rows_two = stage(spread)
    half = both.shape[0] // 2
    places = [(0, 0), (0, half), (1, 0), (2, 0), (3, 0), (3, half), (4, 0), (5, 0)]
    grad_ffn = [grad_near, grad_far, across_core(grad_near), across_core(grad_far)]
    while len(early) < z_count:
        next_hop(early, rows_two[-1])

    def feed(blocks, *others):
        return ffn(ranks, rows_two, places, grad_ffn, blocks, None, others)

    next_hop(late, early[-1])
    held = [in_slots(early)]
    saved = [feed(held[0])]
    next_hop(late, saved[0][0])
    early_terms = ffn(ranks, rows_two, places, grad_ffn, None, saved, [saved[0][0]])
    while len(late) < z_count:
        next_hop(late, early_terms[0])
    held.append(in_slots(late))
    early_hop = up_line(after(early_terms[0], late[-1]))
    saved.append(feed(held[1], early_terms[1]))
    keep_two, send_two = back_rows(
        ranks, [some[1] for some in saved], held, True, [early_terms[1]]
    )

    def next_sum(came, rest, slot, *others):
        return added(after(came, *others), rest[slot])

    early_sum = next_sum(early_hop, early_terms[1], z_count - 2, send_two)
    early_hop = up_line(early_sum)

    send_two = gate(send_two, early_sum)

    def back():
        top, bottom, own = join_group(keep_two, across_core(send_two))
        came_top, came_bottom = across_y(top), across_x(bottom)
        terms = ffn(ranks, rows_two, places, grad_ffn, None, saved[1:], [top])
        return join_pair(own, came_top, came_bottom, [terms[0]]), terms

    (top, bottom, own), late_terms = stage(back)
    early_sum = next_sum(early_hop, early_terms[1], z_count - 3, top)
    early_hop = up_line(early_sum)
    top = gate(top, early_sum)

    def back_middle():
        grad_mid, grad_low, gain_sum = middle_back(
            mid_rows, gain_ffn, grad_out, own, across_x(top), across_y(bottom)
        )

        far = across_y(grad_low)
        keep_out, send_out = back_rows(
            ranks, [some[0] for some in saved], held, False, [grad_low]
        )
        far = after(far, send_out)
        return grad_mid, grad_low, gain_sum, far, keep_out, send_out, across_core(grad_low)

    grad_mid, grad_low, gain_two, far_attn, keep_out, send_out, near_attn = stage(
        back_middle
    )
    for slot in range(z_count - 4, -1, -1):
        early_sum = next_sum(early_hop, early_terms[1], slot, far_attn)
        if slot:
            early_hop = up_line(early_sum)
    came_early = across_x(split_pair(ranks, early_sum))
    late_hop = up_line(after(late_terms[0], far_attn))

    far_attn = gate(far_attn, early_sum)

    def back_attention():
        grad_attn = [grad_low, near_attn, far_attn, across_core(far_attn)]
        return grad_attn, attend_back(
            ranks, grad_attn, rows_one, gain_attn, qkv_blocks, (query, key, value), probs,
            cosine, sine,
        )

    grad_attn, (grad_qkv, bias_sums, gain_one, keep, send) = stage(back_attention)
    came_early = after(came_early, send)
    late_sum = next_sum(late_hop, late_terms[1], z_count - 2, send)
    late_hop = up_line(late_sum)

    send = gate(send, late_sum, came_early)

    def attention_sums():
        came = across_core(send)
        terms = weight_sums(
            ranks, [(rows_one, grad_qkv), (grad_attn, heads_low)], dp_count, [send]
        )
        sent, own = join_near(ranks, keep, came, [terms[0]])
        near, far = terms
        return (
            near,
            far,
            added(across_x(far[-1]), near[z_count - 1]),
            sent,
            own,
            across_core(after(send_out, came)),
        )

    near_terms, far_terms, both_sum, sent, own, came_out = stage(
        attention_sums
    )
    for slot in range(z_count - 3, 0, -1):
        late_sum = next_sum(late_hop, late_terms[1], slot, sent)
        late_hop = up_line(late_sum)

    def joined(total, came, slot):
        return (
            up_line(total).astype(wide) + near_terms[slot].astype(wide) + came.astype(wide)
        ).astype(low)

    sent = gate(sent, late_sum)

    def finish_first():
        came = [None] * z_count
        for slot in range(z_count - 2, -1, -1):
            term = far_terms[slot]
            came[slot] = across_x(after(term, sent if slot == z_count - 2 else came[slot + 1]))
        came_one = across_y(sent)
        top, bottom, own_out = join_group(keep_out, came_out, [came_one])
        came_top, came_bottom = across_y(top), across_x(bottom)
        total = both_sum
        for slot in range(z_count - 2, 0, -1):
            total = joined(total, came[slot], slot)
        return total, came[0], came_one, join_pair(own_out, came_top, came_bottom)

    both_sum, came_both, came_one, ends = stage(finish_first)
    late_sum = next_sum(late_hop, late_terms[1], 0, both_sum)
    came_late = across_x(split_pair(ranks, late_sum))

    both_sum = gate(both_sum, late_sum)

    def finish():
        total = joined(both_sum, came_both, 0)
        top, bottom, own_out = ends
        came_top = across_x(top)
        came_bottom = across_y(bottom)
        grad_tokens = tokens_back(tokens, gain_attn, grad_mid, own, came_one)
        layer_out = layer_rows(mid_rows, own_out, came_top, came_bottom)
        small = all_sum(small_rows(ranks, bias_sums, (gain_two, gain_one)))
        kv_sums = total[:, query_cols:qkv_cols].reshape(2, 2, -1, 2 * HD)
        near_kv = pick(kv_sums, core, 1).astype(wide) + across_core(
            pick(kv_sums, 1 - core, 1)
        ).astype(wide)
        came_kv = across_y(pick(near_kv, 1 - y_rank, 0).astype(low)).astype(wide)
        both_kv = in_order(pick(near_kv, y_rank, 0), came_kv, y_rank, 0).reshape(2, -1, 2, HD)
        return total, small, grad_tokens, layer_out, both_kv

    both_sums, small, grad_tokens, layer_out, both_kv = stage(finish)
    grad_w_gate, grad_w_up, grad_w_down = lay_out(
        ranks, [early_sum, late_sum], [came_early, came_late], cuts, ffn_cols
    )
    grad_w_down = grad_w_down.T
    grad_w_query = both_sums[:, :query_cols].astype(wide)
    grad_w_out = both_sums[:, qkv_cols:].astype(wide).T
    grad_w_key = both_kv[:, :, 0].transpose(1, 0, 2).reshape(-1, KV_HEADS * HD)
    grad_w_value = both_kv[:, :, 1].transpose(1, 0, 2).reshape(-1, KV_HEADS * HD)
    small = small.reshape(-1)

    sizes = (HEADS * HD, KV_HEADS * HD, KV_HEADS * HD, width, width)
    device = dp_rank * lax.axis_size("tensor") + tensor_rank
    small_sums = []
    first = 0
    for size in sizes:
        each = size // (dp_count * lax.axis_size("tensor"))
        small_sums.append(lax.dynamic_slice_in_dim(small, first + device * each, each, 0))
        first += size

    return (
        layer_out,
        grad_tokens,
        small_sums[4],
        grad_w_query,
        small_sums[0],
        grad_w_key,
        small_sums[1],
        grad_w_value,
        small_sums[2],
        grad_w_out,
        small_sums[3],
        grad_w_gate,
        grad_w_up,
        grad_w_down,
    )


def solution(mesh):
    return jax.shard_map(
        on_device,
        mesh=mesh,
        in_specs=(
            P(("dp", "tensor"), None),
            P("dp"),
            P(),
            P("dp", "tensor"),
            P("tensor"),
            P(("dp", "tensor"), None),
            P(),
            P(("dp", "tensor"), None),
            P(),
            P("tensor", "dp"),
            P(),
            P("dp", "tensor"),
            P("dp", "tensor"),
            P("tensor", "dp"),
            P(("dp", "tensor"), None),
        ),
        out_specs=(
            P(("dp", "tensor"), None),
            P(("dp", "tensor"), None),
            P(("dp", "tensor")),
            P("dp", "tensor"),
            P(("dp", "tensor")),
            P(("dp", "tensor"), None),
            P(("dp", "tensor")),
            P(("dp", "tensor"), None),
            P(("dp", "tensor")),
            P("tensor", "dp"),
            P(("dp", "tensor")),
            P("dp", "tensor"),
            P("dp", "tensor"),
            P("tensor", "dp"),
        ),
        check_vma=False,
    )
```

time: 680 us -> 582 us (0.86)
  waiting for transfers between devices: 323 us -> 246 us
  local copies, waits for them, and re-layouts: 61.3 us -> 39.4 us
  Pallas kernels: 183 us -> 204 us
  between operations: 16.1 us -> 1.3 us
  starting transfers between devices: 64.4 us -> 51.7 us
  other arithmetic: 26.9 us -> 33.7 us
    ppermute x84 -> x71, waiting for transfers between devices: 323 us -> 246 us  [moved(): return lax.ppermute(block, axis, route)]
    unnamed x225 -> x58, local copies, waits for them, and re-layouts: 50.5 us -> 4.77 us
    cond x0 -> x58, local copies, waits for them, and re-layouts: none -> 22.5 us
    pallas_call x28, Pallas kernels: 183 us -> 204 us  [call(): pl.pallas_call(body, out_shape=outs, in_specs=list(specs) + [anywhere] *...]
    ppermute x84 -> x71, starting transfers between devices: 64.3 us -> 51.7 us  [moved(): return lax.ppermute(block, axis, route)]
    convert_element_type x9 -> x7, other arithmetic: 15 us -> 18.5 us  [added(): return (came.astype(wide) + part.astype(wide)).astype(low)]
  transfers between devices with their start and end apart: 86 -> 71, of which waited for: 39 -> 37; matrix products, arithmetic and copies ran while one was open for 5% -> 8% of each run, Pallas kernels for 20% -> 34%
where the time goes in v2:
time: 582 us; the launch traced here: 577 us
  waiting for transfers between devices  246 us (42%)
  Pallas kernels  204 us (35%)
  starting transfers between devices  51.7 us (9%)
  local copies, waits for them, and re-layouts  39.4 us (7%)
  other arithmetic  33.7 us (6%)
    ppermute x71, waiting for transfers between devices, moved(): return lax.ppermute(block, axis, route)  246 us
    pallas_call x28, Pallas kernels, call(): pl.pallas_call(body, out_shape=outs, in_specs=list(specs) + [anywhere] *...  204 us
    ppermute x71, starting transfers between devices, moved(): return lax.ppermute(block, axis, route)  51.7 us
    cond x58, local copies, waits for them, and re-layouts  22.5 us
    convert_element_type x7, other arithmetic, added(): return (came.astype(wide) + part.astype(wide)).astype(low)  18.5 us
  transfers between devices with their start and end apart: 71, of which 37 were waited for; matrix products, arithmetic and copies ran while one was open for 8% of the time, Pallas kernels for 34%

profile of v2, /device:TPU:0, one launch (start us, length us, event | category | flops | bytes accessed | tf_op | source)
XLA Modules:
  0.0 576.9 jit_solution(634210700526009869)
XLA Ops:
  1.2 13.8 %conditional.10 = (bf16[192,1024]{1,0:T(8,128)(2,1)}, bf16[256,1536]{1,0:T(8,128)(2,1)}, bf16[3,192,640]{2,1,0:T(8,128)(2,1)}, bf16[3,384,640]{2,1,0:T(8,128)(2,...) conditional(s32[]{:T(128)} %convert_element_type.168, () %tuple.94, (bf16[384,192]{0,1:T(8,128)(2,1)}, ...), branch_computations={%region_0.1_spmd, %region_1.2_spmd} | conditional | flops 599999971328 | bytes 12202355 | solution.py:86
  15.1 64.0 %conditional.11 = (bf16[256,1536]{1,0:T(8,128)(2,1)}, bf16[256,1536]{1,0:T(8,128)(2,1)}, bf16[256,1536]{1,0:T(8,128)(2,1)}, bf16[256,1536]{1,0:T(8,128)(2,1)}, b...) conditional(s32[]{:T(128)} %convert_element_type.168, () %tuple.93, ...), branch_computations={%region_2.3_spmd, %region_3.6_spmd} | conditional | flops 200000585728 | bytes 36013720 | solution.py:86
  22.6 6.2 %collective-permute-done.44.refs_1_ = bf16[192,1024]{1,0:T(8,128)(2,1)S(1)} collective-permute-done((bf16[192,1024]{1,0:T(8,128)(2,1)}, bf16[192,1024]{1,0:T(8,128)(2,1)S(1)}, u32[]{:S(2)}, u32[]{:S(2)}) %collective-permute-start.44) | collective-permute-done | bytes 393248 | tf_op jit(solution)/shard_map/cond/branch_1_fun/ppermute | solution.py:49
  39.4 4.4 collective-permute-done.45
  47.0 6.7 %collective-permute-done.48 = bf16[192,1024]{1,0:T(8,128)(2,1)} collective-permute-done((bf16[192,1024]{1,0:T(8,128)(2,1)S(1)}, bf16[192,1024]{1,0:T(8,128)(2,1)}, u32[]{:S(2)}, u32[]{:S(2)}) %collective-permute-start.48) | collective-permute-done | bytes 393248 | tf_op jit(solution)/shard_map/cond/branch_1_fun/ppermute | solution.py:49
  57.4 8.6 %collective-permute-done.49 = bf16[192,1024]{1,0:T(8,128)(2,1)} collective-permute-done((bf16[192,1024]{1,0:T(8,128)(2,1)}, bf16[192,1024]{1,0:T(8,128)(2,1)}, u32[]{:S(2)}, u32[]{:S(2)}) %collective-permute-start.49) | collective-permute-done | bytes 393248 | tf_op jit(solution)/shard_map/cond/branch_1_fun/ppermute | solution.py:49
  66.0 13.1 %collective-permute-done.51 = bf16[3,192,640]{2,1,0:T(8,128)(2,1)} collective-permute-done((bf16[3,192,640]{2,1,0:T(8,128)(2,1)}, bf16[3,192,640]{2,1,0:T(8,128)(2,1)}, u32[]{:S(2)}, u32[]{:S(2)}) %collective-permute-start.51) | collective-permute-done | bytes 737312 | tf_op jit(solution)/shard_map/cond/branch_1_fun/ppermute | solution.py:49
  91.2 52.5 %conditional.12 = (bf16[1024,384]{1,0:T(8,128)(2,1)}, bf16[1024,128]{1,0:T(8,128)(2,1)}, bf16[1024,128]{1,0:T(8,128)(2,1)}, bf16[1024,384]{1,0:T(8,128)(2,1)}, b...) conditional(s32[]{:T(128)} %convert_element_type.168, ...), branch_computations={%region_6.7_spmd, %region_7.8_spmd} | conditional | flops 799999983616 | bytes 15779132 | solution.py:86
  91.4 14.1 %branch_1_fun.38 = (bf16[1024,384]{1,0:T(8,128)(2,1)}, bf16[1024,128]{1,0:T(8,128)(2,1)}, bf16[1024,128]{1,0:T(8,128)(2,1)}, bf16[1024,384]{1,0:T(8,128)(2,1)}, ...) custom-call(s32[2]{0:T(128)S(1)} %get-tuple-element.304.refs_0_, ...), custom_call_target="tpu_custom_call" | custom-call | flops 199999995904 | bytes 1 | tf_op jit(solution)/shard_map/cond/branch_1_fun/pallas_call | solution.py:123
  105.6 3.4 collective-permute-done.refs_2_
  110.8 18.7 %collective-permute-done.1.refs_2_ = bf16[256,1536]{1,0:T(8,128)(2,1)S(1)} collective-permute-done((bf16[256,1536]{1,0:T(8,128)(2,1)S(1)}, bf16[256,1536]{1,0:T(8,128)(2,1)S(1)}, u32[]{:S(2)}, u32[]{:S(2)}) %collective-permute-start.1) | collective-permute-done | bytes 786464 | tf_op jit(solution)/shard_map/cond/branch_1_fun/ppermute | solution.py:49
  132.6 9.0 %collective-permute-done.2.refs_1_ = bf16[128,1536]{1,0:T(8,128)(2,1)S(1)} collective-permute-done((bf16[128,1536]{1,0:T(8,128)(2,1)S(1)}, bf16[128,1536]{1,0:T(8,128)(2,1)S(1)}, u32[]{:S(2)}, u32[]{:S(2)}) %collective-permute-start.2) | collective-permute-done | bytes 393248 | tf_op jit(solution)/shard_map/cond/branch_1_fun/ppermute | solution.py:49
  145.1 23.8 %conditional.13 = (bf16[512,1536]{1,0:T(8,128)(2,1)S(1)}, bf16[256,1536]{1,0:T(8,128)(2,1)}, bf16[256,1536]{1,0:T(8,128)(2,1)}, bf16[512,1536]{1,0:T(8,128)(2,1)...) conditional(s32[]{:T(128)} %convert_element_type.168, () %tuple.100, (bf16[256,1536]{1,0:T(8,128)(2,1)}, ...), branch_computations={%region_8.9_spmd, %region_9.10_spmd} | conditional | bytes 22020344 | solution.py:86
  147.8 17.4 %collective-permute-done.4 = bf16[256,1536]{1,0:T(8,128)(2,1)} collective-permute-done((bf16[256,1536]{1,0:T(8,128)(2,1)}, bf16[256,1536]{1,0:T(8,128)(2,1)}, u32[]{:S(2)}, u32[]{:S(2)}) %collective-permute-start.4) | collective-permute-done | bytes 786464 | tf_op jit(solution)/shard_map/cond/branch_1_fun/ppermute | solution.py:49
  169.0 11.8 %collective-permute-done.59.refs_0_ = bf16[3,384,640]{2,1,0:T(8,128)(2,1)} collective-permute-done((bf16[3,384,640]{2,1,0:T(8,128)(2,1)}, bf16[3,384,640]{2,1,0:T(8,128)(2,1)}, u32[]{:S(2)}, u32[]{:S(2)}) %collective-permute-start.59) | collective-permute-done | bytes 1474592 | tf_op jit(solution)/shard_map/ppermute | solution.py:49
  180.8 36.1 %collective-permute-done.60.refs_12_.refs_1_.refs_4_ = bf16[3,384,640]{2,1,0:T(8,128)(2,1)S(1)} collective-permute-done((bf16[3,384,640]{2,1,0:T(8,128)(2,1)}, bf16[3,384,640]{2,1,0:T(8,128)(2,1)S(1)}, u32[]{:S(2)}, u32[]{:S(2)}) %collective-permute-start.60) | collective-permute-done | bytes 1474592 | tf_op jit(solution)/shard_map/ppermute | solution.py:49
  218.2 19.1 %shard_map.269 = (bf16[2048,640]{1,0:T(8,128)(2,1)}, bf16[2048,1280]{1,0:T(8,128)(2,1)}) custom-call(s32[2]{0:T(128)S(1)} %copy-done.44, bf16[512,1536]{1,0:T(8,128)(2,1)S(1)} %get-tuple-element.603.refs_1_, bf16[256,1536]{1,0:T(8,128)(2,1)} %get-tuple-element.604.refs_2_, bf16[256,1536]{1,0:T(8,128)(2,1)} %get-tuple-element.605.refs_3_, ...), custom_call_target="tpu_custom_call" | custom-call | flops 199999995904 | bytes 1 | tf_op jit(solution)/shard_map/pallas_call | solution.py:123
  237.3 9.9 %collective-permute-done.61.refs_0_ = bf16[3,384,512]{2,1,0:T(8,128)(2,1)} collective-permute-done((bf16[3,384,512]{2,1,0:T(8,128)(2,1)}, bf16[3,384,512]{2,1,0:T(8,128)(2,1)}, u32[]{:S(2)}, u32[]{:S(2)}) %collective-permute-start.61) | collective-permute-done | bytes 1179680 | tf_op jit(solution)/shard_map/ppermute | solution.py:49
  247.5 22.3 %shard_map.272 = (bf16[3,384,640]{2,1,0:T(8,128)(2,1)}, bf16[3,3,384,640]{3,2,1,0:T(8,128)(2,1)}) custom-call(s32[2]{0:T(128)S(1)} %copy-done.44, bf16[512,1536]{1,0:T(8,128)(2,1)S(1)} %get-tuple-element.603.refs_1_, bf16[256,1536]{1,0:T(8,128)(2,1)} %get-tuple-element.604.refs_2_, bf16[256,1536]{1,0:T(8,128)(2,1)} %get-tuple-element.605.refs_3_, ...), custom_call_target="tpu_custom_call" | custom-call | flops 199999995904 | bytes 1 | tf_op jit(solution)/shard_map/pallas_call | solution.py:123
  269.9 5.7 collective-permute-done.62.refs_12_.refs_8_.refs_1_
  275.8 15.4 %shard_map.273 = (bf16[2048,512]{1,0:T(8,128)(2,1)}, bf16[2048,1024]{1,0:T(8,128)(2,1)}) custom-call(s32[2]{0:T(128)S(1)} %copy-done.44, bf16[512,1536]{1,0:T(8,128)(2,1)S(1)} %get-tuple-element.603.refs_1_, bf16[256,1536]{1,0:T(8,128)(2,1)} %get-tuple-element.604.refs_2_, bf16[256,1536]{1,0:T(8,128)(2,1)} %get-tuple-element.605.refs_3_, ...), custom_call_target="tpu_custom_call" | custom-call | flops 199999995904 | bytes 1 | tf_op jit(solution)/shard_map/pallas_call | solution.py:123
  291.2 24.3 %shard_map.274 = (bf16[1024,1536]{1,0:T(8,128)(2,1)}, bf16[1024,1536]{1,0:T(8,128)(2,1)S(1)}) custom-call(s32[2]{0:T(128)S(1)} %copy-done.44, bf16[2048,1280]{1,0:T(8,128)(2,1)} %get-tuple-element.609.refs_12_.refs_1_, bf16[2048,1024]{1,0:T(8,128)(2,1)} %get-tuple-element.612.refs_2_, ...), custom_call_target="tpu_custom_call" | custom-call | flops 199999995904 | bytes 1 | tf_op jit(solution)/shard_map/pallas_call | solution.py:123
  318.8 36.7 %conditional.14 = (bf16[128,1536]{1,0:T(8,128)(2,1)}, bf16[128,1536]{1,0:T(8,128)(2,1)}, f32[256,1536]{1,0:T(8,128)}, bf16[3,384,512]{2,1,0:T(8,128)(2,1)}, bf16[3,3,384,512]{3,2,1,0:T(8,128)(2,1)}) conditional(s32[]{:T(128)} %convert_element_type.168, () %tuple.99, (bf16[1024,1536]{1,0:T(8,128)(2,1)S(1)}, bf16[1024,1536]{1,0:T(8,128)(2,1)}, ...), branch_computations={%region_10.11_spmd, %region_11.12_spmd} | conditional | flops 599999971328 | bytes 50331952 | solution.py:86
  318.8 5.7 collective-permute-done.9.refs_1_
  324.4 3.5 branch_1_fun.42
  331.1 19.4 %branch_1_fun.43 = (bf16[3,384,512]{2,1,0:T(8,128)(2,1)}, bf16[3,3,384,512]{3,2,1,0:T(8,128)(2,1)}) custom-call(s32[2]{0:T(128)S(1)} %copy-done.52, bf16[512,1536]{1,0:T(8,128)(2,1)S(1)} %copy-done.10, bf16[256,1536]{1,0:T(8,128)(2,1)} %get-tuple-element.351.refs_2_, bf16[256,1536]{1,0:T(8,128)(2,1)} %get-tuple-element.352.refs_3_, ...), custom_call_target="tpu_custom_call" | custom-call | flops 199999995904 | bytes 1 | tf_op jit(solution)/shard_map/cond/branch_1_fun/pallas_call | solution.py:123
  360.0 34.1 %conditional.15 = (f32[256,1536]{1,0:T(8,128)}, bf16[256,1536]{1,0:T(8,128)(2,1)}, f32[1,1536]{1,0:T(1,128)}, bf16[256,1536]{1,0:T(8,128)(2,1)}, bf16[1024,1536]...) conditional(s32[]{:T(128)} %convert_element_type.168, () %tuple.98, ...), branch_computations={%region_12.13_spmd, %region_13.14_spmd} | conditional | flops 399999991808 | bytes 25833804 | solution.py:86
  362.6 8.2 %collective-permute-done.12.refs_4_ = bf16[128,1536]{1,0:T(8,128)(2,1)S(1)} collective-permute-done((bf16[128,1536]{1,0:T(8,128)(2,1)}, bf16[128,1536]{1,0:T(8,128)(2,1)S(1)}, u32[]{:S(2)}, u32[]{:S(2)}) %collective-permute-start.12) | collective-permute-done | bytes 393248 | tf_op jit(solution)/shard_map/cond/branch_1_fun/ppermute | solution.py:49
  371.8 4.4 branch_1_fun.45
  377.3 14.0 %branch_1_fun.46 = (bf16[1024,1536]{1,0:T(8,128)(2,1)}, bf16[1024,1536]{1,0:T(8,128)(2,1)}) custom-call(s32[2]{0:T(128)S(1)} %copy-done.53, bf16[2048,640]{1,0:T(8,128)(2,1)S(1)} %copy-done.8, bf16[2048,512]{1,0:T(8,128)(2,1)} %get-tuple-element.378.refs_2_, bf16[3,384,640]{2,1,0:T(8,128)(2,1)} %get-tuple-element.379.refs_3_, ...), custom_call_target="tpu_custom_call" | custom-call | flops 199999995904 | bytes 1 | tf_op jit(solution)/shard_map/cond/branch_1_fun/pallas_call | solution.py:123
  394.1 4.3 collective-permute-start.66
  404.4 24.9 %conditional.16 = (bf16[256,1536]{1,0:T(8,128)(2,1)}, bf16[256,1536]{1,0:T(8,128)(2,1)}, bf16[256,1536]{1,0:T(8,128)(2,1)}, bf16[256,1536]{1,0:T(8,128)(2,1)}, b...) conditional(s32[]{:T(128)} %convert_element_type.168, () %tuple.97, ...), branch_computations={%region_14.15_spmd, %region_15.16_spmd} | conditional | flops 199999995904 | bytes 7876721 | solution.py:86
  410.7 18.7 %branch_1_fun.48 = (bf16[1024,640]{1,0:T(8,128)(2,1)}, f32[1,640]{1,0:T(1,128)}, f32[1,1536]{1,0:T(1,128)}, bf16[2,256,1536]{2,1,0:T(8,128)(2,1)}, bf16[2,256,1536]{2,1,0:T(8,128)(2,1)}) custom-call(s32[2]{0:T(128)S(1)} %get-tuple-element.392.refs_0_, bf16[256,1536]{1,0:T(8,128)(2,1)} %get-tuple-element.809.refs_1_, ...), custom_call_target="tpu_custom_call" | custom-call | flops 199999995904 | bytes 1 | tf_op jit(solution)/shard_map/cond/branch_1_fun/pallas_call | solution.py:123
  433.8 29.1 %conditional.17 = (bf16[4,192,1024]{2,1,0:T(8,128)(2,1)}, bf16[192,1024]{1,0:T(8,128)(2,1)}, bf16[192,1024]{1,0:T(8,128)(2,1)}, bf16[192,1024]{1,0:T(8,128)(2,1)...) conditional(s32[]{:T(128)} %convert_element_type.168, () %tuple.92, ...), branch_computations={%region_16.17_spmd, %region_17.18_spmd} | conditional | flops 400000778240 | bytes 21627068 | solution.py:86
  434.0 9.5 %branch_1_fun.49 = (bf16[4,192,1024]{2,1,0:T(8,128)(2,1)}, bf16[192,1024]{1,0:T(8,128)(2,1)}, bf16[192,1024]{1,0:T(8,128)(2,1)}, bf16[192,1024]{1,0:T(8,128)(2,1)}, bf16[192,1024]{1,0:T(8,128)(2,1)S(1)}) custom-call(s32[2]{0:T(128)S(1)} %get-tuple-element.420.refs_0_, bf16[256,1536]{1,0:T(8,128)(2,1)} %get-tuple-element.421.refs_1_, ...), custom_call_target="tpu_custom_call" | custom-call | flops 199999995904 | bytes 1 | tf_op jit(solution)/shard_map/cond/branch_1_fun/pallas_call | solution.py:123
  444.5 10.4 %collective-permute-done.20 = bf16[192,1024]{1,0:T(8,128)(2,1)S(1)} collective-permute-done((bf16[192,1024]{1,0:T(8,128)(2,1)S(1)}, bf16[192,1024]{1,0:T(8,128)(2,1)S(1)}, u32[]{:S(2)}, u32[]{:S(2)}) %collective-permute-start.20) | collective-permute-done | bytes 393248 | tf_op jit(solution)/shard_map/cond/branch_1_fun/ppermute | solution.py:49
  456.8 3.6 branch_1_fun.50
  466.1 57.2 %conditional.18 = (bf16[192,1024]{1,0:T(8,128)(2,1)}, bf16[192,1024]{1,0:T(8,128)(2,1)}, bf16[256,1536]{1,0:T(8,128)(2,1)}, bf16[128,1536]{1,0:T(8,128)(2,1)}, b...) conditional(s32[]{:T(128)} %convert_element_type.168, () %tuple.91, (bf16[192,1024]{1,0:T(8,128)(2,1)}, ...), branch_computations={%region_18.19_spmd, %region_19.20_spmd} | conditional | flops 400002351104 | bytes 48759268 | solution.py:86
  468.2 10.2 %collective-permute-done.24.refs_1_ = bf16[192,1024]{1,0:T(8,128)(2,1)S(1)} collective-permute-done((bf16[192,1024]{1,0:T(8,128)(2,1)}, bf16[192,1024]{1,0:T(8,128)(2,1)S(1)}, u32[]{:S(2)}, u32[]{:S(2)}) %collective-permute-start.24) | collective-permute-done | bytes 393248 | tf_op jit(solution)/shard_map/cond/branch_1_fun/ppermute | solution.py:49
  479.7 6.0 %collective-permute-done.28.refs_2_ = bf16[256,1536]{1,0:T(8,128)(2,1)} collective-permute-done((bf16[256,1536]{1,0:T(8,128)(2,1)}, bf16[256,1536]{1,0:T(8,128)(2,1)}, u32[]{:S(2)}, u32[]{:S(2)}) %collective-permute-start.28) | collective-permute-done | bytes 786464 | tf_op jit(solution)/shard_map/cond/branch_1_fun/ppermute | solution.py:49
  485.7 3.5 branch_1_fun.55
  493.0 11.4 %collective-permute-done.23 = bf16[192,1024]{1,0:T(8,128)(2,1)} collective-permute-done((bf16[192,1024]{1,0:T(8,128)(2,1)}, bf16[192,1024]{1,0:T(8,128)(2,1)}, u32[]{:S(2)}, u32[]{:S(2)}) %collective-permute-start.23) | collective-permute-done | bytes 393248 | tf_op jit(solution)/shard_map/cond/branch_1_fun/ppermute | solution.py:49
  506.8 10.9 %collective-permute-done.25 = bf16[192,1024]{1,0:T(8,128)(2,1)} collective-permute-done((bf16[192,1024]{1,0:T(8,128)(2,1)S(1)}, bf16[192,1024]{1,0:T(8,128)(2,1)}, u32[]{:S(2)}, u32[]{:S(2)}) %collective-permute-start.25) | collective-permute-done | bytes 393248 | tf_op jit(solution)/shard_map/cond/branch_1_fun/ppermute | solution.py:49
  527.7 39.7 %conditional.19 = (bf16[192,1024]{1,0:T(8,128)(2,1)}, f32[256,1536]{1,0:T(8,128)}, bf16[256,1536]{1,0:T(8,128)(2,1)}, f32[2,48,2,128]{3,2,1,0:T(2,128)S(1)}, f32[5120]{0:T(1024)}) conditional(s32[]{:T(128)} %convert_element_type.168, () %tuple.90, (bf16[192,1024]{1,0:T(8,128)(2,1)}, bf16[4,192,1024]{2,1,0:T(8,128)(2,1)}, ...), branch_computations={%region_20.21_spmd, %region_21.22_spmd} | conditional | flops 600001282048 | bytes 12280595 | solution.py:86
  534.8 5.9 %collective-permute-done.38 = f32[40,128]{1,0:T(8,128)S(1)} collective-permute-done((f32[40,128]{1,0:T(8,128)S(1)}, f32[40,128]{1,0:T(8,128)S(1)}, u32[]{:S(2)}, u32[]{:S(2)}) %collective-permute-start.38) | collective-permute-done | bytes 20512 | tf_op jit(solution)/shard_map/cond/branch_1_fun/ppermute | solution.py:49
  544.7 3.4 collective-permute-done.39
  548.7 3.9 branch_1_fun.57
  572.7 3.9 shard_map.292
  (334 shorter events, 167.9 us)
Async XLA Ops:
  15.1 13.6 %collective-permute-start.44 = (bf16[192,1024]{1,0:T(8,128)(2,1)}, bf16[192,1024]{1,0:T(8,128)(2,1)S(1)}, u32[]{:S(2)}, u32[]{:S(2)}) collective-permute-start(bf16[192,1024]{1,0:T(8,128)(2,1)} %get-tuple-element.728), channel_id=1, source_target_pairs={{0,8},{4,12},{8,16},{12,20},{16,24},{20,28},{24,0},{28,4},{1,9},{5... | collective-permute-start | bytes 1179656 | tf_op jit(solution)/shard_map/cond/branch_1_fun/ppermute | solution.py:49
  16.9 13.4 %collective-permute-start.47 = (bf16[192,1024]{1,0:T(8,128)(2,1)}, bf16[192,1024]{1,0:T(8,128)(2,1)S(1)}, u32[]{:S(2)}, u32[]{:S(2)}) collective-permute-start(bf16[192,1024]{1,0:T(8,128)(2,1)} %get-tuple-element.728), channel_id=1, source_target_pairs={{0,4},{4,0},{8,12},{12,8},{16,20},{20,16},{24,28},{28,24},{1,5},{5... | collective-permute-start | bytes 1179656 | tf_op jit(solution)/shard_map/cond/branch_1_fun/ppermute | solution.py:49
  18.4 36.7 %collective-permute-start.42 = (bf16[256,1536]{1,0:T(8,128)(2,1)}, bf16[256,1536]{1,0:T(8,128)(2,1)}, u32[]{:S(2)}, u32[]{:S(2)}) collective-permute-start(bf16[256,1536]{1,0:T(8,128)(2,1)} %get-tuple-element.724), channel_id=1, source_target_pairs={{0,2},{1,3},{2,0},{3,1},{4,6},{5,7},{6,4},{7,5},{8,10},{9,11},{10,... | collective-permute-start | bytes 2359304 | tf_op jit(solution)/shard_map/cond/branch_1_fun/ppermute | solution.py:49
  28.7 26.4 %collective-permute-start.52 = (bf16[256,1536]{1,0:T(8,128)(2,1)}, bf16[256,1536]{1,0:T(8,128)(2,1)S(1)}, u32[]{:S(2)}, u32[]{:S(2)}) collective-permute-start(bf16[256,1536]{1,0:T(8,128)(2,1)} %branch_1_fun.36), channel_id=1, source_target_pairs={{0,2},{1,3},{2,0},{3,1},{4,6},{5,7},{6,4},{7,5},{8,10},{9,11},{10,... | collective-permute-start | bytes 2359304 | tf_op jit(solution)/shard_map/cond/branch_1_fun/ppermute | solution.py:49
  30.3 16.6 %collective-permute-start.50 = (bf16[3,192,512]{2,1,0:T(8,128)(2,1)}, bf16[3,192,512]{2,1,0:T(8,128)(2,1)}, u32[]{:S(2)}, u32[]{:S(2)}) collective-permute-start(bf16[3,192,512]{2,1,0:T(8,128)(2,1)} %branch_1_fun.34), channel_id=1, source_target_pairs={{0,4},{4,0},{8,12},{12,8},{16,20},{20,16},{24,28},{28,24},{1,5},{5... | collective-permute-start | bytes 1769480 | tf_op jit(solution)/shard_map/cond/branch_1_fun/ppermute | solution.py:49
  31.9 11.9 %collective-permute-start.45 = (bf16[192,1024]{1,0:T(8,128)(2,1)S(1)}, bf16[192,1024]{1,0:T(8,128)(2,1)}, u32[]{:S(2)}, u32[]{:S(2)}) collective-permute-start(bf16[192,1024]{1,0:T(8,128)(2,1)S(1)} %collective-permute-done.44.refs_1_), channel_id=1, source_target_pairs={{0,8},{4,12},{8,16},{12,20},{16,24},{20,28},{24,0},{28,4},{1,9},{5... | collective-permute-start | bytes 1179656 | tf_op jit(solution)/shard_map/cond/branch_1_fun/ppermute | solution.py:49
  31.9 21.7 %collective-permute-start.48 = (bf16[192,1024]{1,0:T(8,128)(2,1)S(1)}, bf16[192,1024]{1,0:T(8,128)(2,1)}, u32[]{:S(2)}, u32[]{:S(2)}) collective-permute-start(bf16[192,1024]{1,0:T(8,128)(2,1)S(1)} %collective-permute-done.44.refs_1_), channel_id=1, source_target_pairs={{0,4},{4,0},{8,12},{12,8},{16,20},{20,16},{24,28},{28,24},{1,5},{5... | collective-permute-start | bytes 1179656 | tf_op jit(solution)/shard_map/cond/branch_1_fun/ppermute | solution.py:49
  43.8 13.2 %collective-permute-start.41 = (bf16[256,1536]{1,0:T(8,128)(2,1)}, bf16[256,1536]{1,0:T(8,128)(2,1)}, u32[]{:S(2)}, u32[]{:S(2)}) collective-permute-start(bf16[256,1536]{1,0:T(8,128)(2,1)} %get-tuple-element.724), channel_id=1, source_target_pairs={{0,1},{1,0},{2,3},{3,2},{4,5},{5,4},{6,7},{7,6},{8,9},{9,8},{10,11... | collective-permute-start | bytes 2359304 | tf_op jit(solution)/shard_map/cond/branch_1_fun/ppermute | solution.py:49
  53.6 12.4 %collective-permute-start.49 = (bf16[192,1024]{1,0:T(8,128)(2,1)}, bf16[192,1024]{1,0:T(8,128)(2,1)}, u32[]{:S(2)}, u32[]{:S(2)}) collective-permute-start(bf16[192,1024]{1,0:T(8,128)(2,1)} %collective-permute-done.45), channel_id=1, source_target_pairs={{0,4},{4,0},{8,12},{12,8},{16,20},{20,16},{24,28},{28,24},{1,5},{5... | collective-permute-start | bytes 1179656 | tf_op jit(solution)/shard_map/cond/branch_1_fun/ppermute | solution.py:49
  55.1 10.9 %collective-permute-start.43 = (bf16[256,1536]{1,0:T(8,128)(2,1)}, bf16[256,1536]{1,0:T(8,128)(2,1)}, u32[]{:S(2)}, u32[]{:S(2)}) collective-permute-start(bf16[256,1536]{1,0:T(8,128)(2,1)} %collective-permute-done.42), channel_id=1, source_target_pairs={{0,1},{1,0},{2,3},{3,2},{4,5},{5,4},{6,7},{7,6},{8,9},{9,8},{10,11... | collective-permute-start | bytes 2359304 | tf_op jit(solution)/shard_map/cond/branch_1_fun/ppermute | solution.py:49
  55.1 24.0 %collective-permute-start.51 = (bf16[3,192,640]{2,1,0:T(8,128)(2,1)}, bf16[3,192,640]{2,1,0:T(8,128)(2,1)}, u32[]{:S(2)}, u32[]{:S(2)}) collective-permute-start(bf16[3,192,640]{2,1,0:T(8,128)(2,1)} %branch_1_fun.35), channel_id=1, source_target_pairs={{0,4},{4,0},{8,12},{12,8},{16,20},{20,16},{24,28},{28,24},{1,5},{5... | collective-permute-start | bytes 2211848 | tf_op jit(solution)/shard_map/cond/branch_1_fun/ppermute | solution.py:49
  82.7 61.0 %collective-permute-start.56 = (bf16[3,384,640]{2,1,0:T(8,128)(2,1)}, bf16[3,384,640]{2,1,0:T(8,128)(2,1)}, u32[]{:S(2)}, u32[]{:S(2)}) collective-permute-start(bf16[3,384,640]{2,1,0:T(8,128)(2,1)} %constant_dynamic-update-slice_fusion.3.refs_1_.refs_11_.refs_3_), channel_id=1, source_target_pairs={{0,8},{4,12},{8,16},{12,20},{16,24},{20,28},{24,0},{28,4},{1,9},{5... | collective-permute-start | bytes 4423688 | tf_op jit(solution)/shard_map/ppermute | solution.py:49
  88.4 56.7 %collective-permute-start.55 = (bf16[512,1536]{1,0:T(8,128)(2,1)}, bf16[512,1536]{1,0:T(8,128)(2,1)}, u32[]{:S(2)}, u32[]{:S(2)}) collective-permute-start(bf16[512,1536]{1,0:T(8,128)(2,1)} %shard_map.264.refs_7_), channel_id=1, source_target_pairs={{0,4},{4,0},{8,12},{12,8},{16,20},{20,16},{24,28},{28,24},{1,5},{5... | collective-permute-start | bytes 4718600 | tf_op jit(solution)/shard_map/ppermute | solution.py:49
  89.9 55.2 %collective-permute-start.54 = (bf16[3,384,512]{2,1,0:T(8,128)(2,1)}, bf16[3,384,512]{2,1,0:T(8,128)(2,1)}, u32[]{:S(2)}, u32[]{:S(2)}) collective-permute-start(bf16[3,384,512]{2,1,0:T(8,128)(2,1)} %shard_map.261.refs_2_.refs_11_.refs_7_), channel_id=1, source_target_pairs={{0,8},{4,12},{8,16},{12,20},{16,24},{20,28},{24,0},{28,4},{1,9},{5... | collective-permute-start | bytes 3538952 | tf_op jit(solution)/shard_map/ppermute | solution.py:49
  109.9 19.6 %collective-permute-start.1 = (bf16[256,1536]{1,0:T(8,128)(2,1)S(1)}, bf16[256,1536]{1,0:T(8,128)(2,1)S(1)}, u32[]{:S(2)}, u32[]{:S(2)}) collective-permute-start(bf16[256,1536]{1,0:T(8,128)(2,1)S(1)} %get-tuple-element.333), channel_id=1, source_target_pairs={{0,2},{1,3},{2,0},{3,1},{4,6},{5,7},{6,4},{7,5},{8,10},{9,11},{10,... | collective-permute-start | bytes 2359304 | tf_op jit(solution)/shard_map/cond/branch_1_fun/ppermute | solution.py:49
  143.7 74.5 %collective-permute-start.57 = (bf16[512,1536]{1,0:T(8,128)(2,1)}, bf16[512,1536]{1,0:T(8,128)(2,1)}, u32[]{:S(2)}, u32[]{:S(2)}) collective-permute-start(bf16[512,1536]{1,0:T(8,128)(2,1)} %shard_map.264.refs_7_), channel_id=1, source_target_pairs={{0,1},{1,0},{2,3},{3,2},{4,5},{5,4},{6,7},{7,6},{8,9},{9,8},{10,11... | collective-permute-start | bytes 4718600 | tf_op jit(solution)/shard_map/ppermute | solution.py:49
  143.7 37.1 %collective-permute-start.59 = (bf16[3,384,640]{2,1,0:T(8,128)(2,1)}, bf16[3,384,640]{2,1,0:T(8,128)(2,1)}, u32[]{:S(2)}, u32[]{:S(2)}) collective-permute-start(bf16[3,384,640]{2,1,0:T(8,128)(2,1)} %shard_map.266.refs_3_.refs_14_.refs_6_), channel_id=1, source_target_pairs={{0,8},{4,12},{8,16},{12,20},{16,24},{20,28},{24,0},{28,4},{1,9},{5... | collective-permute-start | bytes 4423688 | tf_op jit(solution)/shard_map/ppermute | solution.py:49
  145.1 20.0 %collective-permute-start.4 = (bf16[256,1536]{1,0:T(8,128)(2,1)}, bf16[256,1536]{1,0:T(8,128)(2,1)}, u32[]{:S(2)}, u32[]{:S(2)}) collective-permute-start(bf16[256,1536]{1,0:T(8,128)(2,1)} %get-tuple-element.342), channel_id=1, source_target_pairs={{0,2},{1,3},{2,0},{3,1},{4,6},{5,7},{6,4},{7,5},{8,10},{9,11},{10,... | collective-permute-start | bytes 2359304 | tf_op jit(solution)/shard_map/cond/branch_1_fun/ppermute | solution.py:49
  146.3 19.7 %collective-permute-start.5 = (bf16[256,1536]{1,0:T(8,128)(2,1)}, bf16[256,1536]{1,0:T(8,128)(2,1)}, u32[]{:S(2)}, u32[]{:S(2)}) collective-permute-start(bf16[256,1536]{1,0:T(8,128)(2,1)} %get-tuple-element.343), channel_id=1, source_target_pairs={{0,4},{4,0},{8,12},{12,8},{16,20},{20,16},{24,28},{28,24},{1,5},{5... | collective-permute-start | bytes 2359304 | tf_op jit(solution)/shard_map/cond/branch_1_fun/ppermute | solution.py:49
  147.8 21.1 %collective-permute-start.6 = (bf16[512,1536]{1,0:T(8,128)(2,1)}, bf16[512,1536]{1,0:T(8,128)(2,1)}, u32[]{:S(2)}, u32[]{:S(2)}) collective-permute-start(bf16[512,1536]{1,0:T(8,128)(2,1)} %get-tuple-element.770), channel_id=1, source_target_pairs={{0,1},{1,0},{2,3},{3,2},{4,5},{5,4},{6,7},{7,6},{8,9},{9,8},{10,11... | collective-permute-start | bytes 4718600 | tf_op jit(solution)/shard_map/cond/branch_1_fun/ppermute | solution.py:49
  168.9 49.3 %collective-permute-start.58 = (bf16[512,1536]{1,0:T(8,128)(2,1)}, bf16[512,1536]{1,0:T(8,128)(2,1)}, u32[]{:S(2)}, u32[]{:S(2)}) collective-permute-start(bf16[512,1536]{1,0:T(8,128)(2,1)} %shard_map.265.refs_2_.refs_8_), channel_id=1, source_target_pairs={{0,1},{1,0},{2,3},{3,2},{4,5},{5,4},{6,7},{7,6},{8,9},{9,8},{10,11... | collective-permute-start | bytes 4718600 | tf_op jit(solution)/shard_map/ppermute | solution.py:49
  180.8 36.1 %collective-permute-start.60 = (bf16[3,384,640]{2,1,0:T(8,128)(2,1)}, bf16[3,384,640]{2,1,0:T(8,128)(2,1)S(1)}, u32[]{:S(2)}, u32[]{:S(2)}) collective-permute-start(bf16[3,384,640]{2,1,0:T(8,128)(2,1)} %shard_map.268.refs_13_.refs_5_), channel_id=1, source_target_pairs={{0,8},{4,12},{8,16},{12,20},{16,24},{20,28},{24,0},{28,4},{1,9},{5... | collective-permute-start | bytes 4423688 | tf_op jit(solution)/shard_map/ppermute | solution.py:49
  218.0 29.2 %collective-permute-start.61 = (bf16[3,384,512]{2,1,0:T(8,128)(2,1)}, bf16[3,384,512]{2,1,0:T(8,128)(2,1)}, u32[]{:S(2)}, u32[]{:S(2)}) collective-permute-start(bf16[3,384,512]{2,1,0:T(8,128)(2,1)} %shard_map.270.refs_14_.refs_10_), channel_id=1, source_target_pairs={{0,8},{4,12},{8,16},{12,20},{16,24},{20,28},{24,0},{28,4},{1,9},{5... | collective-permute-start | bytes 3538952 | tf_op jit(solution)/shard_map/ppermute | solution.py:49
  247.1 28.4 %collective-permute-start.62 = (bf16[3,384,512]{2,1,0:T(8,128)(2,1)}, bf16[3,384,512]{2,1,0:T(8,128)(2,1)}, u32[]{:S(2)}, u32[]{:S(2)}) collective-permute-start(bf16[3,384,512]{2,1,0:T(8,128)(2,1)} %shard_map.271.refs_13_.refs_9_), channel_id=1, source_target_pairs={{0,8},{4,12},{8,16},{12,20},{16,24},{20,28},{24,0},{28,4},{1,9},{5... | collective-permute-start | bytes 3538952 | tf_op jit(solution)/shard_map/ppermute | solution.py:49
  275.6 39.9 %collective-permute-start.63 = (bf16[3,384,640]{2,1,0:T(8,128)(2,1)}, bf16[3,384,640]{2,1,0:T(8,128)(2,1)}, u32[]{:S(2)}, u32[]{:S(2)}) collective-permute-start(bf16[3,384,640]{2,1,0:T(8,128)(2,1)} %shard_map.275), channel_id=1, source_target_pairs={{0,8},{4,12},{8,16},{12,20},{16,24},{20,28},{24,0},{28,4},{1,9},{5... | collective-permute-start | bytes 4423688 | tf_op jit(solution)/shard_map/ppermute | solution.py:49
  318.8 36.7 %collective-permute-start.64 = (bf16[3,384,640]{2,1,0:T(8,128)(2,1)}, bf16[3,384,640]{2,1,0:T(8,128)(2,1)}, u32[]{:S(2)}, u32[]{:S(2)}) collective-permute-start(bf16[3,384,640]{2,1,0:T(8,128)(2,1)} %fusion.12.refs_1_), channel_id=1, source_target_pairs={{0,8},{4,12},{8,16},{12,20},{16,24},{20,28},{24,0},{28,4},{1,9},{5... | collective-permute-start | bytes 4423688 | tf_op jit(solution)/shard_map/ppermute | solution.py:49
  329.6 21.0 %collective-permute-start.10 = (bf16[256,1536]{1,0:T(8,128)(2,1)}, bf16[256,1536]{1,0:T(8,128)(2,1)}, u32[]{:S(2)}, u32[]{:S(2)}) collective-permute-start(bf16[256,1536]{1,0:T(8,128)(2,1)} %get-tuple-element.347.refs_13_), channel_id=1, source_target_pairs={{0,2},{1,3},{2,0},{3,1},{4,6},{5,7},{6,4},{7,5},{8,10},{9,11},{10,... | collective-permute-start | bytes 2359304 | tf_op jit(solution)/shard_map/cond/branch_1_fun/ppermute | solution.py:49
  330.6 20.0 %collective-permute-start.11 = (bf16[256,1536]{1,0:T(8,128)(2,1)}, bf16[256,1536]{1,0:T(8,128)(2,1)}, u32[]{:S(2)}, u32[]{:S(2)}) collective-permute-start(bf16[256,1536]{1,0:T(8,128)(2,1)} %get-tuple-element.348), channel_id=1, source_target_pairs={{0,4},{4,0},{8,12},{12,8},{16,20},{20,16},{24,28},{28,24},{1,5},{5... | collective-permute-start | bytes 2359304 | tf_op jit(solution)/shard_map/cond/branch_1_fun/ppermute | solution.py:49
  358.7 39.7 %collective-permute-start.65 = (bf16[3,384,640]{2,1,0:T(8,128)(2,1)}, bf16[3,384,640]{2,1,0:T(8,128)(2,1)}, u32[]{:S(2)}, u32[]{:S(2)}) collective-permute-start(bf16[3,384,640]{2,1,0:T(8,128)(2,1)} %fusion.11.refs_1_), channel_id=1, source_target_pairs={{0,8},{4,12},{8,16},{12,20},{16,24},{20,28},{24,0},{28,4},{1,9},{5... | collective-permute-start | bytes 4423688 | tf_op jit(solution)/shard_map/ppermute | solution.py:49
  376.2 18.0 %collective-permute-start.14 = (bf16[256,1536]{1,0:T(8,128)(2,1)}, bf16[256,1536]{1,0:T(8,128)(2,1)}, u32[]{:S(2)}, u32[]{:S(2)}) collective-permute-start(bf16[256,1536]{1,0:T(8,128)(2,1)} %get-tuple-element.794.refs_11_), channel_id=1, source_target_pairs={{0,2},{1,3},{2,0},{3,1},{4,6},{5,7},{6,4},{7,5},{8,10},{9,11},{10,... | collective-permute-start | bytes 2359304 | tf_op jit(solution)/shard_map/cond/branch_1_fun/ppermute | solution.py:49
  377.3 16.9 %collective-permute-start.15 = (bf16[256,1536]{1,0:T(8,128)(2,1)}, bf16[256,1536]{1,0:T(8,128)(2,1)}, u32[]{:S(2)}, u32[]{:S(2)}) collective-permute-start(bf16[256,1536]{1,0:T(8,128)(2,1)} %get-tuple-element.794.refs_11_), channel_id=1, source_target_pairs={{0,1},{1,0},{2,3},{3,2},{4,5},{5,4},{6,7},{7,6},{8,9},{9,8},{10,11... | collective-permute-start | bytes 2359304 | tf_op jit(solution)/shard_map/cond/branch_1_fun/ppermute | solution.py:49
  394.1 35.3 %collective-permute-start.66 = (bf16[3,384,512]{2,1,0:T(8,128)(2,1)}, bf16[3,384,512]{2,1,0:T(8,128)(2,1)}, u32[]{:S(2)}, u32[]{:S(2)}) collective-permute-start(bf16[3,384,512]{2,1,0:T(8,128)(2,1)} %shard_map.282), channel_id=1, source_target_pairs={{0,8},{4,12},{8,16},{12,20},{16,24},{20,28},{24,0},{28,4},{1,9},{5... | collective-permute-start | bytes 3538952 | tf_op jit(solution)/shard_map/ppermute | solution.py:49
  402.1 31.1 %collective-permute-start.67 = (bf16[3,192,640]{2,1,0:T(8,128)(2,1)}, bf16[3,192,640]{2,1,0:T(8,128)(2,1)}, u32[]{:S(2)}, u32[]{:S(2)}) collective-permute-start(bf16[3,192,640]{2,1,0:T(8,128)(2,1)} %shard_map.284), channel_id=1, source_target_pairs={{0,4},{4,0},{8,12},{12,8},{16,20},{20,16},{24,28},{28,24},{1,5},{5... | collective-permute-start | bytes 2211848 | tf_op jit(solution)/shard_map/ppermute | solution.py:49
  432.4 30.7 %collective-permute-start.68 = (bf16[3,384,512]{2,1,0:T(8,128)(2,1)}, bf16[3,384,512]{2,1,0:T(8,128)(2,1)}, u32[]{:S(2)}, u32[]{:S(2)}) collective-permute-start(bf16[3,384,512]{2,1,0:T(8,128)(2,1)} %fusion.15.refs_1_), channel_id=1, source_target_pairs={{0,8},{4,12},{8,16},{12,20},{16,24},{20,28},{24,0},{28,4},{1,9},{5... | collective-permute-start | bytes 3538952 | tf_op jit(solution)/shard_map/ppermute | solution.py:49
  433.8 23.0 %collective-permute-start.21 = (bf16[2,256,1536]{2,1,0:T(8,128)(2,1)}, bf16[2,256,1536]{2,1,0:T(8,128)(2,1)}, u32[]{:S(2)}, u32[]{:S(2)}) collective-permute-start(bf16[2,256,1536]{2,1,0:T(8,128)(2,1)} %get-tuple-element.431.refs_11_), channel_id=1, source_target_pairs={{0,1},{1,0},{2,3},{3,2},{4,5},{5,4},{6,7},{7,6},{8,9},{9,8},{10,11... | collective-permute-start | bytes 4718600 | tf_op jit(solution)/shard_map/cond/branch_1_fun/ppermute | solution.py:49
  443.6 11.4 %collective-permute-start.20 = (bf16[192,1024]{1,0:T(8,128)(2,1)S(1)}, bf16[192,1024]{1,0:T(8,128)(2,1)S(1)}, u32[]{:S(2)}, u32[]{:S(2)}) collective-permute-start(bf16[192,1024]{1,0:T(8,128)(2,1)S(1)} %get-tuple-element.436), channel_id=1, source_target_pairs={{0,4},{4,0},{8,12},{12,8},{16,20},{20,16},{24,28},{28,24},{1,5},{5... | collective-permute-start | bytes 1179656 | tf_op jit(solution)/shard_map/cond/branch_1_fun/ppermute | solution.py:49
  466.1 57.2 %collective-permute-start.69 = (bf16[3,384,512]{2,1,0:T(8,128)(2,1)}, bf16[3,384,512]{2,1,0:T(8,128)(2,1)}, u32[]{:S(2)}, u32[]{:S(2)}) collective-permute-start(bf16[3,384,512]{2,1,0:T(8,128)(2,1)} %fusion.14.refs_1_), channel_id=1, source_target_pairs={{0,8},{4,12},{8,16},{12,20},{16,24},{20,28},{24,0},{28,4},{1,9},{5... | collective-permute-start | bytes 3538952 | tf_op jit(solution)/shard_map/ppermute | solution.py:49
  466.1 19.6 %collective-permute-start.28 = (bf16[256,1536]{1,0:T(8,128)(2,1)}, bf16[256,1536]{1,0:T(8,128)(2,1)}, u32[]{:S(2)}, u32[]{:S(2)}) collective-permute-start(bf16[256,1536]{1,0:T(8,128)(2,1)} %get-tuple-element.444.refs_1_), channel_id=1, source_target_pairs={{0,2},{1,3},{2,0},{3,1},{4,6},{5,7},{6,4},{7,5},{8,10},{9,11},{10,... | collective-permute-start | bytes 2359304 | tf_op jit(solution)/shard_map/cond/branch_1_fun/ppermute | solution.py:49
  468.2 36.2 %collective-permute-start.23 = (bf16[192,1024]{1,0:T(8,128)(2,1)}, bf16[192,1024]{1,0:T(8,128)(2,1)}, u32[]{:S(2)}, u32[]{:S(2)}) collective-permute-start(bf16[192,1024]{1,0:T(8,128)(2,1)} %get-tuple-element.441), channel_id=1, source_target_pairs={{0,8},{4,12},{8,16},{12,20},{16,24},{20,28},{24,0},{28,4},{1,9},{5... | collective-permute-start | bytes 1179656 | tf_op jit(solution)/shard_map/cond/branch_1_fun/ppermute | solution.py:49
  479.1 26.6 %collective-permute-start.26 = (bf16[192,1024]{1,0:T(8,128)(2,1)}, bf16[192,1024]{1,0:T(8,128)(2,1)}, u32[]{:S(2)}, u32[]{:S(2)}) collective-permute-start(bf16[192,1024]{1,0:T(8,128)(2,1)} %branch_1_fun.53), channel_id=1, source_target_pairs={{0,4},{4,0},{8,12},{12,8},{16,20},{20,16},{24,28},{28,24},{1,5},{5... | collective-permute-start | bytes 1179656 | tf_op jit(solution)/shard_map/cond/branch_1_fun/ppermute | solution.py:49
  491.0 28.9 %collective-permute-start.29 = (bf16[256,1536]{1,0:T(8,128)(2,1)S(1)}, bf16[256,1536]{1,0:T(8,128)(2,1)S(1)}, u32[]{:S(2)}, u32[]{:S(2)}) collective-permute-start(bf16[256,1536]{1,0:T(8,128)(2,1)S(1)} %get-tuple-element.450), channel_id=1, source_target_pairs={{0,2},{1,3},{2,0},{3,1},{4,6},{5,7},{6,4},{7,5},{8,10},{9,11},{10,... | collective-permute-start | bytes 2359304 | tf_op jit(solution)/shard_map/cond/branch_1_fun/ppermute | solution.py:49
  492.4 27.4 %collective-permute-start.30 = (bf16[256,1536]{1,0:T(8,128)(2,1)S(1)}, bf16[256,1536]{1,0:T(8,128)(2,1)S(1)}, u32[]{:S(2)}, u32[]{:S(2)}) collective-permute-start(bf16[256,1536]{1,0:T(8,128)(2,1)S(1)} %get-tuple-element.451), channel_id=1, source_target_pairs={{0,4},{4,0},{8,12},{12,8},{16,20},{20,16},{24,28},{28,24},{1,5},{5... | collective-permute-start | bytes 2359304 | tf_op jit(solution)/shard_map/cond/branch_1_fun/ppermute | solution.py:49
  505.7 11.9 %collective-permute-start.25 = (bf16[192,1024]{1,0:T(8,128)(2,1)S(1)}, bf16[192,1024]{1,0:T(8,128)(2,1)}, u32[]{:S(2)}, u32[]{:S(2)}) collective-permute-start(bf16[192,1024]{1,0:T(8,128)(2,1)S(1)} %fusion.4), channel_id=1, source_target_pairs={{0,8},{4,12},{8,16},{12,20},{16,24},{20,28},{24,0},{28,4},{1,9},{5... | collective-permute-start | bytes 1179656 | tf_op jit(solution)/shard_map/cond/branch_1_fun/ppermute | solution.py:49
  505.8 17.6 %collective-permute-start.27 = (bf16[192,1024]{1,0:T(8,128)(2,1)}, bf16[192,1024]{1,0:T(8,128)(2,1)}, u32[]{:S(2)}, u32[]{:S(2)}) collective-permute-start(bf16[192,1024]{1,0:T(8,128)(2,1)} %branch_1_fun.54), channel_id=1, source_target_pairs={{0,4},{4,0},{8,12},{12,8},{16,20},{20,16},{24,28},{28,24},{1,5},{5... | collective-permute-start | bytes 1179656 | tf_op jit(solution)/shard_map/cond/branch_1_fun/ppermute | solution.py:49
  526.8 46.0 %collective-permute-start.70 = (bf16[3,192,512]{2,1,0:T(8,128)(2,1)}, bf16[3,192,512]{2,1,0:T(8,128)(2,1)}, u32[]{:S(2)}, u32[]{:S(2)}) collective-permute-start(bf16[3,192,512]{2,1,0:T(8,128)(2,1)} %shard_map.291), channel_id=1, source_target_pairs={{0,4},{4,0},{8,12},{12,8},{16,20},{20,16},{24,28},{28,24},{1,5},{5... | collective-permute-start | bytes 1769480 | tf_op jit(solution)/shard_map/ppermute | solution.py:49
  540.7 14.4 %collective-permute-start.31 = (bf16[192,1024]{1,0:T(8,128)(2,1)}, bf16[192,1024]{1,0:T(8,128)(2,1)}, u32[]{:S(2)}, u32[]{:S(2)}) collective-permute-start(bf16[192,1024]{1,0:T(8,128)(2,1)} %get-tuple-element.455), channel_id=1, source_target_pairs={{0,8},{4,12},{8,16},{12,20},{16,24},{20,28},{24,0},{28,4},{1,9},{5... | collective-permute-start | bytes 1179656 | tf_op jit(solution)/shard_map/cond/branch_1_fun/ppermute | solution.py:49
  542.7 16.7 %collective-permute-start.32 = (bf16[128,1536]{1,0:T(8,128)(2,1)}, bf16[128,1536]{1,0:T(8,128)(2,1)}, u32[]{:S(2)}, u32[]{:S(2)}) collective-permute-start(bf16[128,1536]{1,0:T(8,128)(2,1)} %get-tuple-element.465), channel_id=1, source_target_pairs={{0,4},{4,0},{8,12},{12,8},{16,20},{20,16},{24,28},{28,24},{1,5},{5... | collective-permute-start | bytes 1179656 | tf_op jit(solution)/shard_map/cond/branch_1_fun/ppermute | solution.py:49
  543.6 15.8 %collective-permute-start.33 = (bf16[128,1536]{1,0:T(8,128)(2,1)}, bf16[128,1536]{1,0:T(8,128)(2,1)}, u32[]{:S(2)}, u32[]{:S(2)}) collective-permute-start(bf16[128,1536]{1,0:T(8,128)(2,1)} %get-tuple-element.466), channel_id=1, source_target_pairs={{0,2},{1,3},{2,0},{3,1},{4,6},{5,7},{6,4},{7,5},{8,10},{9,11},{10,... | collective-permute-start | bytes 1179656 | tf_op jit(solution)/shard_map/cond/branch_1_fun/ppermute | solution.py:49
  (77 other events, 849.0 us)

commit v3 on v2

--- a/solution.py
+++ b/solution.py
@@ -86,11 +86,10 @@
     return lax.cond(lax.axis_index("tensor") >= 0, work, empty, *args)
 
 
-def all_sum(vector):
+def all_sum(vector, axis, first=0):
     total = vector
-    for axis in ("tensor", "dp"):
-        for bit in range(lax.axis_size(axis).bit_length() - 1):
-            total = total + moved(total, axis, lambda index: index ^ (1 << bit))
+    for bit in range(first, lax.axis_size(axis).bit_length() - 1):
+        total = total + moved(total, axis, lambda index: index ^ (1 << bit))
     return total
 
 
@@ -114,7 +113,7 @@
     return jax.ShapeDtypeStruct(tuple(shape), kind)
 
 
-def call(kernel, args, specs, outs, scratch=(), tokens=(), out_specs=None, room=16):
+def call(kernel, args, specs, outs, scratch=(), tokens=(), out_specs=None, room=16, cost=2 * 10**11):
     tokens = list(tokens)
 
     def body(*refs):
@@ -127,7 +126,7 @@
         out_specs=[in_vmem] * len(outs) if out_specs is None else out_specs,
         scratch_shapes=list(scratch),
         compiler_params=pltpu.CompilerParams(vmem_limit_bytes=room * 2**20),
-        cost_estimate=pl.CostEstimate(flops=2 * 10**11, bytes_accessed=1, transcendentals=0),
+        cost_estimate=pl.CostEstimate(flops=cost, bytes_accessed=1, transcendentals=0),
     )(*args, *tokens)
 
 
@@ -181,7 +180,7 @@
     for cut in cuts:
         outs += [shaped((3, share, size_of(cut))), shaped((3, 2 * share, size_of(cut)))]
     return call(
-        kernel, [ranks, *matrices], [in_smem] + [in_vmem] * 3, outs, tokens=tokens
+        kernel, [ranks, *matrices], [in_smem] + [in_vmem] * 3, outs, tokens=tokens, cost=1
     )
 
 
@@ -226,7 +225,9 @@
         scale = lax.rsqrt(jnp.mean(x * x, axis=1, keepdims=True) + eps_norm)
         out_ref[...] = (x * scale * gain_ref[...]).astype(low)
 
-    return call(kernel, [rows, gain[None]], [in_vmem] * 2, [shaped(rows.shape)], tokens=tokens)[0]
+    return call(
+        kernel, [rows, gain[None]], [in_vmem] * 2, [shaped(rows.shape)], tokens=tokens, cost=1
+    )[0]
 
 
 def join_near(ranks, keep, came, tokens=()):
@@ -286,7 +287,7 @@
     )
 
 
-def join_group(keep, came, tokens=()):
+def join_group(keep, came, tokens=(), **more):
     quarter = keep.shape[0] // 4
 
     def kernel(keep_ref, came_ref, top_ref, bottom_ref, own_ref):
@@ -305,10 +306,11 @@
         [in_vmem] * 2,
         [shaped(shape), shaped(shape), shaped((2 * quarter, keep.shape[1]), wide)],
         tokens=tokens,
-    )
-
-
-def join_pair(own, came_top, came_bottom, tokens=()):
+        **more,
+    )
+
+
+def join_pair(own, came_top, came_bottom, tokens=(), **more):
     half = own.shape[0] // 4
 
     def kernel(own_ref, came_top_ref, came_bottom_ref, top_ref, bottom_ref, out_ref):
@@ -326,6 +328,7 @@
         [in_vmem] * 3,
         [shaped(shape), shaped(shape), shaped((2 * half, own.shape[1]), wide)],
         tokens=tokens,
+        **more,
     )
 
 
@@ -372,6 +375,7 @@
         [in_vmem] * 5,
         [shaped(rows.shape, wide)],
         tokens=tokens,
+        cost=1,
     )[0]
 
 
@@ -384,7 +388,7 @@
             out_ref[here] = (mid_ref[here] + own_ref[here] + came[...].astype(wide)).astype(low)
 
     return call(
-        kernel, [mid, own, came_top, came_bottom], [in_vmem] * 4, [shaped(mid.shape)], tokens=tokens
+        kernel, [mid, own, came_top, came_bottom], [in_vmem] * 4, [shaped(mid.shape)], tokens=tokens, cost=1
     )[0]
 
 
@@ -847,7 +851,7 @@
     return call(kernel, args, specs, outs, scratch, tokens, [anywhere] * len(outs), 62)
 
 
-def back_rows(ranks, lefts, chunks, inner, tokens=()):
+def back_rows(ranks, lefts, chunks, inner, tokens=(), partial=None, whole=False):
     length = lefts[0].shape[0]
     blocks = len(chunks[0])
     width = chunks[0][0].shape[1] * blocks
@@ -865,10 +869,11 @@
 
         left_refs = take(len(chunks))
         weight_refs = [take(blocks) for _ in chunks]
-        keep_ref, send_ref = take(2)
+        partial_refs = take(partial is not None)
+        out_refs = take(1 if whole else 2)
         weight_vs = take(len(chunks))
         left_vs = take(len(chunks))
-        total_v, weight_sems, left_sems, out_sems = refs
+        total_v, weight_sems, left_sems, out_sems = refs[:4]
         copies = []
         for chunk, sources in enumerate(weight_refs):
             target = weight_vs[chunk]
@@ -886,6 +891,12 @@
                     for chunk in range(len(chunks))
                 ]
             )
+            if partial is not None:
+                arriving[-1].append(
+                    pltpu.make_async_copy(
+                        partial_refs[0].at[here], refs[4].at[here], left_sems.at[len(chunks), k]
+                    )
+                )
             for copy in arriving[-1]:
                 copy.start()
         leaving = []
@@ -899,32 +910,36 @@
                 arriving[number][chunk].wait()
                 term = dot_nt(left_vs[chunk][here], weight_vs[chunk][...])
                 total = term if total is None else total + term
+            if partial is not None:
+                arriving[number][-1].wait()
+                total = total + refs[4][here].astype(wide)
             total_v[here] = total.astype(low)
-            target = keep_ref if k < 2 else send_ref
-            leaving.append(
-                pltpu.make_async_copy(
-                    total_v.at[here], target.at[pl.ds(k % 2 * step, step)], out_sems.at[k]
-                )
-            )
+            if whole:
+                target = out_refs[0].at[here]
+            else:
+                target = out_refs[k // 2].at[pl.ds(k % 2 * step, step)]
+            leaving.append(pltpu.make_async_copy(total_v.at[here], target, out_sems.at[k]))
             leaving[-1].start()
         for copy in leaving:
             copy.wait()
 
-    return call(
-        kernel,
-        [ranks, *lefts] + [block for chunk in chunks for block in chunk],
-        [in_smem] + [anywhere] * (len(chunks) * (1 + blocks)),
-        [shaped((length // 2, width))] * 2,
+    extra = [] if partial is None else [partial]
+    return call(
+        kernel,
+        [ranks, *lefts] + [block for chunk in chunks for block in chunk] + extra,
+        [in_smem] + [anywhere] * (len(chunks) * (1 + blocks) + len(extra)),
+        [shaped((length, width))] if whole else [shaped((length // 2, width))] * 2,
         [pltpu.VMEM((width, size), low) for size in wide_sizes]
         + [pltpu.VMEM((length, size), low) for size in wide_sizes]
         + [
             pltpu.VMEM((length, width), low),
             pltpu.SemaphoreType.DMA((len(chunks), blocks, 3)),
-            pltpu.SemaphoreType.DMA((len(chunks), 4)),
+            pltpu.SemaphoreType.DMA((len(chunks) + 1, 4)),
             pltpu.SemaphoreType.DMA((4,)),
-        ],
+        ]
+        + [pltpu.VMEM((length, width), low)] * len(extra),
         tokens,
-        [anywhere] * 2,
+        [anywhere] * (1 if whole else 2),
         60,
     )
 
@@ -956,6 +971,7 @@
         [ranks, biases, *gains],
         [in_smem] + [in_vmem] * (1 + len(gains)),
         [shaped((bias_rows + len(gains) * gain_rows, HD), wide)],
+        cost=1,
     )[0]
 
 
@@ -1038,38 +1054,32 @@
     def begin():
         pair_kv = jnp.concatenate([w_key, w_value], axis=1)
         parts_kv = [pair_kv, across_core(pair_kv), across_y(pair_kv), across_both(pair_kv)]
-        normed = normalize(tokens, gain_attn, [pair_kv])
-        packed = pack(ranks, (w_gate, w_up, w_down.T), cuts, [normed])
-        return attention_block(ranks, w_query, w_out.T, parts_kv), normed, packed
-
-    def along_z(block, normed, *sent):
+        return attention_block(ranks, w_query, w_out.T, parts_kv)
+
+    def pair_block(block, came):
+        return lax.dynamic_update_slice_in_dim(block, came, (1 - dp_rank % 2) * share, 1)
+
+    def along_z(block):
+        line, crossed = [block], []
+        packed = pack(ranks, (w_gate, w_up, w_down.T), cuts, [block])
+        normed = normalize(tokens, gain_attn, [packed[0]])
         far = across_y(normed)
         rows = [normed, across_core(normed), far, across_core(far)]
-        line, crossed = [block], []
         for _ in range(z_count - 1):
             crossed.append(across_x(line[-1]))
             line.append(up_line(line[-1]))
-        came = [across_x(after(sent[1], crossed[0]))]
-        came = [across_x(after(sent[0], came[0])), *came]
+        came = across_x(after(packed[0], crossed[0]))
         (grads,) = stack_rows([grad_out, across_y(after(grad_out, line[1]))], [(0, 1)])
         cosine, sine = angles_of(segment, HD)
         sine = jnp.where(jnp.arange(HD) < HD // 2, -sine, sine)
-        return rows, line, crossed, came, grads, cosine, sine
-
-    block, normed_one, packed = stage(begin)
-    rows_one, line, crossed, came_ffn, grad_near, cosine, sine = stage(
-        along_z, block, normed_one, *packed[::2]
-    )
+        return rows, line, crossed, pair_block(packed[1], came), packed[2:], grads, cosine, sine
+
+    rows_one, line, crossed, block, packed, grad_near, cosine, sine = stage(along_z, stage(begin))
     crossed.append(across_x(line[-1]))
     qkv_blocks = []
     for slot in range(z_count):
         qkv_blocks += [line[-slot % z_count], crossed[-slot % z_count]]
 
-    def pair_block(index, came):
-        return lax.dynamic_update_slice_in_dim(
-            packed[2 * index + 1], came, (1 - dp_rank % 2) * share, 1
-        )
-
     def next_hop(blocks, *others):
         if others:
             blocks[-1] = after(blocks[-1], *others)
@@ -1078,12 +1088,10 @@
     def in_slots(blocks):
         return blocks[:1] + blocks[:0:-1]
 
-    early, late = ([pair_block(index, came)] for index, came in enumerate(came_ffn))
+    early = [block]
     next_hop(early)
-    next_hop(late, crossed[-1])
-    grad_near = after(grad_near, crossed[-1])
-    grad_far = across_x(grad_near)
-    rows_one[0] = gate(rows_one[0], early[0], late[0], crossed[-1])
+    came_late = across_x(after(packed[0], crossed[-1]))
+    rows_one[0] = gate(rows_one[0], early[0], crossed[-1])
     key_bias = lax.dynamic_slice_in_dim(b_key, y_rank * HD, HD, 0)
     value_bias = lax.dynamic_slice_in_dim(b_value, y_rank * HD, HD, 0)
     bias = jnp.concatenate([b_query, key_bias, value_bias])
@@ -1093,17 +1101,27 @@
             ranks, rows_one, qkv_blocks, bias, cosine, sine, segment, others
         )
         sent, own = join_near(ranks, keep, across_core(send))
+        return kept, probs, sent, own
+
+    (query, key, value, heads_low), probs, sent, own = stage(attention)
+    late = [pair_block(packed[1], after(came_late, sent))]
+    next_hop(early, sent)
+    grad_near = after(grad_near, sent)
+    grad_far = across_x(grad_near)
+    sent = gate(sent, early[1], late[0])
+
+    def between():
         mid, top, bottom = middle(tokens, own, across_y(sent), gain_ffn)
         top, bottom, both = stack_rows(
             [top, across_x(top), bottom, across_y(bottom)], [(0, 1), (2, 3), (0, 1, 2, 3)]
         )
-        return kept, probs, mid, top, bottom, both
-
-    (query, key, value, heads_low), probs, mid_rows, top, bottom, both = stage(attention)
+        return mid, top, bottom, both, across_core(grad_near)
+
+    mid_rows, top, bottom, both, other_near = stage(between)
     next_hop(early, both)
-    grad_far, late[1] = after(grad_far, both), after(late[1], both)
-
-    top = gate(top, late[1], grad_far, early[1])
+    grad_far = after(grad_far, both)
+    other_far = across_core(grad_far)
+    top = gate(top, grad_far, early[2])
 
     def spread():
         far_top, far_bottom = across_y(top), across_x(bottom)
@@ -1119,7 +1137,7 @@
     rows_two = stage(spread)
     half = both.shape[0] // 2
     places = [(0, 0), (0, half), (1, 0), (2, 0), (3, 0), (3, half), (4, 0), (5, 0)]
-    grad_ffn = [grad_near, grad_far, across_core(grad_near), across_core(grad_far)]
+    grad_ffn = [grad_near, grad_far, other_near, other_far]
     while len(early) < z_count:
         next_hop(early, rows_two[-1])
 
@@ -1133,11 +1151,12 @@
     early_terms = ffn(ranks, rows_two, places, grad_ffn, None, saved, [saved[0][0]])
     while len(late) < z_count:
         next_hop(late, early_terms[0])
+    (partial,) = back_rows(ranks, [saved[0][1]], held, True, [early_terms[0]], whole=True)
     held.append(in_slots(late))
     early_hop = up_line(after(early_terms[0], late[-1]))
-    saved.append(feed(held[1], early_terms[1]))
+    saved.append(feed(held[1], partial))
     keep_two, send_two = back_rows(
-        ranks, [some[1] for some in saved], held, True, [early_terms[1]]
+        ranks, [saved[1][1]], held[1:], True, [early_terms[1]], partial
     )
 
     def next_sum(came, rest, slot, *others):
@@ -1151,37 +1170,34 @@
     def back():
         top, bottom, own = join_group(keep_two, across_core(send_two))
         came_top, came_bottom = across_y(top), across_x(bottom)
-        terms = ffn(ranks, rows_two, places, grad_ffn, None, saved[1:], [top])
-        return join_pair(own, came_top, came_bottom, [terms[0]]), terms
-
-    (top, bottom, own), late_terms = stage(back)
+        keep_out, send_out = back_rows(ranks, [some[0] for some in saved], held, False, [top])
+        return join_pair(own, came_top, came_bottom, [send_out]), keep_out, send_out
+
+    (top, bottom, own), keep_out, send_out = stage(back)
     early_sum = next_sum(early_hop, early_terms[1], z_count - 3, top)
     early_hop = up_line(early_sum)
     top = gate(top, early_sum)
 
     def back_middle():
+        came_top, came_bottom = across_x(top), across_y(bottom)
+        ends = join_group(keep_out, across_core(send_out))
         grad_mid, grad_low, gain_sum = middle_back(
-            mid_rows, gain_ffn, grad_out, own, across_x(top), across_y(bottom)
+            mid_rows, gain_ffn, grad_out, own, came_top, came_bottom, [ends[0]]
         )
-
         far = across_y(grad_low)
-        keep_out, send_out = back_rows(
-            ranks, [some[0] for some in saved], held, False, [grad_low]
-        )
-        far = after(far, send_out)
-        return grad_mid, grad_low, gain_sum, far, keep_out, send_out, across_core(grad_low)
-
-    grad_mid, grad_low, gain_two, far_attn, keep_out, send_out, near_attn = stage(
-        back_middle
-    )
-    for slot in range(z_count - 4, -1, -1):
+        terms = ffn(ranks, rows_two, places, grad_ffn, None, saved[1:], [grad_low])
+        far = after(far, terms[0])
+        return grad_mid, grad_low, gain_sum, far, ends, terms, across_core(grad_low)
+
+    grad_mid, grad_low, gain_two, far_attn, ends, late_terms, near_attn = stage(back_middle)
+    top_out, bottom_out, own_out = ends
+    came_top_out, came_bottom_out = across_y(top_out), across_x(bottom_out)
+    for slot in range(z_count - 4, 0, -1):
         early_sum = next_sum(early_hop, early_terms[1], slot, far_attn)
-        if slot:
-            early_hop = up_line(early_sum)
-    came_early = across_x(split_pair(ranks, early_sum))
+        early_hop = up_line(early_sum)
     late_hop = up_line(after(late_terms[0], far_attn))
 
-    far_attn = gate(far_attn, early_sum)
+    far_attn = gate(far_attn, early_hop)
 
     def back_attention():
         grad_attn = [grad_low, near_attn, far_attn, across_core(far_attn)]
@@ -1191,11 +1207,11 @@
         )
 
     grad_attn, (grad_qkv, bias_sums, gain_one, keep, send) = stage(back_attention)
-    came_early = after(came_early, send)
     late_sum = next_sum(late_hop, late_terms[1], z_count - 2, send)
     late_hop = up_line(late_sum)
 
-    send = gate(send, late_sum, came_early)
+    came_top_out, came_bottom_out = after(came_top_out, send), after(came_bottom_out, send)
+    send = gate(send, late_sum, came_top_out, came_bottom_out)
 
     def attention_sums():
         came = across_core(send)
@@ -1204,65 +1220,64 @@
         )
         sent, own = join_near(ranks, keep, came, [terms[0]])
         near, far = terms
+        small = all_sum(small_rows(ranks, bias_sums, (gain_two, gain_one)), "tensor")
+        ends = join_pair(own_out, came_top_out, came_bottom_out, [sent])
         return (
             near,
             far,
-            added(across_x(far[-1]), near[z_count - 1]),
+            added(after(across_x(far[-1]), ends[0]), near[z_count - 1]),
+            small,
             sent,
             own,
-            across_core(after(send_out, came)),
+            ends,
         )
 
-    near_terms, far_terms, both_sum, sent, own, came_out = stage(
-        attention_sums
-    )
-    for slot in range(z_count - 3, 0, -1):
-        late_sum = next_sum(late_hop, late_terms[1], slot, sent)
-        late_hop = up_line(late_sum)
-
+    near_terms, far_terms, both_sum, small, sent, own, ends = stage(attention_sums)
     def joined(total, came, slot):
         return (
             up_line(total).astype(wide) + near_terms[slot].astype(wide) + came.astype(wide)
         ).astype(low)
 
+    late_sum = next_sum(late_hop, late_terms[1], z_count - 3, sent)
     sent = gate(sent, late_sum)
 
     def finish_first():
         came = [None] * z_count
         for slot in range(z_count - 2, -1, -1):
-            term = far_terms[slot]
-            came[slot] = across_x(after(term, sent if slot == z_count - 2 else came[slot + 1]))
-        came_one = across_y(sent)
-        top, bottom, own_out = join_group(keep_out, came_out, [came_one])
-        came_top, came_bottom = across_y(top), across_x(bottom)
+            came[slot] = across_x(after(far_terms[slot], sent if slot == z_count - 2 else came[slot + 1]))
+        sums = all_sum(small, "dp")
         total = both_sum
-        for slot in range(z_count - 2, 0, -1):
+        for slot in range(z_count - 2, -1, -1):
             total = joined(total, came[slot], slot)
-        return total, came[0], came_one, join_pair(own_out, came_top, came_bottom)
-
-    both_sum, came_both, came_one, ends = stage(finish_first)
-    late_sum = next_sum(late_hop, late_terms[1], 0, both_sum)
-    came_late = across_x(split_pair(ranks, late_sum))
-
-    both_sum = gate(both_sum, late_sum)
-
-    def finish():
-        total = joined(both_sum, came_both, 0)
+        return total, sums
+
+    both_sums, small = stage(finish_first)
+    for slot in range(z_count - 3, 0, -1):
+        late_sum = after(late_sum, both_sums)
+        late_hop = up_line(late_sum)
+        if slot > 1:
+            late_sum = next_sum(late_hop, late_terms[1], slot - 1)
+    both_sums = gate(both_sums, late_sum)
+
+    def finish_second():
         top, bottom, own_out = ends
-        came_top = across_x(top)
-        came_bottom = across_y(bottom)
+        came_top, came_bottom = across_x(top), across_y(bottom)
+        early = next_sum(early_hop, early_terms[1], 0, both_sums)
+        came_early = across_x(after(split_pair(ranks, early), came_top))
+        came_one = across_y(after(sent, came_bottom))
+        layer_out = layer_rows(mid_rows, own_out, came_top, came_bottom)
         grad_tokens = tokens_back(tokens, gain_attn, grad_mid, own, came_one)
-        layer_out = layer_rows(mid_rows, own_out, came_top, came_bottom)
-        small = all_sum(small_rows(ranks, bias_sums, (gain_two, gain_one)))
-        kv_sums = total[:, query_cols:qkv_cols].reshape(2, 2, -1, 2 * HD)
+        kv_sums = both_sums[:, query_cols:qkv_cols].reshape(2, 2, -1, 2 * HD)
         near_kv = pick(kv_sums, core, 1).astype(wide) + across_core(
             pick(kv_sums, 1 - core, 1)
         ).astype(wide)
         came_kv = across_y(pick(near_kv, 1 - y_rank, 0).astype(low)).astype(wide)
         both_kv = in_order(pick(near_kv, y_rank, 0), came_kv, y_rank, 0).reshape(2, -1, 2, HD)
-        return total, small, grad_tokens, layer_out, both_kv
-
-    both_sums, small, grad_tokens, layer_out, both_kv = stage(finish)
+        return grad_tokens, both_kv, layer_out, early, came_early
+
+    grad_tokens, both_kv, layer_out, early_sum, came_early = stage(finish_second)
+    late_sum = next_sum(late_hop, late_terms[1], 0, grad_tokens)
+    came_late = across_x(split_pair(ranks, late_sum))
     grad_w_gate, grad_w_up, grad_w_down = lay_out(
         ranks, [early_sum, late_sum], [came_early, came_late], cuts, ffn_cols
     )

time: 582 us -> 548 us (0.942)
  waiting for transfers between devices: 246 us -> 218 us
  local copies, waits for them, and re-layouts: 39.4 us -> 29 us
  Pallas kernels: 204 us -> 213 us
    ppermute x71, waiting for transfers between devices: 246 us -> 218 us  [moved(): return lax.ppermute(block, axis, route)]
    cond x58 -> x39, local copies, waits for them, and re-layouts: 22.5 us -> 12.8 us
    pallas_call x28 -> x29, Pallas kernels: 204 us -> 213 us  [call(): pl.pallas_call(body, out_shape=outs, in_specs=list(specs) + [anywhere] *...]
  transfers between devices with their start and end apart: 71 -> 71, of which waited for: 37 -> 41; matrix products, arithmetic and copies ran while one was open for 8% -> 7% of each run, Pallas kernels for 34% -> 38%
where the time goes in v3:
time: 548 us; the launch traced here: 543 us
  waiting for transfers between devices  218 us (40%)
  Pallas kernels  213 us (39%)
  starting transfers between devices  49.7 us (9%)
  other arithmetic  30.9 us (6%)
  local copies, waits for them, and re-layouts  29 us (5%)
    ppermute x71, waiting for transfers between devices, moved(): return lax.ppermute(block, axis, route)  218 us
    pallas_call x29, Pallas kernels, call(): pl.pallas_call(body, out_shape=outs, in_specs=list(specs) + [anywhere] *...  213 us
    ppermute x71, starting transfers between devices, moved(): return lax.ppermute(block, axis, route)  49.7 us
    convert_element_type x7, other arithmetic, added(): return (came.astype(wide) + part.astype(wide)).astype(low)  18.7 us
    cond x39, local copies, waits for them, and re-layouts  12.8 us
  transfers between devices with their start and end apart: 71, of which 41 were waited for; matrix products, arithmetic and copies ran while one was open for 7% of the time, Pallas kernels for 38%

profile of v3, /device:TPU:0, one launch (start us, length us, event | category | flops | bytes accessed | tf_op | source)
XLA Modules:
  0.0 542.9 jit_solution(8934289907241520985)
XLA Ops:
  0.8 10.1 %conditional.11 = (bf16[192,1024]{1,0:T(8,128)(2,1)}) conditional(s32[]{:T(128)} %convert_element_type.169, () %tuple.99, (bf16[384,192]{0,1:T(8,128)(2,1)}, bf16[48,256]{1,0:T(8,128)(2,1)}, bf16[48,256]{1,0:T(8,128)(2,1)}, s32[2]{0:T(128)S(1)}, bf16[192,384]{1,0:T(8,128)(2,1)}) %tuple.100), branch_computations={%region_0.1_spmd, %region_1.2_spmd} | conditional | flops 199999995904 | bytes 688257 | solution.py:86
  10.9 53.1 %conditional.12 = (bf16[256,1536]{1,0:T(8,128)(2,1)}, bf16[256,1536]{1,0:T(8,128)(2,1)}, bf16[256,1536]{1,0:T(8,128)(2,1)}, bf16[256,1536]{1,0:T(8,128)(2,1)}, b...) conditional(s32[]{:T(128)} %convert_element_type.169, () %tuple.98, ...), branch_computations={%region_2.3_spmd, %region_3.6_spmd} | conditional | flops 200000585728 | bytes 38090556 | solution.py:86
  12.5 3.6 branch_1_fun.35
  24.8 7.3 %collective-permute-done.44.refs_1_ = bf16[192,1024]{1,0:T(8,128)(2,1)} collective-permute-done((bf16[192,1024]{1,0:T(8,128)(2,1)}, bf16[192,1024]{1,0:T(8,128)(2,1)}, u32[]{:S(2)}, u32[]{:S(2)}) %collective-permute-start.44) | collective-permute-done | bytes 393248 | tf_op jit(solution)/shard_map/cond/branch_1_fun/ppermute | solution.py:49
  37.9 7.7 %collective-permute-done.45 = bf16[192,1024]{1,0:T(8,128)(2,1)} collective-permute-done((bf16[192,1024]{1,0:T(8,128)(2,1)}, bf16[192,1024]{1,0:T(8,128)(2,1)}, u32[]{:S(2)}, u32[]{:S(2)}) %collective-permute-start.45) | collective-permute-done | bytes 393248 | tf_op jit(solution)/shard_map/cond/branch_1_fun/ppermute | solution.py:49
  48.7 4.9 collective-permute-done.51.refs_1_
  58.1 6.0 %collective-permute-done.49 = bf16[192,1024]{1,0:T(8,128)(2,1)} collective-permute-done((bf16[192,1024]{1,0:T(8,128)(2,1)}, bf16[192,1024]{1,0:T(8,128)(2,1)}, u32[]{:S(2)}, u32[]{:S(2)}) %collective-permute-start.49) | collective-permute-done | bytes 393248 | tf_op jit(solution)/shard_map/cond/branch_1_fun/ppermute | solution.py:49
  65.5 7.8 %collective-permute-done.52.refs_2_.refs_1_ = bf16[192,1024]{1,0:T(8,128)(2,1)S(1)} collective-permute-done((bf16[192,1024]{1,0:T(8,128)(2,1)}, bf16[192,1024]{1,0:T(8,128)(2,1)S(1)}, u32[]{:S(2)}, u32[]{:S(2)}) %collective-permute-start.52) | collective-permute-done | bytes 393248 | tf_op jit(solution)/shard_map/ppermute | solution.py:49
  74.9 20.2 %conditional.13 = (bf16[1024,384]{1,0:T(8,128)(2,1)}, bf16[1024,128]{1,0:T(8,128)(2,1)}, bf16[1024,128]{1,0:T(8,128)(2,1)}, bf16[1024,384]{1,0:T(8,128)(2,1)}, b...) conditional(s32[]{:T(128)} %convert_element_type.169, ...), branch_computations={%region_6.7_spmd, %region_7.8_spmd} | conditional | flops 399999991808 | bytes 8388710 | solution.py:86
  75.1 14.2 %branch_1_fun.40 = (bf16[1024,384]{1,0:T(8,128)(2,1)}, bf16[1024,128]{1,0:T(8,128)(2,1)}, bf16[1024,128]{1,0:T(8,128)(2,1)}, bf16[1024,384]{1,0:T(8,128)(2,1)}, ...) custom-call(s32[2]{0:T(128)S(1)} %get-tuple-element.316.refs_0_, ...), custom_call_target="tpu_custom_call" | custom-call | flops 199999995904 | bytes 1 | tf_op jit(solution)/shard_map/cond/branch_1_fun/pallas_call | solution.py:122
  99.6 42.4 %conditional.14 = (f32[256,1536]{1,0:T(8,128)}, bf16[256,1536]{1,0:T(8,128)(2,1)}, bf16[256,1536]{1,0:T(8,128)(2,1)}, bf16[512,1536]{1,0:T(8,128)(2,1)}, bf16[512,1536]{1,0:T(8,128)(2,1)}) conditional(s32[]{:T(128)} %convert_element_type.169, () %tuple.106, (bf16[256,1536]{1,0:T(8,128)(2,1)}, f32[1536]{0:T(1024)S(1)}, ...), branch_computations={%region_8.9_spmd, %region_9.10_spmd} | conditional | flops 399999991808 | bytes 12595402 | solution.py:86
  100.7 18.4 %collective-permute-done.1.refs_2_ = bf16[256,1536]{1,0:T(8,128)(2,1)S(1)} collective-permute-done((bf16[256,1536]{1,0:T(8,128)(2,1)}, bf16[256,1536]{1,0:T(8,128)(2,1)S(1)}, u32[]{:S(2)}, u32[]{:S(2)}) %collective-permute-start.1) | collective-permute-done | bytes 786464 | tf_op jit(solution)/shard_map/cond/branch_1_fun/ppermute | solution.py:49
  123.7 16.4 %collective-permute-done.2.refs_1_ = bf16[128,1536]{1,0:T(8,128)(2,1)S(1)} collective-permute-done((bf16[128,1536]{1,0:T(8,128)(2,1)S(1)}, bf16[128,1536]{1,0:T(8,128)(2,1)S(1)}, u32[]{:S(2)}, u32[]{:S(2)}) %collective-permute-start.2) | collective-permute-done | bytes 393248 | tf_op jit(solution)/shard_map/cond/branch_1_fun/ppermute | solution.py:49
  142.2 24.0 %conditional.15 = (bf16[512,1536]{1,0:T(8,128)(2,1)S(1)}, bf16[256,1536]{1,0:T(8,128)(2,1)}, bf16[256,1536]{1,0:T(8,128)(2,1)}, bf16[512,1536]{1,0:T(8,128)(2,1)...) conditional(s32[]{:T(128)} %convert_element_type.169, () %tuple.105, (bf16[256,1536]{1,0:T(8,128)(2,1)}, ...), branch_computations={%region_10.11_spmd, %region_11.12_spmd} | conditional | bytes 22020344 | solution.py:86
  144.8 17.6 %collective-permute-done.5 = bf16[256,1536]{1,0:T(8,128)(2,1)} collective-permute-done((bf16[256,1536]{1,0:T(8,128)(2,1)}, bf16[256,1536]{1,0:T(8,128)(2,1)}, u32[]{:S(2)}, u32[]{:S(2)}) %collective-permute-start.5) | collective-permute-done | bytes 786464 | tf_op jit(solution)/shard_map/cond/branch_1_fun/ppermute | solution.py:49
  166.2 12.7 %collective-permute-done.58.refs_1_.refs_12_.refs_3_ = bf16[3,384,640]{2,1,0:T(8,128)(2,1)} collective-permute-done((bf16[3,384,640]{2,1,0:T(8,128)(2,1)}, bf16[3,384,640]{2,1,0:T(8,128)(2,1)}, u32[]{:S(2)}, u32[]{:S(2)}) %collective-permute-start.58) | collective-permute-done | bytes 1474592 | tf_op jit(solution)/shard_map/ppermute | solution.py:49
  179.1 19.1 %shard_map.271 = (bf16[2048,640]{1,0:T(8,128)(2,1)}, bf16[2048,1280]{1,0:T(8,128)(2,1)}) custom-call(s32[2]{0:T(128)S(1)} %copy-done.38, bf16[512,1536]{1,0:T(8,128)(2,1)S(1)} %get-tuple-element.618.refs_1_, bf16[256,1536]{1,0:T(8,128)(2,1)} %get-tuple-element.619.refs_2_, bf16[256,1536]{1,0:T(8,128)(2,1)} %get-tuple-element.620.refs_3_, ...), custom_call_target="tpu_custom_call" | custom-call | flops 199999995904 | bytes 1 | tf_op jit(solution)/shard_map/pallas_call | solution.py:122
  198.2 10.5 %collective-permute-done.59.refs_0_ = bf16[3,384,512]{2,1,0:T(8,128)(2,1)} collective-permute-done((bf16[3,384,512]{2,1,0:T(8,128)(2,1)}, bf16[3,384,512]{2,1,0:T(8,128)(2,1)}, u32[]{:S(2)}, u32[]{:S(2)}) %collective-permute-start.59) | collective-permute-done | bytes 1179680 | tf_op jit(solution)/shard_map/ppermute | solution.py:49
  209.1 22.4 %shard_map.273 = (bf16[3,384,640]{2,1,0:T(8,128)(2,1)}, bf16[3,3,384,640]{3,2,1,0:T(8,128)(2,1)}) custom-call(s32[2]{0:T(128)S(1)} %copy-done.38, bf16[512,1536]{1,0:T(8,128)(2,1)S(1)} %get-tuple-element.618.refs_1_, bf16[256,1536]{1,0:T(8,128)(2,1)} %get-tuple-element.619.refs_2_, bf16[256,1536]{1,0:T(8,128)(2,1)} %get-tuple-element.620.refs_3_, ...), custom_call_target="tpu_custom_call" | custom-call | flops 199999995904 | bytes 1 | tf_op jit(solution)/shard_map/pallas_call | solution.py:122
  231.6 6.3 %collective-permute-done.60.refs_0_ = bf16[3,384,512]{2,1,0:T(8,128)(2,1)} collective-permute-done((bf16[3,384,512]{2,1,0:T(8,128)(2,1)}, bf16[3,384,512]{2,1,0:T(8,128)(2,1)}, u32[]{:S(2)}, u32[]{:S(2)}) %collective-permute-start.60) | collective-permute-done | bytes 1179680 | tf_op jit(solution)/shard_map/ppermute | solution.py:49
  238.0 14.4 %shard_map.275.refs_15_.refs_6_ = bf16[2048,1536]{1,0:T(8,128)(2,1)} custom-call(s32[2]{0:T(128)S(1)} %copy-done.38, bf16[2048,1280]{1,0:T(8,128)(2,1)} %get-tuple-element.626.refs_12_.refs_1_, bf16[3,384,640]{2,1,0:T(8,128)(2,1)} %get-tuple-element.597.refs_1_.refs_11_.refs_2_, bf16[3,384,640]{2,1,0:T(8,128)(2,1)} %collective-permute-done.58.refs_1_.refs_12_.refs_3_, ...), custom_call_target="tpu_custom_call" | custom-call | flops 199999995904 | bytes 1 | tf_op jit(solution)/shard_map/pallas_call | solution.py:122
  252.4 13.4 %collective-permute-done.61.refs_12_.refs_3_.refs_1_ = bf16[3,384,512]{2,1,0:T(8,128)(2,1)} collective-permute-done((bf16[3,384,512]{2,1,0:T(8,128)(2,1)}, bf16[3,384,512]{2,1,0:T(8,128)(2,1)}, u32[]{:S(2)}, u32[]{:S(2)}) %collective-permute-start.61) | collective-permute-done | bytes 1179680 | tf_op jit(solution)/shard_map/ppermute | solution.py:49
  266.0 15.4 %shard_map.276 = (bf16[2048,512]{1,0:T(8,128)(2,1)}, bf16[2048,1024]{1,0:T(8,128)(2,1)}) custom-call(s32[2]{0:T(128)S(1)} %copy-done.38, bf16[512,1536]{1,0:T(8,128)(2,1)S(1)} %copy-done.11, bf16[256,1536]{1,0:T(8,128)(2,1)} %get-tuple-element.619.refs_2_, bf16[256,1536]{1,0:T(8,128)(2,1)} %get-tuple-element.620.refs_3_, ...), custom_call_target="tpu_custom_call" | custom-call | flops 199999995904 | bytes 1 | tf_op jit(solution)/shard_map/pallas_call | solution.py:122
  281.4 15.6 %shard_map.277 = (bf16[1024,1536]{1,0:T(8,128)(2,1)}, bf16[1024,1536]{1,0:T(8,128)(2,1)S(1)}) custom-call(s32[2]{0:T(128)S(1)} %copy-done.38, bf16[2048,1024]{1,0:T(8,128)(2,1)} %get-tuple-element.628.refs_1_, bf16[3,384,512]{2,1,0:T(8,128)(2,1)} %shard_map.270.refs_11_.refs_2_, bf16[3,384,512]{2,1,0:T(8,128)(2,1)} %collective-permute-done.61.refs_12_.refs_3_.refs_1_, ...), custom_call_target="tpu_custom_call" | custom-call | flops 199999995904 | bytes 1 | tf_op jit(solution)/shard_map/pallas_call | solution.py:122
  302.5 32.7 %conditional.16 = (bf16[128,1536]{1,0:T(8,128)(2,1)}, bf16[128,1536]{1,0:T(8,128)(2,1)}, f32[256,1536]{1,0:T(8,128)}, bf16[1024,1536]{1,0:T(8,128)(2,1)}, bf16[1024,1536]{1,0:T(8,128)(2,1)}) conditional(s32[]{:T(128)} %convert_element_type.169, () %tuple.104, (bf16[1024,1536]{1,0:T(8,128)(2,1)S(1)}, bf16[1024,1536]{1,0:T(8,128)(2,1)}, ...), branch_computations={%region_12.13_spmd, %region_13.14_spmd} | conditional | flops 599999971328 | bytes 18874588 | solution.py:86
  302.5 5.7 %collective-permute-done.10.refs_1_ = bf16[1024,1536]{1,0:T(8,128)(2,1)S(1)} collective-permute-done((bf16[1024,1536]{1,0:T(8,128)(2,1)S(1)}, bf16[1024,1536]{1,0:T(8,128)(2,1)S(1)}, u32[]{:S(2)}, u32[]{:S(2)}) %collective-permute-start.10) | collective-permute-done | bytes 3145760 | tf_op jit(solution)/shard_map/cond/branch_1_fun/ppermute | solution.py:49
  314.2 14.8 %branch_1_fun.45 = (bf16[1024,1536]{1,0:T(8,128)(2,1)}, bf16[1024,1536]{1,0:T(8,128)(2,1)}) custom-call(s32[2]{0:T(128)S(1)} %copy-done.42, bf16[2048,640]{1,0:T(8,128)(2,1)} %get-tuple-element.365.refs_1_, bf16[2048,512]{1,0:T(8,128)(2,1)} %get-tuple-element.366.refs_2_, bf16[3,384,640]{2,1,0:T(8,128)(2,1)} %get-tuple-element.367.refs_3_, ...), custom_call_target="tpu_custom_call" | custom-call | flops 199999995904 | bytes 1 | tf_op jit(solution)/shard_map/cond/branch_1_fun/pallas_call | solution.py:122
  339.4 37.5 %conditional.17 = (f32[256,1536]{1,0:T(8,128)}, bf16[256,1536]{1,0:T(8,128)(2,1)}, f32[1,1536]{1,0:T(1,128)}, bf16[256,1536]{1,0:T(8,128)(2,1)}, bf16[256,1536]{...) conditional(s32[]{:T(128)} %convert_element_type.169, ...), branch_computations={%region_14.15_spmd, %region_15.16_spmd} | conditional | flops 599999971328 | bytes 31469964 | solution.py:86
  345.2 4.4 branch_1_fun.47
  352.4 4.4 branch_1_fun.48
  357.8 19.1 %branch_1_fun.49 = (bf16[3,384,512]{2,1,0:T(8,128)(2,1)}, bf16[3,3,384,512]{3,2,1,0:T(8,128)(2,1)}) custom-call(s32[2]{0:T(128)S(1)} %copy-done.43, bf16[512,1536]{1,0:T(8,128)(2,1)S(1)} %copy-done.12, bf16[256,1536]{1,0:T(8,128)(2,1)} %get-tuple-element.394.refs_2_, bf16[256,1536]{1,0:T(8,128)(2,1)} %get-tuple-element.395.refs_3_, ...), custom_call_target="tpu_custom_call" | custom-call | flops 199999995904 | bytes 1 | tf_op jit(solution)/shard_map/cond/branch_1_fun/pallas_call | solution.py:122
  382.7 24.7 %conditional.18 = (bf16[256,1536]{1,0:T(8,128)(2,1)}, bf16[256,1536]{1,0:T(8,128)(2,1)}, bf16[256,1536]{1,0:T(8,128)(2,1)}, bf16[256,1536]{1,0:T(8,128)(2,1)}, b...) conditional(s32[]{:T(128)} %convert_element_type.169, ...), branch_computations={%region_16.17_spmd, %region_17.18_spmd} | conditional | flops 199999995904 | bytes 7876721 | solution.py:86
  388.9 18.4 %branch_1_fun.51 = (bf16[1024,640]{1,0:T(8,128)(2,1)}, f32[1,640]{1,0:T(1,128)}, f32[1,1536]{1,0:T(1,128)}, bf16[2,256,1536]{2,1,0:T(8,128)(2,1)}, bf16[2,256,1536]{2,1,0:T(8,128)(2,1)}) custom-call(s32[2]{0:T(128)S(1)} %get-tuple-element.412.refs_0_, bf16[256,1536]{1,0:T(8,128)(2,1)} %get-tuple-element.829.refs_1_, ...), custom_call_target="tpu_custom_call" | custom-call | flops 199999995904 | bytes 1 | tf_op jit(solution)/shard_map/cond/branch_1_fun/pallas_call | solution.py:122
  413.6 26.6 %conditional.19 = (bf16[4,192,1024]{2,1,0:T(8,128)(2,1)}, bf16[192,1024]{1,0:T(8,128)(2,1)}, bf16[192,1024]{1,0:T(8,128)(2,1)}, bf16[192,1024]{1,0:T(8,128)(2,1)...) conditional(s32[]{:T(128)} %convert_element_type.169, () %tuple.97, ...), branch_computations={%region_18.19_spmd, %region_19.20_spmd} | conditional | flops 600000757760 | bytes 9330941 | solution.py:86
  417.1 9.7 %branch_1_fun.52 = (bf16[4,192,1024]{2,1,0:T(8,128)(2,1)}, bf16[192,1024]{1,0:T(8,128)(2,1)}, bf16[192,1024]{1,0:T(8,128)(2,1)}, bf16[192,1024]{1,0:T(8,128)(2,1)}, bf16[192,1024]{1,0:T(8,128)(2,1)}) custom-call(s32[2]{0:T(128)S(1)} %get-tuple-element.440.refs_0_, bf16[256,1536]{1,0:T(8,128)(2,1)} %get-tuple-element.441.refs_1_, ...), custom_call_target="tpu_custom_call" | custom-call | flops 199999995904 | bytes 1 | tf_op jit(solution)/shard_map/cond/branch_1_fun/pallas_call | solution.py:122
  429.7 3.6 branch_1_fun.53
  433.3 3.8 branch_1_fun.54
  444.6 44.2 %conditional.20 = (bf16[192,1024]{1,0:T(8,128)(2,1)S(1)}, f32[5120]{0:T(1024)S(1)}) conditional(s32[]{:T(128)} %convert_element_type.169, () %tuple.115, (bf16[192,1024]{1,0:T(8,128)(2,1)}, bf16[4,192,1024]{2,1,0:T(8,128)(2,1)}, bf16[192,1024]{1,0:T(8,128)(2,1)}, bf16[256,1536]{1,0:T(8,128)(2,1)}, bf16[192,1024]{1,0:T(8,128)(2,1)}, ...), branch_computations={%region_20.21_spmd, %region_21.22_spmd} | conditional | flops 3554307 | bytes 17732020 | solution.py:86
  446.8 7.5 %collective-permute-done.27.refs_1_ = bf16[192,1024]{1,0:T(8,128)(2,1)S(1)} collective-permute-done((bf16[192,1024]{1,0:T(8,128)(2,1)}, bf16[192,1024]{1,0:T(8,128)(2,1)S(1)}, u32[]{:S(2)}, u32[]{:S(2)}) %collective-permute-start.27) | collective-permute-done | bytes 393248 | tf_op jit(solution)/shard_map/cond/branch_1_fun/ppermute | solution.py:49
  459.2 9.4 %collective-permute-done.28 = bf16[192,1024]{1,0:T(8,128)(2,1)S(1)} collective-permute-done((bf16[192,1024]{1,0:T(8,128)(2,1)S(1)}, bf16[192,1024]{1,0:T(8,128)(2,1)S(1)}, u32[]{:S(2)}, u32[]{:S(2)}) %collective-permute-start.28) | collective-permute-done | bytes 393248 | tf_op jit(solution)/shard_map/cond/branch_1_fun/ppermute | solution.py:49
  472.2 6.2 %collective-permute-done.32 = f32[40,128]{1,0:T(8,128)S(1)} collective-permute-done((f32[40,128]{1,0:T(8,128)}, f32[40,128]{1,0:T(8,128)S(1)}, u32[]{:S(2)}, u32[]{:S(2)}) %collective-permute-start.32) | collective-permute-done | bytes 20512 | tf_op jit(solution)/shard_map/cond/branch_1_fun/ppermute | solution.py:49
  479.2 3.6 collective-permute-done.33
  491.0 33.1 %conditional.21 = (f32[256,1536]{1,0:T(8,128)}, f32[2,48,2,128]{3,2,1,0:T(2,128)}, bf16[256,1536]{1,0:T(8,128)(2,1)}, bf16[3,384,640]{2,1,0:T(8,128)(2,1)}, bf16[3,192,640]{2,1,0:T(8,128)(2,1)}) conditional(s32[]{:T(128)} %convert_element_type.169, () %tuple.96, (f32[1536]{0:T(1024)}, bf16[128,1536]{1,0:T(8,128)(2,1)}, ...), branch_computations={%region_22.23_spmd, %region_23.24_spmd} | conditional | flops 200003092480 | bytes 31716040 | solution.py:86
  494.7 7.2 %collective-permute-done.35.refs_1_.refs_3_ = bf16[128,1536]{1,0:T(8,128)(2,1)S(1)} collective-permute-done((bf16[128,1536]{1,0:T(8,128)(2,1)}, bf16[128,1536]{1,0:T(8,128)(2,1)S(1)}, u32[]{:S(2)}, u32[]{:S(2)}) %collective-permute-start.35) | collective-permute-done | bytes 393248 | tf_op jit(solution)/shard_map/cond/branch_1_fun/ppermute | solution.py:49
  509.2 7.2 %collective-permute-done.38 = bf16[48,256]{1,0:T(8,128)(2,1)S(1)} collective-permute-done((bf16[48,256]{1,0:T(8,128)(2,1)S(1)}, bf16[48,256]{1,0:T(8,128)(2,1)S(1)}, u32[]{:S(2)}, u32[]{:S(2)}) %collective-permute-start.38) | collective-permute-done | bytes 24608 | tf_op jit(solution)/shard_map/cond/branch_1_fun/ppermute | solution.py:49
  520.2 3.9 branch_1_fun.61
  533.2 5.7 %collective-permute-done.70.refs_4_ = bf16[3,192,512]{2,1,0:T(8,128)(2,1)S(1)} collective-permute-done((bf16[3,192,512]{2,1,0:T(8,128)(2,1)S(1)}, bf16[3,192,512]{2,1,0:T(8,128)(2,1)S(1)}, u32[]{:S(2)}, u32[]{:S(2)}) %collective-permute-start.70) | collective-permute-done | bytes 589856 | tf_op jit(solution)/shard_map/ppermute | solution.py:49
  538.9 3.7 shard_map.295
  (326 shorter events, 168.3 us)
Async XLA Ops:
  10.9 11.4 %collective-permute-start.47 = (bf16[192,1024]{1,0:T(8,128)(2,1)}, bf16[192,1024]{1,0:T(8,128)(2,1)S(1)}, u32[]{:S(2)}, u32[]{:S(2)}) collective-permute-start(bf16[192,1024]{1,0:T(8,128)(2,1)} %get-tuple-element.735.refs_4_), channel_id=1, source_target_pairs={{0,4},{4,0},{8,12},{12,8},{16,20},{20,16},{24,28},{28,24},{1,5},{5... | collective-permute-start | bytes 1179656 | tf_op jit(solution)/shard_map/cond/branch_1_fun/ppermute | solution.py:49
  17.3 29.9 %collective-permute-start.42 = (bf16[256,1536]{1,0:T(8,128)(2,1)}, bf16[256,1536]{1,0:T(8,128)(2,1)}, u32[]{:S(2)}, u32[]{:S(2)}) collective-permute-start(bf16[256,1536]{1,0:T(8,128)(2,1)} %branch_1_fun.36), channel_id=1, source_target_pairs={{0,2},{1,3},{2,0},{3,1},{4,6},{5,7},{6,4},{7,5},{8,10},{9,11},{10,... | collective-permute-start | bytes 2359304 | tf_op jit(solution)/shard_map/cond/branch_1_fun/ppermute | solution.py:49
  18.4 36.5 %collective-permute-start.41 = (bf16[256,1536]{1,0:T(8,128)(2,1)}, bf16[256,1536]{1,0:T(8,128)(2,1)}, u32[]{:S(2)}, u32[]{:S(2)}) collective-permute-start(bf16[256,1536]{1,0:T(8,128)(2,1)} %branch_1_fun.36), channel_id=1, source_target_pairs={{0,1},{1,0},{2,3},{3,2},{4,5},{5,4},{6,7},{7,6},{8,9},{9,8},{10,11... | collective-permute-start | bytes 2359304 | tf_op jit(solution)/shard_map/cond/branch_1_fun/ppermute | solution.py:49
  18.4 13.7 %collective-permute-start.44 = (bf16[192,1024]{1,0:T(8,128)(2,1)}, bf16[192,1024]{1,0:T(8,128)(2,1)}, u32[]{:S(2)}, u32[]{:S(2)}) collective-permute-start(bf16[192,1024]{1,0:T(8,128)(2,1)} %get-tuple-element.735.refs_4_), channel_id=1, source_target_pairs={{0,8},{4,12},{8,16},{12,20},{16,24},{20,28},{24,0},{28,4},{1,9},{5... | collective-permute-start | bytes 1179656 | tf_op jit(solution)/shard_map/cond/branch_1_fun/ppermute | solution.py:49
  22.4 23.9 %collective-permute-start.50 = (bf16[3,192,640]{2,1,0:T(8,128)(2,1)}, bf16[3,192,640]{2,1,0:T(8,128)(2,1)S(1)}, u32[]{:S(2)}, u32[]{:S(2)}) collective-permute-start(bf16[3,192,640]{2,1,0:T(8,128)(2,1)} %branch_1_fun.37), channel_id=1, source_target_pairs={{0,4},{4,0},{8,12},{12,8},{16,20},{20,16},{24,28},{28,24},{1,5},{5... | collective-permute-start | bytes 2211848 | tf_op jit(solution)/shard_map/cond/branch_1_fun/ppermute | solution.py:49
  32.1 21.6 %collective-permute-start.51 = (bf16[256,1536]{1,0:T(8,128)(2,1)}, bf16[256,1536]{1,0:T(8,128)(2,1)S(1)}, u32[]{:S(2)}, u32[]{:S(2)}) collective-permute-start(bf16[256,1536]{1,0:T(8,128)(2,1)} %branch_1_fun.38), channel_id=1, source_target_pairs={{0,2},{1,3},{2,0},{3,1},{4,6},{5,7},{6,4},{7,5},{8,10},{9,11},{10,... | collective-permute-start | bytes 2359304 | tf_op jit(solution)/shard_map/cond/branch_1_fun/ppermute | solution.py:49
  33.0 12.7 %collective-permute-start.45 = (bf16[192,1024]{1,0:T(8,128)(2,1)}, bf16[192,1024]{1,0:T(8,128)(2,1)}, u32[]{:S(2)}, u32[]{:S(2)}) collective-permute-start(bf16[192,1024]{1,0:T(8,128)(2,1)} %collective-permute-done.44.refs_1_), channel_id=1, source_target_pairs={{0,8},{4,12},{8,16},{12,20},{16,24},{20,28},{24,0},{28,4},{1,9},{5... | collective-permute-start | bytes 1179656 | tf_op jit(solution)/shard_map/cond/branch_1_fun/ppermute | solution.py:49
  45.7 12.4 %collective-permute-start.48 = (bf16[192,1024]{1,0:T(8,128)(2,1)}, bf16[192,1024]{1,0:T(8,128)(2,1)}, u32[]{:S(2)}, u32[]{:S(2)}) collective-permute-start(bf16[192,1024]{1,0:T(8,128)(2,1)} %collective-permute-done.44.refs_1_), channel_id=1, source_target_pairs={{0,4},{4,0},{8,12},{12,8},{16,20},{20,16},{24,28},{28,24},{1,5},{5... | collective-permute-start | bytes 1179656 | tf_op jit(solution)/shard_map/cond/branch_1_fun/ppermute | solution.py:49
  46.2 11.8 %collective-permute-start.46 = (bf16[192,1024]{1,0:T(8,128)(2,1)}, bf16[192,1024]{1,0:T(8,128)(2,1)}, u32[]{:S(2)}, u32[]{:S(2)}) collective-permute-start(bf16[192,1024]{1,0:T(8,128)(2,1)} %collective-permute-done.45), channel_id=1, source_target_pairs={{0,8},{4,12},{8,16},{12,20},{16,24},{20,28},{24,0},{28,4},{1,9},{5... | collective-permute-start | bytes 1179656 | tf_op jit(solution)/shard_map/cond/branch_1_fun/ppermute | solution.py:49
  47.2 16.9 %collective-permute-start.49 = (bf16[192,1024]{1,0:T(8,128)(2,1)}, bf16[192,1024]{1,0:T(8,128)(2,1)}, u32[]{:S(2)}, u32[]{:S(2)}) collective-permute-start(bf16[192,1024]{1,0:T(8,128)(2,1)} %collective-permute-done.45), channel_id=1, source_target_pairs={{0,4},{4,0},{8,12},{12,8},{16,20},{20,16},{24,28},{28,24},{1,5},{5... | collective-permute-start | bytes 1179656 | tf_op jit(solution)/shard_map/cond/branch_1_fun/ppermute | solution.py:49
  64.6 33.9 %collective-permute-start.53 = (bf16[3,384,640]{2,1,0:T(8,128)(2,1)}, bf16[3,384,640]{2,1,0:T(8,128)(2,1)}, u32[]{:S(2)}, u32[]{:S(2)}) collective-permute-start(bf16[3,384,640]{2,1,0:T(8,128)(2,1)} %get-tuple-element.597.refs_1_.refs_11_.refs_2_), channel_id=1, source_target_pairs={{0,8},{4,12},{8,16},{12,20},{16,24},{20,28},{24,0},{28,4},{1,9},{5... | collective-permute-start | bytes 4423688 | tf_op jit(solution)/shard_map/ppermute | solution.py:49
  73.3 23.2 %collective-permute-start.54 = (bf16[3,192,512]{2,1,0:T(8,128)(2,1)}, bf16[3,192,512]{2,1,0:T(8,128)(2,1)}, u32[]{:S(2)}, u32[]{:S(2)}) collective-permute-start(bf16[3,192,512]{2,1,0:T(8,128)(2,1)} %shard_map.263), channel_id=1, source_target_pairs={{0,4},{4,0},{8,12},{12,8},{16,20},{20,16},{24,28},{28,24},{1,5},{5... | collective-permute-start | bytes 1769480 | tf_op jit(solution)/shard_map/ppermute | solution.py:49
  95.0 47.0 %collective-permute-start.55 = (bf16[512,1536]{1,0:T(8,128)(2,1)}, bf16[512,1536]{1,0:T(8,128)(2,1)}, u32[]{:S(2)}, u32[]{:S(2)}) collective-permute-start(bf16[512,1536]{1,0:T(8,128)(2,1)} %shard_map.266.refs_7_), channel_id=1, source_target_pairs={{0,4},{4,0},{8,12},{12,8},{16,20},{20,16},{24,28},{28,24},{1,5},{5... | collective-permute-start | bytes 4718600 | tf_op jit(solution)/shard_map/ppermute | solution.py:49
  98.5 43.6 %collective-permute-start.56 = (bf16[3,384,640]{2,1,0:T(8,128)(2,1)}, bf16[3,384,640]{2,1,0:T(8,128)(2,1)}, u32[]{:S(2)}, u32[]{:S(2)}) collective-permute-start(bf16[3,384,640]{2,1,0:T(8,128)(2,1)} %shard_map.262.refs_1_.refs_14_.refs_5_), channel_id=1, source_target_pairs={{0,8},{4,12},{8,16},{12,20},{16,24},{20,28},{24,0},{28,4},{1,9},{5... | collective-permute-start | bytes 4423688 | tf_op jit(solution)/shard_map/ppermute | solution.py:49
  99.6 19.5 %collective-permute-start.1 = (bf16[256,1536]{1,0:T(8,128)(2,1)}, bf16[256,1536]{1,0:T(8,128)(2,1)S(1)}, u32[]{:S(2)}, u32[]{:S(2)}) collective-permute-start(bf16[256,1536]{1,0:T(8,128)(2,1)} %get-tuple-element.347), channel_id=1, source_target_pairs={{0,2},{1,3},{2,0},{3,1},{4,6},{5,7},{6,4},{7,5},{8,10},{9,11},{10,... | collective-permute-start | bytes 2359304 | tf_op jit(solution)/shard_map/cond/branch_1_fun/ppermute | solution.py:49
  122.1 18.0 %collective-permute-start.2 = (bf16[128,1536]{1,0:T(8,128)(2,1)S(1)}, bf16[128,1536]{1,0:T(8,128)(2,1)S(1)}, u32[]{:S(2)}, u32[]{:S(2)}) collective-permute-start(bf16[128,1536]{1,0:T(8,128)(2,1)S(1)} %get-tuple-element.350.refs_0_), channel_id=1, source_target_pairs={{0,4},{4,0},{8,12},{12,8},{16,20},{20,16},{24,28},{28,24},{1,5},{5... | collective-permute-start | bytes 1179656 | tf_op jit(solution)/shard_map/cond/branch_1_fun/ppermute | solution.py:49
  122.6 17.5 %collective-permute-start.3 = (bf16[128,1536]{1,0:T(8,128)(2,1)S(1)}, bf16[128,1536]{1,0:T(8,128)(2,1)S(1)}, u32[]{:S(2)}, u32[]{:S(2)}) collective-permute-start(bf16[128,1536]{1,0:T(8,128)(2,1)S(1)} %get-tuple-element.351.refs_2_), channel_id=1, source_target_pairs={{0,2},{1,3},{2,0},{3,1},{4,6},{5,7},{6,4},{7,5},{8,10},{9,11},{10,... | collective-permute-start | bytes 1179656 | tf_op jit(solution)/shard_map/cond/branch_1_fun/ppermute | solution.py:49
  123.7 18.3 %collective-permute-start.4 = (bf16[512,1536]{1,0:T(8,128)(2,1)}, bf16[512,1536]{1,0:T(8,128)(2,1)}, u32[]{:S(2)}, u32[]{:S(2)}) collective-permute-start(bf16[512,1536]{1,0:T(8,128)(2,1)} %get-tuple-element.355), channel_id=1, source_target_pairs={{0,1},{1,0},{2,3},{3,2},{4,5},{5,4},{6,7},{7,6},{8,9},{9,8},{10,11... | collective-permute-start | bytes 4718600 | tf_op jit(solution)/shard_map/cond/branch_1_fun/ppermute | solution.py:49
  142.0 37.1 %collective-permute-start.57 = (bf16[512,1536]{1,0:T(8,128)(2,1)}, bf16[512,1536]{1,0:T(8,128)(2,1)}, u32[]{:S(2)}, u32[]{:S(2)}) collective-permute-start(bf16[512,1536]{1,0:T(8,128)(2,1)} %shard_map.267.refs_1_.refs_8_), channel_id=1, source_target_pairs={{0,1},{1,0},{2,3},{3,2},{4,5},{5,4},{6,7},{7,6},{8,9},{9,8},{10,11... | collective-permute-start | bytes 4718600 | tf_op jit(solution)/shard_map/ppermute | solution.py:49
  142.1 36.8 %collective-permute-start.58 = (bf16[3,384,640]{2,1,0:T(8,128)(2,1)}, bf16[3,384,640]{2,1,0:T(8,128)(2,1)}, u32[]{:S(2)}, u32[]{:S(2)}) collective-permute-start(bf16[3,384,640]{2,1,0:T(8,128)(2,1)} %shard_map.268.refs_2_.refs_13_.refs_4_), channel_id=1, source_target_pairs={{0,8},{4,12},{8,16},{12,20},{16,24},{20,28},{24,0},{28,4},{1,9},{5... | collective-permute-start | bytes 4423688 | tf_op jit(solution)/shard_map/ppermute | solution.py:49
  142.2 20.3 %collective-permute-start.5 = (bf16[256,1536]{1,0:T(8,128)(2,1)}, bf16[256,1536]{1,0:T(8,128)(2,1)}, u32[]{:S(2)}, u32[]{:S(2)}) collective-permute-start(bf16[256,1536]{1,0:T(8,128)(2,1)} %get-tuple-element.357), channel_id=1, source_target_pairs={{0,2},{1,3},{2,0},{3,1},{4,6},{5,7},{6,4},{7,5},{8,10},{9,11},{10,... | collective-permute-start | bytes 2359304 | tf_op jit(solution)/shard_map/cond/branch_1_fun/ppermute | solution.py:49
  143.3 19.9 %collective-permute-start.6 = (bf16[256,1536]{1,0:T(8,128)(2,1)}, bf16[256,1536]{1,0:T(8,128)(2,1)}, u32[]{:S(2)}, u32[]{:S(2)}) collective-permute-start(bf16[256,1536]{1,0:T(8,128)(2,1)} %get-tuple-element.358), channel_id=1, source_target_pairs={{0,4},{4,0},{8,12},{12,8},{16,20},{20,16},{24,28},{28,24},{1,5},{5... | collective-permute-start | bytes 2359304 | tf_op jit(solution)/shard_map/cond/branch_1_fun/ppermute | solution.py:49
  144.8 21.4 %collective-permute-start.7 = (bf16[512,1536]{1,0:T(8,128)(2,1)}, bf16[512,1536]{1,0:T(8,128)(2,1)}, u32[]{:S(2)}, u32[]{:S(2)}) collective-permute-start(bf16[512,1536]{1,0:T(8,128)(2,1)} %get-tuple-element.784), channel_id=1, source_target_pairs={{0,1},{1,0},{2,3},{3,2},{4,5},{5,4},{6,7},{7,6},{8,9},{9,8},{10,11... | collective-permute-start | bytes 4718600 | tf_op jit(solution)/shard_map/cond/branch_1_fun/ppermute | solution.py:49
  178.9 29.8 %collective-permute-start.59 = (bf16[3,384,512]{2,1,0:T(8,128)(2,1)}, bf16[3,384,512]{2,1,0:T(8,128)(2,1)}, u32[]{:S(2)}, u32[]{:S(2)}) collective-permute-start(bf16[3,384,512]{2,1,0:T(8,128)(2,1)} %shard_map.270.refs_11_.refs_2_), channel_id=1, source_target_pairs={{0,8},{4,12},{8,16},{12,20},{16,24},{20,28},{24,0},{28,4},{1,9},{5... | collective-permute-start | bytes 3538952 | tf_op jit(solution)/shard_map/ppermute | solution.py:49
  208.7 29.1 %collective-permute-start.60 = (bf16[3,384,512]{2,1,0:T(8,128)(2,1)}, bf16[3,384,512]{2,1,0:T(8,128)(2,1)}, u32[]{:S(2)}, u32[]{:S(2)}) collective-permute-start(bf16[3,384,512]{2,1,0:T(8,128)(2,1)} %shard_map.272.refs_14_.refs_5_), channel_id=1, source_target_pairs={{0,8},{4,12},{8,16},{12,20},{16,24},{20,28},{24,0},{28,4},{1,9},{5... | collective-permute-start | bytes 3538952 | tf_op jit(solution)/shard_map/ppermute | solution.py:49
  237.8 28.0 %collective-permute-start.61 = (bf16[3,384,512]{2,1,0:T(8,128)(2,1)}, bf16[3,384,512]{2,1,0:T(8,128)(2,1)}, u32[]{:S(2)}, u32[]{:S(2)}) collective-permute-start(bf16[3,384,512]{2,1,0:T(8,128)(2,1)} %shard_map.274.refs_13_.refs_4_), channel_id=1, source_target_pairs={{0,8},{4,12},{8,16},{12,20},{16,24},{20,28},{24,0},{28,4},{1,9},{5... | collective-permute-start | bytes 3538952 | tf_op jit(solution)/shard_map/ppermute | solution.py:49
  265.8 33.4 %collective-permute-start.62 = (bf16[3,384,640]{2,1,0:T(8,128)(2,1)}, bf16[3,384,640]{2,1,0:T(8,128)(2,1)}, u32[]{:S(2)}, u32[]{:S(2)}) collective-permute-start(bf16[3,384,640]{2,1,0:T(8,128)(2,1)} %shard_map.278), channel_id=1, source_target_pairs={{0,8},{4,12},{8,16},{12,20},{16,24},{20,28},{24,0},{28,4},{1,9},{5... | collective-permute-start | bytes 4423688 | tf_op jit(solution)/shard_map/ppermute | solution.py:49
  302.5 32.7 %collective-permute-start.63 = (bf16[3,384,640]{2,1,0:T(8,128)(2,1)}, bf16[3,384,640]{2,1,0:T(8,128)(2,1)}, u32[]{:S(2)}, u32[]{:S(2)}) collective-permute-start(bf16[3,384,640]{2,1,0:T(8,128)(2,1)} %fusion.12.refs_1_), channel_id=1, source_target_pairs={{0,8},{4,12},{8,16},{12,20},{16,24},{20,28},{24,0},{28,4},{1,9},{5... | collective-permute-start | bytes 4423688 | tf_op jit(solution)/shard_map/ppermute | solution.py:49
  311.6 19.9 %collective-permute-start.11 = (bf16[256,1536]{1,0:T(8,128)(2,1)}, bf16[256,1536]{1,0:T(8,128)(2,1)}, u32[]{:S(2)}, u32[]{:S(2)}) collective-permute-start(bf16[256,1536]{1,0:T(8,128)(2,1)} %get-tuple-element.362.refs_11_), channel_id=1, source_target_pairs={{0,2},{1,3},{2,0},{3,1},{4,6},{5,7},{6,4},{7,5},{8,10},{9,11},{10,... | collective-permute-start | bytes 2359304 | tf_op jit(solution)/shard_map/cond/branch_1_fun/ppermute | solution.py:49
  312.7 19.6 %collective-permute-start.12 = (bf16[256,1536]{1,0:T(8,128)(2,1)}, bf16[256,1536]{1,0:T(8,128)(2,1)}, u32[]{:S(2)}, u32[]{:S(2)}) collective-permute-start(bf16[256,1536]{1,0:T(8,128)(2,1)} %get-tuple-element.363), channel_id=1, source_target_pairs={{0,4},{4,0},{8,12},{12,8},{16,20},{20,16},{24,28},{28,24},{1,5},{5... | collective-permute-start | bytes 2359304 | tf_op jit(solution)/shard_map/cond/branch_1_fun/ppermute | solution.py:49
  338.5 43.0 %collective-permute-start.64 = (bf16[3,384,640]{2,1,0:T(8,128)(2,1)}, bf16[3,384,640]{2,1,0:T(8,128)(2,1)}, u32[]{:S(2)}, u32[]{:S(2)}) collective-permute-start(bf16[3,384,640]{2,1,0:T(8,128)(2,1)} %fusion.11.refs_1_), channel_id=1, source_target_pairs={{0,8},{4,12},{8,16},{12,20},{16,24},{20,28},{24,0},{28,4},{1,9},{5... | collective-permute-start | bytes 4423688 | tf_op jit(solution)/shard_map/ppermute | solution.py:49
  339.4 11.8 %collective-permute-start.13 = (bf16[128,1536]{1,0:T(8,128)(2,1)}, bf16[128,1536]{1,0:T(8,128)(2,1)}, u32[]{:S(2)}, u32[]{:S(2)}) collective-permute-start(bf16[128,1536]{1,0:T(8,128)(2,1)} %get-tuple-element.384), channel_id=1, source_target_pairs={{0,4},{4,0},{8,12},{12,8},{16,20},{20,16},{24,28},{28,24},{1,5},{5... | collective-permute-start | bytes 1179656 | tf_op jit(solution)/shard_map/cond/branch_1_fun/ppermute | solution.py:49
  340.9 11.6 %collective-permute-start.14 = (bf16[128,1536]{1,0:T(8,128)(2,1)}, bf16[128,1536]{1,0:T(8,128)(2,1)}, u32[]{:S(2)}, u32[]{:S(2)}) collective-permute-start(bf16[128,1536]{1,0:T(8,128)(2,1)} %get-tuple-element.385), channel_id=1, source_target_pairs={{0,2},{1,3},{2,0},{3,1},{4,6},{5,7},{6,4},{7,5},{8,10},{9,11},{10,... | collective-permute-start | bytes 1179656 | tf_op jit(solution)/shard_map/cond/branch_1_fun/ppermute | solution.py:49
  356.8 20.0 %collective-permute-start.16 = (bf16[256,1536]{1,0:T(8,128)(2,1)}, bf16[256,1536]{1,0:T(8,128)(2,1)}, u32[]{:S(2)}, u32[]{:S(2)}) collective-permute-start(bf16[256,1536]{1,0:T(8,128)(2,1)} %get-tuple-element.811.refs_13_), channel_id=1, source_target_pairs={{0,2},{1,3},{2,0},{3,1},{4,6},{5,7},{6,4},{7,5},{8,10},{9,11},{10,... | collective-permute-start | bytes 2359304 | tf_op jit(solution)/shard_map/cond/branch_1_fun/ppermute | solution.py:49
  357.7 19.1 %collective-permute-start.17 = (bf16[256,1536]{1,0:T(8,128)(2,1)}, bf16[256,1536]{1,0:T(8,128)(2,1)}, u32[]{:S(2)}, u32[]{:S(2)}) collective-permute-start(bf16[256,1536]{1,0:T(8,128)(2,1)} %get-tuple-element.811.refs_13_), channel_id=1, source_target_pairs={{0,1},{1,0},{2,3},{3,2},{4,5},{5,4},{6,7},{7,6},{8,9},{9,8},{10,11... | collective-permute-start | bytes 2359304 | tf_op jit(solution)/shard_map/cond/branch_1_fun/ppermute | solution.py:49
  376.9 36.0 %collective-permute-start.67 = (bf16[256,1536]{1,0:T(8,128)(2,1)}, bf16[256,1536]{1,0:T(8,128)(2,1)}, u32[]{:S(2)}, u32[]{:S(2)}) collective-permute-start(bf16[256,1536]{1,0:T(8,128)(2,1)} %get-tuple-element.659), channel_id=1, source_target_pairs={{0,4},{4,0},{8,12},{12,8},{16,20},{20,16},{24,28},{28,24},{1,5},{5... | collective-permute-start | bytes 2359304 | tf_op jit(solution)/shard_map/ppermute | solution.py:49
  377.5 35.4 %collective-permute-start.66 = (bf16[256,1536]{1,0:T(8,128)(2,1)}, bf16[256,1536]{1,0:T(8,128)(2,1)}, u32[]{:S(2)}, u32[]{:S(2)}) collective-permute-start(bf16[256,1536]{1,0:T(8,128)(2,1)} %get-tuple-element.658), channel_id=1, source_target_pairs={{0,2},{1,3},{2,0},{3,1},{4,6},{5,7},{6,4},{7,5},{8,10},{9,11},{10,... | collective-permute-start | bytes 2359304 | tf_op jit(solution)/shard_map/ppermute | solution.py:49
  378.6 30.4 %collective-permute-start.65 = (bf16[3,384,512]{2,1,0:T(8,128)(2,1)}, bf16[3,384,512]{2,1,0:T(8,128)(2,1)}, u32[]{:S(2)}, u32[]{:S(2)}) collective-permute-start(bf16[3,384,512]{2,1,0:T(8,128)(2,1)} %shard_map.284), channel_id=1, source_target_pairs={{0,8},{4,12},{8,16},{12,20},{16,24},{20,28},{24,0},{28,4},{1,9},{5... | collective-permute-start | bytes 3538952 | tf_op jit(solution)/shard_map/ppermute | solution.py:49
  412.0 29.6 %collective-permute-start.68 = (bf16[3,384,512]{2,1,0:T(8,128)(2,1)}, bf16[3,384,512]{2,1,0:T(8,128)(2,1)}, u32[]{:S(2)}, u32[]{:S(2)}) collective-permute-start(bf16[3,384,512]{2,1,0:T(8,128)(2,1)} %fusion.15.refs_1_), channel_id=1, source_target_pairs={{0,8},{4,12},{8,16},{12,20},{16,24},{20,28},{24,0},{28,4},{1,9},{5... | collective-permute-start | bytes 3538952 | tf_op jit(solution)/shard_map/ppermute | solution.py:49
  414.5 15.3 %collective-permute-start.23 = (bf16[2,256,1536]{2,1,0:T(8,128)(2,1)}, bf16[2,256,1536]{2,1,0:T(8,128)(2,1)}, u32[]{:S(2)}, u32[]{:S(2)}) collective-permute-start(bf16[2,256,1536]{2,1,0:T(8,128)(2,1)} %get-tuple-element.451.refs_11_), channel_id=1, source_target_pairs={{0,1},{1,0},{2,3},{3,2},{4,5},{5,4},{6,7},{7,6},{8,9},{9,8},{10,11... | collective-permute-start | bytes 4718600 | tf_op jit(solution)/shard_map/cond/branch_1_fun/ppermute | solution.py:49
  416.2 12.2 %collective-permute-start.25 = (f32[40,128]{1,0:T(8,128)}, f32[40,128]{1,0:T(8,128)}, u32[]{:S(2)}, u32[]{:S(2)}) collective-permute-start(f32[40,128]{1,0:T(8,128)} %add.90), channel_id=1, source_target_pairs={{0,2},{1,3},{2,0},{3,1},{4,6},{5,7},{6,4},{7,5},{8,10},{9,11},{10,... | collective-permute-start | bytes 61448 | tf_op jit(solution)/shard_map/cond/branch_1_fun/ppermute | solution.py:49
  426.8 11.3 %collective-permute-start.22 = (bf16[192,1024]{1,0:T(8,128)(2,1)}, bf16[192,1024]{1,0:T(8,128)(2,1)}, u32[]{:S(2)}, u32[]{:S(2)}) collective-permute-start(bf16[192,1024]{1,0:T(8,128)(2,1)} %get-tuple-element.456), channel_id=1, source_target_pairs={{0,4},{4,0},{8,12},{12,8},{16,20},{20,16},{24,28},{28,24},{1,5},{5... | collective-permute-start | bytes 1179656 | tf_op jit(solution)/shard_map/cond/branch_1_fun/ppermute | solution.py:49
  470.0 17.6 %collective-permute-start.30 = (bf16[192,1024]{1,0:T(8,128)(2,1)S(1)}, bf16[192,1024]{1,0:T(8,128)(2,1)S(1)}, u32[]{:S(2)}, u32[]{:S(2)}) collective-permute-start(bf16[192,1024]{1,0:T(8,128)(2,1)S(1)} %fusion.4), channel_id=1, source_target_pairs={{0,8},{4,12},{8,16},{12,20},{16,24},{20,28},{24,0},{28,4},{1,9},{5... | collective-permute-start | bytes 1179656 | tf_op jit(solution)/shard_map/cond/branch_1_fun/ppermute | solution.py:49
  470.1 17.5 %collective-permute-start.31 = (bf16[192,1024]{1,0:T(8,128)(2,1)}, bf16[192,1024]{1,0:T(8,128)(2,1)S(1)}, u32[]{:S(2)}, u32[]{:S(2)}) collective-permute-start(bf16[192,1024]{1,0:T(8,128)(2,1)} %branch_1_fun.59), channel_id=1, source_target_pairs={{0,4},{4,0},{8,12},{12,8},{16,20},{20,16},{24,28},{28,24},{1,5},{5... | collective-permute-start | bytes 1179656 | tf_op jit(solution)/shard_map/cond/branch_1_fun/ppermute | solution.py:49
  488.8 37.0 %collective-permute-start.69 = (bf16[3,384,512]{2,1,0:T(8,128)(2,1)}, bf16[3,384,512]{2,1,0:T(8,128)(2,1)}, u32[]{:S(2)}, u32[]{:S(2)}) collective-permute-start(bf16[3,384,512]{2,1,0:T(8,128)(2,1)} %shard_map.291.refs_1_), channel_id=1, source_target_pairs={{0,8},{4,12},{8,16},{12,20},{16,24},{20,28},{24,0},{28,4},{1,9},{5... | collective-permute-start | bytes 3538952 | tf_op jit(solution)/shard_map/ppermute | solution.py:49
  492.0 13.2 %collective-permute-start.39 = (bf16[128,1536]{1,0:T(8,128)(2,1)}, bf16[128,1536]{1,0:T(8,128)(2,1)}, u32[]{:S(2)}, u32[]{:S(2)}) collective-permute-start(bf16[128,1536]{1,0:T(8,128)(2,1)} %get-tuple-element.487), channel_id=1, source_target_pairs={{0,4},{4,0},{8,12},{12,8},{16,20},{20,16},{24,28},{28,24},{1,5},{5... | collective-permute-start | bytes 1179656 | tf_op jit(solution)/shard_map/cond/branch_1_fun/ppermute | solution.py:49
  502.7 17.5 %collective-permute-start.36 = (bf16[256,1536]{1,0:T(8,128)(2,1)}, bf16[256,1536]{1,0:T(8,128)(2,1)}, u32[]{:S(2)}, u32[]{:S(2)}) collective-permute-start(bf16[256,1536]{1,0:T(8,128)(2,1)} %branch_1_fun.60), channel_id=1, source_target_pairs={{0,2},{1,3},{2,0},{3,1},{4,6},{5,7},{6,4},{7,5},{8,10},{9,11},{10,... | collective-permute-start | bytes 2359304 | tf_op jit(solution)/shard_map/cond/branch_1_fun/ppermute | solution.py:49
  505.1 19.0 %collective-permute-start.40 = (bf16[3,192,640]{2,1,0:T(8,128)(2,1)}, bf16[3,192,640]{2,1,0:T(8,128)(2,1)}, u32[]{:S(2)}, u32[]{:S(2)}) collective-permute-start(bf16[3,192,640]{2,1,0:T(8,128)(2,1)} %branch_1_fun.65), channel_id=1, source_target_pairs={{0,4},{4,0},{8,12},{12,8},{16,20},{20,16},{24,28},{28,24},{1,5},{5... | collective-permute-start | bytes 2211848 | tf_op jit(solution)/shard_map/cond/branch_1_fun/ppermute | solution.py:49
  (70 other events, 545.5 us)

commit v4 on v3

--- a/solution.py
+++ b/solution.py
@@ -393,7 +393,7 @@
 
 
 def added(came, part):
-    return (came.astype(wide) + part.astype(wide)).astype(low)
+    return came + part
 
 
 def after(value, *others, cost=1):
@@ -623,7 +623,7 @@
     count = len(pairs[0][0])
     share = width // blocks
     columns = sum(grads.shape[1] for _, grads in pairs)
-    group = max(width // 4, share)
+    group = max(width // 2, share)
 
     def kernel(ranks_ref, *refs):
         piece_refs = [refs[index * (count + 1) : (index + 1) * (count + 1)] for index in range(len(pairs))]
@@ -1059,6 +1059,8 @@
     def pair_block(block, came):
         return lax.dynamic_update_slice_in_dim(block, came, (1 - dp_rank % 2) * share, 1)
 
+    piece = grad_out.shape[0] // 4
+
     def along_z(block):
         line, crossed = [block], []
         packed = pack(ranks, (w_gate, w_up, w_down.T), cuts, [block])
@@ -1069,12 +1071,17 @@
             crossed.append(across_x(line[-1]))
             line.append(up_line(line[-1]))
         came = across_x(after(packed[0], crossed[0]))
-        (grads,) = stack_rows([grad_out, across_y(after(grad_out, line[1]))], [(0, 1)])
+        grad_y = across_y(after(grad_out, line[2 % z_count]))
+        grads, grad_own = stack_rows([grad_out, grad_y], [(0, 1), (0,)])
+        parts = [grad_y[part : part + piece] for part in range(0, 3 * piece, piece)]
         cosine, sine = angles_of(segment, HD)
         sine = jnp.where(jnp.arange(HD) < HD // 2, -sine, sine)
-        return rows, line, crossed, pair_block(packed[1], came), packed[2:], grads, cosine, sine
-
-    rows_one, line, crossed, block, packed, grad_near, cosine, sine = stage(along_z, stage(begin))
+        return rows, line[1:], crossed, pair_block(packed[1], came), packed[2:], [grads, grad_own, parts], cosine, sine
+
+    line = [stage(begin)]
+    rows_one, rest, crossed, block, packed, grads, cosine, sine = stage(along_z, line[0])
+    grad_near, grad_own, grad_parts = grads
+    line += rest
     crossed.append(across_x(line[-1]))
     qkv_blocks = []
     for slot in range(z_count):
@@ -1091,6 +1098,7 @@
     early = [block]
     next_hop(early)
     came_late = across_x(after(packed[0], crossed[-1]))
+    grad_far = [across_x(after(grad_parts[0], crossed[-1]))]
     rows_one[0] = gate(rows_one[0], early[0], crossed[-1])
     key_bias = lax.dynamic_slice_in_dim(b_key, y_rank * HD, HD, 0)
     value_bias = lax.dynamic_slice_in_dim(b_value, y_rank * HD, HD, 0)
@@ -1104,28 +1112,30 @@
         return kept, probs, sent, own
 
     (query, key, value, heads_low), probs, sent, own = stage(attention)
-    late = [pair_block(packed[1], after(came_late, sent))]
     next_hop(early, sent)
-    grad_near = after(grad_near, sent)
-    grad_far = across_x(grad_near)
-    sent = gate(sent, early[1], late[0])
+    grad_x = across_x(after(grad_own, sent))
+    grad_far.append(across_x(after(grad_parts[1], sent)))
+    sent = gate(sent, early[1], came_late, grad_far[0])
 
     def between():
         mid, top, bottom = middle(tokens, own, across_y(sent), gain_ffn)
         top, bottom, both = stack_rows(
             [top, across_x(top), bottom, across_y(bottom)], [(0, 1), (2, 3), (0, 1, 2, 3)]
         )
-        return mid, top, bottom, both, across_core(grad_near)
-
-    mid_rows, top, bottom, both, other_near = stage(between)
+        return mid, top, bottom, both, across_core(grad_near), pair_block(packed[1], came_late)
+
+    mid_rows, top, bottom, both, other_near, block = stage(between)
+    late = [block]
     next_hop(early, both)
-    grad_far = after(grad_far, both)
-    other_far = across_core(grad_far)
-    top = gate(top, grad_far, early[2])
+    grad_far.append(across_x(after(grad_parts[2], both)))
+    grad_x = after(grad_x, both)
+    grad_far.append(across_y(grad_x[3 * piece :]))
+    top = gate(top, *grad_far[:2], grad_x, early[2])
 
     def spread():
         far_top, far_bottom = across_y(top), across_x(bottom)
-        return [
+        (grads,) = stack_rows([grad_x, *grad_far], [range(5)])
+        return [grads, across_core(grads)], [
             both,
             far_top,
             far_bottom,
@@ -1134,7 +1144,7 @@
             across_core(far_bottom),
         ]
 
-    rows_two = stage(spread)
+    (grad_far, other_far), rows_two = stage(spread)
     half = both.shape[0] // 2
     places = [(0, 0), (0, half), (1, 0), (2, 0), (3, 0), (3, half), (4, 0), (5, 0)]
     grad_ffn = [grad_near, grad_far, other_near, other_far]
@@ -1200,13 +1210,14 @@
     far_attn = gate(far_attn, early_hop)
 
     def back_attention():
-        grad_attn = [grad_low, near_attn, far_attn, across_core(far_attn)]
-        return grad_attn, attend_back(
-            ranks, grad_attn, rows_one, gain_attn, qkv_blocks, (query, key, value), probs,
-            cosine, sine,
+        other = across_core(far_attn)
+        return other, attend_back(
+            ranks, [grad_low, near_attn, far_attn, other], rows_one, gain_attn, qkv_blocks,
+            (query, key, value), probs, cosine, sine,
         )
 
-    grad_attn, (grad_qkv, bias_sums, gain_one, keep, send) = stage(back_attention)
+    other_attn, (grad_qkv, bias_sums, gain_one, keep, send) = stage(back_attention)
+    grad_attn = [grad_low, near_attn, far_attn, other_attn]
     late_sum = next_sum(late_hop, late_terms[1], z_count - 2, send)
     late_hop = up_line(late_sum)
 
@@ -1244,14 +1255,19 @@
     def finish_first():
         came = [None] * z_count
         for slot in range(z_count - 2, -1, -1):
-            came[slot] = across_x(after(far_terms[slot], sent if slot == z_count - 2 else came[slot + 1]))
-        sums = all_sum(small, "dp")
+            before = [sent if slot == z_count - 2 else came[slot + 1]]
+            if slot == 0:
+                sums = small + across_x(after(small, *before))
+                before.append(sums)
+            came[slot] = across_x(after(far_terms[slot], *before))
+        sums = all_sum(sums, "dp", 1)
+        came_one = across_y(sent)
         total = both_sum
         for slot in range(z_count - 2, -1, -1):
             total = joined(total, came[slot], slot)
-        return total, sums
-
-    both_sums, small = stage(finish_first)
+        return total, sums, came_one
+
+    both_sums, small, came_one = stage(finish_first)
     for slot in range(z_count - 3, 0, -1):
         late_sum = after(late_sum, both_sums)
         late_hop = up_line(late_sum)
@@ -1264,7 +1280,6 @@
         came_top, came_bottom = across_x(top), across_y(bottom)
         early = next_sum(early_hop, early_terms[1], 0, both_sums)
         came_early = across_x(after(split_pair(ranks, early), came_top))
-        came_one = across_y(after(sent, came_bottom))
         layer_out = layer_rows(mid_rows, own_out, came_top, came_bottom)
         grad_tokens = tokens_back(tokens, gain_attn, grad_mid, own, came_one)
         kv_sums = both_sums[:, query_cols:qkv_cols].reshape(2, 2, -1, 2 * HD)

time: 548 us -> 534 us (0.974)
  waiting for transfers between devices: 218 us -> 181 us
  starting transfers between devices: 49.7 us -> 64.5 us
  Pallas kernels: 213 us -> 223 us
    ppermute x71 -> x75, waiting for transfers between devices: 218 us -> 181 us  [moved(): return lax.ppermute(block, axis, route)]
    convert_element_type x7 -> x0, other arithmetic: 18.7 us -> none  [added(): return (came.astype(wide) + part.astype(wide)).astype(low)]
    add x0 -> x8, other arithmetic: none -> 18.7 us  [the longest x7 17.3 us: added(): return came + part]
    ppermute x71 -> x75, starting transfers between devices: 49.7 us -> 64.5 us  [moved(): return lax.ppermute(block, axis, route)]
    pallas_call x29 -> x30, Pallas kernels: 213 us -> 222 us  [call(): pl.pallas_call(body, out_shape=outs, in_specs=list(specs) + [anywhere] *...]
    cond x39 -> x30, local copies, waits for them, and re-layouts: 12.8 us -> 8.65 us
  transfers between devices with their start and end apart: 71 -> 75, of which waited for: 41 -> 41; matrix products, arithmetic and copies ran while one was open for 7% -> 7% of each run, Pallas kernels for 38% -> 41%
where the time goes in v4:
time: 534 us; the launch traced here: 529 us
  Pallas kernels  223 us (42%)
  waiting for transfers between devices  181 us (34%)
  starting transfers between devices  64.5 us (12%)
  other arithmetic  31 us (6%)
  local copies, waits for them, and re-layouts  27.7 us (5%)
    pallas_call x30, Pallas kernels, call(): pl.pallas_call(body, out_shape=outs, in_specs=list(specs) + [anywhere] *...  222 us
    ppermute x75, waiting for transfers between devices, moved(): return lax.ppermute(block, axis, route)  181 us
    ppermute x75, starting transfers between devices, moved(): return lax.ppermute(block, axis, route)  64.5 us
    add x7, other arithmetic, added(): return came + part  17.3 us
  transfers between devices with their start and end apart: 75, of which 41 were waited for; matrix products, arithmetic and copies ran while one was open for 7% of the time, Pallas kernels for 41%

profile of v4, /device:TPU:0, one launch (start us, length us, event | category | flops | bytes accessed | tf_op | source)
XLA Modules:
  0.0 528.7 jit_solution(11214540023945520794)
XLA Ops:
  0.7 10.1 %conditional.11 = (bf16[192,1024]{1,0:T(8,128)(2,1)}) conditional(s32[]{:T(128)} %convert_element_type.85, () %tuple.102, (bf16[384,192]{0,1:T(8,128)(2,1)}, bf16[48,256]{1,0:T(8,128)(2,1)}, bf16[48,256]{1,0:T(8,128)(2,1)}, s32[2]{0:T(128)S(1)}, bf16[192,384]{1,0:T(8,128)(2,1)}) %tuple.103), branch_computations={%region_0.1_spmd, %region_1.2_spmd} | conditional | flops 199999995904 | bytes 688257 | solution.py:86
  10.9 49.0 %conditional.12 = (bf16[256,1536]{1,0:T(8,128)(2,1)}, bf16[256,1536]{1,0:T(8,128)(2,1)}, bf16[256,1536]{1,0:T(8,128)(2,1)}, bf16[256,1536]{1,0:T(8,128)(2,1)}, b...) conditional(s32[]{:T(128)} %convert_element_type.85, () %tuple.101, ...), branch_computations={%region_2.3_spmd, %region_3.6_spmd} | conditional | flops 200000585728 | bytes 38483796 | solution.py:86
  14.1 3.6 branch_1_fun.36
  27.5 9.4 %collective-permute-done.46.refs_1_ = bf16[192,1024]{1,0:T(8,128)(2,1)} collective-permute-done((bf16[192,1024]{1,0:T(8,128)(2,1)}, bf16[192,1024]{1,0:T(8,128)(2,1)}, u32[]{:S(2)}, u32[]{:S(2)}) %collective-permute-start.46) | collective-permute-done | bytes 393248 | tf_op jit(solution)/shard_map/cond/branch_1_fun/ppermute | solution.py:49
  48.4 6.6 %collective-permute-done.52.refs_1_ = bf16[256,1536]{1,0:T(8,128)(2,1)S(1)} collective-permute-done((bf16[256,1536]{1,0:T(8,128)(2,1)}, bf16[256,1536]{1,0:T(8,128)(2,1)S(1)}, u32[]{:S(2)}, u32[]{:S(2)}) %collective-permute-start.52) | collective-permute-done | bytes 786464 | tf_op jit(solution)/shard_map/cond/branch_1_fun/ppermute | solution.py:49
  63.4 5.8 %collective-permute-done.53.refs_2_.refs_1_ = bf16[192,1024]{1,0:T(8,128)(2,1)S(1)} collective-permute-done((bf16[192,1024]{1,0:T(8,128)(2,1)}, bf16[192,1024]{1,0:T(8,128)(2,1)S(1)}, u32[]{:S(2)}, u32[]{:S(2)}) %collective-permute-start.53) | collective-permute-done | bytes 393248 | tf_op jit(solution)/shard_map/ppermute | solution.py:49
  72.3 20.2 %conditional.13 = (bf16[1024,384]{1,0:T(8,128)(2,1)}, bf16[1024,128]{1,0:T(8,128)(2,1)}, bf16[1024,128]{1,0:T(8,128)(2,1)}, bf16[1024,384]{1,0:T(8,128)(2,1)}, b...) conditional(s32[]{:T(128)} %convert_element_type.85, () %tuple.105, ...), branch_computations={%region_6.7_spmd, %region_7.8_spmd} | conditional | flops 399999991808 | bytes 8388710 | solution.py:86
  72.5 14.2 %branch_1_fun.41 = (bf16[1024,384]{1,0:T(8,128)(2,1)}, bf16[1024,128]{1,0:T(8,128)(2,1)}, bf16[1024,128]{1,0:T(8,128)(2,1)}, bf16[1024,384]{1,0:T(8,128)(2,1)}, ...) custom-call(s32[2]{0:T(128)S(1)} %get-tuple-element.334.refs_0_, ...), custom_call_target="tpu_custom_call" | custom-call | flops 199999995904 | bytes 1 | tf_op jit(solution)/shard_map/cond/branch_1_fun/pallas_call | solution.py:122
  86.9 3.4 collective-permute-done.refs_2_
  97.1 33.1 %conditional.14 = (f32[256,1536]{1,0:T(8,128)}, bf16[256,1536]{1,0:T(8,128)(2,1)}, bf16[256,1536]{1,0:T(8,128)(2,1)}, bf16[512,1536]{1,0:T(8,128)(2,1)}, bf16[51...) conditional(s32[]{:T(128)} %convert_element_type.85, () %tuple.107, (bf16[256,1536]{1,0:T(8,128)(2,1)}, ...), branch_computations={%region_8.9_spmd, %region_9.10_spmd} | conditional | flops 399999991808 | bytes 13775229 | solution.py:86
  98.6 16.7 %collective-permute-done.19.refs_2_ = bf16[256,1536]{1,0:T(8,128)(2,1)S(1)} collective-permute-done((bf16[256,1536]{1,0:T(8,128)(2,1)}, bf16[256,1536]{1,0:T(8,128)(2,1)S(1)}, u32[]{:S(2)}, u32[]{:S(2)}) %collective-permute-start.19) | collective-permute-done | bytes 786464 | tf_op jit(solution)/shard_map/cond/branch_1_fun/ppermute | solution.py:49
  122.4 4.6 collective-permute-done.20.refs_1_
  139.8 26.6 %conditional.15 = (bf16[512,1536]{1,0:T(8,128)(2,1)}, bf16[512,1536]{1,0:T(8,128)(2,1)}, bf16[512,1536]{1,0:T(8,128)(2,1)}, bf16[256,1536]{1,0:T(8,128)(2,1)}, b...) conditional(s32[]{:T(128)} %convert_element_type.85, () %tuple.100, ...), branch_computations={%region_10.11_spmd, %region_11.12_spmd} | conditional | flops 199999995904 | bytes 28311856 | solution.py:86
  144.0 18.7 %collective-permute-done.2 = bf16[256,1536]{1,0:T(8,128)(2,1)} collective-permute-done((bf16[256,1536]{1,0:T(8,128)(2,1)}, bf16[256,1536]{1,0:T(8,128)(2,1)}, u32[]{:S(2)}, u32[]{:S(2)}) %collective-permute-start.2) | collective-permute-done | bytes 786464 | tf_op jit(solution)/shard_map/cond/branch_1_fun/ppermute | solution.py:49
  169.1 22.1 %shard_map.273 = (bf16[2048,640]{1,0:T(8,128)(2,1)}, bf16[2048,1280]{1,0:T(8,128)(2,1)}) custom-call(s32[2]{0:T(128)S(1)} %copy-done.33, bf16[512,1536]{1,0:T(8,128)(2,1)} %get-tuple-element.651.refs_1_, bf16[256,1536]{1,0:T(8,128)(2,1)} %get-tuple-element.652.refs_2_, bf16[256,1536]{1,0:T(8,128)(2,1)} %get-tuple-element.653.refs_3_, ...), custom_call_target="tpu_custom_call" | custom-call | flops 199999995904 | bytes 1 | tf_op jit(solution)/shard_map/pallas_call | solution.py:122
  191.2 6.0 %collective-permute-done.63.refs_0_ = bf16[3,384,512]{2,1,0:T(8,128)(2,1)} collective-permute-done((bf16[3,384,512]{2,1,0:T(8,128)(2,1)}, bf16[3,384,512]{2,1,0:T(8,128)(2,1)}, u32[]{:S(2)}, u32[]{:S(2)}) %collective-permute-start.63) | collective-permute-done | bytes 1179680 | tf_op jit(solution)/shard_map/ppermute | solution.py:49
  197.8 22.7 %shard_map.275 = (bf16[3,384,640]{2,1,0:T(8,128)(2,1)}, bf16[3,3,384,640]{3,2,1,0:T(8,128)(2,1)}) custom-call(s32[2]{0:T(128)S(1)} %copy-done.33, bf16[512,1536]{1,0:T(8,128)(2,1)} %get-tuple-element.651.refs_1_, bf16[256,1536]{1,0:T(8,128)(2,1)} %get-tuple-element.652.refs_2_, bf16[256,1536]{1,0:T(8,128)(2,1)} %get-tuple-element.653.refs_3_, ...), custom_call_target="tpu_custom_call" | custom-call | flops 199999995904 | bytes 1 | tf_op jit(solution)/shard_map/pallas_call | solution.py:122
  220.5 5.6 %collective-permute-done.64.refs_0_ = bf16[3,384,512]{2,1,0:T(8,128)(2,1)} collective-permute-done((bf16[3,384,512]{2,1,0:T(8,128)(2,1)}, bf16[3,384,512]{2,1,0:T(8,128)(2,1)}, u32[]{:S(2)}, u32[]{:S(2)}) %collective-permute-start.64) | collective-permute-done | bytes 1179680 | tf_op jit(solution)/shard_map/ppermute | solution.py:49
  226.3 14.4 %shard_map.277.refs_15_.refs_6_ = bf16[2048,1536]{1,0:T(8,128)(2,1)} custom-call(s32[2]{0:T(128)S(1)} %copy-done.33, bf16[2048,1280]{1,0:T(8,128)(2,1)} %get-tuple-element.662.refs_12_.refs_1_, bf16[3,384,640]{2,1,0:T(8,128)(2,1)} %get-tuple-element.628.refs_1_.refs_11_.refs_2_, bf16[3,384,640]{2,1,0:T(8,128)(2,1)} %collective-permute-done.62.refs_1_.refs_12_.refs_3_, ...), custom_call_target="tpu_custom_call" | custom-call | flops 199999995904 | bytes 1 | tf_op jit(solution)/shard_map/pallas_call | solution.py:122
  240.7 13.4 %collective-permute-done.65.refs_12_.refs_3_.refs_1_ = bf16[3,384,512]{2,1,0:T(8,128)(2,1)} collective-permute-done((bf16[3,384,512]{2,1,0:T(8,128)(2,1)}, bf16[3,384,512]{2,1,0:T(8,128)(2,1)}, u32[]{:S(2)}, u32[]{:S(2)}) %collective-permute-start.65) | collective-permute-done | bytes 1179680 | tf_op jit(solution)/shard_map/ppermute | solution.py:49
  254.5 18.4 %shard_map.278 = (bf16[2048,512]{1,0:T(8,128)(2,1)}, bf16[2048,1024]{1,0:T(8,128)(2,1)}) custom-call(s32[2]{0:T(128)S(1)} %copy-done.33, bf16[512,1536]{1,0:T(8,128)(2,1)} %get-tuple-element.651.refs_1_, bf16[256,1536]{1,0:T(8,128)(2,1)} %get-tuple-element.652.refs_2_, bf16[256,1536]{1,0:T(8,128)(2,1)} %get-tuple-element.653.refs_3_, ...), custom_call_target="tpu_custom_call" | custom-call | flops 199999995904 | bytes 1 | tf_op jit(solution)/shard_map/pallas_call | solution.py:122
  272.9 15.4 %shard_map.279 = (bf16[1024,1536]{1,0:T(8,128)(2,1)}, bf16[1024,1536]{1,0:T(8,128)(2,1)S(1)}) custom-call(s32[2]{0:T(128)S(1)} %copy-done.33, bf16[2048,1024]{1,0:T(8,128)(2,1)} %get-tuple-element.664.refs_1_, bf16[3,384,512]{2,1,0:T(8,128)(2,1)} %shard_map.272.refs_11_.refs_2_, bf16[3,384,512]{2,1,0:T(8,128)(2,1)} %collective-permute-done.65.refs_12_.refs_3_.refs_1_, ...), custom_call_target="tpu_custom_call" | custom-call | flops 199999995904 | bytes 1 | tf_op jit(solution)/shard_map/pallas_call | solution.py:122
  292.0 32.0 %conditional.16 = (bf16[128,1536]{1,0:T(8,128)(2,1)}, bf16[128,1536]{1,0:T(8,128)(2,1)}, f32[256,1536]{1,0:T(8,128)}, bf16[1024,1536]{1,0:T(8,128)(2,1)}, bf16[1024,1536]{1,0:T(8,128)(2,1)}) conditional(s32[]{:T(128)} %convert_element_type.85, () %tuple.99, (bf16[1024,1536]{1,0:T(8,128)(2,1)S(1)}, bf16[1024,1536]{1,0:T(8,128)(2,1)}, s32[2]{0:T(128)}, ...), branch_computations={%region_12.13_spmd, %region_13.14_spmd} | conditional | flops 599999971328 | bytes 18874588 | solution.py:86
  292.0 5.7 %collective-permute-done.7.refs_1_ = bf16[1024,1536]{1,0:T(8,128)(2,1)S(1)} collective-permute-done((bf16[1024,1536]{1,0:T(8,128)(2,1)S(1)}, bf16[1024,1536]{1,0:T(8,128)(2,1)S(1)}, u32[]{:S(2)}, u32[]{:S(2)}) %collective-permute-start.7) | collective-permute-done | bytes 3145760 | tf_op jit(solution)/shard_map/cond/branch_1_fun/ppermute | solution.py:49
  302.7 14.8 %branch_1_fun.47 = (bf16[1024,1536]{1,0:T(8,128)(2,1)}, bf16[1024,1536]{1,0:T(8,128)(2,1)}) custom-call(s32[2]{0:T(128)S(1)} %copy-done.37, bf16[2048,640]{1,0:T(8,128)(2,1)} %get-tuple-element.391.refs_1_, bf16[2048,512]{1,0:T(8,128)(2,1)} %get-tuple-element.392.refs_2_, bf16[3,384,640]{2,1,0:T(8,128)(2,1)} %get-tuple-element.393.refs_3_, ...), custom_call_target="tpu_custom_call" | custom-call | flops 199999995904 | bytes 1 | tf_op jit(solution)/shard_map/cond/branch_1_fun/pallas_call | solution.py:122
  317.4 3.6 collective-permute-done.8.refs_1_
  328.7 38.4 %conditional.17 = (f32[256,1536]{1,0:T(8,128)}, bf16[256,1536]{1,0:T(8,128)(2,1)}, f32[1,1536]{1,0:T(1,128)}, bf16[256,1536]{1,0:T(8,128)(2,1)}, bf16[256,1536]{...) conditional(s32[]{:T(128)} %convert_element_type.85, () %tuple.98, ...), branch_computations={%region_14.15_spmd, %region_15.16_spmd} | conditional | flops 599999971328 | bytes 25178480 | solution.py:86
  334.6 4.4 branch_1_fun.49
  341.8 4.4 branch_1_fun.50
  347.6 19.5 %branch_1_fun.51 = (bf16[3,384,512]{2,1,0:T(8,128)(2,1)}, bf16[3,3,384,512]{3,2,1,0:T(8,128)(2,1)}) custom-call(s32[2]{0:T(128)S(1)} %copy-done.38, bf16[512,1536]{1,0:T(8,128)(2,1)} %get-tuple-element.419.refs_1_, bf16[256,1536]{1,0:T(8,128)(2,1)} %get-tuple-element.420.refs_2_, bf16[256,1536]{1,0:T(8,128)(2,1)} %get-tuple-element.421.refs_3_, ...), custom_call_target="tpu_custom_call" | custom-call | flops 199999995904 | bytes 1 | tf_op jit(solution)/shard_map/cond/branch_1_fun/pallas_call | solution.py:122
  368.3 4.0 collective-permute-start.69
  373.4 21.1 %conditional.18 = (bf16[256,1536]{1,0:T(8,128)(2,1)}, bf16[1024,640]{1,0:T(8,128)(2,1)}, f32[1,640]{1,0:T(1,128)}, f32[1,1536]{1,0:T(1,128)}, bf16[2,256,1536]{2...) conditional(s32[]{:T(128)} %convert_element_type.85, () %tuple.113, (bf16[256,1536]{1,0:T(8,128)(2,1)}, ...), branch_computations={%region_16.17_spmd, %region_17.18_spmd} | conditional | flops 199999995904 | bytes 5251648 | solution.py:86
  376.1 18.4 %branch_1_fun.53 = (bf16[1024,640]{1,0:T(8,128)(2,1)}, f32[1,640]{1,0:T(1,128)}, f32[1,1536]{1,0:T(1,128)}, bf16[2,256,1536]{2,1,0:T(8,128)(2,1)}, bf16[2,256,1536]{2,1,0:T(8,128)(2,1)}) custom-call(s32[2]{0:T(128)S(1)} %get-tuple-element.436.refs_0_, bf16[256,1536]{1,0:T(8,128)(2,1)} %get-tuple-element.437.refs_1_, ...), custom_call_target="tpu_custom_call" | custom-call | flops 199999995904 | bytes 1 | tf_op jit(solution)/shard_map/cond/branch_1_fun/pallas_call | solution.py:122
  394.5 4.4 collective-permute-done.69.refs_0_
  404.0 27.3 %conditional.19 = (bf16[4,192,1024]{2,1,0:T(8,128)(2,1)}, bf16[192,1024]{1,0:T(8,128)(2,1)}, bf16[192,1024]{1,0:T(8,128)(2,1)}, bf16[192,1024]{1,0:T(8,128)(2,1)...) conditional(s32[]{:T(128)} %convert_element_type.85, () %tuple.112, ...), branch_computations={%region_18.19_spmd, %region_19.20_spmd} | conditional | flops 600000167936 | bytes 9330941 | solution.py:86
  408.4 9.7 %branch_1_fun.54 = (bf16[4,192,1024]{2,1,0:T(8,128)(2,1)}, bf16[192,1024]{1,0:T(8,128)(2,1)}, bf16[192,1024]{1,0:T(8,128)(2,1)}, bf16[192,1024]{1,0:T(8,128)(2,1)}, bf16[192,1024]{1,0:T(8,128)(2,1)}) custom-call(s32[2]{0:T(128)S(1)} %get-tuple-element.466.refs_0_, bf16[256,1536]{1,0:T(8,128)(2,1)} %get-tuple-element.467.refs_1_, ...), custom_call_target="tpu_custom_call" | custom-call | flops 199999995904 | bytes 1 | tf_op jit(solution)/shard_map/cond/branch_1_fun/pallas_call | solution.py:122
  420.2 3.6 branch_1_fun.55
  423.8 3.8 branch_1_fun.56
  434.1 41.5 %conditional.20 = (bf16[192,1024]{1,0:T(8,128)(2,1)S(1)}, bf16[256,1536]{1,0:T(8,128)(2,1)}, f32[5120]{0:T(1024)S(1)}) conditional(s32[]{:T(128)} %convert_element_type.85, () %tuple.116, (bf16[192,1024]{1,0:T(8,128)(2,1)}, bf16[4,192,1024]{2,1,0:T(8,128)(2,1)}, bf16[192,1024]{1,0:T(8,128)(2,1)}, bf16[256,1536]{1,0:T(8,128)(2,1)}, ...), branch_computations={%region_20.21_spmd, %region_21.22_spmd} | conditional | flops 3554308 | bytes 20918756 | solution.py:86
  435.1 9.2 %collective-permute-done.28.refs_1_ = bf16[192,1024]{1,0:T(8,128)(2,1)S(1)} collective-permute-done((bf16[192,1024]{1,0:T(8,128)(2,1)}, bf16[192,1024]{1,0:T(8,128)(2,1)S(1)}, u32[]{:S(2)}, u32[]{:S(2)}) %collective-permute-start.28) | collective-permute-done | bytes 393248 | tf_op jit(solution)/shard_map/cond/branch_1_fun/ppermute | solution.py:49
  450.0 4.4 collective-permute-done.30.refs_1_
  462.6 6.3 %collective-permute-done.35 = f32[40,128]{1,0:T(8,128)S(1)} collective-permute-done((f32[40,128]{1,0:T(8,128)}, f32[40,128]{1,0:T(8,128)S(1)}, u32[]{:S(2)}, u32[]{:S(2)}) %collective-permute-start.35) | collective-permute-done | bytes 20512 | tf_op jit(solution)/shard_map/cond/branch_1_fun/ppermute | solution.py:49
  476.9 28.7 %conditional.21 = (f32[256,1536]{1,0:T(8,128)}, f32[2,48,2,128]{3,2,1,0:T(2,128)}, bf16[256,1536]{1,0:T(8,128)(2,1)}, bf16[3,384,640]{2,1,0:T(8,128)(2,1)}, bf16[3,192,640]{2,1,0:T(8,128)(2,1)}) conditional(s32[]{:T(128)} %convert_element_type.85, () %tuple.97, (f32[1536]{0:T(1024)}, bf16[256,1536]{1,0:T(8,128)(2,1)}, f32[256,1536]{1,0:T(8,128)}, ...), branch_computations={%region_22.23_spmd, %region_23.24_spmd} | conditional | flops 200000880640 | bytes 25424488 | solution.py:86
  482.4 4.5 collective-permute-done.39.refs_2_.refs_1_
  489.7 3.9 branch_1_fun.63
  495.8 6.1 %collective-permute-done.38 = bf16[48,256]{1,0:T(8,128)(2,1)S(1)} collective-permute-done((bf16[48,256]{1,0:T(8,128)(2,1)S(1)}, bf16[48,256]{1,0:T(8,128)(2,1)S(1)}, u32[]{:S(2)}, u32[]{:S(2)}) %collective-permute-start.38) | collective-permute-done | bytes 24608 | tf_op jit(solution)/shard_map/cond/branch_1_fun/ppermute | solution.py:49
  514.3 10.5 %collective-permute-done.74.refs_4_ = bf16[3,192,512]{2,1,0:T(8,128)(2,1)S(1)} collective-permute-done((bf16[3,192,512]{2,1,0:T(8,128)(2,1)S(1)}, bf16[3,192,512]{2,1,0:T(8,128)(2,1)S(1)}, u32[]{:S(2)}, u32[]{:S(2)}) %collective-permute-start.74) | collective-permute-done | bytes 589856 | tf_op jit(solution)/shard_map/ppermute | solution.py:49
  524.8 3.7 shard_map.297
  (326 shorter events, 180.4 us)
Async XLA Ops:
  10.9 13.4 %collective-permute-start.45 = (bf16[192,1024]{1,0:T(8,128)(2,1)}, bf16[192,1024]{1,0:T(8,128)(2,1)}, u32[]{:S(2)}, u32[]{:S(2)}) collective-permute-start(bf16[192,1024]{1,0:T(8,128)(2,1)} %get-tuple-element.324.refs_4_), channel_id=1, source_target_pairs={{0,8},{4,12},{8,16},{12,20},{16,24},{20,28},{24,0},{28,4},{1,9},{5... | collective-permute-start | bytes 1179656 | tf_op jit(solution)/shard_map/cond/branch_1_fun/ppermute | solution.py:49
  12.6 12.4 %collective-permute-start.48 = (bf16[192,1024]{1,0:T(8,128)(2,1)}, bf16[192,1024]{1,0:T(8,128)(2,1)S(1)}, u32[]{:S(2)}, u32[]{:S(2)}) collective-permute-start(bf16[192,1024]{1,0:T(8,128)(2,1)} %get-tuple-element.324.refs_4_), channel_id=1, source_target_pairs={{0,4},{4,0},{8,12},{12,8},{16,20},{20,16},{24,28},{28,24},{1,5},{5... | collective-permute-start | bytes 1179656 | tf_op jit(solution)/shard_map/cond/branch_1_fun/ppermute | solution.py:49
  18.9 28.0 %collective-permute-start.43 = (bf16[256,1536]{1,0:T(8,128)(2,1)}, bf16[256,1536]{1,0:T(8,128)(2,1)}, u32[]{:S(2)}, u32[]{:S(2)}) collective-permute-start(bf16[256,1536]{1,0:T(8,128)(2,1)} %branch_1_fun.37), channel_id=1, source_target_pairs={{0,2},{1,3},{2,0},{3,1},{4,6},{5,7},{6,4},{7,5},{8,10},{9,11},{10,... | collective-permute-start | bytes 2359304 | tf_op jit(solution)/shard_map/cond/branch_1_fun/ppermute | solution.py:49
  20.0 37.4 %collective-permute-start.42 = (bf16[256,1536]{1,0:T(8,128)(2,1)}, bf16[256,1536]{1,0:T(8,128)(2,1)}, u32[]{:S(2)}, u32[]{:S(2)}) collective-permute-start(bf16[256,1536]{1,0:T(8,128)(2,1)} %branch_1_fun.37), channel_id=1, source_target_pairs={{0,1},{1,0},{2,3},{3,2},{4,5},{5,4},{6,7},{7,6},{8,9},{9,8},{10,11... | collective-permute-start | bytes 2359304 | tf_op jit(solution)/shard_map/cond/branch_1_fun/ppermute | solution.py:49
  24.3 12.5 %collective-permute-start.46 = (bf16[192,1024]{1,0:T(8,128)(2,1)}, bf16[192,1024]{1,0:T(8,128)(2,1)}, u32[]{:S(2)}, u32[]{:S(2)}) collective-permute-start(bf16[192,1024]{1,0:T(8,128)(2,1)} %collective-permute-done.45), channel_id=1, source_target_pairs={{0,8},{4,12},{8,16},{12,20},{16,24},{20,28},{24,0},{28,4},{1,9},{5... | collective-permute-start | bytes 1179656 | tf_op jit(solution)/shard_map/cond/branch_1_fun/ppermute | solution.py:49
  24.9 18.7 %collective-permute-start.51 = (bf16[3,192,640]{2,1,0:T(8,128)(2,1)}, bf16[3,192,640]{2,1,0:T(8,128)(2,1)S(1)}, u32[]{:S(2)}, u32[]{:S(2)}) collective-permute-start(bf16[3,192,640]{2,1,0:T(8,128)(2,1)} %branch_1_fun.38), channel_id=1, source_target_pairs={{0,4},{4,0},{8,12},{12,8},{16,20},{20,16},{24,28},{28,24},{1,5},{5... | collective-permute-start | bytes 2211848 | tf_op jit(solution)/shard_map/cond/branch_1_fun/ppermute | solution.py:49
  36.9 18.1 %collective-permute-start.52 = (bf16[256,1536]{1,0:T(8,128)(2,1)}, bf16[256,1536]{1,0:T(8,128)(2,1)S(1)}, u32[]{:S(2)}, u32[]{:S(2)}) collective-permute-start(bf16[256,1536]{1,0:T(8,128)(2,1)} %branch_1_fun.39), channel_id=1, source_target_pairs={{0,2},{1,3},{2,0},{3,1},{4,6},{5,7},{6,4},{7,5},{8,10},{9,11},{10,... | collective-permute-start | bytes 2359304 | tf_op jit(solution)/shard_map/cond/branch_1_fun/ppermute | solution.py:49
  41.3 16.1 %collective-permute-start.49 = (bf16[192,1024]{1,0:T(8,128)(2,1)}, bf16[192,1024]{1,0:T(8,128)(2,1)}, u32[]{:S(2)}, u32[]{:S(2)}) collective-permute-start(bf16[192,1024]{1,0:T(8,128)(2,1)} %collective-permute-done.45), channel_id=1, source_target_pairs={{0,4},{4,0},{8,12},{12,8},{16,20},{20,16},{24,28},{28,24},{1,5},{5... | collective-permute-start | bytes 1179656 | tf_op jit(solution)/shard_map/cond/branch_1_fun/ppermute | solution.py:49
  43.6 13.8 %collective-permute-start.47 = (bf16[192,1024]{1,0:T(8,128)(2,1)}, bf16[192,1024]{1,0:T(8,128)(2,1)}, u32[]{:S(2)}, u32[]{:S(2)}) collective-permute-start(bf16[192,1024]{1,0:T(8,128)(2,1)} %collective-permute-done.46.refs_1_), channel_id=1, source_target_pairs={{0,8},{4,12},{8,16},{12,20},{16,24},{20,28},{24,0},{28,4},{1,9},{5... | collective-permute-start | bytes 1179656 | tf_op jit(solution)/shard_map/cond/branch_1_fun/ppermute | solution.py:49
  46.9 13.1 %collective-permute-start.50 = (bf16[192,1024]{1,0:T(8,128)(2,1)}, bf16[192,1024]{1,0:T(8,128)(2,1)}, u32[]{:S(2)}, u32[]{:S(2)}) collective-permute-start(bf16[192,1024]{1,0:T(8,128)(2,1)} %collective-permute-done.46.refs_1_), channel_id=1, source_target_pairs={{0,4},{4,0},{8,12},{12,8},{16,20},{20,16},{24,28},{28,24},{1,5},{5... | collective-permute-start | bytes 1179656 | tf_op jit(solution)/shard_map/cond/branch_1_fun/ppermute | solution.py:49
  61.5 34.5 %collective-permute-start.55 = (bf16[3,384,640]{2,1,0:T(8,128)(2,1)}, bf16[3,384,640]{2,1,0:T(8,128)(2,1)}, u32[]{:S(2)}, u32[]{:S(2)}) collective-permute-start(bf16[3,384,640]{2,1,0:T(8,128)(2,1)} %get-tuple-element.628.refs_1_.refs_11_.refs_2_), channel_id=1, source_target_pairs={{0,8},{4,12},{8,16},{12,20},{16,24},{20,28},{24,0},{28,4},{1,9},{5... | collective-permute-start | bytes 4423688 | tf_op jit(solution)/shard_map/ppermute | solution.py:49
  69.3 26.7 %collective-permute-start.57 = (bf16[64,1536]{1,0:T(8,128)(2,1)}, bf16[64,1536]{1,0:T(8,128)(2,1)}, u32[]{:S(2)}, u32[]{:S(2)}) collective-permute-start(bf16[64,1536]{1,0:T(8,128)(2,1)} %shard_map.265), channel_id=1, source_target_pairs={{0,4},{4,0},{8,12},{12,8},{16,20},{20,16},{24,28},{28,24},{1,5},{5... | collective-permute-start | bytes 589832 | tf_op jit(solution)/shard_map/ppermute | solution.py:49
  70.7 25.2 %collective-permute-start.56 = (bf16[3,192,512]{2,1,0:T(8,128)(2,1)}, bf16[3,192,512]{2,1,0:T(8,128)(2,1)}, u32[]{:S(2)}, u32[]{:S(2)}) collective-permute-start(bf16[3,192,512]{2,1,0:T(8,128)(2,1)} %shard_map.264), channel_id=1, source_target_pairs={{0,4},{4,0},{8,12},{12,8},{16,20},{20,16},{24,28},{28,24},{1,5},{5... | collective-permute-start | bytes 1769480 | tf_op jit(solution)/shard_map/ppermute | solution.py:49
  92.5 39.8 %collective-permute-start.54 = (bf16[256,1536]{1,0:T(8,128)(2,1)}, bf16[256,1536]{1,0:T(8,128)(2,1)}, u32[]{:S(2)}, u32[]{:S(2)}) collective-permute-start(bf16[256,1536]{1,0:T(8,128)(2,1)} %shard_map.262), channel_id=1, source_target_pairs={{0,4},{4,0},{8,12},{12,8},{16,20},{20,16},{24,28},{28,24},{1,5},{5... | collective-permute-start | bytes 2359304 | tf_op jit(solution)/shard_map/ppermute | solution.py:49
  96.0 38.7 %collective-permute-start.61 = (bf16[3,384,640]{2,1,0:T(8,128)(2,1)}, bf16[3,384,640]{2,1,0:T(8,128)(2,1)}, u32[]{:S(2)}, u32[]{:S(2)}) collective-permute-start(bf16[3,384,640]{2,1,0:T(8,128)(2,1)} %shard_map.263.refs_1_.refs_14_.refs_5_), channel_id=1, source_target_pairs={{0,8},{4,12},{8,16},{12,20},{16,24},{20,28},{24,0},{28,4},{1,9},{5... | collective-permute-start | bytes 4423688 | tf_op jit(solution)/shard_map/ppermute | solution.py:49
  97.1 18.2 %collective-permute-start.19 = (bf16[256,1536]{1,0:T(8,128)(2,1)}, bf16[256,1536]{1,0:T(8,128)(2,1)S(1)}, u32[]{:S(2)}, u32[]{:S(2)}) collective-permute-start(bf16[256,1536]{1,0:T(8,128)(2,1)} %get-tuple-element.365), channel_id=1, source_target_pairs={{0,2},{1,3},{2,0},{3,1},{4,6},{5,7},{6,4},{7,5},{8,10},{9,11},{10,... | collective-permute-start | bytes 2359304 | tf_op jit(solution)/shard_map/cond/branch_1_fun/ppermute | solution.py:49
  134.7 32.3 %collective-permute-start.62 = (bf16[3,384,640]{2,1,0:T(8,128)(2,1)}, bf16[3,384,640]{2,1,0:T(8,128)(2,1)}, u32[]{:S(2)}, u32[]{:S(2)}) collective-permute-start(bf16[3,384,640]{2,1,0:T(8,128)(2,1)} %shard_map.270.refs_4_.refs_13_), channel_id=1, source_target_pairs={{0,8},{4,12},{8,16},{12,20},{16,24},{20,28},{24,0},{28,4},{1,9},{5... | collective-permute-start | bytes 4423688 | tf_op jit(solution)/shard_map/ppermute | solution.py:49
  142.4 23.5 %collective-permute-start.1 = (bf16[512,1536]{1,0:T(8,128)(2,1)}, bf16[512,1536]{1,0:T(8,128)(2,1)}, u32[]{:S(2)}, u32[]{:S(2)}) collective-permute-start(bf16[512,1536]{1,0:T(8,128)(2,1)} %branch_1_fun.45), channel_id=1, source_target_pairs={{0,1},{1,0},{2,3},{3,2},{4,5},{5,4},{6,7},{7,6},{8,9},{9,8},{10,11... | collective-permute-start | bytes 4718600 | tf_op jit(solution)/shard_map/cond/branch_1_fun/ppermute | solution.py:49
  142.4 20.3 %collective-permute-start.2 = (bf16[256,1536]{1,0:T(8,128)(2,1)}, bf16[256,1536]{1,0:T(8,128)(2,1)}, u32[]{:S(2)}, u32[]{:S(2)}) collective-permute-start(bf16[256,1536]{1,0:T(8,128)(2,1)} %get-tuple-element.383), channel_id=1, source_target_pairs={{0,2},{1,3},{2,0},{3,1},{4,6},{5,7},{6,4},{7,5},{8,10},{9,11},{10,... | collective-permute-start | bytes 2359304 | tf_op jit(solution)/shard_map/cond/branch_1_fun/ppermute | solution.py:49
  143.2 20.0 %collective-permute-start.3 = (bf16[256,1536]{1,0:T(8,128)(2,1)}, bf16[256,1536]{1,0:T(8,128)(2,1)}, u32[]{:S(2)}, u32[]{:S(2)}) collective-permute-start(bf16[256,1536]{1,0:T(8,128)(2,1)} %get-tuple-element.384), channel_id=1, source_target_pairs={{0,4},{4,0},{8,12},{12,8},{16,20},{20,16},{24,28},{28,24},{1,5},{5... | collective-permute-start | bytes 2359304 | tf_op jit(solution)/shard_map/cond/branch_1_fun/ppermute | solution.py:49
  144.0 22.5 %collective-permute-start.4 = (bf16[512,1536]{1,0:T(8,128)(2,1)}, bf16[512,1536]{1,0:T(8,128)(2,1)}, u32[]{:S(2)}, u32[]{:S(2)}) collective-permute-start(bf16[512,1536]{1,0:T(8,128)(2,1)} %get-tuple-element.833), channel_id=1, source_target_pairs={{0,1},{1,0},{2,3},{3,2},{4,5},{5,4},{6,7},{7,6},{8,9},{9,8},{10,11... | collective-permute-start | bytes 4718600 | tf_op jit(solution)/shard_map/cond/branch_1_fun/ppermute | solution.py:49
  167.0 30.2 %collective-permute-start.63 = (bf16[3,384,512]{2,1,0:T(8,128)(2,1)}, bf16[3,384,512]{2,1,0:T(8,128)(2,1)}, u32[]{:S(2)}, u32[]{:S(2)}) collective-permute-start(bf16[3,384,512]{2,1,0:T(8,128)(2,1)} %shard_map.272.refs_11_.refs_2_), channel_id=1, source_target_pairs={{0,8},{4,12},{8,16},{12,20},{16,24},{20,28},{24,0},{28,4},{1,9},{5... | collective-permute-start | bytes 3538952 | tf_op jit(solution)/shard_map/ppermute | solution.py:49
  197.2 28.9 %collective-permute-start.64 = (bf16[3,384,512]{2,1,0:T(8,128)(2,1)}, bf16[3,384,512]{2,1,0:T(8,128)(2,1)}, u32[]{:S(2)}, u32[]{:S(2)}) collective-permute-start(bf16[3,384,512]{2,1,0:T(8,128)(2,1)} %shard_map.274.refs_14_.refs_5_), channel_id=1, source_target_pairs={{0,8},{4,12},{8,16},{12,20},{16,24},{20,28},{24,0},{28,4},{1,9},{5... | collective-permute-start | bytes 3538952 | tf_op jit(solution)/shard_map/ppermute | solution.py:49
  226.1 28.0 %collective-permute-start.65 = (bf16[3,384,512]{2,1,0:T(8,128)(2,1)}, bf16[3,384,512]{2,1,0:T(8,128)(2,1)}, u32[]{:S(2)}, u32[]{:S(2)}) collective-permute-start(bf16[3,384,512]{2,1,0:T(8,128)(2,1)} %shard_map.276.refs_13_.refs_4_), channel_id=1, source_target_pairs={{0,8},{4,12},{8,16},{12,20},{16,24},{20,28},{24,0},{28,4},{1,9},{5... | collective-permute-start | bytes 3538952 | tf_op jit(solution)/shard_map/ppermute | solution.py:49
  254.1 34.2 %collective-permute-start.66 = (bf16[3,384,640]{2,1,0:T(8,128)(2,1)}, bf16[3,384,640]{2,1,0:T(8,128)(2,1)}, u32[]{:S(2)}, u32[]{:S(2)}) collective-permute-start(bf16[3,384,640]{2,1,0:T(8,128)(2,1)} %shard_map.280), channel_id=1, source_target_pairs={{0,8},{4,12},{8,16},{12,20},{16,24},{20,28},{24,0},{28,4},{1,9},{5... | collective-permute-start | bytes 4423688 | tf_op jit(solution)/shard_map/ppermute | solution.py:49
  291.4 33.2 %collective-permute-start.67 = (bf16[3,384,640]{2,1,0:T(8,128)(2,1)}, bf16[3,384,640]{2,1,0:T(8,128)(2,1)}, u32[]{:S(2)}, u32[]{:S(2)}) collective-permute-start(bf16[3,384,640]{2,1,0:T(8,128)(2,1)} %bitcast_add_fusion.3.refs_1_), channel_id=1, source_target_pairs={{0,8},{4,12},{8,16},{12,20},{16,24},{20,28},{24,0},{28,4},{1,9},{5... | collective-permute-start | bytes 4423688 | tf_op jit(solution)/shard_map/ppermute | solution.py:49
  301.1 19.9 %collective-permute-start.8 = (bf16[256,1536]{1,0:T(8,128)(2,1)}, bf16[256,1536]{1,0:T(8,128)(2,1)}, u32[]{:S(2)}, u32[]{:S(2)}) collective-permute-start(bf16[256,1536]{1,0:T(8,128)(2,1)} %get-tuple-element.388.refs_11_), channel_id=1, source_target_pairs={{0,2},{1,3},{2,0},{3,1},{4,6},{5,7},{6,4},{7,5},{8,10},{9,11},{10,... | collective-permute-start | bytes 2359304 | tf_op jit(solution)/shard_map/cond/branch_1_fun/ppermute | solution.py:49
  301.1 19.8 %collective-permute-start.9 = (bf16[256,1536]{1,0:T(8,128)(2,1)}, bf16[256,1536]{1,0:T(8,128)(2,1)}, u32[]{:S(2)}, u32[]{:S(2)}) collective-permute-start(bf16[256,1536]{1,0:T(8,128)(2,1)} %get-tuple-element.389), channel_id=1, source_target_pairs={{0,4},{4,0},{8,12},{12,8},{16,20},{20,16},{24,28},{28,24},{1,5},{5... | collective-permute-start | bytes 2359304 | tf_op jit(solution)/shard_map/cond/branch_1_fun/ppermute | solution.py:49
  327.7 44.6 %collective-permute-start.68 = (bf16[3,384,640]{2,1,0:T(8,128)(2,1)}, bf16[3,384,640]{2,1,0:T(8,128)(2,1)}, u32[]{:S(2)}, u32[]{:S(2)}) collective-permute-start(bf16[3,384,640]{2,1,0:T(8,128)(2,1)} %bitcast_add_fusion.2.refs_1_), channel_id=1, source_target_pairs={{0,8},{4,12},{8,16},{12,20},{16,24},{20,28},{24,0},{28,4},{1,9},{5... | collective-permute-start | bytes 4423688 | tf_op jit(solution)/shard_map/ppermute | solution.py:49
  328.7 11.8 %collective-permute-start.10 = (bf16[128,1536]{1,0:T(8,128)(2,1)}, bf16[128,1536]{1,0:T(8,128)(2,1)}, u32[]{:S(2)}, u32[]{:S(2)}) collective-permute-start(bf16[128,1536]{1,0:T(8,128)(2,1)} %get-tuple-element.410), channel_id=1, source_target_pairs={{0,4},{4,0},{8,12},{12,8},{16,20},{20,16},{24,28},{28,24},{1,5},{5... | collective-permute-start | bytes 1179656 | tf_op jit(solution)/shard_map/cond/branch_1_fun/ppermute | solution.py:49
  330.2 11.6 %collective-permute-start.11 = (bf16[128,1536]{1,0:T(8,128)(2,1)}, bf16[128,1536]{1,0:T(8,128)(2,1)}, u32[]{:S(2)}, u32[]{:S(2)}) collective-permute-start(bf16[128,1536]{1,0:T(8,128)(2,1)} %get-tuple-element.411), channel_id=1, source_target_pairs={{0,2},{1,3},{2,0},{3,1},{4,6},{5,7},{6,4},{7,5},{8,10},{9,11},{10,... | collective-permute-start | bytes 1179656 | tf_op jit(solution)/shard_map/cond/branch_1_fun/ppermute | solution.py:49
  346.2 20.9 %collective-permute-start.13 = (bf16[256,1536]{1,0:T(8,128)(2,1)}, bf16[256,1536]{1,0:T(8,128)(2,1)}, u32[]{:S(2)}, u32[]{:S(2)}) collective-permute-start(bf16[256,1536]{1,0:T(8,128)(2,1)} %get-tuple-element.860.refs_13_), channel_id=1, source_target_pairs={{0,2},{1,3},{2,0},{3,1},{4,6},{5,7},{6,4},{7,5},{8,10},{9,11},{10,... | collective-permute-start | bytes 2359304 | tf_op jit(solution)/shard_map/cond/branch_1_fun/ppermute | solution.py:49
  347.6 19.5 %collective-permute-start.14 = (bf16[256,1536]{1,0:T(8,128)(2,1)}, bf16[256,1536]{1,0:T(8,128)(2,1)}, u32[]{:S(2)}, u32[]{:S(2)}) collective-permute-start(bf16[256,1536]{1,0:T(8,128)(2,1)} %get-tuple-element.860.refs_13_), channel_id=1, source_target_pairs={{0,1},{1,0},{2,3},{3,2},{4,5},{5,4},{6,7},{7,6},{8,9},{9,8},{10,11... | collective-permute-start | bytes 2359304 | tf_op jit(solution)/shard_map/cond/branch_1_fun/ppermute | solution.py:49
  367.1 36.2 %collective-permute-start.71 = (bf16[256,1536]{1,0:T(8,128)(2,1)}, bf16[256,1536]{1,0:T(8,128)(2,1)}, u32[]{:S(2)}, u32[]{:S(2)}) collective-permute-start(bf16[256,1536]{1,0:T(8,128)(2,1)} %get-tuple-element.693), channel_id=1, source_target_pairs={{0,4},{4,0},{8,12},{12,8},{16,20},{20,16},{24,28},{28,24},{1,5},{5... | collective-permute-start | bytes 2359304 | tf_op jit(solution)/shard_map/ppermute | solution.py:49
  367.6 35.7 %collective-permute-start.70 = (bf16[256,1536]{1,0:T(8,128)(2,1)}, bf16[256,1536]{1,0:T(8,128)(2,1)}, u32[]{:S(2)}, u32[]{:S(2)}) collective-permute-start(bf16[256,1536]{1,0:T(8,128)(2,1)} %get-tuple-element.692), channel_id=1, source_target_pairs={{0,2},{1,3},{2,0},{3,1},{4,6},{5,7},{6,4},{7,5},{8,10},{9,11},{10,... | collective-permute-start | bytes 2359304 | tf_op jit(solution)/shard_map/ppermute | solution.py:49
  368.3 30.5 %collective-permute-start.69 = (bf16[3,384,512]{2,1,0:T(8,128)(2,1)}, bf16[3,384,512]{2,1,0:T(8,128)(2,1)}, u32[]{:S(2)}, u32[]{:S(2)}) collective-permute-start(bf16[3,384,512]{2,1,0:T(8,128)(2,1)} %shard_map.286), channel_id=1, source_target_pairs={{0,8},{4,12},{8,16},{12,20},{16,24},{20,28},{24,0},{28,4},{1,9},{5... | collective-permute-start | bytes 3538952 | tf_op jit(solution)/shard_map/ppermute | solution.py:49
  401.6 29.7 %collective-permute-start.72 = (bf16[3,384,512]{2,1,0:T(8,128)(2,1)}, bf16[3,384,512]{2,1,0:T(8,128)(2,1)}, u32[]{:S(2)}, u32[]{:S(2)}) collective-permute-start(bf16[3,384,512]{2,1,0:T(8,128)(2,1)} %bitcast_add_fusion.6.refs_1_), channel_id=1, source_target_pairs={{0,8},{4,12},{8,16},{12,20},{16,24},{20,28},{24,0},{28,4},{1,9},{5... | collective-permute-start | bytes 3538952 | tf_op jit(solution)/shard_map/ppermute | solution.py:49
  404.8 15.4 %collective-permute-start.24 = (bf16[2,256,1536]{2,1,0:T(8,128)(2,1)}, bf16[2,256,1536]{2,1,0:T(8,128)(2,1)}, u32[]{:S(2)}, u32[]{:S(2)}) collective-permute-start(bf16[2,256,1536]{2,1,0:T(8,128)(2,1)} %get-tuple-element.477.refs_11_), channel_id=1, source_target_pairs={{0,1},{1,0},{2,3},{3,2},{4,5},{5,4},{6,7},{7,6},{8,9},{9,8},{10,11... | collective-permute-start | bytes 4718600 | tf_op jit(solution)/shard_map/cond/branch_1_fun/ppermute | solution.py:49
  406.6 12.3 %collective-permute-start.26 = (f32[40,128]{1,0:T(8,128)}, f32[40,128]{1,0:T(8,128)}, u32[]{:S(2)}, u32[]{:S(2)}) collective-permute-start(f32[40,128]{1,0:T(8,128)} %add.92), channel_id=1, source_target_pairs={{0,2},{1,3},{2,0},{3,1},{4,6},{5,7},{6,4},{7,5},{8,10},{9,11},{10,... | collective-permute-start | bytes 61448 | tf_op jit(solution)/shard_map/cond/branch_1_fun/ppermute | solution.py:49
  418.1 11.3 %collective-permute-start.23 = (bf16[192,1024]{1,0:T(8,128)(2,1)}, bf16[192,1024]{1,0:T(8,128)(2,1)}, u32[]{:S(2)}, u32[]{:S(2)}) collective-permute-start(bf16[192,1024]{1,0:T(8,128)(2,1)} %get-tuple-element.482), channel_id=1, source_target_pairs={{0,4},{4,0},{8,12},{12,8},{16,20},{20,16},{24,28},{28,24},{1,5},{5... | collective-permute-start | bytes 1179656 | tf_op jit(solution)/shard_map/cond/branch_1_fun/ppermute | solution.py:49
  434.9 11.7 %collective-permute-start.27 = (bf16[192,1024]{1,0:T(8,128)(2,1)}, bf16[192,1024]{1,0:T(8,128)(2,1)S(1)}, u32[]{:S(2)}, u32[]{:S(2)}) collective-permute-start(bf16[192,1024]{1,0:T(8,128)(2,1)} %get-tuple-element.495), channel_id=1, source_target_pairs={{0,8},{4,12},{8,16},{12,20},{16,24},{20,28},{24,0},{28,4},{1,9},{5... | collective-permute-start | bytes 1179656 | tf_op jit(solution)/shard_map/cond/branch_1_fun/ppermute | solution.py:49
  447.9 27.6 %collective-permute-start.34 = (bf16[256,1536]{1,0:T(8,128)(2,1)}, bf16[256,1536]{1,0:T(8,128)(2,1)}, u32[]{:S(2)}, u32[]{:S(2)}) collective-permute-start(bf16[256,1536]{1,0:T(8,128)(2,1)} %get-tuple-element.498.refs_1_), channel_id=1, source_target_pairs={{0,2},{1,3},{2,0},{3,1},{4,6},{5,7},{6,4},{7,5},{8,10},{9,11},{10,... | collective-permute-start | bytes 2359304 | tf_op jit(solution)/shard_map/cond/branch_1_fun/ppermute | solution.py:49
  459.8 14.5 %collective-permute-start.31 = (bf16[192,1024]{1,0:T(8,128)(2,1)S(1)}, bf16[192,1024]{1,0:T(8,128)(2,1)S(1)}, u32[]{:S(2)}, u32[]{:S(2)}) collective-permute-start(bf16[192,1024]{1,0:T(8,128)(2,1)S(1)} %fusion.3), channel_id=1, source_target_pairs={{0,8},{4,12},{8,16},{12,20},{16,24},{20,28},{24,0},{28,4},{1,9},{5... | collective-permute-start | bytes 1179656 | tf_op jit(solution)/shard_map/cond/branch_1_fun/ppermute | solution.py:49
  461.2 13.1 %collective-permute-start.33 = (bf16[192,1024]{1,0:T(8,128)(2,1)}, bf16[192,1024]{1,0:T(8,128)(2,1)S(1)}, u32[]{:S(2)}, u32[]{:S(2)}) collective-permute-start(bf16[192,1024]{1,0:T(8,128)(2,1)} %branch_1_fun.62), channel_id=1, source_target_pairs={{0,4},{4,0},{8,12},{12,8},{16,20},{20,16},{24,28},{28,24},{1,5},{5... | collective-permute-start | bytes 1179656 | tf_op jit(solution)/shard_map/cond/branch_1_fun/ppermute | solution.py:49
  475.6 31.8 %collective-permute-start.73 = (bf16[3,384,512]{2,1,0:T(8,128)(2,1)}, bf16[3,384,512]{2,1,0:T(8,128)(2,1)}, u32[]{:S(2)}, u32[]{:S(2)}) collective-permute-start(bf16[3,384,512]{2,1,0:T(8,128)(2,1)} %shard_map.293.refs_1_), channel_id=1, source_target_pairs={{0,8},{4,12},{8,16},{12,20},{16,24},{20,28},{24,0},{28,4},{1,9},{5... | collective-permute-start | bytes 3538952 | tf_op jit(solution)/shard_map/ppermute | solution.py:49
  486.9 18.7 %collective-permute-start.41 = (bf16[3,192,640]{2,1,0:T(8,128)(2,1)}, bf16[3,192,640]{2,1,0:T(8,128)(2,1)}, u32[]{:S(2)}, u32[]{:S(2)}) collective-permute-start(bf16[3,192,640]{2,1,0:T(8,128)(2,1)} %branch_1_fun.67), channel_id=1, source_target_pairs={{0,4},{4,0},{8,12},{12,8},{16,20},{20,16},{24,28},{28,24},{1,5},{5... | collective-permute-start | bytes 2211848 | tf_op jit(solution)/shard_map/cond/branch_1_fun/ppermute | solution.py:49
  489.6 13.0 %collective-permute-start.40 = (bf16[128,1536]{1,0:T(8,128)(2,1)}, bf16[128,1536]{1,0:T(8,128)(2,1)S(1)}, u32[]{:S(2)}, u32[]{:S(2)}) collective-permute-start(bf16[128,1536]{1,0:T(8,128)(2,1)} %get-tuple-element.513), channel_id=1, source_target_pairs={{0,2},{1,3},{2,0},{3,1},{4,6},{5,7},{6,4},{7,5},{8,10},{9,11},{10,... | collective-permute-start | bytes 1179656 | tf_op jit(solution)/shard_map/cond/branch_1_fun/ppermute | solution.py:49
  509.7 15.1 %collective-permute-start.74 = (bf16[3,192,512]{2,1,0:T(8,128)(2,1)S(1)}, bf16[3,192,512]{2,1,0:T(8,128)(2,1)S(1)}, u32[]{:S(2)}, u32[]{:S(2)}) collective-permute-start(bf16[3,192,512]{2,1,0:T(8,128)(2,1)S(1)} %shard_map.296), channel_id=1, source_target_pairs={{0,4},{4,0},{8,12},{12,8},{16,20},{20,16},{24,28},{28,24},{1,5},{5... | collective-permute-start | bytes 1769480 | tf_op jit(solution)/shard_map/ppermute | solution.py:49
  (69 other events, 477.2 us)

commit v5 on v4

--- a/solution.py
+++ b/solution.py
@@ -269,20 +269,24 @@
 
 
 def stack_rows(parts, outs):
+    outs = [
+        [piece if isinstance(piece, tuple) else (piece, 0, parts[piece].shape[0]) for piece in pieces]
+        for pieces in outs
+    ]
+
     def kernel(*refs):
-        for index, numbers in enumerate(outs):
+        for index, pieces in enumerate(outs):
             begin = 0
-            for number in numbers:
-                ref = refs[number]
-                refs[len(parts) + index][begin : begin + ref.shape[0]] = ref[...]
-                begin += ref.shape[0]
+            for number, first, last in pieces:
+                refs[len(parts) + index][begin : begin + last - first] = refs[number][first:last]
+                begin += last - first
 
     width = parts[0].shape[1]
     return call(
         kernel,
         parts,
         [in_vmem] * len(parts),
-        [shaped((sum(parts[number].shape[0] for number in numbers), width)) for numbers in outs],
+        [shaped((sum(last - first for _, first, last in pieces), width)) for pieces in outs],
         room=24,
     )
 
@@ -1059,7 +1063,8 @@
     def pair_block(block, came):
         return lax.dynamic_update_slice_in_dim(block, came, (1 - dp_rank % 2) * share, 1)
 
-    piece = grad_out.shape[0] // 4
+    held = grad_out.shape[0]
+    most = 3 * held // 4
 
     def along_z(block):
         line, crossed = [block], []
@@ -1072,15 +1077,17 @@
             line.append(up_line(line[-1]))
         came = across_x(after(packed[0], crossed[0]))
         grad_y = across_y(after(grad_out, line[2 % z_count]))
-        grads, grad_own = stack_rows([grad_out, grad_y], [(0, 1), (0,)])
-        parts = [grad_y[part : part + piece] for part in range(0, 3 * piece, piece)]
+        grads, grad_most, grad_end = stack_rows(
+            [grad_out, grad_y],
+            [(0, 1), [(0, 0, most), (1, 0, most)], [(0, most, held)]],
+        )
         cosine, sine = angles_of(segment, HD)
         sine = jnp.where(jnp.arange(HD) < HD // 2, -sine, sine)
-        return rows, line[1:], crossed, pair_block(packed[1], came), packed[2:], [grads, grad_own, parts], cosine, sine
+        return rows, line[1:], crossed, pair_block(packed[1], came), packed[2:], [grads, grad_most, grad_end], cosine, sine
 
     line = [stage(begin)]
     rows_one, rest, crossed, block, packed, grads, cosine, sine = stage(along_z, line[0])
-    grad_near, grad_own, grad_parts = grads
+    grad_near, grad_most, grad_end = grads
     line += rest
     crossed.append(across_x(line[-1]))
     qkv_blocks = []
@@ -1098,7 +1105,7 @@
     early = [block]
     next_hop(early)
     came_late = across_x(after(packed[0], crossed[-1]))
-    grad_far = [across_x(after(grad_parts[0], crossed[-1]))]
+    grad_end = across_x(after(grad_end, crossed[-1]))
     rows_one[0] = gate(rows_one[0], early[0], crossed[-1])
     key_bias = lax.dynamic_slice_in_dim(b_key, y_rank * HD, HD, 0)
     value_bias = lax.dynamic_slice_in_dim(b_value, y_rank * HD, HD, 0)
@@ -1109,32 +1116,32 @@
             ranks, rows_one, qkv_blocks, bias, cosine, sine, segment, others
         )
         sent, own = join_near(ranks, keep, across_core(send))
-        return kept, probs, sent, own
-
-    (query, key, value, heads_low), probs, sent, own = stage(attention)
+        return kept, probs, sent, own, across_core(grad_near)
+
+    (query, key, value, heads_low), probs, sent, own, other_near = stage(attention)
     next_hop(early, sent)
-    grad_x = across_x(after(grad_own, sent))
-    grad_far.append(across_x(after(grad_parts[1], sent)))
-    sent = gate(sent, early[1], came_late, grad_far[0])
+    grad_most = across_x(after(grad_most, sent))
+    sent = gate(sent, early[1], came_late, grad_end)
 
     def between():
-        mid, top, bottom = middle(tokens, own, across_y(sent), gain_ffn)
+        came = across_y(sent)
+        mid, top, bottom = middle(tokens, own, came, gain_ffn)
         top, bottom, both = stack_rows(
             [top, across_x(top), bottom, across_y(bottom)], [(0, 1), (2, 3), (0, 1, 2, 3)]
         )
-        return mid, top, bottom, both, across_core(grad_near), pair_block(packed[1], came_late)
-
-    mid_rows, top, bottom, both, other_near, block = stage(between)
+        last = across_y(after(grad_end, came))
+        return mid, top, bottom, both, pair_block(packed[1], came_late), last
+
+    mid_rows, top, bottom, both, block, grad_last = stage(between)
     late = [block]
     next_hop(early, both)
-    grad_far.append(across_x(after(grad_parts[2], both)))
-    grad_x = after(grad_x, both)
-    grad_far.append(across_y(grad_x[3 * piece :]))
-    top = gate(top, *grad_far[:2], grad_x, early[2])
+    top = gate(top, grad_most, early[2])
 
     def spread():
         far_top, far_bottom = across_y(top), across_x(bottom)
-        (grads,) = stack_rows([grad_x, *grad_far], [range(5)])
+        (grads,) = stack_rows(
+            [grad_most, grad_end, grad_last], [[(0, 0, most), 1, (0, most, 2 * most), 2]]
+        )
         return [grads, across_core(grads)], [
             both,
             far_top,

time: 534 us -> 528 us (0.989)
  waiting for transfers between devices: 181 us -> 173 us
    ppermute x75 -> x73, waiting for transfers between devices: 181 us -> 173 us  [moved(): return lax.ppermute(block, axis, route)]
    ppermute x75 -> x73, starting transfers between devices: 64.5 us -> 66.2 us  [moved(): return lax.ppermute(block, axis, route)]
  transfers between devices with their start and end apart: 75 -> 73, of which waited for: 41 -> 41; matrix products, arithmetic and copies ran while one was open for 7% -> 7% of each run, Pallas kernels for 41% -> 42%
where the time goes in v5:
time: 528 us; the launch traced here: 522 us
  Pallas kernels  223 us (42%)
  waiting for transfers between devices  173 us (33%)
  starting transfers between devices  66.2 us (13%)
  other arithmetic  31 us (6%)
  local copies, waits for them, and re-layouts  26.8 us (5%)
    pallas_call x30, Pallas kernels, call(): pl.pallas_call(body, out_shape=outs, in_specs=list(specs) + [anywhere] *...  223 us
    ppermute x73, waiting for transfers between devices, moved(): return lax.ppermute(block, axis, route)  173 us
    ppermute x73, starting transfers between devices, moved(): return lax.ppermute(block, axis, route)  66.2 us
    add x7, other arithmetic, added(): return came + part  17.3 us
  transfers between devices with their start and end apart: 73, of which 41 were waited for; matrix products, arithmetic and copies ran while one was open for 7% of the time, Pallas kernels for 42%

profile of v5, /device:TPU:0, one launch (start us, length us, event | category | flops | bytes accessed | tf_op | source)
XLA Modules:
  0.0 522.3 jit_solution(13281898609869460694)
XLA Ops:
  0.7 10.1 %conditional.11 = (bf16[192,1024]{1,0:T(8,128)(2,1)}) conditional(s32[]{:T(128)} %convert_element_type.85, () %tuple.102, (bf16[384,192]{0,1:T(8,128)(2,1)}, bf16[48,256]{1,0:T(8,128)(2,1)}, bf16[48,256]{1,0:T(8,128)(2,1)}, s32[2]{0:T(128)S(1)}, bf16[192,384]{1,0:T(8,128)(2,1)}) %tuple.103), branch_computations={%region_0.1_spmd, %region_1.2_spmd} | conditional | flops 199999995904 | bytes 688257 | solution.py:86
  10.9 49.0 %conditional.12 = (bf16[256,1536]{1,0:T(8,128)(2,1)}, bf16[256,1536]{1,0:T(8,128)(2,1)}, bf16[256,1536]{1,0:T(8,128)(2,1)}, bf16[256,1536]{1,0:T(8,128)(2,1)}, b...) conditional(s32[]{:T(128)} %convert_element_type.85, () %tuple.101, ...), branch_computations={%region_2.3_spmd, %region_3.6_spmd} | conditional | flops 200000585728 | bytes 37304132 | solution.py:86
  14.0 3.6 branch_1_fun.37
  27.5 9.4 %collective-permute-done.47.refs_1_ = bf16[192,1024]{1,0:T(8,128)(2,1)} collective-permute-done((bf16[192,1024]{1,0:T(8,128)(2,1)}, bf16[192,1024]{1,0:T(8,128)(2,1)}, u32[]{:S(2)}, u32[]{:S(2)}) %collective-permute-start.47) | collective-permute-done | bytes 393248 | tf_op jit(solution)/shard_map/cond/branch_1_fun/ppermute | solution.py:49
  48.4 6.6 %collective-permute-done.53.refs_1_ = bf16[256,1536]{1,0:T(8,128)(2,1)S(1)} collective-permute-done((bf16[256,1536]{1,0:T(8,128)(2,1)}, bf16[256,1536]{1,0:T(8,128)(2,1)S(1)}, u32[]{:S(2)}, u32[]{:S(2)}) %collective-permute-start.53) | collective-permute-done | bytes 786464 | tf_op jit(solution)/shard_map/cond/branch_1_fun/ppermute | solution.py:49
  63.4 5.8 %collective-permute-done.54.refs_2_.refs_1_ = bf16[192,1024]{1,0:T(8,128)(2,1)S(1)} collective-permute-done((bf16[192,1024]{1,0:T(8,128)(2,1)}, bf16[192,1024]{1,0:T(8,128)(2,1)S(1)}, u32[]{:S(2)}, u32[]{:S(2)}) %collective-permute-start.54) | collective-permute-done | bytes 393248 | tf_op jit(solution)/shard_map/ppermute | solution.py:49
  72.3 21.6 %conditional.13 = (bf16[1024,384]{1,0:T(8,128)(2,1)}, bf16[1024,128]{1,0:T(8,128)(2,1)}, bf16[1024,128]{1,0:T(8,128)(2,1)}, bf16[1024,384]{1,0:T(8,128)(2,1)}, b...) conditional(s32[]{:T(128)} %convert_element_type.85, () %tuple.105, ...), branch_computations={%region_6.7_spmd, %region_7.8_spmd} | conditional | flops 399999991808 | bytes 12596394 | solution.py:86
  72.5 14.2 %branch_1_fun.42 = (bf16[1024,384]{1,0:T(8,128)(2,1)}, bf16[1024,128]{1,0:T(8,128)(2,1)}, bf16[1024,128]{1,0:T(8,128)(2,1)}, bf16[1024,384]{1,0:T(8,128)(2,1)}, ...) custom-call(s32[2]{0:T(128)S(1)} %get-tuple-element.333.refs_0_, ...), custom_call_target="tpu_custom_call" | custom-call | flops 199999995904 | bytes 1 | tf_op jit(solution)/shard_map/cond/branch_1_fun/pallas_call | solution.py:122
  87.3 4.4 collective-permute-done.refs_2_
  97.5 37.1 %conditional.14 = (f32[256,1536]{1,0:T(8,128)}, bf16[256,1536]{1,0:T(8,128)(2,1)}, bf16[256,1536]{1,0:T(8,128)(2,1)}, bf16[512,1536]{1,0:T(8,128)(2,1)}, bf16[3,...) conditional(s32[]{:T(128)} %convert_element_type.85, () %tuple.107, (bf16[256,1536]{1,0:T(8,128)(2,1)}, ...), branch_computations={%region_8.9_spmd, %region_9.10_spmd} | conditional | flops 399999991808 | bytes 11809178 | solution.py:86
  98.9 17.9 %collective-permute-done.20.refs_2_.refs_1_ = bf16[256,1536]{1,0:T(8,128)(2,1)S(1)} collective-permute-done((bf16[256,1536]{1,0:T(8,128)(2,1)}, bf16[256,1536]{1,0:T(8,128)(2,1)S(1)}, u32[]{:S(2)}, u32[]{:S(2)}) %collective-permute-start.20) | collective-permute-done | bytes 786464 | tf_op jit(solution)/shard_map/cond/branch_1_fun/ppermute | solution.py:49
  126.4 4.1 collective-permute-done.21.refs_1_
  136.2 26.7 %conditional.15 = (bf16[512,1536]{1,0:T(8,128)(2,1)}, bf16[512,1536]{1,0:T(8,128)(2,1)}, bf16[512,1536]{1,0:T(8,128)(2,1)}, bf16[256,1536]{1,0:T(8,128)(2,1)}, b...) conditional(s32[]{:T(128)} %convert_element_type.85, () %tuple.100, ...), branch_computations={%region_10.11_spmd, %region_11.12_spmd} | conditional | flops 199999995904 | bytes 28311856 | solution.py:86
  141.4 17.8 %collective-permute-done.3 = bf16[256,1536]{1,0:T(8,128)(2,1)} collective-permute-done((bf16[256,1536]{1,0:T(8,128)(2,1)}, bf16[256,1536]{1,0:T(8,128)(2,1)}, u32[]{:S(2)}, u32[]{:S(2)}) %collective-permute-start.3) | collective-permute-done | bytes 786464 | tf_op jit(solution)/shard_map/cond/branch_1_fun/ppermute | solution.py:49
  162.9 5.5 %collective-permute-done.60.refs_1_.refs_12_.refs_3_ = bf16[3,384,640]{2,1,0:T(8,128)(2,1)} collective-permute-done((bf16[3,384,640]{2,1,0:T(8,128)(2,1)}, bf16[3,384,640]{2,1,0:T(8,128)(2,1)}, u32[]{:S(2)}, u32[]{:S(2)}) %collective-permute-start.60) | collective-permute-done | bytes 1474592 | tf_op jit(solution)/shard_map/ppermute | solution.py:49
  169.1 22.2 %shard_map.270 = (bf16[2048,640]{1,0:T(8,128)(2,1)}, bf16[2048,1280]{1,0:T(8,128)(2,1)}) custom-call(s32[2]{0:T(128)S(1)} %copy-done.34, bf16[512,1536]{1,0:T(8,128)(2,1)} %get-tuple-element.647.refs_1_, bf16[256,1536]{1,0:T(8,128)(2,1)} %get-tuple-element.648.refs_2_, bf16[256,1536]{1,0:T(8,128)(2,1)} %get-tuple-element.649.refs_3_, ...), custom_call_target="tpu_custom_call" | custom-call | flops 199999995904 | bytes 1 | tf_op jit(solution)/shard_map/pallas_call | solution.py:122
  191.3 4.2 collective-permute-done.61.refs_0_
  195.6 22.7 %shard_map.272 = (bf16[3,384,640]{2,1,0:T(8,128)(2,1)}, bf16[3,3,384,640]{3,2,1,0:T(8,128)(2,1)}) custom-call(s32[2]{0:T(128)S(1)} %copy-done.34, bf16[512,1536]{1,0:T(8,128)(2,1)} %get-tuple-element.647.refs_1_, bf16[256,1536]{1,0:T(8,128)(2,1)} %get-tuple-element.648.refs_2_, bf16[256,1536]{1,0:T(8,128)(2,1)} %get-tuple-element.649.refs_3_, ...), custom_call_target="tpu_custom_call" | custom-call | flops 199999995904 | bytes 1 | tf_op jit(solution)/shard_map/pallas_call | solution.py:122
  221.8 14.4 %shard_map.274.refs_15_.refs_6_ = bf16[2048,1536]{1,0:T(8,128)(2,1)} custom-call(s32[2]{0:T(128)S(1)} %copy-done.34, bf16[2048,1280]{1,0:T(8,128)(2,1)} %get-tuple-element.658.refs_12_.refs_1_, bf16[3,384,640]{2,1,0:T(8,128)(2,1)} %get-tuple-element.625.refs_1_.refs_11_.refs_2_, bf16[3,384,640]{2,1,0:T(8,128)(2,1)} %collective-permute-done.60.refs_1_.refs_12_.refs_3_, ...), custom_call_target="tpu_custom_call" | custom-call | flops 199999995904 | bytes 1 | tf_op jit(solution)/shard_map/pallas_call | solution.py:122
  236.2 11.3 %collective-permute-done.63.refs_12_.refs_3_.refs_1_ = bf16[3,384,512]{2,1,0:T(8,128)(2,1)} collective-permute-done((bf16[3,384,512]{2,1,0:T(8,128)(2,1)}, bf16[3,384,512]{2,1,0:T(8,128)(2,1)}, u32[]{:S(2)}, u32[]{:S(2)}) %collective-permute-start.63) | collective-permute-done | bytes 1179680 | tf_op jit(solution)/shard_map/ppermute | solution.py:49
  247.9 18.5 %shard_map.275 = (bf16[2048,512]{1,0:T(8,128)(2,1)}, bf16[2048,1024]{1,0:T(8,128)(2,1)}) custom-call(s32[2]{0:T(128)S(1)} %copy-done.34, bf16[512,1536]{1,0:T(8,128)(2,1)} %get-tuple-element.647.refs_1_, bf16[256,1536]{1,0:T(8,128)(2,1)} %get-tuple-element.648.refs_2_, bf16[256,1536]{1,0:T(8,128)(2,1)} %get-tuple-element.649.refs_3_, ...), custom_call_target="tpu_custom_call" | custom-call | flops 199999995904 | bytes 1 | tf_op jit(solution)/shard_map/pallas_call | solution.py:122
  266.4 15.4 %shard_map.276 = (bf16[1024,1536]{1,0:T(8,128)(2,1)}, bf16[1024,1536]{1,0:T(8,128)(2,1)S(1)}) custom-call(s32[2]{0:T(128)S(1)} %copy-done.34, bf16[2048,1024]{1,0:T(8,128)(2,1)} %get-tuple-element.660.refs_1_, bf16[3,384,512]{2,1,0:T(8,128)(2,1)} %shard_map.269.refs_11_.refs_2_, bf16[3,384,512]{2,1,0:T(8,128)(2,1)} %collective-permute-done.63.refs_12_.refs_3_.refs_1_, ...), custom_call_target="tpu_custom_call" | custom-call | flops 199999995904 | bytes 1 | tf_op jit(solution)/shard_map/pallas_call | solution.py:122
  284.9 33.5 %conditional.16 = (bf16[128,1536]{1,0:T(8,128)(2,1)}, bf16[128,1536]{1,0:T(8,128)(2,1)}, f32[256,1536]{1,0:T(8,128)}, bf16[1024,1536]{1,0:T(8,128)(2,1)}, bf16[1024,1536]{1,0:T(8,128)(2,1)}) conditional(s32[]{:T(128)} %convert_element_type.85, () %tuple.99, (bf16[1024,1536]{1,0:T(8,128)(2,1)S(1)}, bf16[1024,1536]{1,0:T(8,128)(2,1)}, s32[2]{0:T(128)}, ...), branch_computations={%region_12.13_spmd, %region_13.14_spmd} | conditional | flops 599999971328 | bytes 18874588 | solution.py:86
  284.9 5.7 %collective-permute-done.8.refs_1_ = bf16[1024,1536]{1,0:T(8,128)(2,1)S(1)} collective-permute-done((bf16[1024,1536]{1,0:T(8,128)(2,1)S(1)}, bf16[1024,1536]{1,0:T(8,128)(2,1)S(1)}, u32[]{:S(2)}, u32[]{:S(2)}) %collective-permute-start.8) | collective-permute-done | bytes 3145760 | tf_op jit(solution)/shard_map/cond/branch_1_fun/ppermute | solution.py:49
  297.5 14.7 %branch_1_fun.49 = (bf16[1024,1536]{1,0:T(8,128)(2,1)}, bf16[1024,1536]{1,0:T(8,128)(2,1)}) custom-call(s32[2]{0:T(128)S(1)} %copy-done.38, bf16[2048,640]{1,0:T(8,128)(2,1)} %get-tuple-element.389.refs_1_, bf16[2048,512]{1,0:T(8,128)(2,1)} %get-tuple-element.390.refs_2_, bf16[3,384,640]{2,1,0:T(8,128)(2,1)} %get-tuple-element.391.refs_3_, ...), custom_call_target="tpu_custom_call" | custom-call | flops 199999995904 | bytes 1 | tf_op jit(solution)/shard_map/cond/branch_1_fun/pallas_call | solution.py:122
  323.9 37.3 %conditional.17 = (f32[256,1536]{1,0:T(8,128)}, bf16[256,1536]{1,0:T(8,128)(2,1)}, f32[1,1536]{1,0:T(1,128)}, bf16[256,1536]{1,0:T(8,128)(2,1)}, bf16[256,1536]{...) conditional(s32[]{:T(128)} %convert_element_type.85, () %tuple.98, ...), branch_computations={%region_14.15_spmd, %region_15.16_spmd} | conditional | flops 599999971328 | bytes 25178480 | solution.py:86
  325.9 3.8 collective-permute-done.13.refs_1_
  329.8 4.3 branch_1_fun.51
  337.2 4.3 branch_1_fun.52
  341.8 19.4 %branch_1_fun.53 = (bf16[3,384,512]{2,1,0:T(8,128)(2,1)}, bf16[3,3,384,512]{3,2,1,0:T(8,128)(2,1)}) custom-call(s32[2]{0:T(128)S(1)} %copy-done.39, bf16[512,1536]{1,0:T(8,128)(2,1)} %get-tuple-element.417.refs_1_, bf16[256,1536]{1,0:T(8,128)(2,1)} %get-tuple-element.418.refs_2_, bf16[256,1536]{1,0:T(8,128)(2,1)} %get-tuple-element.419.refs_3_, ...), custom_call_target="tpu_custom_call" | custom-call | flops 199999995904 | bytes 1 | tf_op jit(solution)/shard_map/cond/branch_1_fun/pallas_call | solution.py:122
  363.3 3.7 collective-permute-start.67
  368.1 21.1 %conditional.18 = (bf16[256,1536]{1,0:T(8,128)(2,1)}, bf16[1024,640]{1,0:T(8,128)(2,1)}, f32[1,640]{1,0:T(1,128)}, f32[1,1536]{1,0:T(1,128)}, bf16[2,256,1536]{2...) conditional(s32[]{:T(128)} %convert_element_type.85, () %tuple.113, (bf16[256,1536]{1,0:T(8,128)(2,1)}, ...), branch_computations={%region_16.17_spmd, %region_17.18_spmd} | conditional | flops 199999995904 | bytes 5251648 | solution.py:86
  370.8 18.4 %branch_1_fun.55 = (bf16[1024,640]{1,0:T(8,128)(2,1)}, f32[1,640]{1,0:T(1,128)}, f32[1,1536]{1,0:T(1,128)}, bf16[2,256,1536]{2,1,0:T(8,128)(2,1)}, bf16[2,256,1536]{2,1,0:T(8,128)(2,1)}) custom-call(s32[2]{0:T(128)S(1)} %get-tuple-element.434.refs_0_, bf16[256,1536]{1,0:T(8,128)(2,1)} %get-tuple-element.435.refs_1_, ...), custom_call_target="tpu_custom_call" | custom-call | flops 199999995904 | bytes 1 | tf_op jit(solution)/shard_map/cond/branch_1_fun/pallas_call | solution.py:122
  389.2 4.5 collective-permute-done.67.refs_0_
  398.8 25.9 %conditional.19 = (bf16[4,192,1024]{2,1,0:T(8,128)(2,1)}, bf16[192,1024]{1,0:T(8,128)(2,1)}, bf16[192,1024]{1,0:T(8,128)(2,1)}, bf16[192,1024]{1,0:T(8,128)(2,1)...) conditional(s32[]{:T(128)} %convert_element_type.85, () %tuple.112, ...), branch_computations={%region_18.19_spmd, %region_19.20_spmd} | conditional | flops 600000167936 | bytes 9330941 | solution.py:86
  401.8 9.7 %branch_1_fun.56 = (bf16[4,192,1024]{2,1,0:T(8,128)(2,1)}, bf16[192,1024]{1,0:T(8,128)(2,1)}, bf16[192,1024]{1,0:T(8,128)(2,1)}, bf16[192,1024]{1,0:T(8,128)(2,1)}, bf16[192,1024]{1,0:T(8,128)(2,1)}) custom-call(s32[2]{0:T(128)S(1)} %get-tuple-element.464.refs_0_, bf16[256,1536]{1,0:T(8,128)(2,1)} %get-tuple-element.465.refs_1_, ...), custom_call_target="tpu_custom_call" | custom-call | flops 199999995904 | bytes 1 | tf_op jit(solution)/shard_map/cond/branch_1_fun/pallas_call | solution.py:122
  414.5 3.6 branch_1_fun.57
  418.1 3.8 branch_1_fun.58
  428.5 39.4 %conditional.20 = (bf16[192,1024]{1,0:T(8,128)(2,1)S(1)}, bf16[256,1536]{1,0:T(8,128)(2,1)}, f32[5120]{0:T(1024)S(1)}) conditional(s32[]{:T(128)} %convert_element_type.85, () %tuple.116, (bf16[192,1024]{1,0:T(8,128)(2,1)}, bf16[4,192,1024]{2,1,0:T(8,128)(2,1)}, bf16[192,1024]{1,0:T(8,128)(2,1)}, bf16[256,1536]{1,0:T(8,128)(2,1)}, ...), branch_computations={%region_20.21_spmd, %region_21.22_spmd} | conditional | flops 3554308 | bytes 20918756 | solution.py:86
  430.1 7.9 %collective-permute-done.29.refs_1_ = bf16[192,1024]{1,0:T(8,128)(2,1)S(1)} collective-permute-done((bf16[192,1024]{1,0:T(8,128)(2,1)}, bf16[192,1024]{1,0:T(8,128)(2,1)S(1)}, u32[]{:S(2)}, u32[]{:S(2)}) %collective-permute-start.29) | collective-permute-done | bytes 393248 | tf_op jit(solution)/shard_map/cond/branch_1_fun/ppermute | solution.py:49
  455.5 5.7 %collective-permute-done.36 = f32[40,128]{1,0:T(8,128)S(1)} collective-permute-done((f32[40,128]{1,0:T(8,128)}, f32[40,128]{1,0:T(8,128)S(1)}, u32[]{:S(2)}, u32[]{:S(2)}) %collective-permute-start.36) | collective-permute-done | bytes 20512 | tf_op jit(solution)/shard_map/cond/branch_1_fun/ppermute | solution.py:49
  469.3 29.8 %conditional.21 = (f32[256,1536]{1,0:T(8,128)}, f32[2,48,2,128]{3,2,1,0:T(2,128)}, bf16[256,1536]{1,0:T(8,128)(2,1)}, bf16[3,384,640]{2,1,0:T(8,128)(2,1)}, bf16[3,192,640]{2,1,0:T(8,128)(2,1)}) conditional(s32[]{:T(128)} %convert_element_type.85, () %tuple.97, (f32[1536]{0:T(1024)}, bf16[256,1536]{1,0:T(8,128)(2,1)}, f32[256,1536]{1,0:T(8,128)}, ...), branch_computations={%region_22.23_spmd, %region_23.24_spmd} | conditional | flops 200000880640 | bytes 25424488 | solution.py:86
  474.0 4.8 collective-permute-done.40.refs_2_.refs_1_
  480.7 4.3 collective-permute-start.41
  485.0 3.9 branch_1_fun.65
  489.0 6.4 %collective-permute-done.39 = bf16[48,256]{1,0:T(8,128)(2,1)S(1)} collective-permute-done((bf16[48,256]{1,0:T(8,128)(2,1)S(1)}, bf16[48,256]{1,0:T(8,128)(2,1)S(1)}, u32[]{:S(2)}, u32[]{:S(2)}) %collective-permute-start.39) | collective-permute-done | bytes 24608 | tf_op jit(solution)/shard_map/cond/branch_1_fun/ppermute | solution.py:49
  507.5 10.8 %collective-permute-done.72.refs_4_ = bf16[3,192,512]{2,1,0:T(8,128)(2,1)S(1)} collective-permute-done((bf16[3,192,512]{2,1,0:T(8,128)(2,1)S(1)}, bf16[3,192,512]{2,1,0:T(8,128)(2,1)S(1)}, u32[]{:S(2)}, u32[]{:S(2)}) %collective-permute-start.72) | collective-permute-done | bytes 589856 | tf_op jit(solution)/shard_map/ppermute | solution.py:49
  518.4 3.7 shard_map.294
  (321 shorter events, 178.7 us)
Async XLA Ops:
  10.9 13.4 %collective-permute-start.46 = (bf16[192,1024]{1,0:T(8,128)(2,1)}, bf16[192,1024]{1,0:T(8,128)(2,1)}, u32[]{:S(2)}, u32[]{:S(2)}) collective-permute-start(bf16[192,1024]{1,0:T(8,128)(2,1)} %get-tuple-element.322.refs_4_), channel_id=1, source_target_pairs={{0,8},{4,12},{8,16},{12,20},{16,24},{20,28},{24,0},{28,4},{1,9},{5... | collective-permute-start | bytes 1179656 | tf_op jit(solution)/shard_map/cond/branch_1_fun/ppermute | solution.py:49
  12.6 12.4 %collective-permute-start.49 = (bf16[192,1024]{1,0:T(8,128)(2,1)}, bf16[192,1024]{1,0:T(8,128)(2,1)S(1)}, u32[]{:S(2)}, u32[]{:S(2)}) collective-permute-start(bf16[192,1024]{1,0:T(8,128)(2,1)} %get-tuple-element.322.refs_4_), channel_id=1, source_target_pairs={{0,4},{4,0},{8,12},{12,8},{16,20},{20,16},{24,28},{28,24},{1,5},{5... | collective-permute-start | bytes 1179656 | tf_op jit(solution)/shard_map/cond/branch_1_fun/ppermute | solution.py:49
  18.9 28.0 %collective-permute-start.44 = (bf16[256,1536]{1,0:T(8,128)(2,1)}, bf16[256,1536]{1,0:T(8,128)(2,1)}, u32[]{:S(2)}, u32[]{:S(2)}) collective-permute-start(bf16[256,1536]{1,0:T(8,128)(2,1)} %branch_1_fun.38), channel_id=1, source_target_pairs={{0,2},{1,3},{2,0},{3,1},{4,6},{5,7},{6,4},{7,5},{8,10},{9,11},{10,... | collective-permute-start | bytes 2359304 | tf_op jit(solution)/shard_map/cond/branch_1_fun/ppermute | solution.py:49
  20.0 36.8 %collective-permute-start.43 = (bf16[256,1536]{1,0:T(8,128)(2,1)}, bf16[256,1536]{1,0:T(8,128)(2,1)}, u32[]{:S(2)}, u32[]{:S(2)}) collective-permute-start(bf16[256,1536]{1,0:T(8,128)(2,1)} %branch_1_fun.38), channel_id=1, source_target_pairs={{0,1},{1,0},{2,3},{3,2},{4,5},{5,4},{6,7},{7,6},{8,9},{9,8},{10,11... | collective-permute-start | bytes 2359304 | tf_op jit(solution)/shard_map/cond/branch_1_fun/ppermute | solution.py:49
  24.3 12.5 %collective-permute-start.47 = (bf16[192,1024]{1,0:T(8,128)(2,1)}, bf16[192,1024]{1,0:T(8,128)(2,1)}, u32[]{:S(2)}, u32[]{:S(2)}) collective-permute-start(bf16[192,1024]{1,0:T(8,128)(2,1)} %collective-permute-done.46), channel_id=1, source_target_pairs={{0,8},{4,12},{8,16},{12,20},{16,24},{20,28},{24,0},{28,4},{1,9},{5... | collective-permute-start | bytes 1179656 | tf_op jit(solution)/shard_map/cond/branch_1_fun/ppermute | solution.py:49
  24.9 18.7 %collective-permute-start.52 = (bf16[3,192,640]{2,1,0:T(8,128)(2,1)}, bf16[3,192,640]{2,1,0:T(8,128)(2,1)S(1)}, u32[]{:S(2)}, u32[]{:S(2)}) collective-permute-start(bf16[3,192,640]{2,1,0:T(8,128)(2,1)} %branch_1_fun.39), channel_id=1, source_target_pairs={{0,4},{4,0},{8,12},{12,8},{16,20},{20,16},{24,28},{28,24},{1,5},{5... | collective-permute-start | bytes 2211848 | tf_op jit(solution)/shard_map/cond/branch_1_fun/ppermute | solution.py:49
  36.8 18.1 %collective-permute-start.53 = (bf16[256,1536]{1,0:T(8,128)(2,1)}, bf16[256,1536]{1,0:T(8,128)(2,1)S(1)}, u32[]{:S(2)}, u32[]{:S(2)}) collective-permute-start(bf16[256,1536]{1,0:T(8,128)(2,1)} %branch_1_fun.40), channel_id=1, source_target_pairs={{0,2},{1,3},{2,0},{3,1},{4,6},{5,7},{6,4},{7,5},{8,10},{9,11},{10,... | collective-permute-start | bytes 2359304 | tf_op jit(solution)/shard_map/cond/branch_1_fun/ppermute | solution.py:49
  41.2 15.5 %collective-permute-start.50 = (bf16[192,1024]{1,0:T(8,128)(2,1)}, bf16[192,1024]{1,0:T(8,128)(2,1)}, u32[]{:S(2)}, u32[]{:S(2)}) collective-permute-start(bf16[192,1024]{1,0:T(8,128)(2,1)} %collective-permute-done.46), channel_id=1, source_target_pairs={{0,4},{4,0},{8,12},{12,8},{16,20},{20,16},{24,28},{28,24},{1,5},{5... | collective-permute-start | bytes 1179656 | tf_op jit(solution)/shard_map/cond/branch_1_fun/ppermute | solution.py:49
  43.6 13.1 %collective-permute-start.48 = (bf16[192,1024]{1,0:T(8,128)(2,1)}, bf16[192,1024]{1,0:T(8,128)(2,1)}, u32[]{:S(2)}, u32[]{:S(2)}) collective-permute-start(bf16[192,1024]{1,0:T(8,128)(2,1)} %collective-permute-done.47.refs_1_), channel_id=1, source_target_pairs={{0,8},{4,12},{8,16},{12,20},{16,24},{20,28},{24,0},{28,4},{1,9},{5... | collective-permute-start | bytes 1179656 | tf_op jit(solution)/shard_map/cond/branch_1_fun/ppermute | solution.py:49
  46.9 13.1 %collective-permute-start.51 = (bf16[192,1024]{1,0:T(8,128)(2,1)}, bf16[192,1024]{1,0:T(8,128)(2,1)}, u32[]{:S(2)}, u32[]{:S(2)}) collective-permute-start(bf16[192,1024]{1,0:T(8,128)(2,1)} %collective-permute-done.47.refs_1_), channel_id=1, source_target_pairs={{0,4},{4,0},{8,12},{12,8},{16,20},{20,16},{24,28},{28,24},{1,5},{5... | collective-permute-start | bytes 1179656 | tf_op jit(solution)/shard_map/cond/branch_1_fun/ppermute | solution.py:49
  61.5 34.5 %collective-permute-start.57 = (bf16[3,384,640]{2,1,0:T(8,128)(2,1)}, bf16[3,384,640]{2,1,0:T(8,128)(2,1)}, u32[]{:S(2)}, u32[]{:S(2)}) collective-permute-start(bf16[3,384,640]{2,1,0:T(8,128)(2,1)} %get-tuple-element.625.refs_1_.refs_11_.refs_2_), channel_id=1, source_target_pairs={{0,8},{4,12},{8,16},{12,20},{16,24},{20,28},{24,0},{28,4},{1,9},{5... | collective-permute-start | bytes 4423688 | tf_op jit(solution)/shard_map/ppermute | solution.py:49
  69.2 27.1 %collective-permute-start.56 = (bf16[64,1536]{1,0:T(8,128)(2,1)}, bf16[64,1536]{1,0:T(8,128)(2,1)}, u32[]{:S(2)}, u32[]{:S(2)}) collective-permute-start(bf16[64,1536]{1,0:T(8,128)(2,1)} %shard_map.263), channel_id=1, source_target_pairs={{0,4},{4,0},{8,12},{12,8},{16,20},{20,16},{24,28},{28,24},{1,5},{5... | collective-permute-start | bytes 589832 | tf_op jit(solution)/shard_map/ppermute | solution.py:49
  70.7 25.7 %collective-permute-start.58 = (bf16[3,192,512]{2,1,0:T(8,128)(2,1)}, bf16[3,192,512]{2,1,0:T(8,128)(2,1)}, u32[]{:S(2)}, u32[]{:S(2)}) collective-permute-start(bf16[3,192,512]{2,1,0:T(8,128)(2,1)} %shard_map.265), channel_id=1, source_target_pairs={{0,4},{4,0},{8,12},{12,8},{16,20},{20,16},{24,28},{28,24},{1,5},{5... | collective-permute-start | bytes 1769480 | tf_op jit(solution)/shard_map/ppermute | solution.py:49
  93.9 42.3 %collective-permute-start.55 = (bf16[384,1536]{1,0:T(8,128)(2,1)}, bf16[384,1536]{1,0:T(8,128)(2,1)}, u32[]{:S(2)}, u32[]{:S(2)}) collective-permute-start(bf16[384,1536]{1,0:T(8,128)(2,1)} %shard_map.262), channel_id=1, source_target_pairs={{0,4},{4,0},{8,12},{12,8},{16,20},{20,16},{24,28},{28,24},{1,5},{5... | collective-permute-start | bytes 3538952 | tf_op jit(solution)/shard_map/ppermute | solution.py:49
  95.9 38.7 %collective-permute-start.59 = (bf16[3,384,640]{2,1,0:T(8,128)(2,1)}, bf16[3,384,640]{2,1,0:T(8,128)(2,1)}, u32[]{:S(2)}, u32[]{:S(2)}) collective-permute-start(bf16[3,384,640]{2,1,0:T(8,128)(2,1)} %shard_map.264.refs_1_.refs_14_.refs_5_), channel_id=1, source_target_pairs={{0,8},{4,12},{8,16},{12,20},{16,24},{20,28},{24,0},{28,4},{1,9},{5... | collective-permute-start | bytes 4423688 | tf_op jit(solution)/shard_map/ppermute | solution.py:49
  97.5 19.2 %collective-permute-start.20 = (bf16[256,1536]{1,0:T(8,128)(2,1)}, bf16[256,1536]{1,0:T(8,128)(2,1)S(1)}, u32[]{:S(2)}, u32[]{:S(2)}) collective-permute-start(bf16[256,1536]{1,0:T(8,128)(2,1)} %get-tuple-element.365), channel_id=1, source_target_pairs={{0,2},{1,3},{2,0},{3,1},{4,6},{5,7},{6,4},{7,5},{8,10},{9,11},{10,... | collective-permute-start | bytes 2359304 | tf_op jit(solution)/shard_map/cond/branch_1_fun/ppermute | solution.py:49
  120.8 11.6 %collective-permute-start.22 = (bf16[128,1536]{1,0:T(8,128)(2,1)S(1)}, bf16[128,1536]{1,0:T(8,128)(2,1)S(1)}, u32[]{:S(2)}, u32[]{:S(2)}) collective-permute-start(bf16[128,1536]{1,0:T(8,128)(2,1)S(1)} %get-tuple-element.369.refs_2_), channel_id=1, source_target_pairs={{0,2},{1,3},{2,0},{3,1},{4,6},{5,7},{6,4},{7,5},{8,10},{9,11},{10,... | collective-permute-start | bytes 1179656 | tf_op jit(solution)/shard_map/cond/branch_1_fun/ppermute | solution.py:49
  134.7 33.8 %collective-permute-start.60 = (bf16[3,384,640]{2,1,0:T(8,128)(2,1)}, bf16[3,384,640]{2,1,0:T(8,128)(2,1)}, u32[]{:S(2)}, u32[]{:S(2)}) collective-permute-start(bf16[3,384,640]{2,1,0:T(8,128)(2,1)} %shard_map.267.refs_2_.refs_13_.refs_4_), channel_id=1, source_target_pairs={{0,8},{4,12},{8,16},{12,20},{16,24},{20,28},{24,0},{28,4},{1,9},{5... | collective-permute-start | bytes 4423688 | tf_op jit(solution)/shard_map/ppermute | solution.py:49
  138.9 23.8 %collective-permute-start.2 = (bf16[512,1536]{1,0:T(8,128)(2,1)}, bf16[512,1536]{1,0:T(8,128)(2,1)}, u32[]{:S(2)}, u32[]{:S(2)}) collective-permute-start(bf16[512,1536]{1,0:T(8,128)(2,1)} %branch_1_fun.47), channel_id=1, source_target_pairs={{0,1},{1,0},{2,3},{3,2},{4,5},{5,4},{6,7},{7,6},{8,9},{9,8},{10,11... | collective-permute-start | bytes 4718600 | tf_op jit(solution)/shard_map/cond/branch_1_fun/ppermute | solution.py:49
  138.9 20.3 %collective-permute-start.3 = (bf16[256,1536]{1,0:T(8,128)(2,1)}, bf16[256,1536]{1,0:T(8,128)(2,1)}, u32[]{:S(2)}, u32[]{:S(2)}) collective-permute-start(bf16[256,1536]{1,0:T(8,128)(2,1)} %get-tuple-element.381), channel_id=1, source_target_pairs={{0,2},{1,3},{2,0},{3,1},{4,6},{5,7},{6,4},{7,5},{8,10},{9,11},{10,... | collective-permute-start | bytes 2359304 | tf_op jit(solution)/shard_map/cond/branch_1_fun/ppermute | solution.py:49
  140.0 20.0 %collective-permute-start.4 = (bf16[256,1536]{1,0:T(8,128)(2,1)}, bf16[256,1536]{1,0:T(8,128)(2,1)}, u32[]{:S(2)}, u32[]{:S(2)}) collective-permute-start(bf16[256,1536]{1,0:T(8,128)(2,1)} %get-tuple-element.382), channel_id=1, source_target_pairs={{0,4},{4,0},{8,12},{12,8},{16,20},{20,16},{24,28},{28,24},{1,5},{5... | collective-permute-start | bytes 2359304 | tf_op jit(solution)/shard_map/cond/branch_1_fun/ppermute | solution.py:49
  141.4 21.5 %collective-permute-start.5 = (bf16[512,1536]{1,0:T(8,128)(2,1)}, bf16[512,1536]{1,0:T(8,128)(2,1)}, u32[]{:S(2)}, u32[]{:S(2)}) collective-permute-start(bf16[512,1536]{1,0:T(8,128)(2,1)} %get-tuple-element.824), channel_id=1, source_target_pairs={{0,1},{1,0},{2,3},{3,2},{4,5},{5,4},{6,7},{7,6},{8,9},{9,8},{10,11... | collective-permute-start | bytes 4718600 | tf_op jit(solution)/shard_map/cond/branch_1_fun/ppermute | solution.py:49
  168.4 27.0 %collective-permute-start.61 = (bf16[3,384,512]{2,1,0:T(8,128)(2,1)}, bf16[3,384,512]{2,1,0:T(8,128)(2,1)}, u32[]{:S(2)}, u32[]{:S(2)}) collective-permute-start(bf16[3,384,512]{2,1,0:T(8,128)(2,1)} %shard_map.269.refs_11_.refs_2_), channel_id=1, source_target_pairs={{0,8},{4,12},{8,16},{12,20},{16,24},{20,28},{24,0},{28,4},{1,9},{5... | collective-permute-start | bytes 3538952 | tf_op jit(solution)/shard_map/ppermute | solution.py:49
  195.5 26.1 %collective-permute-start.62 = (bf16[3,384,512]{2,1,0:T(8,128)(2,1)}, bf16[3,384,512]{2,1,0:T(8,128)(2,1)}, u32[]{:S(2)}, u32[]{:S(2)}) collective-permute-start(bf16[3,384,512]{2,1,0:T(8,128)(2,1)} %shard_map.271.refs_14_.refs_5_), channel_id=1, source_target_pairs={{0,8},{4,12},{8,16},{12,20},{16,24},{20,28},{24,0},{28,4},{1,9},{5... | collective-permute-start | bytes 3538952 | tf_op jit(solution)/shard_map/ppermute | solution.py:49
  221.6 25.9 %collective-permute-start.63 = (bf16[3,384,512]{2,1,0:T(8,128)(2,1)}, bf16[3,384,512]{2,1,0:T(8,128)(2,1)}, u32[]{:S(2)}, u32[]{:S(2)}) collective-permute-start(bf16[3,384,512]{2,1,0:T(8,128)(2,1)} %shard_map.273.refs_13_.refs_4_), channel_id=1, source_target_pairs={{0,8},{4,12},{8,16},{12,20},{16,24},{20,28},{24,0},{28,4},{1,9},{5... | collective-permute-start | bytes 3538952 | tf_op jit(solution)/shard_map/ppermute | solution.py:49
  247.5 34.3 %collective-permute-start.64 = (bf16[3,384,640]{2,1,0:T(8,128)(2,1)}, bf16[3,384,640]{2,1,0:T(8,128)(2,1)}, u32[]{:S(2)}, u32[]{:S(2)}) collective-permute-start(bf16[3,384,640]{2,1,0:T(8,128)(2,1)} %shard_map.277), channel_id=1, source_target_pairs={{0,8},{4,12},{8,16},{12,20},{16,24},{20,28},{24,0},{28,4},{1,9},{5... | collective-permute-start | bytes 4423688 | tf_op jit(solution)/shard_map/ppermute | solution.py:49
  284.9 33.5 %collective-permute-start.65 = (bf16[3,384,640]{2,1,0:T(8,128)(2,1)}, bf16[3,384,640]{2,1,0:T(8,128)(2,1)}, u32[]{:S(2)}, u32[]{:S(2)}) collective-permute-start(bf16[3,384,640]{2,1,0:T(8,128)(2,1)} %bitcast_add_fusion.3.refs_1_), channel_id=1, source_target_pairs={{0,8},{4,12},{8,16},{12,20},{16,24},{20,28},{24,0},{28,4},{1,9},{5... | collective-permute-start | bytes 4423688 | tf_op jit(solution)/shard_map/ppermute | solution.py:49
  293.9 20.0 %collective-permute-start.9 = (bf16[256,1536]{1,0:T(8,128)(2,1)}, bf16[256,1536]{1,0:T(8,128)(2,1)}, u32[]{:S(2)}, u32[]{:S(2)}) collective-permute-start(bf16[256,1536]{1,0:T(8,128)(2,1)} %get-tuple-element.386.refs_11_), channel_id=1, source_target_pairs={{0,2},{1,3},{2,0},{3,1},{4,6},{5,7},{6,4},{7,5},{8,10},{9,11},{10,... | collective-permute-start | bytes 2359304 | tf_op jit(solution)/shard_map/cond/branch_1_fun/ppermute | solution.py:49
  295.8 19.6 %collective-permute-start.10 = (bf16[256,1536]{1,0:T(8,128)(2,1)}, bf16[256,1536]{1,0:T(8,128)(2,1)}, u32[]{:S(2)}, u32[]{:S(2)}) collective-permute-start(bf16[256,1536]{1,0:T(8,128)(2,1)} %get-tuple-element.387), channel_id=1, source_target_pairs={{0,4},{4,0},{8,12},{12,8},{16,20},{20,16},{24,28},{28,24},{1,5},{5... | collective-permute-start | bytes 2359304 | tf_op jit(solution)/shard_map/cond/branch_1_fun/ppermute | solution.py:49
  321.4 45.6 %collective-permute-start.66 = (bf16[3,384,640]{2,1,0:T(8,128)(2,1)}, bf16[3,384,640]{2,1,0:T(8,128)(2,1)}, u32[]{:S(2)}, u32[]{:S(2)}) collective-permute-start(bf16[3,384,640]{2,1,0:T(8,128)(2,1)} %bitcast_add_fusion.2.refs_1_), channel_id=1, source_target_pairs={{0,8},{4,12},{8,16},{12,20},{16,24},{20,28},{24,0},{28,4},{1,9},{5... | collective-permute-start | bytes 4423688 | tf_op jit(solution)/shard_map/ppermute | solution.py:49
  323.9 11.8 %collective-permute-start.11 = (bf16[128,1536]{1,0:T(8,128)(2,1)}, bf16[128,1536]{1,0:T(8,128)(2,1)}, u32[]{:S(2)}, u32[]{:S(2)}) collective-permute-start(bf16[128,1536]{1,0:T(8,128)(2,1)} %get-tuple-element.408), channel_id=1, source_target_pairs={{0,4},{4,0},{8,12},{12,8},{16,20},{20,16},{24,28},{28,24},{1,5},{5... | collective-permute-start | bytes 1179656 | tf_op jit(solution)/shard_map/cond/branch_1_fun/ppermute | solution.py:49
  325.7 11.6 %collective-permute-start.12 = (bf16[128,1536]{1,0:T(8,128)(2,1)}, bf16[128,1536]{1,0:T(8,128)(2,1)}, u32[]{:S(2)}, u32[]{:S(2)}) collective-permute-start(bf16[128,1536]{1,0:T(8,128)(2,1)} %get-tuple-element.409), channel_id=1, source_target_pairs={{0,2},{1,3},{2,0},{3,1},{4,6},{5,7},{6,4},{7,5},{8,10},{9,11},{10,... | collective-permute-start | bytes 1179656 | tf_op jit(solution)/shard_map/cond/branch_1_fun/ppermute | solution.py:49
  341.5 19.7 %collective-permute-start.14 = (bf16[256,1536]{1,0:T(8,128)(2,1)}, bf16[256,1536]{1,0:T(8,128)(2,1)}, u32[]{:S(2)}, u32[]{:S(2)}) collective-permute-start(bf16[256,1536]{1,0:T(8,128)(2,1)} %get-tuple-element.851.refs_13_), channel_id=1, source_target_pairs={{0,2},{1,3},{2,0},{3,1},{4,6},{5,7},{6,4},{7,5},{8,10},{9,11},{10,... | collective-permute-start | bytes 2359304 | tf_op jit(solution)/shard_map/cond/branch_1_fun/ppermute | solution.py:49
  341.8 19.4 %collective-permute-start.15 = (bf16[256,1536]{1,0:T(8,128)(2,1)}, bf16[256,1536]{1,0:T(8,128)(2,1)}, u32[]{:S(2)}, u32[]{:S(2)}) collective-permute-start(bf16[256,1536]{1,0:T(8,128)(2,1)} %get-tuple-element.851.refs_13_), channel_id=1, source_target_pairs={{0,1},{1,0},{2,3},{3,2},{4,5},{5,4},{6,7},{7,6},{8,9},{9,8},{10,11... | collective-permute-start | bytes 2359304 | tf_op jit(solution)/shard_map/cond/branch_1_fun/ppermute | solution.py:49
  361.2 36.9 %collective-permute-start.69 = (bf16[256,1536]{1,0:T(8,128)(2,1)}, bf16[256,1536]{1,0:T(8,128)(2,1)}, u32[]{:S(2)}, u32[]{:S(2)}) collective-permute-start(bf16[256,1536]{1,0:T(8,128)(2,1)} %get-tuple-element.689), channel_id=1, source_target_pairs={{0,4},{4,0},{8,12},{12,8},{16,20},{20,16},{24,28},{28,24},{1,5},{5... | collective-permute-start | bytes 2359304 | tf_op jit(solution)/shard_map/ppermute | solution.py:49
  362.0 36.2 %collective-permute-start.68 = (bf16[256,1536]{1,0:T(8,128)(2,1)}, bf16[256,1536]{1,0:T(8,128)(2,1)}, u32[]{:S(2)}, u32[]{:S(2)}) collective-permute-start(bf16[256,1536]{1,0:T(8,128)(2,1)} %get-tuple-element.688), channel_id=1, source_target_pairs={{0,2},{1,3},{2,0},{3,1},{4,6},{5,7},{6,4},{7,5},{8,10},{9,11},{10,... | collective-permute-start | bytes 2359304 | tf_op jit(solution)/shard_map/ppermute | solution.py:49
  363.3 30.4 %collective-permute-start.67 = (bf16[3,384,512]{2,1,0:T(8,128)(2,1)}, bf16[3,384,512]{2,1,0:T(8,128)(2,1)}, u32[]{:S(2)}, u32[]{:S(2)}) collective-permute-start(bf16[3,384,512]{2,1,0:T(8,128)(2,1)} %shard_map.283), channel_id=1, source_target_pairs={{0,8},{4,12},{8,16},{12,20},{16,24},{20,28},{24,0},{28,4},{1,9},{5... | collective-permute-start | bytes 3538952 | tf_op jit(solution)/shard_map/ppermute | solution.py:49
  396.5 29.3 %collective-permute-start.70 = (bf16[3,384,512]{2,1,0:T(8,128)(2,1)}, bf16[3,384,512]{2,1,0:T(8,128)(2,1)}, u32[]{:S(2)}, u32[]{:S(2)}) collective-permute-start(bf16[3,384,512]{2,1,0:T(8,128)(2,1)} %bitcast_add_fusion.6.refs_1_), channel_id=1, source_target_pairs={{0,8},{4,12},{8,16},{12,20},{16,24},{20,28},{24,0},{28,4},{1,9},{5... | collective-permute-start | bytes 3538952 | tf_op jit(solution)/shard_map/ppermute | solution.py:49
  399.6 14.9 %collective-permute-start.25 = (bf16[2,256,1536]{2,1,0:T(8,128)(2,1)}, bf16[2,256,1536]{2,1,0:T(8,128)(2,1)}, u32[]{:S(2)}, u32[]{:S(2)}) collective-permute-start(bf16[2,256,1536]{2,1,0:T(8,128)(2,1)} %get-tuple-element.475.refs_11_), channel_id=1, source_target_pairs={{0,1},{1,0},{2,3},{3,2},{4,5},{5,4},{6,7},{7,6},{8,9},{9,8},{10,11... | collective-permute-start | bytes 4718600 | tf_op jit(solution)/shard_map/cond/branch_1_fun/ppermute | solution.py:49
  401.4 11.7 %collective-permute-start.27 = (f32[40,128]{1,0:T(8,128)}, f32[40,128]{1,0:T(8,128)}, u32[]{:S(2)}, u32[]{:S(2)}) collective-permute-start(f32[40,128]{1,0:T(8,128)} %add.92), channel_id=1, source_target_pairs={{0,2},{1,3},{2,0},{3,1},{4,6},{5,7},{6,4},{7,5},{8,10},{9,11},{10,... | collective-permute-start | bytes 61448 | tf_op jit(solution)/shard_map/cond/branch_1_fun/ppermute | solution.py:49
  411.5 11.3 %collective-permute-start.24 = (bf16[192,1024]{1,0:T(8,128)(2,1)}, bf16[192,1024]{1,0:T(8,128)(2,1)}, u32[]{:S(2)}, u32[]{:S(2)}) collective-permute-start(bf16[192,1024]{1,0:T(8,128)(2,1)} %get-tuple-element.480), channel_id=1, source_target_pairs={{0,4},{4,0},{8,12},{12,8},{16,20},{20,16},{24,28},{28,24},{1,5},{5... | collective-permute-start | bytes 1179656 | tf_op jit(solution)/shard_map/cond/branch_1_fun/ppermute | solution.py:49
  442.4 25.5 %collective-permute-start.35 = (bf16[256,1536]{1,0:T(8,128)(2,1)}, bf16[256,1536]{1,0:T(8,128)(2,1)}, u32[]{:S(2)}, u32[]{:S(2)}) collective-permute-start(bf16[256,1536]{1,0:T(8,128)(2,1)} %get-tuple-element.496.refs_1_), channel_id=1, source_target_pairs={{0,2},{1,3},{2,0},{3,1},{4,6},{5,7},{6,4},{7,5},{8,10},{9,11},{10,... | collective-permute-start | bytes 2359304 | tf_op jit(solution)/shard_map/cond/branch_1_fun/ppermute | solution.py:49
  453.5 13.2 %collective-permute-start.32 = (bf16[192,1024]{1,0:T(8,128)(2,1)S(1)}, bf16[192,1024]{1,0:T(8,128)(2,1)S(1)}, u32[]{:S(2)}, u32[]{:S(2)}) collective-permute-start(bf16[192,1024]{1,0:T(8,128)(2,1)S(1)} %fusion.3), channel_id=1, source_target_pairs={{0,8},{4,12},{8,16},{12,20},{16,24},{20,28},{24,0},{28,4},{1,9},{5... | collective-permute-start | bytes 1179656 | tf_op jit(solution)/shard_map/cond/branch_1_fun/ppermute | solution.py:49
  454.9 11.8 %collective-permute-start.34 = (bf16[192,1024]{1,0:T(8,128)(2,1)}, bf16[192,1024]{1,0:T(8,128)(2,1)S(1)}, u32[]{:S(2)}, u32[]{:S(2)}) collective-permute-start(bf16[192,1024]{1,0:T(8,128)(2,1)} %branch_1_fun.64), channel_id=1, source_target_pairs={{0,4},{4,0},{8,12},{12,8},{16,20},{20,16},{24,28},{28,24},{1,5},{5... | collective-permute-start | bytes 1179656 | tf_op jit(solution)/shard_map/cond/branch_1_fun/ppermute | solution.py:49
  467.9 32.9 %collective-permute-start.71 = (bf16[3,384,512]{2,1,0:T(8,128)(2,1)}, bf16[3,384,512]{2,1,0:T(8,128)(2,1)}, u32[]{:S(2)}, u32[]{:S(2)}) collective-permute-start(bf16[3,384,512]{2,1,0:T(8,128)(2,1)} %shard_map.290.refs_1_), channel_id=1, source_target_pairs={{0,8},{4,12},{8,16},{12,20},{16,24},{20,28},{24,0},{28,4},{1,9},{5... | collective-permute-start | bytes 3538952 | tf_op jit(solution)/shard_map/ppermute | solution.py:49
  478.8 20.3 %collective-permute-start.42 = (bf16[3,192,640]{2,1,0:T(8,128)(2,1)}, bf16[3,192,640]{2,1,0:T(8,128)(2,1)}, u32[]{:S(2)}, u32[]{:S(2)}) collective-permute-start(bf16[3,192,640]{2,1,0:T(8,128)(2,1)} %branch_1_fun.69), channel_id=1, source_target_pairs={{0,4},{4,0},{8,12},{12,8},{16,20},{20,16},{24,28},{28,24},{1,5},{5... | collective-permute-start | bytes 2211848 | tf_op jit(solution)/shard_map/cond/branch_1_fun/ppermute | solution.py:49
  480.7 15.5 %collective-permute-start.41 = (bf16[128,1536]{1,0:T(8,128)(2,1)}, bf16[128,1536]{1,0:T(8,128)(2,1)S(1)}, u32[]{:S(2)}, u32[]{:S(2)}) collective-permute-start(bf16[128,1536]{1,0:T(8,128)(2,1)} %get-tuple-element.511), channel_id=1, source_target_pairs={{0,2},{1,3},{2,0},{3,1},{4,6},{5,7},{6,4},{7,5},{8,10},{9,11},{10,... | collective-permute-start | bytes 1179656 | tf_op jit(solution)/shard_map/cond/branch_1_fun/ppermute | solution.py:49
  503.2 15.1 %collective-permute-start.72 = (bf16[3,192,512]{2,1,0:T(8,128)(2,1)S(1)}, bf16[3,192,512]{2,1,0:T(8,128)(2,1)S(1)}, u32[]{:S(2)}, u32[]{:S(2)}) collective-permute-start(bf16[3,192,512]{2,1,0:T(8,128)(2,1)S(1)} %shard_map.293), channel_id=1, source_target_pairs={{0,4},{4,0},{8,12},{12,8},{16,20},{20,16},{24,28},{28,24},{1,5},{5... | collective-permute-start | bytes 1769480 | tf_op jit(solution)/shard_map/ppermute | solution.py:49
  (68 other events, 476.2 us)

commit v6 on v5

--- a/solution.py
+++ b/solution.py
@@ -1143,7 +1143,6 @@
             [grad_most, grad_end, grad_last], [[(0, 0, most), 1, (0, most, 2 * most), 2]]
         )
         return [grads, across_core(grads)], [
-            both,
             far_top,
             far_bottom,
             across_core(both),
@@ -1152,6 +1151,7 @@
         ]
 
     (grad_far, other_far), rows_two = stage(spread)
+    rows_two = [both, *rows_two]
     half = both.shape[0] // 2
     places = [(0, 0), (0, half), (1, 0), (2, 0), (3, 0), (3, half), (4, 0), (5, 0)]
     grad_ffn = [grad_near, grad_far, other_near, other_far]

time: 528 us -> 527 us (level)
  transfers between devices with their start and end apart: 73 -> 73, of which waited for: 41 -> 42; matrix products, arithmetic and copies ran while one was open for 7% -> 7% of each run, Pallas kernels for 42% -> 42%
where the time goes in v6:
time: 527 us; the launch traced here: 522 us
  Pallas kernels  223 us (42%)
  waiting for transfers between devices  176 us (33%)
  starting transfers between devices  66.1 us (13%)
  other arithmetic  31 us (6%)
  local copies, waits for them, and re-layouts  24.1 us (5%)
    pallas_call x30, Pallas kernels, call(): pl.pallas_call(body, out_shape=outs, in_specs=list(specs) + [anywhere] *...  223 us
    ppermute x73, waiting for transfers between devices, moved(): return lax.ppermute(block, axis, route)  176 us
    ppermute x73, starting transfers between devices, moved(): return lax.ppermute(block, axis, route)  66.1 us
    add x7, other arithmetic, added(): return came + part  17.3 us
  transfers between devices with their start and end apart: 73, of which 42 were waited for; matrix products, arithmetic and copies ran while one was open for 7% of the time, Pallas kernels for 42%

profile of v6, /device:TPU:0, one launch (start us, length us, event | category | flops | bytes accessed | tf_op | source)
XLA Modules:
  0.0 522.0 jit_solution(17241198042504914051)
XLA Ops:
  0.7 10.1 %conditional.11 = (bf16[192,1024]{1,0:T(8,128)(2,1)}) conditional(s32[]{:T(128)} %convert_element_type.85, () %tuple.103, (bf16[384,192]{0,1:T(8,128)(2,1)}, bf16[48,256]{1,0:T(8,128)(2,1)}, bf16[48,256]{1,0:T(8,128)(2,1)}, s32[2]{0:T(128)S(1)}, bf16[192,384]{1,0:T(8,128)(2,1)}) %tuple.104), branch_computations={%region_0.1_spmd, %region_1.2_spmd} | conditional | flops 199999995904 | bytes 688257 | solution.py:86
  10.9 49.0 %conditional.12 = (bf16[256,1536]{1,0:T(8,128)(2,1)}, bf16[256,1536]{1,0:T(8,128)(2,1)}, bf16[256,1536]{1,0:T(8,128)(2,1)}, bf16[256,1536]{1,0:T(8,128)(2,1)}, b...) conditional(s32[]{:T(128)} %convert_element_type.85, () %tuple.102, ...), branch_computations={%region_2.3_spmd, %region_3.6_spmd} | conditional | flops 200000585728 | bytes 37304132 | solution.py:86
  14.0 3.6 branch_1_fun.37
  27.5 9.4 %collective-permute-done.47.refs_1_ = bf16[192,1024]{1,0:T(8,128)(2,1)} collective-permute-done((bf16[192,1024]{1,0:T(8,128)(2,1)}, bf16[192,1024]{1,0:T(8,128)(2,1)}, u32[]{:S(2)}, u32[]{:S(2)}) %collective-permute-start.47) | collective-permute-done | bytes 393248 | tf_op jit(solution)/shard_map/cond/branch_1_fun/ppermute | solution.py:49
  48.4 6.6 %collective-permute-done.53.refs_1_ = bf16[256,1536]{1,0:T(8,128)(2,1)S(1)} collective-permute-done((bf16[256,1536]{1,0:T(8,128)(2,1)}, bf16[256,1536]{1,0:T(8,128)(2,1)S(1)}, u32[]{:S(2)}, u32[]{:S(2)}) %collective-permute-start.53) | collective-permute-done | bytes 786464 | tf_op jit(solution)/shard_map/cond/branch_1_fun/ppermute | solution.py:49
  63.4 5.8 %collective-permute-done.54.refs_2_.refs_1_ = bf16[192,1024]{1,0:T(8,128)(2,1)S(1)} collective-permute-done((bf16[192,1024]{1,0:T(8,128)(2,1)}, bf16[192,1024]{1,0:T(8,128)(2,1)S(1)}, u32[]{:S(2)}, u32[]{:S(2)}) %collective-permute-start.54) | collective-permute-done | bytes 393248 | tf_op jit(solution)/shard_map/ppermute | solution.py:49
  72.3 21.6 %conditional.13 = (bf16[1024,384]{1,0:T(8,128)(2,1)}, bf16[1024,128]{1,0:T(8,128)(2,1)}, bf16[1024,128]{1,0:T(8,128)(2,1)}, bf16[1024,384]{1,0:T(8,128)(2,1)}, b...) conditional(s32[]{:T(128)} %convert_element_type.85, () %tuple.101, ...), branch_computations={%region_6.7_spmd, %region_7.8_spmd} | conditional | flops 399999991808 | bytes 12596394 | solution.py:86
  72.5 14.2 %branch_1_fun.42 = (bf16[1024,384]{1,0:T(8,128)(2,1)}, bf16[1024,128]{1,0:T(8,128)(2,1)}, bf16[1024,128]{1,0:T(8,128)(2,1)}, bf16[1024,384]{1,0:T(8,128)(2,1)}, ...) custom-call(s32[2]{0:T(128)S(1)} %get-tuple-element.333.refs_0_, ...), custom_call_target="tpu_custom_call" | custom-call | flops 199999995904 | bytes 1 | tf_op jit(solution)/shard_map/cond/branch_1_fun/pallas_call | solution.py:122
  87.3 4.4 collective-permute-done.refs_2_
  97.5 37.1 %conditional.14 = (f32[256,1536]{1,0:T(8,128)}, bf16[256,1536]{1,0:T(8,128)(2,1)}, bf16[256,1536]{1,0:T(8,128)(2,1)}, bf16[512,1536]{1,0:T(8,128)(2,1)}, bf16[3,...) conditional(s32[]{:T(128)} %convert_element_type.85, () %tuple.100, (bf16[256,1536]{1,0:T(8,128)(2,1)}, ...), branch_computations={%region_8.9_spmd, %region_9.10_spmd} | conditional | flops 399999991808 | bytes 11809178 | solution.py:86
  98.9 17.9 %collective-permute-done.20.refs_2_.refs_1_ = bf16[256,1536]{1,0:T(8,128)(2,1)S(1)} collective-permute-done((bf16[256,1536]{1,0:T(8,128)(2,1)}, bf16[256,1536]{1,0:T(8,128)(2,1)S(1)}, u32[]{:S(2)}, u32[]{:S(2)}) %collective-permute-start.20) | collective-permute-done | bytes 786464 | tf_op jit(solution)/shard_map/cond/branch_1_fun/ppermute | solution.py:49
  126.4 4.1 collective-permute-done.21.refs_1_
  136.2 26.7 %conditional.15 = (bf16[512,1536]{1,0:T(8,128)(2,1)}, bf16[512,1536]{1,0:T(8,128)(2,1)}, bf16[256,1536]{1,0:T(8,128)(2,1)}, bf16[256,1536]{1,0:T(8,128)(2,1)}, b...) conditional(s32[]{:T(128)} %convert_element_type.85, () %tuple.108, ...), branch_computations={%region_10.11_spmd, %region_11.12_spmd} | conditional | flops 199999995904 | bytes 25166120 | solution.py:86
  141.4 17.8 %collective-permute-done.3 = bf16[256,1536]{1,0:T(8,128)(2,1)} collective-permute-done((bf16[256,1536]{1,0:T(8,128)(2,1)}, bf16[256,1536]{1,0:T(8,128)(2,1)}, u32[]{:S(2)}, u32[]{:S(2)}) %collective-permute-start.3) | collective-permute-done | bytes 786464 | tf_op jit(solution)/shard_map/cond/branch_1_fun/ppermute | solution.py:49
  162.9 5.5 %collective-permute-done.60.refs_1_.refs_12_.refs_3_ = bf16[3,384,640]{2,1,0:T(8,128)(2,1)} collective-permute-done((bf16[3,384,640]{2,1,0:T(8,128)(2,1)}, bf16[3,384,640]{2,1,0:T(8,128)(2,1)}, u32[]{:S(2)}, u32[]{:S(2)}) %collective-permute-start.60) | collective-permute-done | bytes 1474592 | tf_op jit(solution)/shard_map/ppermute | solution.py:49
  169.1 22.1 %shard_map.270 = (bf16[2048,640]{1,0:T(8,128)(2,1)}, bf16[2048,1280]{1,0:T(8,128)(2,1)}) custom-call(s32[2]{0:T(128)S(1)} %copy-done.34, bf16[512,1536]{1,0:T(8,128)(2,1)} %get-tuple-element.641.refs_1_, bf16[256,1536]{1,0:T(8,128)(2,1)} %get-tuple-element.646.refs_2_, bf16[256,1536]{1,0:T(8,128)(2,1)} %get-tuple-element.647.refs_3_, ...), custom_call_target="tpu_custom_call" | custom-call | flops 199999995904 | bytes 1 | tf_op jit(solution)/shard_map/pallas_call | solution.py:122
  191.2 4.2 collective-permute-done.61.refs_0_
  195.6 22.7 %shard_map.272 = (bf16[3,384,640]{2,1,0:T(8,128)(2,1)}, bf16[3,3,384,640]{3,2,1,0:T(8,128)(2,1)}) custom-call(s32[2]{0:T(128)S(1)} %copy-done.34, bf16[512,1536]{1,0:T(8,128)(2,1)} %get-tuple-element.641.refs_1_, bf16[256,1536]{1,0:T(8,128)(2,1)} %get-tuple-element.646.refs_2_, bf16[256,1536]{1,0:T(8,128)(2,1)} %get-tuple-element.647.refs_3_, ...), custom_call_target="tpu_custom_call" | custom-call | flops 199999995904 | bytes 1 | tf_op jit(solution)/shard_map/pallas_call | solution.py:122
  221.8 14.4 %shard_map.274.refs_15_.refs_6_ = bf16[2048,1536]{1,0:T(8,128)(2,1)} custom-call(s32[2]{0:T(128)S(1)} %copy-done.34, bf16[2048,1280]{1,0:T(8,128)(2,1)} %get-tuple-element.656.refs_12_.refs_1_, bf16[3,384,640]{2,1,0:T(8,128)(2,1)} %get-tuple-element.623.refs_1_.refs_11_.refs_2_, bf16[3,384,640]{2,1,0:T(8,128)(2,1)} %collective-permute-done.60.refs_1_.refs_12_.refs_3_, ...), custom_call_target="tpu_custom_call" | custom-call | flops 199999995904 | bytes 1 | tf_op jit(solution)/shard_map/pallas_call | solution.py:122
  236.2 11.3 %collective-permute-done.63.refs_12_.refs_3_.refs_1_ = bf16[3,384,512]{2,1,0:T(8,128)(2,1)} collective-permute-done((bf16[3,384,512]{2,1,0:T(8,128)(2,1)}, bf16[3,384,512]{2,1,0:T(8,128)(2,1)}, u32[]{:S(2)}, u32[]{:S(2)}) %collective-permute-start.63) | collective-permute-done | bytes 1179680 | tf_op jit(solution)/shard_map/ppermute | solution.py:49
  247.9 18.5 %shard_map.275 = (bf16[2048,512]{1,0:T(8,128)(2,1)}, bf16[2048,1024]{1,0:T(8,128)(2,1)}) custom-call(s32[2]{0:T(128)S(1)} %copy-done.34, bf16[512,1536]{1,0:T(8,128)(2,1)} %get-tuple-element.641.refs_1_, bf16[256,1536]{1,0:T(8,128)(2,1)} %get-tuple-element.646.refs_2_, bf16[256,1536]{1,0:T(8,128)(2,1)} %get-tuple-element.647.refs_3_, ...), custom_call_target="tpu_custom_call" | custom-call | flops 199999995904 | bytes 1 | tf_op jit(solution)/shard_map/pallas_call | solution.py:122
  266.4 15.4 %shard_map.276 = (bf16[1024,1536]{1,0:T(8,128)(2,1)}, bf16[1024,1536]{1,0:T(8,128)(2,1)S(1)}) custom-call(s32[2]{0:T(128)S(1)} %copy-done.34, bf16[2048,1024]{1,0:T(8,128)(2,1)} %get-tuple-element.658.refs_1_, bf16[3,384,512]{2,1,0:T(8,128)(2,1)} %shard_map.269.refs_11_.refs_2_, bf16[3,384,512]{2,1,0:T(8,128)(2,1)} %collective-permute-done.63.refs_12_.refs_3_.refs_1_, ...), custom_call_target="tpu_custom_call" | custom-call | flops 199999995904 | bytes 1 | tf_op jit(solution)/shard_map/pallas_call | solution.py:122
  284.9 33.5 %conditional.16 = (bf16[128,1536]{1,0:T(8,128)(2,1)}, bf16[128,1536]{1,0:T(8,128)(2,1)}, f32[256,1536]{1,0:T(8,128)}, bf16[1024,1536]{1,0:T(8,128)(2,1)}, bf16[1024,1536]{1,0:T(8,128)(2,1)}) conditional(s32[]{:T(128)} %convert_element_type.85, () %tuple.99, (bf16[1024,1536]{1,0:T(8,128)(2,1)S(1)}, bf16[1024,1536]{1,0:T(8,128)(2,1)}, s32[2]{0:T(128)}, ...), branch_computations={%region_12.13_spmd, %region_13.14_spmd} | conditional | flops 599999971328 | bytes 18874588 | solution.py:86
  284.9 5.7 %collective-permute-done.8.refs_1_ = bf16[1024,1536]{1,0:T(8,128)(2,1)S(1)} collective-permute-done((bf16[1024,1536]{1,0:T(8,128)(2,1)S(1)}, bf16[1024,1536]{1,0:T(8,128)(2,1)S(1)}, u32[]{:S(2)}, u32[]{:S(2)}) %collective-permute-start.8) | collective-permute-done | bytes 3145760 | tf_op jit(solution)/shard_map/cond/branch_1_fun/ppermute | solution.py:49
  297.2 14.7 %branch_1_fun.49 = (bf16[1024,1536]{1,0:T(8,128)(2,1)}, bf16[1024,1536]{1,0:T(8,128)(2,1)}) custom-call(s32[2]{0:T(128)S(1)} %copy-done.38, bf16[2048,640]{1,0:T(8,128)(2,1)} %get-tuple-element.389.refs_1_, bf16[2048,512]{1,0:T(8,128)(2,1)} %get-tuple-element.390.refs_2_, bf16[3,384,640]{2,1,0:T(8,128)(2,1)} %get-tuple-element.391.refs_3_, ...), custom_call_target="tpu_custom_call" | custom-call | flops 199999995904 | bytes 1 | tf_op jit(solution)/shard_map/cond/branch_1_fun/pallas_call | solution.py:122
  323.8 37.3 %conditional.17 = (f32[256,1536]{1,0:T(8,128)}, bf16[256,1536]{1,0:T(8,128)(2,1)}, f32[1,1536]{1,0:T(1,128)}, bf16[256,1536]{1,0:T(8,128)(2,1)}, bf16[256,1536]{...) conditional(s32[]{:T(128)} %convert_element_type.85, () %tuple.98, ...), branch_computations={%region_14.15_spmd, %region_15.16_spmd} | conditional | flops 599999971328 | bytes 25178480 | solution.py:86
  325.8 3.8 collective-permute-done.13.refs_1_
  329.6 4.4 branch_1_fun.51
  337.1 4.3 branch_1_fun.52
  341.6 19.4 %branch_1_fun.53 = (bf16[3,384,512]{2,1,0:T(8,128)(2,1)}, bf16[3,3,384,512]{3,2,1,0:T(8,128)(2,1)}) custom-call(s32[2]{0:T(128)S(1)} %copy-done.39, bf16[512,1536]{1,0:T(8,128)(2,1)} %get-tuple-element.417.refs_1_, bf16[256,1536]{1,0:T(8,128)(2,1)} %get-tuple-element.418.refs_2_, bf16[256,1536]{1,0:T(8,128)(2,1)} %get-tuple-element.419.refs_3_, ...), custom_call_target="tpu_custom_call" | custom-call | flops 199999995904 | bytes 1 | tf_op jit(solution)/shard_map/cond/branch_1_fun/pallas_call | solution.py:122
  363.1 3.5 collective-permute-start.67
  367.8 21.1 %conditional.18 = (bf16[256,1536]{1,0:T(8,128)(2,1)}, bf16[1024,640]{1,0:T(8,128)(2,1)}, f32[1,640]{1,0:T(1,128)}, f32[1,1536]{1,0:T(1,128)}, bf16[2,256,1536]{2...) conditional(s32[]{:T(128)} %convert_element_type.85, () %tuple.113, (bf16[256,1536]{1,0:T(8,128)(2,1)}, ...), branch_computations={%region_16.17_spmd, %region_17.18_spmd} | conditional | flops 199999995904 | bytes 5251648 | solution.py:86
  370.4 18.4 %branch_1_fun.55 = (bf16[1024,640]{1,0:T(8,128)(2,1)}, f32[1,640]{1,0:T(1,128)}, f32[1,1536]{1,0:T(1,128)}, bf16[2,256,1536]{2,1,0:T(8,128)(2,1)}, bf16[2,256,1536]{2,1,0:T(8,128)(2,1)}) custom-call(s32[2]{0:T(128)S(1)} %get-tuple-element.434.refs_0_, bf16[256,1536]{1,0:T(8,128)(2,1)} %get-tuple-element.435.refs_1_, ...), custom_call_target="tpu_custom_call" | custom-call | flops 199999995904 | bytes 1 | tf_op jit(solution)/shard_map/cond/branch_1_fun/pallas_call | solution.py:122
  388.9 4.7 collective-permute-done.67.refs_0_
  398.5 25.9 %conditional.19 = (bf16[4,192,1024]{2,1,0:T(8,128)(2,1)}, bf16[192,1024]{1,0:T(8,128)(2,1)}, bf16[192,1024]{1,0:T(8,128)(2,1)}, bf16[192,1024]{1,0:T(8,128)(2,1)...) conditional(s32[]{:T(128)} %convert_element_type.85, () %tuple.112, ...), branch_computations={%region_18.19_spmd, %region_19.20_spmd} | conditional | flops 600000167936 | bytes 9330941 | solution.py:86
  401.5 9.7 %branch_1_fun.56 = (bf16[4,192,1024]{2,1,0:T(8,128)(2,1)}, bf16[192,1024]{1,0:T(8,128)(2,1)}, bf16[192,1024]{1,0:T(8,128)(2,1)}, bf16[192,1024]{1,0:T(8,128)(2,1)}, bf16[192,1024]{1,0:T(8,128)(2,1)}) custom-call(s32[2]{0:T(128)S(1)} %get-tuple-element.464.refs_0_, bf16[256,1536]{1,0:T(8,128)(2,1)} %get-tuple-element.465.refs_1_, ...), custom_call_target="tpu_custom_call" | custom-call | flops 199999995904 | bytes 1 | tf_op jit(solution)/shard_map/cond/branch_1_fun/pallas_call | solution.py:122
  414.2 3.6 branch_1_fun.57
  417.8 3.8 branch_1_fun.58
  428.4 39.4 %conditional.20 = (bf16[192,1024]{1,0:T(8,128)(2,1)S(1)}, bf16[256,1536]{1,0:T(8,128)(2,1)}, f32[5120]{0:T(1024)S(1)}) conditional(s32[]{:T(128)} %convert_element_type.85, () %tuple.116, (bf16[192,1024]{1,0:T(8,128)(2,1)}, bf16[4,192,1024]{2,1,0:T(8,128)(2,1)}, bf16[192,1024]{1,0:T(8,128)(2,1)}, bf16[256,1536]{1,0:T(8,128)(2,1)}, ...), branch_computations={%region_20.21_spmd, %region_21.22_spmd} | conditional | flops 3554308 | bytes 20918756 | solution.py:86
  430.0 7.9 %collective-permute-done.29.refs_1_ = bf16[192,1024]{1,0:T(8,128)(2,1)S(1)} collective-permute-done((bf16[192,1024]{1,0:T(8,128)(2,1)}, bf16[192,1024]{1,0:T(8,128)(2,1)S(1)}, u32[]{:S(2)}, u32[]{:S(2)}) %collective-permute-start.29) | collective-permute-done | bytes 393248 | tf_op jit(solution)/shard_map/cond/branch_1_fun/ppermute | solution.py:49
  455.4 5.7 %collective-permute-done.36 = f32[40,128]{1,0:T(8,128)S(1)} collective-permute-done((f32[40,128]{1,0:T(8,128)}, f32[40,128]{1,0:T(8,128)S(1)}, u32[]{:S(2)}, u32[]{:S(2)}) %collective-permute-start.36) | collective-permute-done | bytes 20512 | tf_op jit(solution)/shard_map/cond/branch_1_fun/ppermute | solution.py:49
  469.1 29.7 %conditional.21 = (f32[256,1536]{1,0:T(8,128)}, f32[2,48,2,128]{3,2,1,0:T(2,128)}, bf16[256,1536]{1,0:T(8,128)(2,1)}, bf16[3,384,640]{2,1,0:T(8,128)(2,1)}, bf16[3,192,640]{2,1,0:T(8,128)(2,1)}) conditional(s32[]{:T(128)} %convert_element_type.85, () %tuple.97, (f32[1536]{0:T(1024)}, bf16[256,1536]{1,0:T(8,128)(2,1)}, f32[256,1536]{1,0:T(8,128)}, ...), branch_computations={%region_22.23_spmd, %region_23.24_spmd} | conditional | flops 200000880640 | bytes 25424488 | solution.py:86
  473.9 4.8 collective-permute-done.40.refs_2_.refs_1_
  480.5 4.1 collective-permute-start.41
  484.7 3.9 branch_1_fun.65
  488.7 6.4 %collective-permute-done.39 = bf16[48,256]{1,0:T(8,128)(2,1)S(1)} collective-permute-done((bf16[48,256]{1,0:T(8,128)(2,1)S(1)}, bf16[48,256]{1,0:T(8,128)(2,1)S(1)}, u32[]{:S(2)}, u32[]{:S(2)}) %collective-permute-start.39) | collective-permute-done | bytes 24608 | tf_op jit(solution)/shard_map/cond/branch_1_fun/ppermute | solution.py:49
  508.5 9.6 %collective-permute-done.72.refs_4_ = bf16[3,192,512]{2,1,0:T(8,128)(2,1)S(1)} collective-permute-done((bf16[3,192,512]{2,1,0:T(8,128)(2,1)S(1)}, bf16[3,192,512]{2,1,0:T(8,128)(2,1)S(1)}, u32[]{:S(2)}, u32[]{:S(2)}) %collective-permute-start.72) | collective-permute-done | bytes 589856 | tf_op jit(solution)/shard_map/ppermute | solution.py:49
  518.0 3.7 shard_map.294
  (320 shorter events, 179.7 us)
Async XLA Ops:
  10.9 13.4 %collective-permute-start.46 = (bf16[192,1024]{1,0:T(8,128)(2,1)}, bf16[192,1024]{1,0:T(8,128)(2,1)}, u32[]{:S(2)}, u32[]{:S(2)}) collective-permute-start(bf16[192,1024]{1,0:T(8,128)(2,1)} %get-tuple-element.322.refs_4_), channel_id=1, source_target_pairs={{0,8},{4,12},{8,16},{12,20},{16,24},{20,28},{24,0},{28,4},{1,9},{5... | collective-permute-start | bytes 1179656 | tf_op jit(solution)/shard_map/cond/branch_1_fun/ppermute | solution.py:49
  12.6 12.4 %collective-permute-start.49 = (bf16[192,1024]{1,0:T(8,128)(2,1)}, bf16[192,1024]{1,0:T(8,128)(2,1)S(1)}, u32[]{:S(2)}, u32[]{:S(2)}) collective-permute-start(bf16[192,1024]{1,0:T(8,128)(2,1)} %get-tuple-element.322.refs_4_), channel_id=1, source_target_pairs={{0,4},{4,0},{8,12},{12,8},{16,20},{20,16},{24,28},{28,24},{1,5},{5... | collective-permute-start | bytes 1179656 | tf_op jit(solution)/shard_map/cond/branch_1_fun/ppermute | solution.py:49
  18.9 28.0 %collective-permute-start.44 = (bf16[256,1536]{1,0:T(8,128)(2,1)}, bf16[256,1536]{1,0:T(8,128)(2,1)}, u32[]{:S(2)}, u32[]{:S(2)}) collective-permute-start(bf16[256,1536]{1,0:T(8,128)(2,1)} %branch_1_fun.38), channel_id=1, source_target_pairs={{0,2},{1,3},{2,0},{3,1},{4,6},{5,7},{6,4},{7,5},{8,10},{9,11},{10,... | collective-permute-start | bytes 2359304 | tf_op jit(solution)/shard_map/cond/branch_1_fun/ppermute | solution.py:49
  20.0 36.8 %collective-permute-start.43 = (bf16[256,1536]{1,0:T(8,128)(2,1)}, bf16[256,1536]{1,0:T(8,128)(2,1)}, u32[]{:S(2)}, u32[]{:S(2)}) collective-permute-start(bf16[256,1536]{1,0:T(8,128)(2,1)} %branch_1_fun.38), channel_id=1, source_target_pairs={{0,1},{1,0},{2,3},{3,2},{4,5},{5,4},{6,7},{7,6},{8,9},{9,8},{10,11... | collective-permute-start | bytes 2359304 | tf_op jit(solution)/shard_map/cond/branch_1_fun/ppermute | solution.py:49
  24.3 12.5 %collective-permute-start.47 = (bf16[192,1024]{1,0:T(8,128)(2,1)}, bf16[192,1024]{1,0:T(8,128)(2,1)}, u32[]{:S(2)}, u32[]{:S(2)}) collective-permute-start(bf16[192,1024]{1,0:T(8,128)(2,1)} %collective-permute-done.46), channel_id=1, source_target_pairs={{0,8},{4,12},{8,16},{12,20},{16,24},{20,28},{24,0},{28,4},{1,9},{5... | collective-permute-start | bytes 1179656 | tf_op jit(solution)/shard_map/cond/branch_1_fun/ppermute | solution.py:49
  24.9 18.7 %collective-permute-start.52 = (bf16[3,192,640]{2,1,0:T(8,128)(2,1)}, bf16[3,192,640]{2,1,0:T(8,128)(2,1)S(1)}, u32[]{:S(2)}, u32[]{:S(2)}) collective-permute-start(bf16[3,192,640]{2,1,0:T(8,128)(2,1)} %branch_1_fun.39), channel_id=1, source_target_pairs={{0,4},{4,0},{8,12},{12,8},{16,20},{20,16},{24,28},{28,24},{1,5},{5... | collective-permute-start | bytes 2211848 | tf_op jit(solution)/shard_map/cond/branch_1_fun/ppermute | solution.py:49
  36.8 18.1 %collective-permute-start.53 = (bf16[256,1536]{1,0:T(8,128)(2,1)}, bf16[256,1536]{1,0:T(8,128)(2,1)S(1)}, u32[]{:S(2)}, u32[]{:S(2)}) collective-permute-start(bf16[256,1536]{1,0:T(8,128)(2,1)} %branch_1_fun.40), channel_id=1, source_target_pairs={{0,2},{1,3},{2,0},{3,1},{4,6},{5,7},{6,4},{7,5},{8,10},{9,11},{10,... | collective-permute-start | bytes 2359304 | tf_op jit(solution)/shard_map/cond/branch_1_fun/ppermute | solution.py:49
  41.2 15.5 %collective-permute-start.50 = (bf16[192,1024]{1,0:T(8,128)(2,1)}, bf16[192,1024]{1,0:T(8,128)(2,1)}, u32[]{:S(2)}, u32[]{:S(2)}) collective-permute-start(bf16[192,1024]{1,0:T(8,128)(2,1)} %collective-permute-done.46), channel_id=1, source_target_pairs={{0,4},{4,0},{8,12},{12,8},{16,20},{20,16},{24,28},{28,24},{1,5},{5... | collective-permute-start | bytes 1179656 | tf_op jit(solution)/shard_map/cond/branch_1_fun/ppermute | solution.py:49
  43.6 13.1 %collective-permute-start.48 = (bf16[192,1024]{1,0:T(8,128)(2,1)}, bf16[192,1024]{1,0:T(8,128)(2,1)}, u32[]{:S(2)}, u32[]{:S(2)}) collective-permute-start(bf16[192,1024]{1,0:T(8,128)(2,1)} %collective-permute-done.47.refs_1_), channel_id=1, source_target_pairs={{0,8},{4,12},{8,16},{12,20},{16,24},{20,28},{24,0},{28,4},{1,9},{5... | collective-permute-start | bytes 1179656 | tf_op jit(solution)/shard_map/cond/branch_1_fun/ppermute | solution.py:49
  46.9 13.1 %collective-permute-start.51 = (bf16[192,1024]{1,0:T(8,128)(2,1)}, bf16[192,1024]{1,0:T(8,128)(2,1)}, u32[]{:S(2)}, u32[]{:S(2)}) collective-permute-start(bf16[192,1024]{1,0:T(8,128)(2,1)} %collective-permute-done.47.refs_1_), channel_id=1, source_target_pairs={{0,4},{4,0},{8,12},{12,8},{16,20},{20,16},{24,28},{28,24},{1,5},{5... | collective-permute-start | bytes 1179656 | tf_op jit(solution)/shard_map/cond/branch_1_fun/ppermute | solution.py:49
  61.5 34.5 %collective-permute-start.55 = (bf16[3,384,640]{2,1,0:T(8,128)(2,1)}, bf16[3,384,640]{2,1,0:T(8,128)(2,1)}, u32[]{:S(2)}, u32[]{:S(2)}) collective-permute-start(bf16[3,384,640]{2,1,0:T(8,128)(2,1)} %get-tuple-element.623.refs_1_.refs_11_.refs_2_), channel_id=1, source_target_pairs={{0,8},{4,12},{8,16},{12,20},{16,24},{20,28},{24,0},{28,4},{1,9},{5... | collective-permute-start | bytes 4423688 | tf_op jit(solution)/shard_map/ppermute | solution.py:49
  69.2 27.1 %collective-permute-start.57 = (bf16[64,1536]{1,0:T(8,128)(2,1)}, bf16[64,1536]{1,0:T(8,128)(2,1)}, u32[]{:S(2)}, u32[]{:S(2)}) collective-permute-start(bf16[64,1536]{1,0:T(8,128)(2,1)} %shard_map.264), channel_id=1, source_target_pairs={{0,4},{4,0},{8,12},{12,8},{16,20},{20,16},{24,28},{28,24},{1,5},{5... | collective-permute-start | bytes 589832 | tf_op jit(solution)/shard_map/ppermute | solution.py:49
  70.7 25.7 %collective-permute-start.56 = (bf16[3,192,512]{2,1,0:T(8,128)(2,1)}, bf16[3,192,512]{2,1,0:T(8,128)(2,1)}, u32[]{:S(2)}, u32[]{:S(2)}) collective-permute-start(bf16[3,192,512]{2,1,0:T(8,128)(2,1)} %shard_map.263), channel_id=1, source_target_pairs={{0,4},{4,0},{8,12},{12,8},{16,20},{20,16},{24,28},{28,24},{1,5},{5... | collective-permute-start | bytes 1769480 | tf_op jit(solution)/shard_map/ppermute | solution.py:49
  93.9 42.3 %collective-permute-start.58 = (bf16[384,1536]{1,0:T(8,128)(2,1)}, bf16[384,1536]{1,0:T(8,128)(2,1)}, u32[]{:S(2)}, u32[]{:S(2)}) collective-permute-start(bf16[384,1536]{1,0:T(8,128)(2,1)} %shard_map.266), channel_id=1, source_target_pairs={{0,4},{4,0},{8,12},{12,8},{16,20},{20,16},{24,28},{28,24},{1,5},{5... | collective-permute-start | bytes 3538952 | tf_op jit(solution)/shard_map/ppermute | solution.py:49
  95.9 38.7 %collective-permute-start.59 = (bf16[3,384,640]{2,1,0:T(8,128)(2,1)}, bf16[3,384,640]{2,1,0:T(8,128)(2,1)}, u32[]{:S(2)}, u32[]{:S(2)}) collective-permute-start(bf16[3,384,640]{2,1,0:T(8,128)(2,1)} %shard_map.262.refs_1_.refs_14_.refs_5_), channel_id=1, source_target_pairs={{0,8},{4,12},{8,16},{12,20},{16,24},{20,28},{24,0},{28,4},{1,9},{5... | collective-permute-start | bytes 4423688 | tf_op jit(solution)/shard_map/ppermute | solution.py:49
  97.5 19.2 %collective-permute-start.20 = (bf16[256,1536]{1,0:T(8,128)(2,1)}, bf16[256,1536]{1,0:T(8,128)(2,1)S(1)}, u32[]{:S(2)}, u32[]{:S(2)}) collective-permute-start(bf16[256,1536]{1,0:T(8,128)(2,1)} %get-tuple-element.365), channel_id=1, source_target_pairs={{0,2},{1,3},{2,0},{3,1},{4,6},{5,7},{6,4},{7,5},{8,10},{9,11},{10,... | collective-permute-start | bytes 2359304 | tf_op jit(solution)/shard_map/cond/branch_1_fun/ppermute | solution.py:49
  120.8 11.6 %collective-permute-start.22 = (bf16[128,1536]{1,0:T(8,128)(2,1)S(1)}, bf16[128,1536]{1,0:T(8,128)(2,1)S(1)}, u32[]{:S(2)}, u32[]{:S(2)}) collective-permute-start(bf16[128,1536]{1,0:T(8,128)(2,1)S(1)} %get-tuple-element.369.refs_2_), channel_id=1, source_target_pairs={{0,2},{1,3},{2,0},{3,1},{4,6},{5,7},{6,4},{7,5},{8,10},{9,11},{10,... | collective-permute-start | bytes 1179656 | tf_op jit(solution)/shard_map/cond/branch_1_fun/ppermute | solution.py:49
  134.7 33.8 %collective-permute-start.60 = (bf16[3,384,640]{2,1,0:T(8,128)(2,1)}, bf16[3,384,640]{2,1,0:T(8,128)(2,1)}, u32[]{:S(2)}, u32[]{:S(2)}) collective-permute-start(bf16[3,384,640]{2,1,0:T(8,128)(2,1)} %shard_map.267.refs_2_.refs_13_.refs_4_), channel_id=1, source_target_pairs={{0,8},{4,12},{8,16},{12,20},{16,24},{20,28},{24,0},{28,4},{1,9},{5... | collective-permute-start | bytes 4423688 | tf_op jit(solution)/shard_map/ppermute | solution.py:49
  138.9 21.2 %collective-permute-start.2 = (bf16[512,1536]{1,0:T(8,128)(2,1)}, bf16[512,1536]{1,0:T(8,128)(2,1)}, u32[]{:S(2)}, u32[]{:S(2)}) collective-permute-start(bf16[512,1536]{1,0:T(8,128)(2,1)} %branch_1_fun.47), channel_id=1, source_target_pairs={{0,1},{1,0},{2,3},{3,2},{4,5},{5,4},{6,7},{7,6},{8,9},{9,8},{10,11... | collective-permute-start | bytes 4718600 | tf_op jit(solution)/shard_map/cond/branch_1_fun/ppermute | solution.py:49
  138.9 20.3 %collective-permute-start.3 = (bf16[256,1536]{1,0:T(8,128)(2,1)}, bf16[256,1536]{1,0:T(8,128)(2,1)}, u32[]{:S(2)}, u32[]{:S(2)}) collective-permute-start(bf16[256,1536]{1,0:T(8,128)(2,1)} %get-tuple-element.380), channel_id=1, source_target_pairs={{0,2},{1,3},{2,0},{3,1},{4,6},{5,7},{6,4},{7,5},{8,10},{9,11},{10,... | collective-permute-start | bytes 2359304 | tf_op jit(solution)/shard_map/cond/branch_1_fun/ppermute | solution.py:49
  140.0 20.0 %collective-permute-start.4 = (bf16[256,1536]{1,0:T(8,128)(2,1)}, bf16[256,1536]{1,0:T(8,128)(2,1)}, u32[]{:S(2)}, u32[]{:S(2)}) collective-permute-start(bf16[256,1536]{1,0:T(8,128)(2,1)} %get-tuple-element.381), channel_id=1, source_target_pairs={{0,4},{4,0},{8,12},{12,8},{16,20},{20,16},{24,28},{28,24},{1,5},{5... | collective-permute-start | bytes 2359304 | tf_op jit(solution)/shard_map/cond/branch_1_fun/ppermute | solution.py:49
  141.4 21.5 %collective-permute-start.5 = (bf16[512,1536]{1,0:T(8,128)(2,1)}, bf16[512,1536]{1,0:T(8,128)(2,1)}, u32[]{:S(2)}, u32[]{:S(2)}) collective-permute-start(bf16[512,1536]{1,0:T(8,128)(2,1)} %get-tuple-element.382), channel_id=1, source_target_pairs={{0,1},{1,0},{2,3},{3,2},{4,5},{5,4},{6,7},{7,6},{8,9},{9,8},{10,11... | collective-permute-start | bytes 4718600 | tf_op jit(solution)/shard_map/cond/branch_1_fun/ppermute | solution.py:49
  168.4 27.0 %collective-permute-start.61 = (bf16[3,384,512]{2,1,0:T(8,128)(2,1)}, bf16[3,384,512]{2,1,0:T(8,128)(2,1)}, u32[]{:S(2)}, u32[]{:S(2)}) collective-permute-start(bf16[3,384,512]{2,1,0:T(8,128)(2,1)} %shard_map.269.refs_11_.refs_2_), channel_id=1, source_target_pairs={{0,8},{4,12},{8,16},{12,20},{16,24},{20,28},{24,0},{28,4},{1,9},{5... | collective-permute-start | bytes 3538952 | tf_op jit(solution)/shard_map/ppermute | solution.py:49
  195.5 26.1 %collective-permute-start.62 = (bf16[3,384,512]{2,1,0:T(8,128)(2,1)}, bf16[3,384,512]{2,1,0:T(8,128)(2,1)}, u32[]{:S(2)}, u32[]{:S(2)}) collective-permute-start(bf16[3,384,512]{2,1,0:T(8,128)(2,1)} %shard_map.271.refs_14_.refs_5_), channel_id=1, source_target_pairs={{0,8},{4,12},{8,16},{12,20},{16,24},{20,28},{24,0},{28,4},{1,9},{5... | collective-permute-start | bytes 3538952 | tf_op jit(solution)/shard_map/ppermute | solution.py:49
  221.6 25.9 %collective-permute-start.63 = (bf16[3,384,512]{2,1,0:T(8,128)(2,1)}, bf16[3,384,512]{2,1,0:T(8,128)(2,1)}, u32[]{:S(2)}, u32[]{:S(2)}) collective-permute-start(bf16[3,384,512]{2,1,0:T(8,128)(2,1)} %shard_map.273.refs_13_.refs_4_), channel_id=1, source_target_pairs={{0,8},{4,12},{8,16},{12,20},{16,24},{20,28},{24,0},{28,4},{1,9},{5... | collective-permute-start | bytes 3538952 | tf_op jit(solution)/shard_map/ppermute | solution.py:49
  247.5 34.3 %collective-permute-start.64 = (bf16[3,384,640]{2,1,0:T(8,128)(2,1)}, bf16[3,384,640]{2,1,0:T(8,128)(2,1)}, u32[]{:S(2)}, u32[]{:S(2)}) collective-permute-start(bf16[3,384,640]{2,1,0:T(8,128)(2,1)} %shard_map.277), channel_id=1, source_target_pairs={{0,8},{4,12},{8,16},{12,20},{16,24},{20,28},{24,0},{28,4},{1,9},{5... | collective-permute-start | bytes 4423688 | tf_op jit(solution)/shard_map/ppermute | solution.py:49
  284.8 33.7 %collective-permute-start.65 = (bf16[3,384,640]{2,1,0:T(8,128)(2,1)}, bf16[3,384,640]{2,1,0:T(8,128)(2,1)}, u32[]{:S(2)}, u32[]{:S(2)}) collective-permute-start(bf16[3,384,640]{2,1,0:T(8,128)(2,1)} %bitcast_add_fusion.3.refs_1_), channel_id=1, source_target_pairs={{0,8},{4,12},{8,16},{12,20},{16,24},{20,28},{24,0},{28,4},{1,9},{5... | collective-permute-start | bytes 4423688 | tf_op jit(solution)/shard_map/ppermute | solution.py:49
  294.0 20.1 %collective-permute-start.9 = (bf16[256,1536]{1,0:T(8,128)(2,1)}, bf16[256,1536]{1,0:T(8,128)(2,1)}, u32[]{:S(2)}, u32[]{:S(2)}) collective-permute-start(bf16[256,1536]{1,0:T(8,128)(2,1)} %get-tuple-element.386.refs_11_), channel_id=1, source_target_pairs={{0,2},{1,3},{2,0},{3,1},{4,6},{5,7},{6,4},{7,5},{8,10},{9,11},{10,... | collective-permute-start | bytes 2359304 | tf_op jit(solution)/shard_map/cond/branch_1_fun/ppermute | solution.py:49
  295.9 19.6 %collective-permute-start.10 = (bf16[256,1536]{1,0:T(8,128)(2,1)}, bf16[256,1536]{1,0:T(8,128)(2,1)}, u32[]{:S(2)}, u32[]{:S(2)}) collective-permute-start(bf16[256,1536]{1,0:T(8,128)(2,1)} %get-tuple-element.387), channel_id=1, source_target_pairs={{0,4},{4,0},{8,12},{12,8},{16,20},{20,16},{24,28},{28,24},{1,5},{5... | collective-permute-start | bytes 2359304 | tf_op jit(solution)/shard_map/cond/branch_1_fun/ppermute | solution.py:49
  321.6 45.1 %collective-permute-start.66 = (bf16[3,384,640]{2,1,0:T(8,128)(2,1)}, bf16[3,384,640]{2,1,0:T(8,128)(2,1)}, u32[]{:S(2)}, u32[]{:S(2)}) collective-permute-start(bf16[3,384,640]{2,1,0:T(8,128)(2,1)} %bitcast_add_fusion.2.refs_1_), channel_id=1, source_target_pairs={{0,8},{4,12},{8,16},{12,20},{16,24},{20,28},{24,0},{28,4},{1,9},{5... | collective-permute-start | bytes 4423688 | tf_op jit(solution)/shard_map/ppermute | solution.py:49
  323.8 11.8 %collective-permute-start.11 = (bf16[128,1536]{1,0:T(8,128)(2,1)}, bf16[128,1536]{1,0:T(8,128)(2,1)}, u32[]{:S(2)}, u32[]{:S(2)}) collective-permute-start(bf16[128,1536]{1,0:T(8,128)(2,1)} %get-tuple-element.408), channel_id=1, source_target_pairs={{0,4},{4,0},{8,12},{12,8},{16,20},{20,16},{24,28},{28,24},{1,5},{5... | collective-permute-start | bytes 1179656 | tf_op jit(solution)/shard_map/cond/branch_1_fun/ppermute | solution.py:49
  325.5 11.6 %collective-permute-start.12 = (bf16[128,1536]{1,0:T(8,128)(2,1)}, bf16[128,1536]{1,0:T(8,128)(2,1)}, u32[]{:S(2)}, u32[]{:S(2)}) collective-permute-start(bf16[128,1536]{1,0:T(8,128)(2,1)} %get-tuple-element.409), channel_id=1, source_target_pairs={{0,2},{1,3},{2,0},{3,1},{4,6},{5,7},{6,4},{7,5},{8,10},{9,11},{10,... | collective-permute-start | bytes 1179656 | tf_op jit(solution)/shard_map/cond/branch_1_fun/ppermute | solution.py:49
  341.3 19.7 %collective-permute-start.14 = (bf16[256,1536]{1,0:T(8,128)(2,1)}, bf16[256,1536]{1,0:T(8,128)(2,1)}, u32[]{:S(2)}, u32[]{:S(2)}) collective-permute-start(bf16[256,1536]{1,0:T(8,128)(2,1)} %get-tuple-element.847.refs_13_), channel_id=1, source_target_pairs={{0,2},{1,3},{2,0},{3,1},{4,6},{5,7},{6,4},{7,5},{8,10},{9,11},{10,... | collective-permute-start | bytes 2359304 | tf_op jit(solution)/shard_map/cond/branch_1_fun/ppermute | solution.py:49
  341.6 19.4 %collective-permute-start.15 = (bf16[256,1536]{1,0:T(8,128)(2,1)}, bf16[256,1536]{1,0:T(8,128)(2,1)}, u32[]{:S(2)}, u32[]{:S(2)}) collective-permute-start(bf16[256,1536]{1,0:T(8,128)(2,1)} %get-tuple-element.847.refs_13_), channel_id=1, source_target_pairs={{0,1},{1,0},{2,3},{3,2},{4,5},{5,4},{6,7},{7,6},{8,9},{9,8},{10,11... | collective-permute-start | bytes 2359304 | tf_op jit(solution)/shard_map/cond/branch_1_fun/ppermute | solution.py:49
  361.0 36.8 %collective-permute-start.69 = (bf16[256,1536]{1,0:T(8,128)(2,1)}, bf16[256,1536]{1,0:T(8,128)(2,1)}, u32[]{:S(2)}, u32[]{:S(2)}) collective-permute-start(bf16[256,1536]{1,0:T(8,128)(2,1)} %get-tuple-element.687), channel_id=1, source_target_pairs={{0,4},{4,0},{8,12},{12,8},{16,20},{20,16},{24,28},{28,24},{1,5},{5... | collective-permute-start | bytes 2359304 | tf_op jit(solution)/shard_map/ppermute | solution.py:49
  361.6 36.2 %collective-permute-start.68 = (bf16[256,1536]{1,0:T(8,128)(2,1)}, bf16[256,1536]{1,0:T(8,128)(2,1)}, u32[]{:S(2)}, u32[]{:S(2)}) collective-permute-start(bf16[256,1536]{1,0:T(8,128)(2,1)} %get-tuple-element.686), channel_id=1, source_target_pairs={{0,2},{1,3},{2,0},{3,1},{4,6},{5,7},{6,4},{7,5},{8,10},{9,11},{10,... | collective-permute-start | bytes 2359304 | tf_op jit(solution)/shard_map/ppermute | solution.py:49
  363.1 30.4 %collective-permute-start.67 = (bf16[3,384,512]{2,1,0:T(8,128)(2,1)}, bf16[3,384,512]{2,1,0:T(8,128)(2,1)}, u32[]{:S(2)}, u32[]{:S(2)}) collective-permute-start(bf16[3,384,512]{2,1,0:T(8,128)(2,1)} %shard_map.283), channel_id=1, source_target_pairs={{0,8},{4,12},{8,16},{12,20},{16,24},{20,28},{24,0},{28,4},{1,9},{5... | collective-permute-start | bytes 3538952 | tf_op jit(solution)/shard_map/ppermute | solution.py:49
  396.3 29.3 %collective-permute-start.70 = (bf16[3,384,512]{2,1,0:T(8,128)(2,1)}, bf16[3,384,512]{2,1,0:T(8,128)(2,1)}, u32[]{:S(2)}, u32[]{:S(2)}) collective-permute-start(bf16[3,384,512]{2,1,0:T(8,128)(2,1)} %bitcast_add_fusion.6.refs_1_), channel_id=1, source_target_pairs={{0,8},{4,12},{8,16},{12,20},{16,24},{20,28},{24,0},{28,4},{1,9},{5... | collective-permute-start | bytes 3538952 | tf_op jit(solution)/shard_map/ppermute | solution.py:49
  399.3 14.9 %collective-permute-start.25 = (bf16[2,256,1536]{2,1,0:T(8,128)(2,1)}, bf16[2,256,1536]{2,1,0:T(8,128)(2,1)}, u32[]{:S(2)}, u32[]{:S(2)}) collective-permute-start(bf16[2,256,1536]{2,1,0:T(8,128)(2,1)} %get-tuple-element.475.refs_11_), channel_id=1, source_target_pairs={{0,1},{1,0},{2,3},{3,2},{4,5},{5,4},{6,7},{7,6},{8,9},{9,8},{10,11... | collective-permute-start | bytes 4718600 | tf_op jit(solution)/shard_map/cond/branch_1_fun/ppermute | solution.py:49
  401.1 11.7 %collective-permute-start.27 = (f32[40,128]{1,0:T(8,128)}, f32[40,128]{1,0:T(8,128)}, u32[]{:S(2)}, u32[]{:S(2)}) collective-permute-start(f32[40,128]{1,0:T(8,128)} %add.92), channel_id=1, source_target_pairs={{0,2},{1,3},{2,0},{3,1},{4,6},{5,7},{6,4},{7,5},{8,10},{9,11},{10,... | collective-permute-start | bytes 61448 | tf_op jit(solution)/shard_map/cond/branch_1_fun/ppermute | solution.py:49
  411.2 11.3 %collective-permute-start.24 = (bf16[192,1024]{1,0:T(8,128)(2,1)}, bf16[192,1024]{1,0:T(8,128)(2,1)}, u32[]{:S(2)}, u32[]{:S(2)}) collective-permute-start(bf16[192,1024]{1,0:T(8,128)(2,1)} %get-tuple-element.480), channel_id=1, source_target_pairs={{0,4},{4,0},{8,12},{12,8},{16,20},{20,16},{24,28},{28,24},{1,5},{5... | collective-permute-start | bytes 1179656 | tf_op jit(solution)/shard_map/cond/branch_1_fun/ppermute | solution.py:49
  442.3 25.5 %collective-permute-start.35 = (bf16[256,1536]{1,0:T(8,128)(2,1)}, bf16[256,1536]{1,0:T(8,128)(2,1)}, u32[]{:S(2)}, u32[]{:S(2)}) collective-permute-start(bf16[256,1536]{1,0:T(8,128)(2,1)} %get-tuple-element.496.refs_1_), channel_id=1, source_target_pairs={{0,2},{1,3},{2,0},{3,1},{4,6},{5,7},{6,4},{7,5},{8,10},{9,11},{10,... | collective-permute-start | bytes 2359304 | tf_op jit(solution)/shard_map/cond/branch_1_fun/ppermute | solution.py:49
  453.3 13.2 %collective-permute-start.32 = (bf16[192,1024]{1,0:T(8,128)(2,1)S(1)}, bf16[192,1024]{1,0:T(8,128)(2,1)S(1)}, u32[]{:S(2)}, u32[]{:S(2)}) collective-permute-start(bf16[192,1024]{1,0:T(8,128)(2,1)S(1)} %fusion.3), channel_id=1, source_target_pairs={{0,8},{4,12},{8,16},{12,20},{16,24},{20,28},{24,0},{28,4},{1,9},{5... | collective-permute-start | bytes 1179656 | tf_op jit(solution)/shard_map/cond/branch_1_fun/ppermute | solution.py:49
  454.8 11.8 %collective-permute-start.34 = (bf16[192,1024]{1,0:T(8,128)(2,1)}, bf16[192,1024]{1,0:T(8,128)(2,1)S(1)}, u32[]{:S(2)}, u32[]{:S(2)}) collective-permute-start(bf16[192,1024]{1,0:T(8,128)(2,1)} %branch_1_fun.64), channel_id=1, source_target_pairs={{0,4},{4,0},{8,12},{12,8},{16,20},{20,16},{24,28},{28,24},{1,5},{5... | collective-permute-start | bytes 1179656 | tf_op jit(solution)/shard_map/cond/branch_1_fun/ppermute | solution.py:49
  467.8 32.7 %collective-permute-start.71 = (bf16[3,384,512]{2,1,0:T(8,128)(2,1)}, bf16[3,384,512]{2,1,0:T(8,128)(2,1)}, u32[]{:S(2)}, u32[]{:S(2)}) collective-permute-start(bf16[3,384,512]{2,1,0:T(8,128)(2,1)} %shard_map.290.refs_1_), channel_id=1, source_target_pairs={{0,8},{4,12},{8,16},{12,20},{16,24},{20,28},{24,0},{28,4},{1,9},{5... | collective-permute-start | bytes 3538952 | tf_op jit(solution)/shard_map/ppermute | solution.py:49
  478.6 20.2 %collective-permute-start.42 = (bf16[3,192,640]{2,1,0:T(8,128)(2,1)}, bf16[3,192,640]{2,1,0:T(8,128)(2,1)}, u32[]{:S(2)}, u32[]{:S(2)}) collective-permute-start(bf16[3,192,640]{2,1,0:T(8,128)(2,1)} %branch_1_fun.69), channel_id=1, source_target_pairs={{0,4},{4,0},{8,12},{12,8},{16,20},{20,16},{24,28},{28,24},{1,5},{5... | collective-permute-start | bytes 2211848 | tf_op jit(solution)/shard_map/cond/branch_1_fun/ppermute | solution.py:49
  480.5 15.3 %collective-permute-start.41 = (bf16[128,1536]{1,0:T(8,128)(2,1)}, bf16[128,1536]{1,0:T(8,128)(2,1)S(1)}, u32[]{:S(2)}, u32[]{:S(2)}) collective-permute-start(bf16[128,1536]{1,0:T(8,128)(2,1)} %get-tuple-element.511), channel_id=1, source_target_pairs={{0,2},{1,3},{2,0},{3,1},{4,6},{5,7},{6,4},{7,5},{8,10},{9,11},{10,... | collective-permute-start | bytes 1179656 | tf_op jit(solution)/shard_map/cond/branch_1_fun/ppermute | solution.py:49
  502.9 15.1 %collective-permute-start.72 = (bf16[3,192,512]{2,1,0:T(8,128)(2,1)S(1)}, bf16[3,192,512]{2,1,0:T(8,128)(2,1)S(1)}, u32[]{:S(2)}, u32[]{:S(2)}) collective-permute-start(bf16[3,192,512]{2,1,0:T(8,128)(2,1)S(1)} %shard_map.293), channel_id=1, source_target_pairs={{0,4},{4,0},{8,12},{12,8},{16,20},{20,16},{24,28},{28,24},{1,5},{5... | collective-permute-start | bytes 1769480 | tf_op jit(solution)/shard_map/ppermute | solution.py:49
  (68 other events, 478.1 us)
